TPU v7x, 32 devices: a whole 2x2x4 slice. The times are simulated.
32 devices in a mesh: grp: 8 (over y, x, core), seq: 4 (over z).
Axes of the slice: x: 2, y: 2, z: 4, core: 2. Of those that a mesh axis runs over, the one named last changes fastest.
Arguments:
- q_space: bfloat16 [32, 256, 576], P(('grp', 'seq')), may hold values from -96 to 96
- k_space: bfloat16 [32, 256, 576], P(('grp', 'seq')), may hold values from -96 to 96
- v_space: bfloat16 [32, 256, 576], P(('grp', 'seq')), may hold values from -6 to 6
- cot_space: bfloat16 [32, 256, 576], P(('grp', 'seq')), may hold values from -6 to 6
- q_time: bfloat16 [32, 256, 576], P(('grp', 'seq')), may hold values from -96 to 96
- k_time: bfloat16 [32, 256, 576], P(('grp', 'seq')), may hold values from -96 to 96
- v_time: bfloat16 [32, 256, 576], P(('grp', 'seq')), may hold values from -6 to 6
- cot_time: bfloat16 [32, 256, 576], P(('grp', 'seq')), may hold values from -6 to 6
- clip_len: int32 [16], replicated, may hold values from 1 to 4, 32 in all
Outputs:
- grad_q_space: bfloat16 [32, 256, 576], P(('grp', 'seq'))
- grad_k_space: bfloat16 [32, 256, 576], P(('grp', 'seq'))
- grad_v_space: bfloat16 [32, 256, 576], P(('grp', 'seq'))
- grad_q_time: bfloat16 [32, 256, 576], P(('grp', 'seq'))
- grad_k_time: bfloat16 [32, 256, 576], P(('grp', 'seq'))
- grad_v_time: bfloat16 [32, 256, 576], P(('grp', 'seq'))
Inputs may be any that keep to these rules, and one draw needn't show every extreme that they name: `clip_len`: the 16 frame counts sum to 32; some clip has exactly 4 frames.
All inputs are finite; a program needn't handle non-finite values.
Results may differ from a plain program's by a relative error of at most 0.013.
Values may be sent and summed in bfloat16 or wider, within the bound.
No kernel may reach another device: no remote copies, remote signals or barrier semaphores. Data moves between devices by JAX's collectives and lax.ppermute only.
A program may use at most 64 MiB of HBM per device.

v0:
```python
import functools
import math

import jax
import jax.numpy as jnp
from jax import lax
from jax.experimental import pallas as pl
from jax.experimental.pallas import tpu as pltpu
from jax.sharding import PartitionSpec as P

HEADS = 8
HDIM = 72
WIDTH = HEADS * HDIM
LANES = 128
SCALING = 1.0 / math.sqrt(HDIM)
CHUNKS = (4, 4)
masked_score = -1e30


def dot(left, right, left_dim, right_dim):
    dims = (((left_dim,), (right_dim,)), ((), ()))
    return lax.dot_general(left, right, dims, preferred_element_type=jnp.float32)


def rounded(value):
    return value.astype(jnp.bfloat16).astype(jnp.float32)


def frame_kernel(q_ref, k_ref, v_ref, g_ref, dq_ref, dk_ref, dv_ref):
    pair = 2 * HDIM
    reach = -(-HDIM // 16) * 16
    row = lax.broadcasted_iota(jnp.int32, (reach, 1), 0)
    for begin in range(0, WIDTH, pair):
        found = [[], [], []]
        for low, own in ((0, 0), (pair - reach, reach - HDIM)):
            span = slice(begin + low, begin + low + reach)
            mask = ((row >= own) & (row < own + HDIM)).astype(jnp.float32).astype(jnp.bfloat16)
            queries, keys = q_ref[0, span, :], k_ref[0, span, :]
            cotangent = g_ref[0, span, :]
            scores = dot(keys * mask, queries, 0, 0) * SCALING
            weight_grad = dot(v_ref[0, span, :] * mask, cotangent, 0, 0)
            raised = jnp.exp(scores - jnp.max(scores, axis=0, keepdims=True))
            weights = raised * (1.0 / jnp.sum(raised, axis=0, keepdims=True))
            weights_low = weights.astype(jnp.bfloat16)
            dots = jnp.sum(weights_low.astype(jnp.float32) * weight_grad, axis=0, keepdims=True)
            score_grad = (weights * (weight_grad - dots)).astype(jnp.bfloat16)
            rows = slice(own, own + HDIM)
            found[0].append(dot(keys, score_grad, 1, 0)[rows] * SCALING)
            found[1].append(dot(queries, score_grad, 1, 1)[rows] * SCALING)
            found[2].append(dot(cotangent, weights_low, 1, 1)[rows])
        for out, parts in zip((dq_ref, dk_ref, dv_ref), found):
            out[0, begin : begin + pair, :] = jnp.concatenate(parts, axis=0).astype(jnp.bfloat16)


def space_grads(queries, keys, values, cotangent):
    tokens = queries.shape[2]
    shape = jax.ShapeDtypeStruct(queries.shape, jnp.bfloat16)
    return pl.pallas_call(
        frame_kernel,
        out_shape=(shape, shape, shape),
        compiler_params=pltpu.CompilerParams(vmem_limit_bytes=60 * 2**20),
        cost_estimate=pl.CostEstimate(
            flops=12 * tokens * tokens * 256 * HEADS,
            bytes_accessed=14 * tokens * WIDTH,
            transcendentals=tokens * tokens * HEADS,
        ),
        name="space",
    )(queries, keys, values, cotangent)


def part_of(device, sharing, rows):
    row = pl.multiple_of(device % sharing * rows, 16)
    return row, pl.ds(pl.multiple_of(device // sharing * LANES, LANES), LANES)


def split_kernel(sharing, rows, span, *refs):
    ins, outs, sent = refs[:4], refs[4:-1], refs[-1]
    copies = []
    for step in far_first(len(outs)):
        row, tokens = part_of(lax.axis_index("seq") ^ step, sharing, rows)
        for i, array in enumerate(ins):
            given = array.at[0, pl.ds(span.start + row, rows), tokens]
            copies.append(pltpu.make_async_copy(given, outs[step].at[i], sent.at[step, i]))
            copies[-1].start()
    for copy in copies:
        copy.wait()


def split(arrays, span, n, sharing):
    rows = (span.stop - span.start) // sharing
    hbm = pl.BlockSpec(memory_space=pltpu.HBM)
    return pl.pallas_call(
        functools.partial(split_kernel, sharing, rows, span),
        in_specs=[hbm] * 4,
        out_specs=[hbm] * n,
        out_shape=[jax.ShapeDtypeStruct((4, rows, LANES), jnp.bfloat16)] * n,
        scratch_shapes=[pltpu.SemaphoreType.DMA((n, 4))],
        compiler_params=pltpu.CompilerParams(vmem_limit_bytes=60 * 2**20),
        name="pack",
    )(*arrays)


def far_first(n):
    return [*range(n // 2, n), *range(n // 2)]


def swap(block, axis, pairs):
    return lax.ppermute(block, axis, [(i, j) for i, j in pairs] + [(j, i) for i, j in pairs])


def exchange(blocks):
    n = len(blocks)
    moved = list(blocks)
    for step in reversed(range(1, n)):
        pairs = [[i, i ^ step] for i in range(n) if i < i ^ step]
        moved[step] = swap(blocks[step], "seq", pairs)
    return moved


def sides_kernel(n, *refs):
    ins, outs = refs[:n], refs[n:]
    is_odd = lax.axis_index("grp") & 1
    for step, ref in enumerate(ins):
        frame = lax.axis_index("seq") ^ step
        for start, out in zip((1, 0), outs):
            at = frame - jnp.where(is_odd == start, 1, 0)

            @pl.when((at >= 0) & (at < n - 1))
            def _():
                out[jnp.clip(at, 0, n - 2)] = ref[...]


def sides(blocks):
    n = len(blocks)
    shape = jax.ShapeDtypeStruct((n - 1, *blocks[0].shape), jnp.bfloat16)
    vmem = pl.BlockSpec(memory_space=pltpu.VMEM)
    return pl.pallas_call(
        functools.partial(sides_kernel, n),
        in_specs=[vmem] * n,
        out_specs=[vmem] * 2,
        out_shape=[shape] * 2,
        compiler_params=pltpu.CompilerParams(vmem_limit_bytes=24 * 2**20),
        name="sides",
    )(*blocks)


def gated(values, *earlier):
    return lax.optimization_barrier((values, *earlier))


def neighbours(block, start):
    count = lax.axis_size("grp")
    return swap(block, "grp", [(i, i + 1) for i in range(start, count - 1, 2)])


def join_kernel(sharing, span, *refs):
    outs, sent = refs[-4:-1], refs[-1]
    rows = refs[0].shape[1]
    n = sent.shape[0]
    copies = []
    for at, step in enumerate(far_first(n)):
        row, tokens = part_of(lax.axis_index("seq") ^ step, sharing, rows)
        for i, out in enumerate(outs):
            given = out.at[0, pl.ds(span.start + row, rows), tokens]
            copies.append(pltpu.make_async_copy(refs[at].at[i], given, sent.at[step, i]))
            copies[-1].start()
    for copy in copies:
        copy.wait()


def join(blocks, span, tokens, sharing, earlier):
    n = len(blocks)
    shape = jax.ShapeDtypeStruct((1, WIDTH, tokens), jnp.bfloat16)
    hbm = pl.BlockSpec(memory_space=pltpu.HBM)
    earlier = [] if earlier is None else list(earlier)
    return pl.pallas_call(
        functools.partial(join_kernel, sharing, span),
        in_specs=[pl.BlockSpec(memory_space=pltpu.VMEM)] * n + [hbm] * len(earlier),
        out_specs=[hbm] * 3,
        out_shape=[shape] * 3,
        scratch_shapes=[pltpu.SemaphoreType.DMA((n, 3))],
        input_output_aliases={n + i: i for i in range(len(earlier))},
        compiler_params=pltpu.CompilerParams(vmem_limit_bytes=24 * 2**20),
        name="unpack",
    )(*(blocks[step] for step in far_first(n)), *earlier)


def clip_kernel(window, heads, given_bounds, *refs):
    own, sides_of = refs[:window], refs[window : window + 2]
    outs, refs = refs[window + 2 : 2 * window + 2], refs[2 * window + 2 :]
    wide, score_ref, grad_ref, weight_ref, found, bounds, arrived = refs
    copy = pltpu.make_async_copy(given_bounds, bounds, arrived)
    copy.start()
    halo = window - 1
    extent = window + 2 * halo
    queries, keys, values, cotangent = range(4)

    def widen(ref, frame):
        for i in range(4):
            wide[i, frame] = ref[i].astype(jnp.float32)

    for step, ref in enumerate(own):
        widen(ref, halo + (lax.axis_index("seq") ^ step))
    copy.wait()
    lowest, highest = bounds[0, halo], bounds[1, halo + window - 1]
    for start, ref in zip((1, 0), sides_of):
        is_next = (lax.axis_index("grp") & 1) == start
        for at in range(halo):
            frame = at + jnp.where(is_next, halo + window, 0)
            needed = (frame >= lowest) & (frame < highest)
            pl.when(needed)(functools.partial(widen, ref.at[at], frame))

    def partners(frame):
        first, last = bounds[0, frame], bounds[1, frame]
        return first, last - first, [jnp.minimum(first + t, last - 1) for t in range(window)]

    def products(frame, carry):
        first, count, others = partners(frame)
        scores, grads = [[] for _ in others], [[] for _ in others]
        for head in range(heads):
            span = slice(head * HDIM, (head + 1) * HDIM)
            query, cot = wide[queries, frame, span, :], wide[cotangent, frame, span, :]
            for t, other in enumerate(others):
                score = jnp.sum(query * wide[keys, other, span, :], axis=0, keepdims=True)
                grad = jnp.sum(cot * wide[values, other, span, :], axis=0, keepdims=True)
                scores[t].append(score)
                grads[t].append(grad)
        for t in range(window):
            bias = jnp.where(t < count, 0.0, masked_score)
            score_ref[t, frame] = jnp.concatenate(scores[t], axis=0) * SCALING + bias
            grad_ref[t, frame] = jnp.concatenate(grads[t], axis=0)
        return carry

    lax.fori_loop(lowest, highest, products, 0)
    scores, grads = [score_ref[t] for t in range(window)], [grad_ref[t] for t in range(window)]
    peak = functools.reduce(jnp.maximum, scores)
    raised = [jnp.exp(score - peak) for score in scores]
    inverse = 1.0 / functools.reduce(jnp.add, raised)
    weights = [part * inverse for part in raised]
    weights_low = [rounded(part) for part in weights]
    dots = functools.reduce(jnp.add, [w * d for w, d in zip(weights_low, grads)])
    for t in range(window):
        weight_ref[t] = weights_low[t]
        score_ref[t] = rounded(weights[t] * (grads[t] - dots))

    def gradients(at, carry):
        frame = halo + at
        first, count, others = partners(frame)
        place = frame - first
        sums = [[], [], []]
        for head in range(heads):
            span, row = slice(head * HDIM, (head + 1) * HDIM), slice(head, head + 1)
            totals = [None] * 3
            for t, other in enumerate(others):
                score_back = jnp.where(t < count, score_ref[place, other, row, :], 0.0)
                weight_back = jnp.where(t < count, weight_ref[place, other, row, :], 0.0)
                terms = (
                    score_ref[t, frame, row, :] * wide[keys, other, span, :],
                    score_back * wide[queries, other, span, :],
                    weight_back * wide[cotangent, other, span, :],
                )
                totals = [x if y is None else y + x for x, y in zip(terms, totals)]
            for held, total, scale in zip(sums, totals, (SCALING, SCALING, None)):
                held.append(total if scale is None else total * scale)
        for i, parts in enumerate(sums):
            found[at, i] = jnp.concatenate(parts, axis=0).astype(jnp.bfloat16)
        return carry

    lax.fori_loop(0, window, gradients, 0)
    for step, out in enumerate(outs):
        out[...] = found[lax.axis_index("seq") ^ step]


def clip_grads(bounds, own, beside):
    window = len(own)
    _, rows, lanes = own[0].shape
    heads = rows // HDIM
    extent = 3 * window - 2
    vmem = pl.BlockSpec(memory_space=pltpu.VMEM)
    shape = (3, rows, lanes)
    slots = pltpu.VMEM((window, extent, heads, lanes), jnp.float32)
    return pl.pallas_call(
        functools.partial(clip_kernel, window, heads),
        out_shape=[jax.ShapeDtypeStruct(shape, jnp.bfloat16)] * window,
        in_specs=[pl.BlockSpec(memory_space=pl.ANY)] + [vmem] * (window + 2),
        out_specs=[vmem] * window,
        scratch_shapes=[
            pltpu.VMEM((4, extent, rows, lanes), jnp.float32),
            slots,
            slots,
            slots,
            pltpu.VMEM((window, *shape), jnp.bfloat16),
            pltpu.SMEM(bounds.shape, jnp.int32),
            pltpu.SemaphoreType.DMA,
        ],
        compiler_params=pltpu.CompilerParams(vmem_limit_bytes=48 * 2**20),
        cost_estimate=pl.CostEstimate(
            flops=800 * extent * window * rows * lanes,
            bytes_accessed=2 * sum(block.size for block in (*own, *beside)),
            transcendentals=extent * window * heads * lanes,
        ),
        name="clips",
    )(bounds, *own, *beside)


def clip_bounds(clip_len, window):
    halo = window - 1
    extent = window + 2 * halo
    start = lax.axis_index("grp") * window - halo
    frames = start + jnp.arange(extent, dtype=jnp.int32)
    order = jnp.arange(clip_len.shape[0])
    ends = jnp.sum(jnp.where(order[:, None] <= order[None, :], clip_len[:, None], 0), axis=0)
    begins = ends - clip_len
    holds = (begins[None, :] <= frames[:, None]) & (frames[:, None] < ends[None, :])
    first = jnp.sum(jnp.where(holds, begins[None, :], 0), axis=1) - start
    last = jnp.sum(jnp.where(holds, ends[None, :], 0), axis=1) - start
    return jnp.stack([first, last]).astype(jnp.int32)


def tile_shards(q_space, k_space, v_space, cot_space, q_time, k_time, v_time, cot_time, clip_len):
    def turned(*arrays):
        return tuple(array.transpose(0, 2, 1) for array in arrays)

    n = lax.axis_size("seq")
    window = q_time.shape[0] * n
    tokens = q_time.shape[1]
    sharing = n * LANES // tokens
    bounds = clip_bounds(clip_len, window)
    time = turned(q_time, k_time, v_time, cot_time)
    spans = []
    head = 0
    for heads in CHUNKS:
        spans.append(slice(head * HDIM, (head + heads) * HDIM))
        head += heads
    space_in = turned(q_space, k_space, v_space, cot_space)
    packed = [list(split(time, span, n, sharing)) for span in spans]
    own = [exchange(packed[0])]
    space = space_grads(*space_in)
    packed[1][2:], own[0][2], space = gated(packed[1][2:], own[0][2], space)
    own.append(exchange(packed[1]))
    beside = [
        [neighbours(ends, start) for ends, start in zip(sides(blocks), (1, 0))] for blocks in own
    ]
    back, grads = [], None
    for blocks, near in zip(own, beside):
        back.append(exchange(clip_grads(bounds, blocks, near)))
    for span, blocks in zip(spans, back):
        grads = join(blocks, span, tokens, sharing, grads)
    return turned(*space, *grads)


def whole_tiles(mesh, tokens):
    n = mesh.shape["seq"]
    sharing = n * LANES // tokens
    return (
        tokens % LANES == 0
        and n % 4 == 0
        and n & (n - 1) == 0
        and sharing * tokens == n * LANES
        and all(heads % sharing == 0 and heads // sharing * HDIM % 16 == 0 for heads in CHUNKS)
    )


def padded(block, sides, width):
    for axis, dim in sides:
        count = lax.axis_size(axis)
        forward = [(i, i + 1) for i in range(count - 1)]
        backward = [(target, source) for source, target in forward]
        low = lax.ppermute(
            lax.slice_in_dim(block, block.shape[dim] - width, None, axis=dim), axis, forward
        )
        high = lax.ppermute(lax.slice_in_dim(block, 0, width, axis=dim), axis, backward)
        block = jnp.concatenate([low, block, high], axis=dim)
    return block


def shifted(value, axis, by):
    count = lax.axis_size(axis)
    pairs = [(i, i + by) for i in range(count) if 0 <= i + by < count]
    return lax.ppermute(value, axis, pairs)


def clip_labels(clip_len, first_frame, count, frame_total):
    frame_ids = first_frame + jnp.arange(count, dtype=jnp.int32)
    clip_ends = jnp.cumsum(clip_len)
    labels = jnp.sum((clip_ends[None, :] <= frame_ids[:, None]).astype(jnp.int32), axis=1)
    inside = (frame_ids >= 0) & (frame_ids < frame_total)
    return (labels, inside)


def frame_grads(queries, keys, values, cotangent):
    scaling = 1.0 / math.sqrt(HDIM)
    tokens = queries.shape[0]
    q_heads = queries.reshape(tokens, HEADS, HDIM)
    k_heads = keys.reshape(tokens, HEADS, HDIM)
    v_heads = values.reshape(tokens, HEADS, HDIM)
    g_heads = cotangent.reshape(tokens, HEADS, HDIM)
    scores = (
        jnp.einsum("qhd,khd->hqk", q_heads, k_heads, preferred_element_type=jnp.float32) * scaling
    )
    row_max = jnp.max(scores, axis=-1, keepdims=True)
    log_total = row_max + jnp.log(jnp.sum(jnp.exp(scores - row_max), axis=-1, keepdims=True))
    weights = jnp.exp(scores - log_total)
    weights_low = weights.astype(jnp.bfloat16)
    attended = jnp.einsum("hqk,khd->qhd", weights_low, v_heads, preferred_element_type=jnp.float32)
    row_dot = jnp.einsum("qhd,qhd->hq", g_heads.astype(jnp.float32), attended)
    weight_grad = jnp.einsum("qhd,khd->hqk", g_heads, v_heads, preferred_element_type=jnp.float32)
    score_grad = (weights * (weight_grad - row_dot[:, :, None])).astype(jnp.bfloat16)
    grad_query = (
        jnp.einsum("hqk,khd->qhd", score_grad, k_heads, preferred_element_type=jnp.float32)
        * scaling
    )
    grad_key = (
        jnp.einsum("hqk,qhd->khd", score_grad, q_heads, preferred_element_type=jnp.float32)
        * scaling
    )
    grad_value = jnp.einsum(
        "hqk,qhd->khd", weights_low, g_heads, preferred_element_type=jnp.float32
    )
    flat_shape = (1, tokens, HEADS * HDIM)
    return (
        grad_query.reshape(flat_shape).astype(jnp.bfloat16),
        grad_key.reshape(flat_shape).astype(jnp.bfloat16),
        grad_value.reshape(flat_shape).astype(jnp.bfloat16),
    )


def shards(q_space, k_space, v_space, cot_space, q_time, k_time, v_time, cot_time, clip_len):
    scaling = 1.0 / math.sqrt(HDIM)
    grad_qs, grad_ks, grad_vs = frame_grads(q_space[0], k_space[0], v_space[0], cot_space[0])
    moved = (
        lax.all_to_all(q_time, "seq", split_axis=1, concat_axis=0, tiled=True),
        lax.all_to_all(k_time, "seq", split_axis=1, concat_axis=0, tiled=True),
        lax.all_to_all(v_time, "seq", split_axis=1, concat_axis=0, tiled=True),
        lax.all_to_all(cot_time, "seq", split_axis=1, concat_axis=0, tiled=True),
    )
    query_win, key_win, value_win, cot_win = moved
    window = query_win.shape[0]
    places = query_win.shape[1]
    channels = query_win.shape[2]
    group_id = lax.axis_index("grp")
    frame_total = window * lax.axis_size("grp")
    first_frame = group_id * window

    def split_heads(array):
        return array.reshape(array.shape[0], places, HEADS, HDIM)

    key_pair = padded(jnp.stack([key_win, value_win]), (("grp", 1),), window)
    q_own = split_heads(query_win)
    g_own = split_heads(cot_win)
    k_ext = split_heads(key_pair[0])
    v_ext = split_heads(key_pair[1])
    own_label, own_inside = clip_labels(clip_len, first_frame, window, frame_total)
    ext_label, ext_inside = clip_labels(clip_len, first_frame - window, 3 * window, frame_total)
    allowed = (own_label[:, None] == ext_label[None, :]) & ext_inside[None, :]
    scores = (
        jnp.einsum("iphd,jphd->phij", q_own, k_ext, preferred_element_type=jnp.float32) * scaling
    )
    scores = jnp.where(allowed, scores, masked_score)
    row_max = jnp.max(scores, axis=-1)
    log_total = row_max + jnp.log(jnp.sum(jnp.exp(scores - row_max[..., None]), axis=-1))
    weights = jnp.where(allowed, jnp.exp(scores - log_total[..., None]), 0.0)
    weights_low = weights.astype(jnp.bfloat16)
    attended = jnp.einsum("phij,jphd->iphd", weights_low, v_ext, preferred_element_type=jnp.float32)
    row_dot = jnp.einsum("iphd,iphd->phi", g_own.astype(jnp.float32), attended)
    weight_grad = jnp.einsum("iphd,jphd->phij", g_own, v_ext, preferred_element_type=jnp.float32)
    score_grad = (weights * (weight_grad - row_dot[..., None])).astype(jnp.bfloat16)
    grad_query = (
        jnp.einsum("phij,jphd->iphd", score_grad, k_ext, preferred_element_type=jnp.float32)
        * scaling
    )
    key_terms = (
        jnp.einsum("phij,iphd->jphd", score_grad, q_own, preferred_element_type=jnp.float32)
        * scaling
    )
    value_terms = jnp.einsum(
        "phij,iphd->jphd", weights_low, g_own, preferred_element_type=jnp.float32
    )
    both_terms = jnp.stack([key_terms, value_terms]).reshape(2, 3 * window, places, channels)
    from_after = shifted(both_terms[:, :window], "grp", -1)
    from_before = shifted(both_terms[:, 2 * window :], "grp", 1)
    summed = both_terms[:, window : 2 * window] + from_after + from_before
    grad_key = summed[0]
    grad_value = summed[1]
    grad_qt, grad_kt, grad_vt = (
        lax.all_to_all(
            grad_query.reshape(window, places, channels).astype(jnp.bfloat16),
            "seq",
            split_axis=0,
            concat_axis=1,
            tiled=True,
        ),
        lax.all_to_all(
            grad_key.astype(jnp.bfloat16), "seq", split_axis=0, concat_axis=1, tiled=True
        ),
        lax.all_to_all(
            grad_value.astype(jnp.bfloat16), "seq", split_axis=0, concat_axis=1, tiled=True
        ),
    )
    return (grad_qs, grad_ks, grad_vs, grad_qt, grad_kt, grad_vt)


def solution(mesh):
    split_spec = P(("grp", "seq"), None, None)

    def mapped(body):
        return jax.shard_map(
            body,
            mesh=mesh,
            in_specs=(split_spec,) * 8 + (P(),),
            out_specs=(split_spec,) * 6,
            check_vma=False,
        )

    def grads(*arrays):
        return mapped(tile_shards if whole_tiles(mesh, arrays[0].shape[1]) else shards)(*arrays)

    return grads
```

profile of v0, /device:TPU:0, one launch (start us, length us, event | category | flops | bytes accessed | tf_op | source)
XLA Modules:
  0.0 92.7 jit_solution(2758860163832351563)
XLA Ops:
  0.6 19.1 %pack.3 = (bf16[4,144,128]{2,1,0:T(8,128)(2,1)}, bf16[4,144,128]{2,1,0:T(8,128)(2,1)}, bf16[4,144,128]{2,1,0:T(8,128)(2,1)}, bf16[4,144,128]{2,1,0:T(8,128)(2,1)}) custom-call(bf16[1,576,256]{2,1,0:T(8,128)(2,1)} %bitcast.18, bf16[1,576,256]{2,1,0:T(8,128)(2,1)} %bitcast.20, bf16[1,576,256]{2,1,0:T(8,128)(2,1)} %bitcast.22, bf16[1,576,256]{2,1,0:T(8,128)(2,1)} %bitcast.24), custom_call_target="tpu_custom_call" | custom-call | tf_op jit(solution)/shard_map/pack/pallas_call | solution.py:92
  19.8 4.1 %collective-permute-start = (bf16[4,144,128]{2,1,0:T(8,128)(2,1)}, bf16[4,144,128]{2,1,0:T(8,128)(2,1)S(1)}, u32[]{:S(2)}, u32[]{:S(2)}) collective-permute-start(bf16[4,144,128]{2,1,0:T(8,128)(2,1)} %get-tuple-element.43), channel_id=1, source_target_pairs={{0,2},{1,3},{2,0},{3,1},{4,6},{5,7},{6,4},{7,5},{8,10},{9,11},{10,... | collective-permute-start | bytes 442376 | tf_op jit(solution)/shard_map/ppermute | solution.py:108
  23.9 1.6 %collective-permute-start.9 = (bf16[4,144,128]{2,1,0:T(8,128)(2,1)}, bf16[4,144,128]{2,1,0:T(8,128)(2,1)S(1)}, u32[]{:S(2)}, u32[]{:S(2)}) collective-permute-start(bf16[4,144,128]{2,1,0:T(8,128)(2,1)} %get-tuple-element.61), channel_id=1, source_target_pairs={{0,1},{2,3},{1,0},{3,2},{4,5},{6,7},{5,4},{7,6},{8,9},{10,11},{9,8... | collective-permute-start | bytes 442376 | tf_op jit(solution)/shard_map/ppermute | solution.py:108
  25.5 0.0 collective-permute-start.10
  25.5 19.1 %pack.2 = (bf16[4,144,128]{2,1,0:T(8,128)(2,1)}, bf16[4,144,128]{2,1,0:T(8,128)(2,1)}, bf16[4,144,128]{2,1,0:T(8,128)(2,1)}, bf16[4,144,128]{2,1,0:T(8,128)(2,1)}) custom-call(bf16[1,576,256]{2,1,0:T(8,128)(2,1)} %bitcast.19, bf16[1,576,256]{2,1,0:T(8,128)(2,1)} %bitcast.21, bf16[1,576,256]{2,1,0:T(8,128)(2,1)} %bitcast.23, bf16[1,576,256]{2,1,0:T(8,128)(2,1)} %bitcast.25), custom_call_target="tpu_custom_call" | custom-call | tf_op jit(solution)/shard_map/pack/pallas_call | solution.py:92
  44.6 1.0 %collective-permute-start.1 = (bf16[4,144,128]{2,1,0:T(8,128)(2,1)}, bf16[4,144,128]{2,1,0:T(8,128)(2,1)S(1)}, u32[]{:S(2)}, u32[]{:S(2)}) collective-permute-start(bf16[4,144,128]{2,1,0:T(8,128)(2,1)} %get-tuple-element.51), channel_id=1, source_target_pairs={{0,1},{2,3},{1,0},{3,2},{4,5},{6,7},{5,4},{7,6},{8,9},{10,11},{9,8... | collective-permute-start | bytes 442376 | tf_op jit(solution)/shard_map/ppermute | solution.py:108
  45.5 0.0 copy-start.4
  45.5 0.0 copy-start.3
  45.5 0.0 copy-start.2
  45.5 0.0 copy-start.1
  45.5 5.6 %space.1 = (bf16[1,576,256]{2,1,0:T(8,128)(2,1)}, bf16[1,576,256]{2,1,0:T(8,128)(2,1)}, bf16[1,576,256]{2,1,0:T(8,128)(2,1)}) custom-call(bf16[1,576,256]{2,1,0:T(8,128)(2,1)} %bitcast.29, bf16[1,576,256]{2,1,0:T(8,128)(2,1)} %bitcast.30, bf16[1,576,256]{2,1,0:T(8,128)(2,1)} %bitcast.31, bf16[1,576,256]{2,1,0:T(8,128)(2,1)} %bitcast.32), custom_call_target="tpu_custom_call" | custom-call | flops 1610612736 | bytes 2064384 | tf_op jit(solution)/shard_map/space/pallas_call | solution.py:58
  51.1 0.0 copy-done.4
  51.1 0.1 select_reduce_fusion.2
  51.2 0.0 collective-permute-done.refs_2_
  51.2 0.0 copy-done.3
  51.2 3.5 %collective-permute-start.2 = (bf16[4,144,128]{2,1,0:T(8,128)(2,1)S(1)}, bf16[4,144,128]{2,1,0:T(8,128)(2,1)S(1)}, u32[]{:S(2)}, u32[]{:S(2)}) collective-permute-start(bf16[4,144,128]{2,1,0:T(8,128)(2,1)S(1)} %copy-done.3), channel_id=1, source_target_pairs={{0,2},{1,3},{2,0},{3,1},{4,6},{5,7},{6,4},{7,5},{8,10},{9,11},{10,... | collective-permute-start | bytes 442376 | tf_op jit(solution)/shard_map/ppermute | solution.py:108
  54.8 0.0 copy-done.2
  54.8 0.0 collective-permute-start.3
  54.8 0.0 collective-permute-done.9.refs_1_
  54.8 0.0 collective-permute-done.10.refs_3_
  54.8 0.0 copy-done.1
  54.8 0.0 copy-start
  54.8 0.1 sides.3
  55.0 0.7 collective-permute-start.11
  55.7 3.1 %collective-permute-start.12 = (bf16[3,4,144,128]{3,2,1,0:T(8,128)(2,1)S(1)}, bf16[3,4,144,128]{3,2,1,0:T(8,128)(2,1)S(1)}, u32[]{:S(2)}, u32[]{:S(2)}) collective-permute-start(bf16[3,4,144,128]{3,2,1,0:T(8,128)(2,1)S(1)} %get-tuple-element.65), channel_id=1, source_target_pairs={{0,4},{8,12},{16,20},{24,28},{4,0},{12,8},{20,16},{28,24},{1,5},{9... | collective-permute-start | bytes 1327112 | tf_op jit(solution)/shard_map/ppermute | solution.py:108
  58.8 0.2 select_reduce_fusion.1
  59.0 0.0 collective-permute-done.1.refs_1_
  59.0 5.3 %collective-permute-done.2.refs_2_ = bf16[4,144,128]{2,1,0:T(8,128)(2,1)S(1)} collective-permute-done((bf16[4,144,128]{2,1,0:T(8,128)(2,1)S(1)}, bf16[4,144,128]{2,1,0:T(8,128)(2,1)S(1)}, u32[]{:S(2)}, u32[]{:S(2)}) %collective-permute-start.2) | collective-permute-done | bytes 147488 | tf_op jit(solution)/shard_map/ppermute | solution.py:108
  64.3 0.0 collective-permute-done.3.refs_3_
  64.3 0.0 copy-done
  64.3 0.1 sides.2
  64.4 0.7 collective-permute-start.4
  65.1 2.9 %collective-permute-start.5 = (bf16[3,4,144,128]{3,2,1,0:T(8,128)(2,1)S(1)}, bf16[3,4,144,128]{3,2,1,0:T(8,128)(2,1)S(1)}, u32[]{:S(2)}, u32[]{:S(2)}) collective-permute-start(bf16[3,4,144,128]{3,2,1,0:T(8,128)(2,1)S(1)} %get-tuple-element.55), channel_id=1, source_target_pairs={{0,4},{8,12},{16,20},{24,28},{4,0},{12,8},{20,16},{28,24},{1,5},{9... | collective-permute-start | bytes 1327112 | tf_op jit(solution)/shard_map/ppermute | solution.py:108
  68.0 0.0 collective-permute-done.11.refs_4_
  68.0 0.0 collective-permute-done.12.refs_5_
  68.0 1.4 %clips.3 = (bf16[3,144,128]{2,1,0:T(8,128)(2,1)S(1)}, bf16[3,144,128]{2,1,0:T(8,128)(2,1)S(1)}, bf16[3,144,128]{2,1,0:T(8,128)(2,1)S(1)}, bf16[3,144,128]{2,1,0:T(8,128)(2,1)S(1)}) custom-call(s32[2,10]{1,0:T(2,128)S(1)} %pad_add_fusion.given_bounds, bf16[4,144,128]{2,1,0:T(8,128)(2,1)S(1)} %copy-done.1, ...), custom_call_target="tpu_custom_call" | custom-call | flops 589824000 | bytes 1474560 | tf_op jit(solution)/shard_map/clips/pallas_call | solution.py:282
  69.4 4.3 %collective-permute-start.13 = (bf16[3,144,128]{2,1,0:T(8,128)(2,1)S(1)}, bf16[3,144,128]{2,1,0:T(8,128)(2,1)S(1)}, u32[]{:S(2)}, u32[]{:S(2)}) collective-permute-start(bf16[3,144,128]{2,1,0:T(8,128)(2,1)S(1)} %get-tuple-element.66), channel_id=1, source_target_pairs={{0,2},{1,3},{2,0},{3,1},{4,6},{5,7},{6,4},{7,5},{8,10},{9,11},{10,... | collective-permute-start | bytes 331784 | tf_op jit(solution)/shard_map/ppermute | solution.py:108
  73.7 1.4 %collective-permute-start.14 = (bf16[3,144,128]{2,1,0:T(8,128)(2,1)S(1)}, bf16[3,144,128]{2,1,0:T(8,128)(2,1)S(1)}, u32[]{:S(2)}, u32[]{:S(2)}) collective-permute-start(bf16[3,144,128]{2,1,0:T(8,128)(2,1)S(1)} %get-tuple-element.67), channel_id=1, source_target_pairs={{0,3},{1,2},{3,0},{2,1},{4,7},{5,6},{7,4},{6,5},{8,11},{9,10},{11,... | collective-permute-start | bytes 331784 | tf_op jit(solution)/shard_map/ppermute | solution.py:108
  75.1 0.0 collective-permute-start.15
  75.1 0.0 collective-permute-done.4.refs_4_
  75.1 0.0 collective-permute-done.5.refs_5_
  75.1 1.4 %clips.2 = (bf16[3,144,128]{2,1,0:T(8,128)(2,1)S(1)}, bf16[3,144,128]{2,1,0:T(8,128)(2,1)S(1)}, bf16[3,144,128]{2,1,0:T(8,128)(2,1)S(1)}, bf16[3,144,128]{2,1,0:T(8,128)(2,1)S(1)}) custom-call(s32[2,10]{1,0:T(2,128)S(1)} %pad_add_fusion.given_bounds, bf16[4,144,128]{2,1,0:T(8,128)(2,1)S(1)} %copy-done, ...), custom_call_target="tpu_custom_call" | custom-call | flops 589824000 | bytes 1474560 | tf_op jit(solution)/shard_map/clips/pallas_call | solution.py:282
  76.5 3.0 %collective-permute-start.6 = (bf16[3,144,128]{2,1,0:T(8,128)(2,1)S(1)}, bf16[3,144,128]{2,1,0:T(8,128)(2,1)S(1)}, u32[]{:S(2)}, u32[]{:S(2)}) collective-permute-start(bf16[3,144,128]{2,1,0:T(8,128)(2,1)S(1)} %get-tuple-element.56), channel_id=1, source_target_pairs={{0,2},{1,3},{2,0},{3,1},{4,6},{5,7},{6,4},{7,5},{8,10},{9,11},{10,... | collective-permute-start | bytes 331784 | tf_op jit(solution)/shard_map/ppermute | solution.py:108
  79.5 1.4 %collective-permute-start.7 = (bf16[3,144,128]{2,1,0:T(8,128)(2,1)S(1)}, bf16[3,144,128]{2,1,0:T(8,128)(2,1)S(1)}, u32[]{:S(2)}, u32[]{:S(2)}) collective-permute-start(bf16[3,144,128]{2,1,0:T(8,128)(2,1)S(1)} %get-tuple-element.57), channel_id=1, source_target_pairs={{0,3},{1,2},{3,0},{2,1},{4,7},{5,6},{7,4},{6,5},{8,11},{9,10},{11,... | collective-permute-start | bytes 331784 | tf_op jit(solution)/shard_map/ppermute | solution.py:108
  80.9 1.4 %collective-permute-done.13.refs_0_ = bf16[3,144,128]{2,1,0:T(8,128)(2,1)S(1)} collective-permute-done((bf16[3,144,128]{2,1,0:T(8,128)(2,1)S(1)}, bf16[3,144,128]{2,1,0:T(8,128)(2,1)S(1)}, u32[]{:S(2)}, u32[]{:S(2)}) %collective-permute-start.13) | collective-permute-done | bytes 110624 | tf_op jit(solution)/shard_map/ppermute | solution.py:108
  82.3 0.0 collective-permute-start.8
  82.3 0.0 collective-permute-done.14.refs_1_
  82.3 0.7 collective-permute-done.15.refs_3_
  83.0 0.9 unpack.2
  83.9 8.0 %collective-permute-done.6.refs_0_ = bf16[3,144,128]{2,1,0:T(8,128)(2,1)S(1)} collective-permute-done((bf16[3,144,128]{2,1,0:T(8,128)(2,1)S(1)}, bf16[3,144,128]{2,1,0:T(8,128)(2,1)S(1)}, u32[]{:S(2)}, u32[]{:S(2)}) %collective-permute-start.6) | collective-permute-done | bytes 110624 | tf_op jit(solution)/shard_map/ppermute | solution.py:108
  91.8 0.0 collective-permute-done.7.refs_1_
  91.8 0.0 collective-permute-done.8.refs_3_
  91.8 0.9 unpack.3
  (4 shorter events, 0.0 us)
Async XLA Ops:
  19.8 31.5 %collective-permute-start = (bf16[4,144,128]{2,1,0:T(8,128)(2,1)}, bf16[4,144,128]{2,1,0:T(8,128)(2,1)S(1)}, u32[]{:S(2)}, u32[]{:S(2)}) collective-permute-start(bf16[4,144,128]{2,1,0:T(8,128)(2,1)} %get-tuple-element.43), channel_id=1, source_target_pairs={{0,2},{1,3},{2,0},{3,1},{4,6},{5,7},{6,4},{7,5},{8,10},{9,11},{10,... | collective-permute-start | bytes 442376 | tf_op jit(solution)/shard_map/ppermute | solution.py:108
  23.9 30.9 %collective-permute-start.9 = (bf16[4,144,128]{2,1,0:T(8,128)(2,1)}, bf16[4,144,128]{2,1,0:T(8,128)(2,1)S(1)}, u32[]{:S(2)}, u32[]{:S(2)}) collective-permute-start(bf16[4,144,128]{2,1,0:T(8,128)(2,1)} %get-tuple-element.61), channel_id=1, source_target_pairs={{0,1},{2,3},{1,0},{3,2},{4,5},{6,7},{5,4},{7,6},{8,9},{10,11},{9,8... | collective-permute-start | bytes 442376 | tf_op jit(solution)/shard_map/ppermute | solution.py:108
  25.5 29.4 %collective-permute-start.10 = (bf16[4,144,128]{2,1,0:T(8,128)(2,1)}, bf16[4,144,128]{2,1,0:T(8,128)(2,1)S(1)}, u32[]{:S(2)}, u32[]{:S(2)}) collective-permute-start(bf16[4,144,128]{2,1,0:T(8,128)(2,1)} %get-tuple-element.63), channel_id=1, source_target_pairs={{0,3},{1,2},{3,0},{2,1},{4,7},{5,6},{7,4},{6,5},{8,11},{9,10},{11,... | collective-permute-start | bytes 442376 | tf_op jit(solution)/shard_map/ppermute | solution.py:108
  44.6 14.4 %collective-permute-start.1 = (bf16[4,144,128]{2,1,0:T(8,128)(2,1)}, bf16[4,144,128]{2,1,0:T(8,128)(2,1)S(1)}, u32[]{:S(2)}, u32[]{:S(2)}) collective-permute-start(bf16[4,144,128]{2,1,0:T(8,128)(2,1)} %get-tuple-element.51), channel_id=1, source_target_pairs={{0,1},{2,3},{1,0},{3,2},{4,5},{6,7},{5,4},{7,6},{8,9},{10,11},{9,8... | collective-permute-start | bytes 442376 | tf_op jit(solution)/shard_map/ppermute | solution.py:108
  45.5 5.6 %copy-start.4 = (s32[16]{0:T(128)S(1)}, s32[16]{0:T(128)}, u32[]{:S(2)}) copy-start(s32[16]{0:T(128)} %param.17) | copy-start | bytes 196
  45.5 5.7 %copy-start.3 = (bf16[4,144,128]{2,1,0:T(8,128)(2,1)S(1)}, bf16[4,144,128]{2,1,0:T(8,128)(2,1)}, u32[]{:S(2)}) copy-start(bf16[4,144,128]{2,1,0:T(8,128)(2,1)} %get-tuple-element.52) | copy-start | bytes 442372
  45.5 9.2 %copy-start.2 = (bf16[4,144,128]{2,1,0:T(8,128)(2,1)S(1)}, bf16[4,144,128]{2,1,0:T(8,128)(2,1)}, u32[]{:S(2)}) copy-start(bf16[4,144,128]{2,1,0:T(8,128)(2,1)} %get-tuple-element.53) | copy-start | bytes 442372
  45.5 9.3 %copy-start.1 = (bf16[4,144,128]{2,1,0:T(8,128)(2,1)S(1)}, bf16[4,144,128]{2,1,0:T(8,128)(2,1)}, u32[]{:S(2)}) copy-start(bf16[4,144,128]{2,1,0:T(8,128)(2,1)} %get-tuple-element.60.refs_0_) | copy-start | bytes 442372
  51.2 13.1 %collective-permute-start.2 = (bf16[4,144,128]{2,1,0:T(8,128)(2,1)S(1)}, bf16[4,144,128]{2,1,0:T(8,128)(2,1)S(1)}, u32[]{:S(2)}, u32[]{:S(2)}) collective-permute-start(bf16[4,144,128]{2,1,0:T(8,128)(2,1)S(1)} %copy-done.3), channel_id=1, source_target_pairs={{0,2},{1,3},{2,0},{3,1},{4,6},{5,7},{6,4},{7,5},{8,10},{9,11},{10,... | collective-permute-start | bytes 442376 | tf_op jit(solution)/shard_map/ppermute | solution.py:108
  54.8 9.5 %collective-permute-start.3 = (bf16[4,144,128]{2,1,0:T(8,128)(2,1)S(1)}, bf16[4,144,128]{2,1,0:T(8,128)(2,1)S(1)}, u32[]{:S(2)}, u32[]{:S(2)}) collective-permute-start(bf16[4,144,128]{2,1,0:T(8,128)(2,1)S(1)} %copy-done.2), channel_id=1, source_target_pairs={{0,3},{1,2},{3,0},{2,1},{4,7},{5,6},{7,4},{6,5},{8,11},{9,10},{11,... | collective-permute-start | bytes 442376 | tf_op jit(solution)/shard_map/ppermute | solution.py:108
  54.8 9.5 %copy-start = (bf16[4,144,128]{2,1,0:T(8,128)(2,1)S(1)}, bf16[4,144,128]{2,1,0:T(8,128)(2,1)}, u32[]{:S(2)}) copy-start(bf16[4,144,128]{2,1,0:T(8,128)(2,1)} %get-tuple-element.50.refs_0_) | copy-start | bytes 442372
  55.0 13.0 %collective-permute-start.11 = (bf16[3,4,144,128]{3,2,1,0:T(8,128)(2,1)S(1)}, bf16[3,4,144,128]{3,2,1,0:T(8,128)(2,1)S(1)}, u32[]{:S(2)}, u32[]{:S(2)}) collective-permute-start(bf16[3,4,144,128]{3,2,1,0:T(8,128)(2,1)S(1)} %get-tuple-element.64), channel_id=1, source_target_pairs={{4,8},{12,16},{20,24},{8,4},{16,12},{24,20},{5,9},{13,17},{21,25},... | collective-permute-start | bytes 1327112 | tf_op jit(solution)/shard_map/ppermute | solution.py:108
  55.7 12.3 %collective-permute-start.12 = (bf16[3,4,144,128]{3,2,1,0:T(8,128)(2,1)S(1)}, bf16[3,4,144,128]{3,2,1,0:T(8,128)(2,1)S(1)}, u32[]{:S(2)}, u32[]{:S(2)}) collective-permute-start(bf16[3,4,144,128]{3,2,1,0:T(8,128)(2,1)S(1)} %get-tuple-element.65), channel_id=1, source_target_pairs={{0,4},{8,12},{16,20},{24,28},{4,0},{12,8},{20,16},{28,24},{1,5},{9... | collective-permute-start | bytes 1327112 | tf_op jit(solution)/shard_map/ppermute | solution.py:108
  64.4 10.7 %collective-permute-start.4 = (bf16[3,4,144,128]{3,2,1,0:T(8,128)(2,1)S(1)}, bf16[3,4,144,128]{3,2,1,0:T(8,128)(2,1)S(1)}, u32[]{:S(2)}, u32[]{:S(2)}) collective-permute-start(bf16[3,4,144,128]{3,2,1,0:T(8,128)(2,1)S(1)} %get-tuple-element.54), channel_id=1, source_target_pairs={{4,8},{12,16},{20,24},{8,4},{16,12},{24,20},{5,9},{13,17},{21,25},... | collective-permute-start | bytes 1327112 | tf_op jit(solution)/shard_map/ppermute | solution.py:108
  65.1 10.0 %collective-permute-start.5 = (bf16[3,4,144,128]{3,2,1,0:T(8,128)(2,1)S(1)}, bf16[3,4,144,128]{3,2,1,0:T(8,128)(2,1)S(1)}, u32[]{:S(2)}, u32[]{:S(2)}) collective-permute-start(bf16[3,4,144,128]{3,2,1,0:T(8,128)(2,1)S(1)} %get-tuple-element.55), channel_id=1, source_target_pairs={{0,4},{8,12},{16,20},{24,28},{4,0},{12,8},{20,16},{28,24},{1,5},{9... | collective-permute-start | bytes 1327112 | tf_op jit(solution)/shard_map/ppermute | solution.py:108
  69.4 12.9 %collective-permute-start.13 = (bf16[3,144,128]{2,1,0:T(8,128)(2,1)S(1)}, bf16[3,144,128]{2,1,0:T(8,128)(2,1)S(1)}, u32[]{:S(2)}, u32[]{:S(2)}) collective-permute-start(bf16[3,144,128]{2,1,0:T(8,128)(2,1)S(1)} %get-tuple-element.66), channel_id=1, source_target_pairs={{0,2},{1,3},{2,0},{3,1},{4,6},{5,7},{6,4},{7,5},{8,10},{9,11},{10,... | collective-permute-start | bytes 331784 | tf_op jit(solution)/shard_map/ppermute | solution.py:108
  73.7 8.7 %collective-permute-start.14 = (bf16[3,144,128]{2,1,0:T(8,128)(2,1)S(1)}, bf16[3,144,128]{2,1,0:T(8,128)(2,1)S(1)}, u32[]{:S(2)}, u32[]{:S(2)}) collective-permute-start(bf16[3,144,128]{2,1,0:T(8,128)(2,1)S(1)} %get-tuple-element.67), channel_id=1, source_target_pairs={{0,3},{1,2},{3,0},{2,1},{4,7},{5,6},{7,4},{6,5},{8,11},{9,10},{11,... | collective-permute-start | bytes 331784 | tf_op jit(solution)/shard_map/ppermute | solution.py:108
  75.1 7.9 %collective-permute-start.15 = (bf16[3,144,128]{2,1,0:T(8,128)(2,1)S(1)}, bf16[3,144,128]{2,1,0:T(8,128)(2,1)S(1)}, u32[]{:S(2)}, u32[]{:S(2)}) collective-permute-start(bf16[3,144,128]{2,1,0:T(8,128)(2,1)S(1)} %get-tuple-element.69), channel_id=1, source_target_pairs={{0,1},{2,3},{1,0},{3,2},{4,5},{6,7},{5,4},{7,6},{8,9},{10,11},{9,8... | collective-permute-start | bytes 331784 | tf_op jit(solution)/shard_map/ppermute | solution.py:108
  76.5 15.3 %collective-permute-start.6 = (bf16[3,144,128]{2,1,0:T(8,128)(2,1)S(1)}, bf16[3,144,128]{2,1,0:T(8,128)(2,1)S(1)}, u32[]{:S(2)}, u32[]{:S(2)}) collective-permute-start(bf16[3,144,128]{2,1,0:T(8,128)(2,1)S(1)} %get-tuple-element.56), channel_id=1, source_target_pairs={{0,2},{1,3},{2,0},{3,1},{4,6},{5,7},{6,4},{7,5},{8,10},{9,11},{10,... | collective-permute-start | bytes 331784 | tf_op jit(solution)/shard_map/ppermute | solution.py:108
  79.5 12.3 %collective-permute-start.7 = (bf16[3,144,128]{2,1,0:T(8,128)(2,1)S(1)}, bf16[3,144,128]{2,1,0:T(8,128)(2,1)S(1)}, u32[]{:S(2)}, u32[]{:S(2)}) collective-permute-start(bf16[3,144,128]{2,1,0:T(8,128)(2,1)S(1)} %get-tuple-element.57), channel_id=1, source_target_pairs={{0,3},{1,2},{3,0},{2,1},{4,7},{5,6},{7,4},{6,5},{8,11},{9,10},{11,... | collective-permute-start | bytes 331784 | tf_op jit(solution)/shard_map/ppermute | solution.py:108
  82.3 9.5 %collective-permute-start.8 = (bf16[3,144,128]{2,1,0:T(8,128)(2,1)S(1)}, bf16[3,144,128]{2,1,0:T(8,128)(2,1)S(1)}, u32[]{:S(2)}, u32[]{:S(2)}) collective-permute-start(bf16[3,144,128]{2,1,0:T(8,128)(2,1)S(1)} %get-tuple-element.59), channel_id=1, source_target_pairs={{0,1},{2,3},{1,0},{3,2},{4,5},{6,7},{5,4},{7,6},{8,9},{10,11},{9,8... | collective-permute-start | bytes 331784 | tf_op jit(solution)/shard_map/ppermute | solution.py:108
where the time goes:
time: 93 us; the launch traced here: 92.7 us
  Pallas kernels  48.5 us (52%)
  starting transfers between devices  27.7 us (30%)
  waiting for transfers between devices  15.4 us (17%)
    pallas_call x2, Pallas kernels, split(): pl.pallas_call(functools.partial(split_kernel, sharing, rows, span), in_s...  38.2 us
    ppermute x16, starting transfers between devices, swap(): lax.ppermute(block, axis, [(i, j) for i, j in pairs] + [(j, i) for i, j i...  27.7 us
    ppermute x16, waiting for transfers between devices, swap(): lax.ppermute(block, axis, [(i, j) for i, j in pairs] + [(j, i) for i, j i...  15.4 us
    pallas_call x1, Pallas kernels, space_grads(): pl.pallas_call(frame_kernel, out_shape=(shape, shape, shape), compiler_pa...  5.59 us
    pallas_call x2, Pallas kernels, clip_grads(): pl.pallas_call(functools.partial(clip_kernel, window, heads), out_shape=[...  2.72 us
  transfers between devices with their start and end apart: 16, of which 4 were waited for; matrix products, arithmetic and copies ran while one was open for 0% of the time, Pallas kernels for 31%

commit v1 on v0

--- a/solution.py
+++ b/solution.py
@@ -74,15 +74,20 @@
 
 
 def split_kernel(sharing, rows, span, *refs):
-    ins, outs, sent = refs[:4], refs[4:-1], refs[-1]
-    copies = []
+    ins, outs, (held, arrived, sent) = refs[:4], refs[4:-3], refs[-3:]
+    loads, stores = {}, []
     for step in far_first(len(outs)):
         row, tokens = part_of(lax.axis_index("seq") ^ step, sharing, rows)
         for i, array in enumerate(ins):
             given = array.at[0, pl.ds(span.start + row, rows), tokens]
-            copies.append(pltpu.make_async_copy(given, outs[step].at[i], sent.at[step, i]))
-            copies[-1].start()
-    for copy in copies:
+            loads[step, i] = pltpu.make_async_copy(given, held.at[step, i], arrived.at[step, i])
+            loads[step, i].start()
+    for step in far_first(len(outs)):
+        for i in range(len(ins)):
+            loads[step, i].wait()
+        stores.append(pltpu.make_async_copy(held.at[step], outs[step], sent.at[step]))
+        stores[-1].start()
+    for copy in stores:
         copy.wait()
 
 
@@ -94,7 +99,11 @@
         in_specs=[hbm] * 4,
         out_specs=[hbm] * n,
         out_shape=[jax.ShapeDtypeStruct((4, rows, LANES), jnp.bfloat16)] * n,
-        scratch_shapes=[pltpu.SemaphoreType.DMA((n, 4))],
+        scratch_shapes=[
+            pltpu.VMEM((n, 4, rows, LANES), jnp.bfloat16),
+            pltpu.SemaphoreType.DMA((n, 4)),
+            pltpu.SemaphoreType.DMA((n,)),
+        ],
         compiler_params=pltpu.CompilerParams(vmem_limit_bytes=60 * 2**20),
         name="pack",
     )(*arrays)

time: 93 us -> 60.5 us (0.65)
  Pallas kernels: 48.5 us -> 14.4 us
  waiting for transfers between devices: 15.4 us -> 17.2 us
    pallas_call x2, Pallas kernels: 38.2 us -> 3.77 us  [split(): pl.pallas_call(functools.partial(split_kernel, sharing, rows, span), in_s...]
    ppermute x16, waiting for transfers between devices: 15.4 us -> 17.2 us  [swap(): lax.ppermute(block, axis, [(i, j) for i, j in pairs] + [(j, i) for i, j i...]
  transfers between devices with their start and end apart: 16 -> 16, of which waited for: 4 -> 5; matrix products, arithmetic and copies ran while one was open for 0% -> 0% of each run, Pallas kernels for 31% -> 19%
where the time goes in v1:
time: 60.5 us; the launch traced here: 60.1 us
  starting transfers between devices  27.5 us (45%)
  waiting for transfers between devices  17.2 us (28%)
  Pallas kernels  14.4 us (24%)
  between operations  0.78 us (1%)
    ppermute x16, starting transfers between devices, swap(): lax.ppermute(block, axis, [(i, j) for i, j in pairs] + [(j, i) for i, j i...  27.5 us
    ppermute x16, waiting for transfers between devices, swap(): lax.ppermute(block, axis, [(i, j) for i, j in pairs] + [(j, i) for i, j i...  17.2 us
    pallas_call x1, Pallas kernels, space_grads(): pl.pallas_call(frame_kernel, out_shape=(shape, shape, shape), compiler_pa...  5.58 us
    pallas_call x2, Pallas kernels, split(): pl.pallas_call(functools.partial(split_kernel, sharing, rows, span), in_s...  3.77 us
    pallas_call x2, Pallas kernels, clip_grads(): pl.pallas_call(functools.partial(clip_kernel, window, heads), out_shape=[...  3.08 us
    pallas_call x2, Pallas kernels, join(): pl.pallas_call(functools.partial(join_kernel, sharing, span), in_specs=[p...  1.71 us
  transfers between devices with their start and end apart: 16, of which 5 were waited for; matrix products, arithmetic and copies ran while one was open for 0% of the time, Pallas kernels for 19%

profile of v1, /device:TPU:0, one launch (start us, length us, event | category | flops | bytes accessed | tf_op | source)
XLA Modules:
  0.0 60.1 jit_solution(15734596148676124047)
XLA Ops:
  0.6 1.9 %pack.3 = (bf16[4,144,128]{2,1,0:T(8,128)(2,1)}, bf16[4,144,128]{2,1,0:T(8,128)(2,1)}, bf16[4,144,128]{2,1,0:T(8,128)(2,1)}, bf16[4,144,128]{2,1,0:T(8,128)(2,1)}) custom-call(bf16[1,576,256]{2,1,0:T(8,128)(2,1)} %bitcast.18, bf16[1,576,256]{2,1,0:T(8,128)(2,1)} %bitcast.20, bf16[1,576,256]{2,1,0:T(8,128)(2,1)} %bitcast.22, bf16[1,576,256]{2,1,0:T(8,128)(2,1)} %bitcast.24), custom_call_target="tpu_custom_call" | custom-call | tf_op jit(solution)/shard_map/pack/pallas_call | solution.py:97
  2.5 4.1 %collective-permute-start = (bf16[4,144,128]{2,1,0:T(8,128)(2,1)}, bf16[4,144,128]{2,1,0:T(8,128)(2,1)S(1)}, u32[]{:S(2)}, u32[]{:S(2)}) collective-permute-start(bf16[4,144,128]{2,1,0:T(8,128)(2,1)} %get-tuple-element.43), channel_id=1, source_target_pairs={{0,2},{1,3},{2,0},{3,1},{4,6},{5,7},{6,4},{7,5},{8,10},{9,11},{10,... | collective-permute-start | bytes 442376 | tf_op jit(solution)/shard_map/ppermute | solution.py:117
  6.6 1.6 %collective-permute-start.9 = (bf16[4,144,128]{2,1,0:T(8,128)(2,1)}, bf16[4,144,128]{2,1,0:T(8,128)(2,1)S(1)}, u32[]{:S(2)}, u32[]{:S(2)}) collective-permute-start(bf16[4,144,128]{2,1,0:T(8,128)(2,1)} %get-tuple-element.61), channel_id=1, source_target_pairs={{0,1},{2,3},{1,0},{3,2},{4,5},{6,7},{5,4},{7,6},{8,9},{10,11},{9,8... | collective-permute-start | bytes 442376 | tf_op jit(solution)/shard_map/ppermute | solution.py:117
  8.2 0.0 collective-permute-start.10
  8.2 1.9 %pack.2 = (bf16[4,144,128]{2,1,0:T(8,128)(2,1)}, bf16[4,144,128]{2,1,0:T(8,128)(2,1)}, bf16[4,144,128]{2,1,0:T(8,128)(2,1)}, bf16[4,144,128]{2,1,0:T(8,128)(2,1)}) custom-call(bf16[1,576,256]{2,1,0:T(8,128)(2,1)} %bitcast.19, bf16[1,576,256]{2,1,0:T(8,128)(2,1)} %bitcast.21, bf16[1,576,256]{2,1,0:T(8,128)(2,1)} %bitcast.23, bf16[1,576,256]{2,1,0:T(8,128)(2,1)} %bitcast.25), custom_call_target="tpu_custom_call" | custom-call | tf_op jit(solution)/shard_map/pack/pallas_call | solution.py:97
  10.1 1.0 %collective-permute-start.1 = (bf16[4,144,128]{2,1,0:T(8,128)(2,1)}, bf16[4,144,128]{2,1,0:T(8,128)(2,1)S(1)}, u32[]{:S(2)}, u32[]{:S(2)}) collective-permute-start(bf16[4,144,128]{2,1,0:T(8,128)(2,1)} %get-tuple-element.51), channel_id=1, source_target_pairs={{0,1},{2,3},{1,0},{3,2},{4,5},{6,7},{5,4},{7,6},{8,9},{10,11},{9,8... | collective-permute-start | bytes 442376 | tf_op jit(solution)/shard_map/ppermute | solution.py:117
  11.1 0.0 copy-start.4
  11.1 0.0 copy-start.3
  11.1 0.0 copy-start.2
  11.1 0.0 copy-start.1
  11.1 5.6 %space.1 = (bf16[1,576,256]{2,1,0:T(8,128)(2,1)}, bf16[1,576,256]{2,1,0:T(8,128)(2,1)}, bf16[1,576,256]{2,1,0:T(8,128)(2,1)}) custom-call(bf16[1,576,256]{2,1,0:T(8,128)(2,1)} %bitcast.29, bf16[1,576,256]{2,1,0:T(8,128)(2,1)} %bitcast.30, bf16[1,576,256]{2,1,0:T(8,128)(2,1)} %bitcast.31, bf16[1,576,256]{2,1,0:T(8,128)(2,1)} %bitcast.32), custom_call_target="tpu_custom_call" | custom-call | flops 1610612736 | bytes 2064384 | tf_op jit(solution)/shard_map/space/pallas_call | solution.py:58
  16.7 0.0 copy-done.4
  16.7 0.1 select_reduce_fusion.2
  16.7 0.0 collective-permute-done.refs_2_
  16.7 0.0 copy-done.3
  16.8 3.6 %collective-permute-start.2 = (bf16[4,144,128]{2,1,0:T(8,128)(2,1)S(1)}, bf16[4,144,128]{2,1,0:T(8,128)(2,1)S(1)}, u32[]{:S(2)}, u32[]{:S(2)}) collective-permute-start(bf16[4,144,128]{2,1,0:T(8,128)(2,1)S(1)} %copy-done.3), channel_id=1, source_target_pairs={{0,2},{1,3},{2,0},{3,1},{4,6},{5,7},{6,4},{7,5},{8,10},{9,11},{10,... | collective-permute-start | bytes 442376 | tf_op jit(solution)/shard_map/ppermute | solution.py:117
  20.3 0.0 copy-done.2
  20.3 0.0 collective-permute-start.3
  20.3 0.0 collective-permute-done.9.refs_1_
  20.3 0.0 collective-permute-done.10.refs_3_
  20.4 0.0 copy-done.1
  20.4 0.0 copy-start
  20.4 0.1 sides.3
  20.5 0.7 %collective-permute-start.11 = (bf16[3,4,144,128]{3,2,1,0:T(8,128)(2,1)S(1)}, bf16[3,4,144,128]{3,2,1,0:T(8,128)(2,1)S(1)}, u32[]{:S(2)}, u32[]{:S(2)}) collective-permute-start(bf16[3,4,144,128]{3,2,1,0:T(8,128)(2,1)S(1)} %get-tuple-element.64), channel_id=1, source_target_pairs={{4,8},{12,16},{20,24},{8,4},{16,12},{24,20},{5,9},{13,17},{21,25},... | collective-permute-start | bytes 1327112 | tf_op jit(solution)/shard_map/ppermute | solution.py:117
  21.2 3.1 %collective-permute-start.12 = (bf16[3,4,144,128]{3,2,1,0:T(8,128)(2,1)S(1)}, bf16[3,4,144,128]{3,2,1,0:T(8,128)(2,1)S(1)}, u32[]{:S(2)}, u32[]{:S(2)}) collective-permute-start(bf16[3,4,144,128]{3,2,1,0:T(8,128)(2,1)S(1)} %get-tuple-element.65), channel_id=1, source_target_pairs={{0,4},{8,12},{16,20},{24,28},{4,0},{12,8},{20,16},{28,24},{1,5},{9... | collective-permute-start | bytes 1327112 | tf_op jit(solution)/shard_map/ppermute | solution.py:117
  24.3 0.2 select_reduce_fusion.1
  24.5 0.0 collective-permute-done.1.refs_1_
  24.5 6.1 %collective-permute-done.2.refs_2_ = bf16[4,144,128]{2,1,0:T(8,128)(2,1)S(1)} collective-permute-done((bf16[4,144,128]{2,1,0:T(8,128)(2,1)S(1)}, bf16[4,144,128]{2,1,0:T(8,128)(2,1)S(1)}, u32[]{:S(2)}, u32[]{:S(2)}) %collective-permute-start.2) | collective-permute-done | bytes 147488 | tf_op jit(solution)/shard_map/ppermute | solution.py:117
  30.6 0.0 collective-permute-done.3.refs_3_
  30.6 0.0 copy-done
  30.6 0.1 sides.2
  30.7 0.7 %collective-permute-start.4 = (bf16[3,4,144,128]{3,2,1,0:T(8,128)(2,1)S(1)}, bf16[3,4,144,128]{3,2,1,0:T(8,128)(2,1)S(1)}, u32[]{:S(2)}, u32[]{:S(2)}) collective-permute-start(bf16[3,4,144,128]{3,2,1,0:T(8,128)(2,1)S(1)} %get-tuple-element.54), channel_id=1, source_target_pairs={{4,8},{12,16},{20,24},{8,4},{16,12},{24,20},{5,9},{13,17},{21,25},... | collective-permute-start | bytes 1327112 | tf_op jit(solution)/shard_map/ppermute | solution.py:117
  31.4 2.9 %collective-permute-start.5 = (bf16[3,4,144,128]{3,2,1,0:T(8,128)(2,1)S(1)}, bf16[3,4,144,128]{3,2,1,0:T(8,128)(2,1)S(1)}, u32[]{:S(2)}, u32[]{:S(2)}) collective-permute-start(bf16[3,4,144,128]{3,2,1,0:T(8,128)(2,1)S(1)} %get-tuple-element.55), channel_id=1, source_target_pairs={{0,4},{8,12},{16,20},{24,28},{4,0},{12,8},{20,16},{28,24},{1,5},{9... | collective-permute-start | bytes 1327112 | tf_op jit(solution)/shard_map/ppermute | solution.py:117
  34.3 0.0 collective-permute-done.11.refs_4_
  34.3 0.0 collective-permute-done.12.refs_5_
  34.3 1.5 %clips.3 = (bf16[3,144,128]{2,1,0:T(8,128)(2,1)S(1)}, bf16[3,144,128]{2,1,0:T(8,128)(2,1)S(1)}, bf16[3,144,128]{2,1,0:T(8,128)(2,1)S(1)}, bf16[3,144,128]{2,1,0:T(8,128)(2,1)S(1)}) custom-call(s32[2,10]{1,0:T(2,128)S(1)} %pad_add_fusion.given_bounds, bf16[4,144,128]{2,1,0:T(8,128)(2,1)S(1)} %copy-done.1, ...), custom_call_target="tpu_custom_call" | custom-call | flops 589824000 | bytes 1474560 | tf_op jit(solution)/shard_map/clips/pallas_call | solution.py:291
  35.9 5.0 %collective-permute-start.13 = (bf16[3,144,128]{2,1,0:T(8,128)(2,1)S(1)}, bf16[3,144,128]{2,1,0:T(8,128)(2,1)S(1)}, u32[]{:S(2)}, u32[]{:S(2)}) collective-permute-start(bf16[3,144,128]{2,1,0:T(8,128)(2,1)S(1)} %get-tuple-element.66), channel_id=1, source_target_pairs={{0,2},{1,3},{2,0},{3,1},{4,6},{5,7},{6,4},{7,5},{8,10},{9,11},{10,... | collective-permute-start | bytes 331784 | tf_op jit(solution)/shard_map/ppermute | solution.py:117
  40.9 0.4 collective-permute-start.14
  41.3 0.2 collective-permute-start.15
  41.5 0.0 collective-permute-done.4.refs_4_
  41.5 0.0 collective-permute-done.5.refs_5_
  41.5 1.5 %clips.2 = (bf16[3,144,128]{2,1,0:T(8,128)(2,1)S(1)}, bf16[3,144,128]{2,1,0:T(8,128)(2,1)S(1)}, bf16[3,144,128]{2,1,0:T(8,128)(2,1)S(1)}, bf16[3,144,128]{2,1,0:T(8,128)(2,1)S(1)}) custom-call(s32[2,10]{1,0:T(2,128)S(1)} %pad_add_fusion.given_bounds, bf16[4,144,128]{2,1,0:T(8,128)(2,1)S(1)} %copy-done, ...), custom_call_target="tpu_custom_call" | custom-call | flops 589824000 | bytes 1474560 | tf_op jit(solution)/shard_map/clips/pallas_call | solution.py:291
  43.1 3.8 %collective-permute-start.6 = (bf16[3,144,128]{2,1,0:T(8,128)(2,1)S(1)}, bf16[3,144,128]{2,1,0:T(8,128)(2,1)S(1)}, u32[]{:S(2)}, u32[]{:S(2)}) collective-permute-start(bf16[3,144,128]{2,1,0:T(8,128)(2,1)S(1)} %get-tuple-element.56), channel_id=1, source_target_pairs={{0,2},{1,3},{2,0},{3,1},{4,6},{5,7},{6,4},{7,5},{8,10},{9,11},{10,... | collective-permute-start | bytes 331784 | tf_op jit(solution)/shard_map/ppermute | solution.py:117
  46.9 0.4 collective-permute-start.7
  47.3 1.8 %collective-permute-done.13.refs_0_ = bf16[3,144,128]{2,1,0:T(8,128)(2,1)S(1)} collective-permute-done((bf16[3,144,128]{2,1,0:T(8,128)(2,1)S(1)}, bf16[3,144,128]{2,1,0:T(8,128)(2,1)S(1)}, u32[]{:S(2)}, u32[]{:S(2)}) %collective-permute-start.13) | collective-permute-done | bytes 110624 | tf_op jit(solution)/shard_map/ppermute | solution.py:117
  49.2 0.0 collective-permute-start.8
  49.2 0.0 collective-permute-done.14.refs_1_
  49.2 1.1 %collective-permute-done.15.refs_3_ = bf16[3,144,128]{2,1,0:T(8,128)(2,1)S(1)} collective-permute-done((bf16[3,144,128]{2,1,0:T(8,128)(2,1)S(1)}, bf16[3,144,128]{2,1,0:T(8,128)(2,1)S(1)}, u32[]{:S(2)}, u32[]{:S(2)}) %collective-permute-start.15) | collective-permute-done | bytes 110624 | tf_op jit(solution)/shard_map/ppermute | solution.py:117
  50.2 0.9 %unpack.2 = (bf16[1,576,256]{2,1,0:T(8,128)(2,1)}, bf16[1,576,256]{2,1,0:T(8,128)(2,1)}, bf16[1,576,256]{2,1,0:T(8,128)(2,1)}) custom-call(bf16[3,144,128]{2,1,0:T(8,128)(2,1)S(1)} %collective-permute-done.13.refs_0_, bf16[3,144,128]{2,1,0:T(8,128)(2,1)S(1)} %collective-permute-done.14.refs_1_, bf16[3,144,128]{2,1,0:T(8,128)(2,1)S(1)} %get-tuple-element.68.refs_2_, ...), custom_call_target="tpu_custom_call" | custom-call | tf_op jit(solution)/shard_map/unpack/pallas_call | solution.py:185
  51.1 7.5 %collective-permute-done.6.refs_0_ = bf16[3,144,128]{2,1,0:T(8,128)(2,1)S(1)} collective-permute-done((bf16[3,144,128]{2,1,0:T(8,128)(2,1)S(1)}, bf16[3,144,128]{2,1,0:T(8,128)(2,1)S(1)}, u32[]{:S(2)}, u32[]{:S(2)}) %collective-permute-start.6) | collective-permute-done | bytes 110624 | tf_op jit(solution)/shard_map/ppermute | solution.py:117
  58.6 0.0 collective-permute-done.7.refs_1_
  58.6 0.6 %collective-permute-done.8.refs_3_ = bf16[3,144,128]{2,1,0:T(8,128)(2,1)S(1)} collective-permute-done((bf16[3,144,128]{2,1,0:T(8,128)(2,1)S(1)}, bf16[3,144,128]{2,1,0:T(8,128)(2,1)S(1)}, u32[]{:S(2)}, u32[]{:S(2)}) %collective-permute-start.8) | collective-permute-done | bytes 110624 | tf_op jit(solution)/shard_map/ppermute | solution.py:117
  59.3 0.9 %unpack.3 = (bf16[1,576,256]{2,1,0:T(8,128)(2,1)}, bf16[1,576,256]{2,1,0:T(8,128)(2,1)}, bf16[1,576,256]{2,1,0:T(8,128)(2,1)}) custom-call(bf16[3,144,128]{2,1,0:T(8,128)(2,1)S(1)} %collective-permute-done.6.refs_0_, bf16[3,144,128]{2,1,0:T(8,128)(2,1)S(1)} %collective-permute-done.7.refs_1_, ...), custom_call_target="tpu_custom_call", output_to_operand_aliasing={{0}: (4, {}), {1}: (5, {}), {2}: (6, {})} | custom-call | tf_op jit(solution)/shard_map/unpack/pallas_call | solution.py:185
  (4 shorter events, 0.0 us)
Async XLA Ops:
  2.5 14.2 %collective-permute-start = (bf16[4,144,128]{2,1,0:T(8,128)(2,1)}, bf16[4,144,128]{2,1,0:T(8,128)(2,1)S(1)}, u32[]{:S(2)}, u32[]{:S(2)}) collective-permute-start(bf16[4,144,128]{2,1,0:T(8,128)(2,1)} %get-tuple-element.43), channel_id=1, source_target_pairs={{0,2},{1,3},{2,0},{3,1},{4,6},{5,7},{6,4},{7,5},{8,10},{9,11},{10,... | collective-permute-start | bytes 442376 | tf_op jit(solution)/shard_map/ppermute | solution.py:117
  6.6 13.7 %collective-permute-start.9 = (bf16[4,144,128]{2,1,0:T(8,128)(2,1)}, bf16[4,144,128]{2,1,0:T(8,128)(2,1)S(1)}, u32[]{:S(2)}, u32[]{:S(2)}) collective-permute-start(bf16[4,144,128]{2,1,0:T(8,128)(2,1)} %get-tuple-element.61), channel_id=1, source_target_pairs={{0,1},{2,3},{1,0},{3,2},{4,5},{6,7},{5,4},{7,6},{8,9},{10,11},{9,8... | collective-permute-start | bytes 442376 | tf_op jit(solution)/shard_map/ppermute | solution.py:117
  8.2 12.1 %collective-permute-start.10 = (bf16[4,144,128]{2,1,0:T(8,128)(2,1)}, bf16[4,144,128]{2,1,0:T(8,128)(2,1)S(1)}, u32[]{:S(2)}, u32[]{:S(2)}) collective-permute-start(bf16[4,144,128]{2,1,0:T(8,128)(2,1)} %get-tuple-element.63), channel_id=1, source_target_pairs={{0,3},{1,2},{3,0},{2,1},{4,7},{5,6},{7,4},{6,5},{8,11},{9,10},{11,... | collective-permute-start | bytes 442376 | tf_op jit(solution)/shard_map/ppermute | solution.py:117
  10.1 14.4 %collective-permute-start.1 = (bf16[4,144,128]{2,1,0:T(8,128)(2,1)}, bf16[4,144,128]{2,1,0:T(8,128)(2,1)S(1)}, u32[]{:S(2)}, u32[]{:S(2)}) collective-permute-start(bf16[4,144,128]{2,1,0:T(8,128)(2,1)} %get-tuple-element.51), channel_id=1, source_target_pairs={{0,1},{2,3},{1,0},{3,2},{4,5},{6,7},{5,4},{7,6},{8,9},{10,11},{9,8... | collective-permute-start | bytes 442376 | tf_op jit(solution)/shard_map/ppermute | solution.py:117
  11.1 5.6 %copy-start.4 = (s32[16]{0:T(128)S(1)}, s32[16]{0:T(128)}, u32[]{:S(2)}) copy-start(s32[16]{0:T(128)} %param.17) | copy-start | bytes 196
  11.1 5.7 %copy-start.3 = (bf16[4,144,128]{2,1,0:T(8,128)(2,1)S(1)}, bf16[4,144,128]{2,1,0:T(8,128)(2,1)}, u32[]{:S(2)}) copy-start(bf16[4,144,128]{2,1,0:T(8,128)(2,1)} %get-tuple-element.52) | copy-start | bytes 442372
  11.1 9.2 %copy-start.2 = (bf16[4,144,128]{2,1,0:T(8,128)(2,1)S(1)}, bf16[4,144,128]{2,1,0:T(8,128)(2,1)}, u32[]{:S(2)}) copy-start(bf16[4,144,128]{2,1,0:T(8,128)(2,1)} %get-tuple-element.53) | copy-start | bytes 442372
  11.1 9.3 %copy-start.1 = (bf16[4,144,128]{2,1,0:T(8,128)(2,1)S(1)}, bf16[4,144,128]{2,1,0:T(8,128)(2,1)}, u32[]{:S(2)}) copy-start(bf16[4,144,128]{2,1,0:T(8,128)(2,1)} %get-tuple-element.60.refs_0_) | copy-start | bytes 442372
  16.8 13.8 %collective-permute-start.2 = (bf16[4,144,128]{2,1,0:T(8,128)(2,1)S(1)}, bf16[4,144,128]{2,1,0:T(8,128)(2,1)S(1)}, u32[]{:S(2)}, u32[]{:S(2)}) collective-permute-start(bf16[4,144,128]{2,1,0:T(8,128)(2,1)S(1)} %copy-done.3), channel_id=1, source_target_pairs={{0,2},{1,3},{2,0},{3,1},{4,6},{5,7},{6,4},{7,5},{8,10},{9,11},{10,... | collective-permute-start | bytes 442376 | tf_op jit(solution)/shard_map/ppermute | solution.py:117
  20.3 10.3 %collective-permute-start.3 = (bf16[4,144,128]{2,1,0:T(8,128)(2,1)S(1)}, bf16[4,144,128]{2,1,0:T(8,128)(2,1)S(1)}, u32[]{:S(2)}, u32[]{:S(2)}) collective-permute-start(bf16[4,144,128]{2,1,0:T(8,128)(2,1)S(1)} %copy-done.2), channel_id=1, source_target_pairs={{0,3},{1,2},{3,0},{2,1},{4,7},{5,6},{7,4},{6,5},{8,11},{9,10},{11,... | collective-permute-start | bytes 442376 | tf_op jit(solution)/shard_map/ppermute | solution.py:117
  20.4 10.2 %copy-start = (bf16[4,144,128]{2,1,0:T(8,128)(2,1)S(1)}, bf16[4,144,128]{2,1,0:T(8,128)(2,1)}, u32[]{:S(2)}) copy-start(bf16[4,144,128]{2,1,0:T(8,128)(2,1)} %get-tuple-element.50.refs_0_) | copy-start | bytes 442372
  20.5 13.8 %collective-permute-start.11 = (bf16[3,4,144,128]{3,2,1,0:T(8,128)(2,1)S(1)}, bf16[3,4,144,128]{3,2,1,0:T(8,128)(2,1)S(1)}, u32[]{:S(2)}, u32[]{:S(2)}) collective-permute-start(bf16[3,4,144,128]{3,2,1,0:T(8,128)(2,1)S(1)} %get-tuple-element.64), channel_id=1, source_target_pairs={{4,8},{12,16},{20,24},{8,4},{16,12},{24,20},{5,9},{13,17},{21,25},... | collective-permute-start | bytes 1327112 | tf_op jit(solution)/shard_map/ppermute | solution.py:117
  21.2 13.1 %collective-permute-start.12 = (bf16[3,4,144,128]{3,2,1,0:T(8,128)(2,1)S(1)}, bf16[3,4,144,128]{3,2,1,0:T(8,128)(2,1)S(1)}, u32[]{:S(2)}, u32[]{:S(2)}) collective-permute-start(bf16[3,4,144,128]{3,2,1,0:T(8,128)(2,1)S(1)} %get-tuple-element.65), channel_id=1, source_target_pairs={{0,4},{8,12},{16,20},{24,28},{4,0},{12,8},{20,16},{28,24},{1,5},{9... | collective-permute-start | bytes 1327112 | tf_op jit(solution)/shard_map/ppermute | solution.py:117
  30.7 10.8 %collective-permute-start.4 = (bf16[3,4,144,128]{3,2,1,0:T(8,128)(2,1)S(1)}, bf16[3,4,144,128]{3,2,1,0:T(8,128)(2,1)S(1)}, u32[]{:S(2)}, u32[]{:S(2)}) collective-permute-start(bf16[3,4,144,128]{3,2,1,0:T(8,128)(2,1)S(1)} %get-tuple-element.54), channel_id=1, source_target_pairs={{4,8},{12,16},{20,24},{8,4},{16,12},{24,20},{5,9},{13,17},{21,25},... | collective-permute-start | bytes 1327112 | tf_op jit(solution)/shard_map/ppermute | solution.py:117
  31.4 10.1 %collective-permute-start.5 = (bf16[3,4,144,128]{3,2,1,0:T(8,128)(2,1)S(1)}, bf16[3,4,144,128]{3,2,1,0:T(8,128)(2,1)S(1)}, u32[]{:S(2)}, u32[]{:S(2)}) collective-permute-start(bf16[3,4,144,128]{3,2,1,0:T(8,128)(2,1)S(1)} %get-tuple-element.55), channel_id=1, source_target_pairs={{0,4},{8,12},{16,20},{24,28},{4,0},{12,8},{20,16},{28,24},{1,5},{9... | collective-permute-start | bytes 1327112 | tf_op jit(solution)/shard_map/ppermute | solution.py:117
  35.9 13.3 %collective-permute-start.13 = (bf16[3,144,128]{2,1,0:T(8,128)(2,1)S(1)}, bf16[3,144,128]{2,1,0:T(8,128)(2,1)S(1)}, u32[]{:S(2)}, u32[]{:S(2)}) collective-permute-start(bf16[3,144,128]{2,1,0:T(8,128)(2,1)S(1)} %get-tuple-element.66), channel_id=1, source_target_pairs={{0,2},{1,3},{2,0},{3,1},{4,6},{5,7},{6,4},{7,5},{8,10},{9,11},{10,... | collective-permute-start | bytes 331784 | tf_op jit(solution)/shard_map/ppermute | solution.py:117
  40.9 8.3 %collective-permute-start.14 = (bf16[3,144,128]{2,1,0:T(8,128)(2,1)S(1)}, bf16[3,144,128]{2,1,0:T(8,128)(2,1)S(1)}, u32[]{:S(2)}, u32[]{:S(2)}) collective-permute-start(bf16[3,144,128]{2,1,0:T(8,128)(2,1)S(1)} %get-tuple-element.67), channel_id=1, source_target_pairs={{0,3},{1,2},{3,0},{2,1},{4,7},{5,6},{7,4},{6,5},{8,11},{9,10},{11,... | collective-permute-start | bytes 331784 | tf_op jit(solution)/shard_map/ppermute | solution.py:117
  41.3 8.9 %collective-permute-start.15 = (bf16[3,144,128]{2,1,0:T(8,128)(2,1)S(1)}, bf16[3,144,128]{2,1,0:T(8,128)(2,1)S(1)}, u32[]{:S(2)}, u32[]{:S(2)}) collective-permute-start(bf16[3,144,128]{2,1,0:T(8,128)(2,1)S(1)} %get-tuple-element.69), channel_id=1, source_target_pairs={{0,1},{2,3},{1,0},{3,2},{4,5},{6,7},{5,4},{7,6},{8,9},{10,11},{9,8... | collective-permute-start | bytes 331784 | tf_op jit(solution)/shard_map/ppermute | solution.py:117
  43.1 15.6 %collective-permute-start.6 = (bf16[3,144,128]{2,1,0:T(8,128)(2,1)S(1)}, bf16[3,144,128]{2,1,0:T(8,128)(2,1)S(1)}, u32[]{:S(2)}, u32[]{:S(2)}) collective-permute-start(bf16[3,144,128]{2,1,0:T(8,128)(2,1)S(1)} %get-tuple-element.56), channel_id=1, source_target_pairs={{0,2},{1,3},{2,0},{3,1},{4,6},{5,7},{6,4},{7,5},{8,10},{9,11},{10,... | collective-permute-start | bytes 331784 | tf_op jit(solution)/shard_map/ppermute | solution.py:117
  46.9 11.8 %collective-permute-start.7 = (bf16[3,144,128]{2,1,0:T(8,128)(2,1)S(1)}, bf16[3,144,128]{2,1,0:T(8,128)(2,1)S(1)}, u32[]{:S(2)}, u32[]{:S(2)}) collective-permute-start(bf16[3,144,128]{2,1,0:T(8,128)(2,1)S(1)} %get-tuple-element.57), channel_id=1, source_target_pairs={{0,3},{1,2},{3,0},{2,1},{4,7},{5,6},{7,4},{6,5},{8,11},{9,10},{11,... | collective-permute-start | bytes 331784 | tf_op jit(solution)/shard_map/ppermute | solution.py:117
  49.2 10.1 %collective-permute-start.8 = (bf16[3,144,128]{2,1,0:T(8,128)(2,1)S(1)}, bf16[3,144,128]{2,1,0:T(8,128)(2,1)S(1)}, u32[]{:S(2)}, u32[]{:S(2)}) collective-permute-start(bf16[3,144,128]{2,1,0:T(8,128)(2,1)S(1)} %get-tuple-element.59), channel_id=1, source_target_pairs={{0,1},{2,3},{1,0},{3,2},{4,5},{6,7},{5,4},{7,6},{8,9},{10,11},{9,8... | collective-permute-start | bytes 331784 | tf_op jit(solution)/shard_map/ppermute | solution.py:117

commit v2 on v1

--- a/solution.py
+++ b/solution.py
@@ -110,7 +110,7 @@
 
 
 def far_first(n):
-    return [*range(n // 2, n), *range(n // 2)]
+    return [*reversed(range(n // 2, n)), *range(n // 2)]
 
 
 def swap(block, axis, pairs):

time: 60.5 us -> 60.5 us (level)
  starting transfers between devices: 27.5 us -> 28.4 us
  waiting for transfers between devices: 17.2 us -> 16.5 us
    ppermute x16, starting transfers between devices: 27.5 us -> 28.4 us  [swap(): lax.ppermute(block, axis, [(i, j) for i, j in pairs] + [(j, i) for i, j i...]
    ppermute x16, waiting for transfers between devices: 17.2 us -> 16.5 us  [swap(): lax.ppermute(block, axis, [(i, j) for i, j in pairs] + [(j, i) for i, j i...]
  transfers between devices with their start and end apart: 16 -> 16, of which waited for: 5 -> 3; matrix products, arithmetic and copies ran while one was open for 0% -> 0% of each run, Pallas kernels for 19% -> 19%
where the time goes in v2:
time: 60.5 us; the launch traced here: 60.2 us
  starting transfers between devices  28.4 us (47%)
  waiting for transfers between devices  16.5 us (27%)
  Pallas kernels  14.2 us (23%)
  between operations  0.79 us (1%)
    ppermute x16, starting transfers between devices, swap(): lax.ppermute(block, axis, [(i, j) for i, j in pairs] + [(j, i) for i, j i...  28.4 us
    ppermute x16, waiting for transfers between devices, swap(): lax.ppermute(block, axis, [(i, j) for i, j in pairs] + [(j, i) for i, j i...  16.5 us
    pallas_call x1, Pallas kernels, space_grads(): pl.pallas_call(frame_kernel, out_shape=(shape, shape, shape), compiler_pa...  5.58 us
    pallas_call x2, Pallas kernels, split(): pl.pallas_call(functools.partial(split_kernel, sharing, rows, span), in_s...  3.77 us
    pallas_call x2, Pallas kernels, clip_grads(): pl.pallas_call(functools.partial(clip_kernel, window, heads), out_shape=[...  2.89 us
    pallas_call x2, Pallas kernels, join(): pl.pallas_call(functools.partial(join_kernel, sharing, span), in_specs=[p...  1.71 us
  transfers between devices with their start and end apart: 16, of which 3 were waited for; matrix products, arithmetic and copies ran while one was open for 0% of the time, Pallas kernels for 19%

profile of v2, /device:TPU:0, one launch (start us, length us, event | category | flops | bytes accessed | tf_op | source)
XLA Modules:
  0.0 60.2 jit_solution(5517093877318822671)
XLA Ops:
  0.6 1.9 %pack.3 = (bf16[4,144,128]{2,1,0:T(8,128)(2,1)}, bf16[4,144,128]{2,1,0:T(8,128)(2,1)}, bf16[4,144,128]{2,1,0:T(8,128)(2,1)}, bf16[4,144,128]{2,1,0:T(8,128)(2,1)}) custom-call(bf16[1,576,256]{2,1,0:T(8,128)(2,1)} %bitcast.18, bf16[1,576,256]{2,1,0:T(8,128)(2,1)} %bitcast.20, bf16[1,576,256]{2,1,0:T(8,128)(2,1)} %bitcast.22, bf16[1,576,256]{2,1,0:T(8,128)(2,1)} %bitcast.24), custom_call_target="tpu_custom_call" | custom-call | tf_op jit(solution)/shard_map/pack/pallas_call | solution.py:97
  2.5 4.1 %collective-permute-start = (bf16[4,144,128]{2,1,0:T(8,128)(2,1)}, bf16[4,144,128]{2,1,0:T(8,128)(2,1)S(1)}, u32[]{:S(2)}, u32[]{:S(2)}) collective-permute-start(bf16[4,144,128]{2,1,0:T(8,128)(2,1)} %get-tuple-element.43), channel_id=1, source_target_pairs={{0,2},{1,3},{2,0},{3,1},{4,6},{5,7},{6,4},{7,5},{8,10},{9,11},{10,... | collective-permute-start | bytes 442376 | tf_op jit(solution)/shard_map/ppermute | solution.py:117
  6.6 1.6 %collective-permute-start.9 = (bf16[4,144,128]{2,1,0:T(8,128)(2,1)}, bf16[4,144,128]{2,1,0:T(8,128)(2,1)S(1)}, u32[]{:S(2)}, u32[]{:S(2)}) collective-permute-start(bf16[4,144,128]{2,1,0:T(8,128)(2,1)} %get-tuple-element.61), channel_id=1, source_target_pairs={{0,1},{2,3},{1,0},{3,2},{4,5},{6,7},{5,4},{7,6},{8,9},{10,11},{9,8... | collective-permute-start | bytes 442376 | tf_op jit(solution)/shard_map/ppermute | solution.py:117
  8.2 0.0 collective-permute-start.10
  8.2 1.9 %pack.2 = (bf16[4,144,128]{2,1,0:T(8,128)(2,1)}, bf16[4,144,128]{2,1,0:T(8,128)(2,1)}, bf16[4,144,128]{2,1,0:T(8,128)(2,1)}, bf16[4,144,128]{2,1,0:T(8,128)(2,1)}) custom-call(bf16[1,576,256]{2,1,0:T(8,128)(2,1)} %bitcast.19, bf16[1,576,256]{2,1,0:T(8,128)(2,1)} %bitcast.21, bf16[1,576,256]{2,1,0:T(8,128)(2,1)} %bitcast.23, bf16[1,576,256]{2,1,0:T(8,128)(2,1)} %bitcast.25), custom_call_target="tpu_custom_call" | custom-call | tf_op jit(solution)/shard_map/pack/pallas_call | solution.py:97
  10.1 1.0 %collective-permute-start.1 = (bf16[4,144,128]{2,1,0:T(8,128)(2,1)}, bf16[4,144,128]{2,1,0:T(8,128)(2,1)S(1)}, u32[]{:S(2)}, u32[]{:S(2)}) collective-permute-start(bf16[4,144,128]{2,1,0:T(8,128)(2,1)} %get-tuple-element.51), channel_id=1, source_target_pairs={{0,1},{2,3},{1,0},{3,2},{4,5},{6,7},{5,4},{7,6},{8,9},{10,11},{9,8... | collective-permute-start | bytes 442376 | tf_op jit(solution)/shard_map/ppermute | solution.py:117
  11.1 0.0 copy-start.4
  11.1 0.0 copy-start.3
  11.1 0.0 copy-start.2
  11.1 0.0 copy-start.1
  11.1 5.6 %space.1 = (bf16[1,576,256]{2,1,0:T(8,128)(2,1)}, bf16[1,576,256]{2,1,0:T(8,128)(2,1)}, bf16[1,576,256]{2,1,0:T(8,128)(2,1)}) custom-call(bf16[1,576,256]{2,1,0:T(8,128)(2,1)} %bitcast.29, bf16[1,576,256]{2,1,0:T(8,128)(2,1)} %bitcast.30, bf16[1,576,256]{2,1,0:T(8,128)(2,1)} %bitcast.31, bf16[1,576,256]{2,1,0:T(8,128)(2,1)} %bitcast.32), custom_call_target="tpu_custom_call" | custom-call | flops 1610612736 | bytes 2064384 | tf_op jit(solution)/shard_map/space/pallas_call | solution.py:58
  16.7 0.0 copy-done.4
  16.7 0.1 select_reduce_fusion.2
  16.7 0.0 collective-permute-done.refs_2_
  16.7 0.0 copy-done.3
  16.8 3.6 %collective-permute-start.2 = (bf16[4,144,128]{2,1,0:T(8,128)(2,1)S(1)}, bf16[4,144,128]{2,1,0:T(8,128)(2,1)S(1)}, u32[]{:S(2)}, u32[]{:S(2)}) collective-permute-start(bf16[4,144,128]{2,1,0:T(8,128)(2,1)S(1)} %copy-done.3), channel_id=1, source_target_pairs={{0,2},{1,3},{2,0},{3,1},{4,6},{5,7},{6,4},{7,5},{8,10},{9,11},{10,... | collective-permute-start | bytes 442376 | tf_op jit(solution)/shard_map/ppermute | solution.py:117
  20.3 0.0 copy-done.2
  20.3 0.0 collective-permute-start.3
  20.3 0.0 collective-permute-done.9.refs_1_
  20.3 0.0 collective-permute-done.10.refs_3_
  20.4 0.0 copy-done.1
  20.4 0.0 copy-start
  20.4 0.1 sides.3
  20.5 0.7 %collective-permute-start.11 = (bf16[3,4,144,128]{3,2,1,0:T(8,128)(2,1)S(1)}, bf16[3,4,144,128]{3,2,1,0:T(8,128)(2,1)S(1)}, u32[]{:S(2)}, u32[]{:S(2)}) collective-permute-start(bf16[3,4,144,128]{3,2,1,0:T(8,128)(2,1)S(1)} %get-tuple-element.64), channel_id=1, source_target_pairs={{4,8},{12,16},{20,24},{8,4},{16,12},{24,20},{5,9},{13,17},{21,25},... | collective-permute-start | bytes 1327112 | tf_op jit(solution)/shard_map/ppermute | solution.py:117
  21.2 3.1 %collective-permute-start.12 = (bf16[3,4,144,128]{3,2,1,0:T(8,128)(2,1)S(1)}, bf16[3,4,144,128]{3,2,1,0:T(8,128)(2,1)S(1)}, u32[]{:S(2)}, u32[]{:S(2)}) collective-permute-start(bf16[3,4,144,128]{3,2,1,0:T(8,128)(2,1)S(1)} %get-tuple-element.65), channel_id=1, source_target_pairs={{0,4},{8,12},{16,20},{24,28},{4,0},{12,8},{20,16},{28,24},{1,5},{9... | collective-permute-start | bytes 1327112 | tf_op jit(solution)/shard_map/ppermute | solution.py:117
  24.3 0.2 select_reduce_fusion.1
  24.5 0.0 collective-permute-done.1.refs_1_
  24.5 6.1 %collective-permute-done.2.refs_2_ = bf16[4,144,128]{2,1,0:T(8,128)(2,1)S(1)} collective-permute-done((bf16[4,144,128]{2,1,0:T(8,128)(2,1)S(1)}, bf16[4,144,128]{2,1,0:T(8,128)(2,1)S(1)}, u32[]{:S(2)}, u32[]{:S(2)}) %collective-permute-start.2) | collective-permute-done | bytes 147488 | tf_op jit(solution)/shard_map/ppermute | solution.py:117
  30.6 0.0 collective-permute-done.3.refs_3_
  30.6 0.0 copy-done
  30.6 0.1 sides.2
  30.7 0.7 %collective-permute-start.4 = (bf16[3,4,144,128]{3,2,1,0:T(8,128)(2,1)S(1)}, bf16[3,4,144,128]{3,2,1,0:T(8,128)(2,1)S(1)}, u32[]{:S(2)}, u32[]{:S(2)}) collective-permute-start(bf16[3,4,144,128]{3,2,1,0:T(8,128)(2,1)S(1)} %get-tuple-element.54), channel_id=1, source_target_pairs={{4,8},{12,16},{20,24},{8,4},{16,12},{24,20},{5,9},{13,17},{21,25},... | collective-permute-start | bytes 1327112 | tf_op jit(solution)/shard_map/ppermute | solution.py:117
  31.4 2.9 %collective-permute-start.5 = (bf16[3,4,144,128]{3,2,1,0:T(8,128)(2,1)S(1)}, bf16[3,4,144,128]{3,2,1,0:T(8,128)(2,1)S(1)}, u32[]{:S(2)}, u32[]{:S(2)}) collective-permute-start(bf16[3,4,144,128]{3,2,1,0:T(8,128)(2,1)S(1)} %get-tuple-element.55), channel_id=1, source_target_pairs={{0,4},{8,12},{16,20},{24,28},{4,0},{12,8},{20,16},{28,24},{1,5},{9... | collective-permute-start | bytes 1327112 | tf_op jit(solution)/shard_map/ppermute | solution.py:117
  34.3 0.0 collective-permute-done.11.refs_4_
  34.3 0.0 collective-permute-done.12.refs_5_
  34.3 1.4 %clips.3 = (bf16[3,144,128]{2,1,0:T(8,128)(2,1)S(1)}, bf16[3,144,128]{2,1,0:T(8,128)(2,1)S(1)}, bf16[3,144,128]{2,1,0:T(8,128)(2,1)S(1)}, bf16[3,144,128]{2,1,0:T(8,128)(2,1)S(1)}) custom-call(s32[2,10]{1,0:T(2,128)S(1)} %pad_add_fusion.given_bounds, bf16[4,144,128]{2,1,0:T(8,128)(2,1)S(1)} %copy-done.1, ...), custom_call_target="tpu_custom_call" | custom-call | flops 589824000 | bytes 1474560 | tf_op jit(solution)/shard_map/clips/pallas_call | solution.py:291
  35.8 2.9 %collective-permute-start.13 = (bf16[3,144,128]{2,1,0:T(8,128)(2,1)S(1)}, bf16[3,144,128]{2,1,0:T(8,128)(2,1)S(1)}, u32[]{:S(2)}, u32[]{:S(2)}) collective-permute-start(bf16[3,144,128]{2,1,0:T(8,128)(2,1)S(1)} %get-tuple-element.66), channel_id=1, source_target_pairs={{0,3},{1,2},{3,0},{2,1},{4,7},{5,6},{7,4},{6,5},{8,11},{9,10},{11,... | collective-permute-start | bytes 331784 | tf_op jit(solution)/shard_map/ppermute | solution.py:117
  38.7 2.2 %collective-permute-start.14 = (bf16[3,144,128]{2,1,0:T(8,128)(2,1)S(1)}, bf16[3,144,128]{2,1,0:T(8,128)(2,1)S(1)}, u32[]{:S(2)}, u32[]{:S(2)}) collective-permute-start(bf16[3,144,128]{2,1,0:T(8,128)(2,1)S(1)} %get-tuple-element.67), channel_id=1, source_target_pairs={{0,2},{1,3},{2,0},{3,1},{4,6},{5,7},{6,4},{7,5},{8,10},{9,11},{10,... | collective-permute-start | bytes 331784 | tf_op jit(solution)/shard_map/ppermute | solution.py:117
  40.9 0.5 collective-permute-start.15
  41.3 0.0 collective-permute-done.4.refs_4_
  41.3 0.0 collective-permute-done.5.refs_5_
  41.3 1.4 %clips.2 = (bf16[3,144,128]{2,1,0:T(8,128)(2,1)S(1)}, bf16[3,144,128]{2,1,0:T(8,128)(2,1)S(1)}, bf16[3,144,128]{2,1,0:T(8,128)(2,1)S(1)}, bf16[3,144,128]{2,1,0:T(8,128)(2,1)S(1)}) custom-call(s32[2,10]{1,0:T(2,128)S(1)} %pad_add_fusion.given_bounds, bf16[4,144,128]{2,1,0:T(8,128)(2,1)S(1)} %copy-done, ...), custom_call_target="tpu_custom_call" | custom-call | flops 589824000 | bytes 1474560 | tf_op jit(solution)/shard_map/clips/pallas_call | solution.py:291
  42.8 2.4 %collective-permute-start.6 = (bf16[3,144,128]{2,1,0:T(8,128)(2,1)S(1)}, bf16[3,144,128]{2,1,0:T(8,128)(2,1)S(1)}, u32[]{:S(2)}, u32[]{:S(2)}) collective-permute-start(bf16[3,144,128]{2,1,0:T(8,128)(2,1)S(1)} %get-tuple-element.56), channel_id=1, source_target_pairs={{0,3},{1,2},{3,0},{2,1},{4,7},{5,6},{7,4},{6,5},{8,11},{9,10},{11,... | collective-permute-start | bytes 331784 | tf_op jit(solution)/shard_map/ppermute | solution.py:117
  45.2 0.6 %collective-permute-start.7 = (bf16[3,144,128]{2,1,0:T(8,128)(2,1)S(1)}, bf16[3,144,128]{2,1,0:T(8,128)(2,1)S(1)}, u32[]{:S(2)}, u32[]{:S(2)}) collective-permute-start(bf16[3,144,128]{2,1,0:T(8,128)(2,1)S(1)} %get-tuple-element.57), channel_id=1, source_target_pairs={{0,2},{1,3},{2,0},{3,1},{4,6},{5,7},{6,4},{7,5},{8,10},{9,11},{10,... | collective-permute-start | bytes 331784 | tf_op jit(solution)/shard_map/ppermute | solution.py:117
  45.9 0.0 collective-permute-done.13.refs_0_
  45.9 2.2 %collective-permute-start.8 = (bf16[3,144,128]{2,1,0:T(8,128)(2,1)S(1)}, bf16[3,144,128]{2,1,0:T(8,128)(2,1)S(1)}, u32[]{:S(2)}, u32[]{:S(2)}) collective-permute-start(bf16[3,144,128]{2,1,0:T(8,128)(2,1)S(1)} %get-tuple-element.59), channel_id=1, source_target_pairs={{0,1},{2,3},{1,0},{3,2},{4,5},{6,7},{5,4},{7,6},{8,9},{10,11},{9,8... | collective-permute-start | bytes 331784 | tf_op jit(solution)/shard_map/ppermute | solution.py:117
  48.0 5.4 %collective-permute-done.14.refs_1_ = bf16[3,144,128]{2,1,0:T(8,128)(2,1)S(1)} collective-permute-done((bf16[3,144,128]{2,1,0:T(8,128)(2,1)S(1)}, bf16[3,144,128]{2,1,0:T(8,128)(2,1)S(1)}, u32[]{:S(2)}, u32[]{:S(2)}) %collective-permute-start.14) | collective-permute-done | bytes 110624 | tf_op jit(solution)/shard_map/ppermute | solution.py:117
  53.4 0.0 collective-permute-done.15.refs_3_
  53.4 0.9 %unpack.2 = (bf16[1,576,256]{2,1,0:T(8,128)(2,1)}, bf16[1,576,256]{2,1,0:T(8,128)(2,1)}, bf16[1,576,256]{2,1,0:T(8,128)(2,1)}) custom-call(bf16[3,144,128]{2,1,0:T(8,128)(2,1)S(1)} %collective-permute-done.13.refs_0_, bf16[3,144,128]{2,1,0:T(8,128)(2,1)S(1)} %collective-permute-done.14.refs_1_, bf16[3,144,128]{2,1,0:T(8,128)(2,1)S(1)} %get-tuple-element.68.refs_2_, ...), custom_call_target="tpu_custom_call" | custom-call | tf_op jit(solution)/shard_map/unpack/pallas_call | solution.py:185
  54.3 0.0 collective-permute-done.6.refs_0_
  54.3 5.0 %collective-permute-done.7.refs_1_ = bf16[3,144,128]{2,1,0:T(8,128)(2,1)S(1)} collective-permute-done((bf16[3,144,128]{2,1,0:T(8,128)(2,1)S(1)}, bf16[3,144,128]{2,1,0:T(8,128)(2,1)S(1)}, u32[]{:S(2)}, u32[]{:S(2)}) %collective-permute-start.7) | collective-permute-done | bytes 110624 | tf_op jit(solution)/shard_map/ppermute | solution.py:117
  59.3 0.0 collective-permute-done.8.refs_3_
  59.3 0.9 %unpack.3 = (bf16[1,576,256]{2,1,0:T(8,128)(2,1)}, bf16[1,576,256]{2,1,0:T(8,128)(2,1)}, bf16[1,576,256]{2,1,0:T(8,128)(2,1)}) custom-call(bf16[3,144,128]{2,1,0:T(8,128)(2,1)S(1)} %collective-permute-done.6.refs_0_, bf16[3,144,128]{2,1,0:T(8,128)(2,1)S(1)} %collective-permute-done.7.refs_1_, ...), custom_call_target="tpu_custom_call", output_to_operand_aliasing={{0}: (4, {}), {1}: (5, {}), {2}: (6, {})} | custom-call | tf_op jit(solution)/shard_map/unpack/pallas_call | solution.py:185
  (4 shorter events, 0.0 us)
Async XLA Ops:
  2.5 14.2 %collective-permute-start = (bf16[4,144,128]{2,1,0:T(8,128)(2,1)}, bf16[4,144,128]{2,1,0:T(8,128)(2,1)S(1)}, u32[]{:S(2)}, u32[]{:S(2)}) collective-permute-start(bf16[4,144,128]{2,1,0:T(8,128)(2,1)} %get-tuple-element.43), channel_id=1, source_target_pairs={{0,2},{1,3},{2,0},{3,1},{4,6},{5,7},{6,4},{7,5},{8,10},{9,11},{10,... | collective-permute-start | bytes 442376 | tf_op jit(solution)/shard_map/ppermute | solution.py:117
  6.6 13.7 %collective-permute-start.9 = (bf16[4,144,128]{2,1,0:T(8,128)(2,1)}, bf16[4,144,128]{2,1,0:T(8,128)(2,1)S(1)}, u32[]{:S(2)}, u32[]{:S(2)}) collective-permute-start(bf16[4,144,128]{2,1,0:T(8,128)(2,1)} %get-tuple-element.61), channel_id=1, source_target_pairs={{0,1},{2,3},{1,0},{3,2},{4,5},{6,7},{5,4},{7,6},{8,9},{10,11},{9,8... | collective-permute-start | bytes 442376 | tf_op jit(solution)/shard_map/ppermute | solution.py:117
  8.2 12.1 %collective-permute-start.10 = (bf16[4,144,128]{2,1,0:T(8,128)(2,1)}, bf16[4,144,128]{2,1,0:T(8,128)(2,1)S(1)}, u32[]{:S(2)}, u32[]{:S(2)}) collective-permute-start(bf16[4,144,128]{2,1,0:T(8,128)(2,1)} %get-tuple-element.63), channel_id=1, source_target_pairs={{0,3},{1,2},{3,0},{2,1},{4,7},{5,6},{7,4},{6,5},{8,11},{9,10},{11,... | collective-permute-start | bytes 442376 | tf_op jit(solution)/shard_map/ppermute | solution.py:117
  10.1 14.4 %collective-permute-start.1 = (bf16[4,144,128]{2,1,0:T(8,128)(2,1)}, bf16[4,144,128]{2,1,0:T(8,128)(2,1)S(1)}, u32[]{:S(2)}, u32[]{:S(2)}) collective-permute-start(bf16[4,144,128]{2,1,0:T(8,128)(2,1)} %get-tuple-element.51), channel_id=1, source_target_pairs={{0,1},{2,3},{1,0},{3,2},{4,5},{6,7},{5,4},{7,6},{8,9},{10,11},{9,8... | collective-permute-start | bytes 442376 | tf_op jit(solution)/shard_map/ppermute | solution.py:117
  11.1 5.6 %copy-start.4 = (s32[16]{0:T(128)S(1)}, s32[16]{0:T(128)}, u32[]{:S(2)}) copy-start(s32[16]{0:T(128)} %param.17) | copy-start | bytes 196
  11.1 5.7 %copy-start.3 = (bf16[4,144,128]{2,1,0:T(8,128)(2,1)S(1)}, bf16[4,144,128]{2,1,0:T(8,128)(2,1)}, u32[]{:S(2)}) copy-start(bf16[4,144,128]{2,1,0:T(8,128)(2,1)} %get-tuple-element.52) | copy-start | bytes 442372
  11.1 9.2 %copy-start.2 = (bf16[4,144,128]{2,1,0:T(8,128)(2,1)S(1)}, bf16[4,144,128]{2,1,0:T(8,128)(2,1)}, u32[]{:S(2)}) copy-start(bf16[4,144,128]{2,1,0:T(8,128)(2,1)} %get-tuple-element.53) | copy-start | bytes 442372
  11.1 9.3 %copy-start.1 = (bf16[4,144,128]{2,1,0:T(8,128)(2,1)S(1)}, bf16[4,144,128]{2,1,0:T(8,128)(2,1)}, u32[]{:S(2)}) copy-start(bf16[4,144,128]{2,1,0:T(8,128)(2,1)} %get-tuple-element.60.refs_0_) | copy-start | bytes 442372
  16.8 13.8 %collective-permute-start.2 = (bf16[4,144,128]{2,1,0:T(8,128)(2,1)S(1)}, bf16[4,144,128]{2,1,0:T(8,128)(2,1)S(1)}, u32[]{:S(2)}, u32[]{:S(2)}) collective-permute-start(bf16[4,144,128]{2,1,0:T(8,128)(2,1)S(1)} %copy-done.3), channel_id=1, source_target_pairs={{0,2},{1,3},{2,0},{3,1},{4,6},{5,7},{6,4},{7,5},{8,10},{9,11},{10,... | collective-permute-start | bytes 442376 | tf_op jit(solution)/shard_map/ppermute | solution.py:117
  20.3 10.3 %collective-permute-start.3 = (bf16[4,144,128]{2,1,0:T(8,128)(2,1)S(1)}, bf16[4,144,128]{2,1,0:T(8,128)(2,1)S(1)}, u32[]{:S(2)}, u32[]{:S(2)}) collective-permute-start(bf16[4,144,128]{2,1,0:T(8,128)(2,1)S(1)} %copy-done.2), channel_id=1, source_target_pairs={{0,3},{1,2},{3,0},{2,1},{4,7},{5,6},{7,4},{6,5},{8,11},{9,10},{11,... | collective-permute-start | bytes 442376 | tf_op jit(solution)/shard_map/ppermute | solution.py:117
  20.4 10.2 %copy-start = (bf16[4,144,128]{2,1,0:T(8,128)(2,1)S(1)}, bf16[4,144,128]{2,1,0:T(8,128)(2,1)}, u32[]{:S(2)}) copy-start(bf16[4,144,128]{2,1,0:T(8,128)(2,1)} %get-tuple-element.50.refs_0_) | copy-start | bytes 442372
  20.5 13.8 %collective-permute-start.11 = (bf16[3,4,144,128]{3,2,1,0:T(8,128)(2,1)S(1)}, bf16[3,4,144,128]{3,2,1,0:T(8,128)(2,1)S(1)}, u32[]{:S(2)}, u32[]{:S(2)}) collective-permute-start(bf16[3,4,144,128]{3,2,1,0:T(8,128)(2,1)S(1)} %get-tuple-element.64), channel_id=1, source_target_pairs={{4,8},{12,16},{20,24},{8,4},{16,12},{24,20},{5,9},{13,17},{21,25},... | collective-permute-start | bytes 1327112 | tf_op jit(solution)/shard_map/ppermute | solution.py:117
  21.2 13.1 %collective-permute-start.12 = (bf16[3,4,144,128]{3,2,1,0:T(8,128)(2,1)S(1)}, bf16[3,4,144,128]{3,2,1,0:T(8,128)(2,1)S(1)}, u32[]{:S(2)}, u32[]{:S(2)}) collective-permute-start(bf16[3,4,144,128]{3,2,1,0:T(8,128)(2,1)S(1)} %get-tuple-element.65), channel_id=1, source_target_pairs={{0,4},{8,12},{16,20},{24,28},{4,0},{12,8},{20,16},{28,24},{1,5},{9... | collective-permute-start | bytes 1327112 | tf_op jit(solution)/shard_map/ppermute | solution.py:117
  30.7 10.6 %collective-permute-start.4 = (bf16[3,4,144,128]{3,2,1,0:T(8,128)(2,1)S(1)}, bf16[3,4,144,128]{3,2,1,0:T(8,128)(2,1)S(1)}, u32[]{:S(2)}, u32[]{:S(2)}) collective-permute-start(bf16[3,4,144,128]{3,2,1,0:T(8,128)(2,1)S(1)} %get-tuple-element.54), channel_id=1, source_target_pairs={{4,8},{12,16},{20,24},{8,4},{16,12},{24,20},{5,9},{13,17},{21,25},... | collective-permute-start | bytes 1327112 | tf_op jit(solution)/shard_map/ppermute | solution.py:117
  31.4 9.9 %collective-permute-start.5 = (bf16[3,4,144,128]{3,2,1,0:T(8,128)(2,1)S(1)}, bf16[3,4,144,128]{3,2,1,0:T(8,128)(2,1)S(1)}, u32[]{:S(2)}, u32[]{:S(2)}) collective-permute-start(bf16[3,4,144,128]{3,2,1,0:T(8,128)(2,1)S(1)} %get-tuple-element.55), channel_id=1, source_target_pairs={{0,4},{8,12},{16,20},{24,28},{4,0},{12,8},{20,16},{28,24},{1,5},{9... | collective-permute-start | bytes 1327112 | tf_op jit(solution)/shard_map/ppermute | solution.py:117
  35.8 10.1 %collective-permute-start.13 = (bf16[3,144,128]{2,1,0:T(8,128)(2,1)S(1)}, bf16[3,144,128]{2,1,0:T(8,128)(2,1)S(1)}, u32[]{:S(2)}, u32[]{:S(2)}) collective-permute-start(bf16[3,144,128]{2,1,0:T(8,128)(2,1)S(1)} %get-tuple-element.66), channel_id=1, source_target_pairs={{0,3},{1,2},{3,0},{2,1},{4,7},{5,6},{7,4},{6,5},{8,11},{9,10},{11,... | collective-permute-start | bytes 331784 | tf_op jit(solution)/shard_map/ppermute | solution.py:117
  38.7 14.8 %collective-permute-start.14 = (bf16[3,144,128]{2,1,0:T(8,128)(2,1)S(1)}, bf16[3,144,128]{2,1,0:T(8,128)(2,1)S(1)}, u32[]{:S(2)}, u32[]{:S(2)}) collective-permute-start(bf16[3,144,128]{2,1,0:T(8,128)(2,1)S(1)} %get-tuple-element.67), channel_id=1, source_target_pairs={{0,2},{1,3},{2,0},{3,1},{4,6},{5,7},{6,4},{7,5},{8,10},{9,11},{10,... | collective-permute-start | bytes 331784 | tf_op jit(solution)/shard_map/ppermute | solution.py:117
  40.9 12.6 %collective-permute-start.15 = (bf16[3,144,128]{2,1,0:T(8,128)(2,1)S(1)}, bf16[3,144,128]{2,1,0:T(8,128)(2,1)S(1)}, u32[]{:S(2)}, u32[]{:S(2)}) collective-permute-start(bf16[3,144,128]{2,1,0:T(8,128)(2,1)S(1)} %get-tuple-element.69), channel_id=1, source_target_pairs={{0,1},{2,3},{1,0},{3,2},{4,5},{6,7},{5,4},{7,6},{8,9},{10,11},{9,8... | collective-permute-start | bytes 331784 | tf_op jit(solution)/shard_map/ppermute | solution.py:117
  42.8 11.5 %collective-permute-start.6 = (bf16[3,144,128]{2,1,0:T(8,128)(2,1)S(1)}, bf16[3,144,128]{2,1,0:T(8,128)(2,1)S(1)}, u32[]{:S(2)}, u32[]{:S(2)}) collective-permute-start(bf16[3,144,128]{2,1,0:T(8,128)(2,1)S(1)} %get-tuple-element.56), channel_id=1, source_target_pairs={{0,3},{1,2},{3,0},{2,1},{4,7},{5,6},{7,4},{6,5},{8,11},{9,10},{11,... | collective-permute-start | bytes 331784 | tf_op jit(solution)/shard_map/ppermute | solution.py:117
  45.2 14.1 %collective-permute-start.7 = (bf16[3,144,128]{2,1,0:T(8,128)(2,1)S(1)}, bf16[3,144,128]{2,1,0:T(8,128)(2,1)S(1)}, u32[]{:S(2)}, u32[]{:S(2)}) collective-permute-start(bf16[3,144,128]{2,1,0:T(8,128)(2,1)S(1)} %get-tuple-element.57), channel_id=1, source_target_pairs={{0,2},{1,3},{2,0},{3,1},{4,6},{5,7},{6,4},{7,5},{8,10},{9,11},{10,... | collective-permute-start | bytes 331784 | tf_op jit(solution)/shard_map/ppermute | solution.py:117
  45.9 13.4 %collective-permute-start.8 = (bf16[3,144,128]{2,1,0:T(8,128)(2,1)S(1)}, bf16[3,144,128]{2,1,0:T(8,128)(2,1)S(1)}, u32[]{:S(2)}, u32[]{:S(2)}) collective-permute-start(bf16[3,144,128]{2,1,0:T(8,128)(2,1)S(1)} %get-tuple-element.59), channel_id=1, source_target_pairs={{0,1},{2,3},{1,0},{3,2},{4,5},{6,7},{5,4},{7,6},{8,9},{10,11},{9,8... | collective-permute-start | bytes 331784 | tf_op jit(solution)/shard_map/ppermute | solution.py:117

commit v3 on v2

--- a/solution.py
+++ b/solution.py
@@ -342,11 +342,9 @@
         spans.append(slice(head * HDIM, (head + heads) * HDIM))
         head += heads
     space_in = turned(q_space, k_space, v_space, cot_space)
-    packed = [list(split(time, span, n, sharing)) for span in spans]
-    own = [exchange(packed[0])]
+    packed = [split(time, span, n, sharing) for span in spans]
+    own = [exchange(blocks) for blocks in packed]
     space = space_grads(*space_in)
-    packed[1][2:], own[0][2], space = gated(packed[1][2:], own[0][2], space)
-    own.append(exchange(packed[1]))
     beside = [
         [neighbours(ends, start) for ends, start in zip(sides(blocks), (1, 0))] for blocks in own
     ]

time: 60.5 us -> 61.2 us (1.012)
  starting transfers between devices: 28.4 us -> 30.9 us
  waiting for transfers between devices: 16.5 us -> 14.9 us
    ppermute x16, starting transfers between devices: 28.4 us -> 30.9 us  [swap(): lax.ppermute(block, axis, [(i, j) for i, j in pairs] + [(j, i) for i, j i...]
    ppermute x16, waiting for transfers between devices: 16.5 us -> 14.9 us  [swap(): lax.ppermute(block, axis, [(i, j) for i, j in pairs] + [(j, i) for i, j i...]
  transfers between devices with their start and end apart: 16 -> 16, of which waited for: 3 -> 4; matrix products, arithmetic and copies ran while one was open for 0% -> 0% of each run, Pallas kernels for 19% -> 19%
where the time goes in v3:
time: 61.2 us; the launch traced here: 61 us
  starting transfers between devices  30.9 us (50%)
  waiting for transfers between devices  14.9 us (24%)
  Pallas kernels  14.1 us (23%)
  between operations  0.75 us (1%)
    ppermute x16, starting transfers between devices, swap(): lax.ppermute(block, axis, [(i, j) for i, j in pairs] + [(j, i) for i, j i...  30.9 us
    ppermute x16, waiting for transfers between devices, swap(): lax.ppermute(block, axis, [(i, j) for i, j in pairs] + [(j, i) for i, j i...  14.9 us
    pallas_call x1, Pallas kernels, space_grads(): pl.pallas_call(frame_kernel, out_shape=(shape, shape, shape), compiler_pa...  5.53 us
    pallas_call x2, Pallas kernels, split(): pl.pallas_call(functools.partial(split_kernel, sharing, rows, span), in_s...  3.76 us
    pallas_call x2, Pallas kernels, clip_grads(): pl.pallas_call(functools.partial(clip_kernel, window, heads), out_shape=[...  2.89 us
    pallas_call x2, Pallas kernels, join(): pl.pallas_call(functools.partial(join_kernel, sharing, span), in_specs=[p...  1.71 us
  transfers between devices with their start and end apart: 16, of which 4 were waited for; matrix products, arithmetic and copies ran while one was open for 0% of the time, Pallas kernels for 19%

profile of v3, /device:TPU:0, one launch (start us, length us, event | category | flops | bytes accessed | tf_op | source)
XLA Modules:
  0.0 61.0 jit_solution(12871220020392421816)
XLA Ops:
  0.6 1.9 %pack.3 = (bf16[4,144,128]{2,1,0:T(8,128)(2,1)}, bf16[4,144,128]{2,1,0:T(8,128)(2,1)}, bf16[4,144,128]{2,1,0:T(8,128)(2,1)}, bf16[4,144,128]{2,1,0:T(8,128)(2,1)}) custom-call(bf16[1,576,256]{2,1,0:T(8,128)(2,1)} %bitcast.18, bf16[1,576,256]{2,1,0:T(8,128)(2,1)} %bitcast.20, bf16[1,576,256]{2,1,0:T(8,128)(2,1)} %bitcast.22, bf16[1,576,256]{2,1,0:T(8,128)(2,1)} %bitcast.24), custom_call_target="tpu_custom_call" | custom-call | tf_op jit(solution)/shard_map/pack/pallas_call | solution.py:97
  2.5 5.1 %collective-permute-start.10 = (bf16[4,144,128]{2,1,0:T(8,128)(2,1)}, bf16[4,144,128]{2,1,0:T(8,128)(2,1)S(1)}, u32[]{:S(2)}, u32[]{:S(2)}) collective-permute-start(bf16[4,144,128]{2,1,0:T(8,128)(2,1)} %get-tuple-element.51), channel_id=1, source_target_pairs={{0,3},{1,2},{3,0},{2,1},{4,7},{5,6},{7,4},{6,5},{8,11},{9,10},{11,... | collective-permute-start | bytes 442376 | tf_op jit(solution)/shard_map/ppermute | solution.py:117
  7.6 0.0 collective-permute-start.8
  7.7 0.0 copy-start.1
  7.7 0.6 %collective-permute-start.9 = (bf16[4,144,128]{2,1,0:T(8,128)(2,1)}, bf16[4,144,128]{2,1,0:T(8,128)(2,1)S(1)}, u32[]{:S(2)}, u32[]{:S(2)}) collective-permute-start(bf16[4,144,128]{2,1,0:T(8,128)(2,1)} %get-tuple-element.50), channel_id=1, source_target_pairs={{0,2},{1,3},{2,0},{3,1},{4,6},{5,7},{6,4},{7,5},{8,10},{9,11},{10,... | collective-permute-start | bytes 442376 | tf_op jit(solution)/shard_map/ppermute | solution.py:117
  8.3 1.9 %pack.2 = (bf16[4,144,128]{2,1,0:T(8,128)(2,1)}, bf16[4,144,128]{2,1,0:T(8,128)(2,1)}, bf16[4,144,128]{2,1,0:T(8,128)(2,1)}, bf16[4,144,128]{2,1,0:T(8,128)(2,1)}) custom-call(bf16[1,576,256]{2,1,0:T(8,128)(2,1)} %bitcast.19, bf16[1,576,256]{2,1,0:T(8,128)(2,1)} %bitcast.21, bf16[1,576,256]{2,1,0:T(8,128)(2,1)} %bitcast.23, bf16[1,576,256]{2,1,0:T(8,128)(2,1)} %bitcast.25), custom_call_target="tpu_custom_call" | custom-call | tf_op jit(solution)/shard_map/pack/pallas_call | solution.py:97
  10.2 0.0 copy-start.2
  10.2 1.5 %collective-permute-start = (bf16[4,144,128]{2,1,0:T(8,128)(2,1)}, bf16[4,144,128]{2,1,0:T(8,128)(2,1)S(1)}, u32[]{:S(2)}, u32[]{:S(2)}) collective-permute-start(bf16[4,144,128]{2,1,0:T(8,128)(2,1)} %get-tuple-element.39), channel_id=1, source_target_pairs={{0,1},{2,3},{1,0},{3,2},{4,5},{6,7},{5,4},{7,6},{8,9},{10,11},{9,8... | collective-permute-start | bytes 442376 | tf_op jit(solution)/shard_map/ppermute | solution.py:117
  11.7 2.9 %collective-permute-start.1 = (bf16[4,144,128]{2,1,0:T(8,128)(2,1)}, bf16[4,144,128]{2,1,0:T(8,128)(2,1)S(1)}, u32[]{:S(2)}, u32[]{:S(2)}) collective-permute-start(bf16[4,144,128]{2,1,0:T(8,128)(2,1)} %get-tuple-element.40), channel_id=1, source_target_pairs={{0,2},{1,3},{2,0},{3,1},{4,6},{5,7},{6,4},{7,5},{8,10},{9,11},{10,... | collective-permute-start | bytes 442376 | tf_op jit(solution)/shard_map/ppermute | solution.py:117
  14.6 0.0 copy-done.2
  14.6 0.1 select_reduce_fusion.2
  14.6 0.0 collective-permute-done.10.refs_3_
  14.7 1.7 %collective-permute-start.2 = (bf16[4,144,128]{2,1,0:T(8,128)(2,1)}, bf16[4,144,128]{2,1,0:T(8,128)(2,1)S(1)}, u32[]{:S(2)}, u32[]{:S(2)}) collective-permute-start(bf16[4,144,128]{2,1,0:T(8,128)(2,1)} %get-tuple-element.41), channel_id=1, source_target_pairs={{0,3},{1,2},{3,0},{2,1},{4,7},{5,6},{7,4},{6,5},{8,11},{9,10},{11,... | collective-permute-start | bytes 442376 | tf_op jit(solution)/shard_map/ppermute | solution.py:117
  16.4 0.0 collective-permute-done.8.refs_1_
  16.4 5.8 %collective-permute-done.9.refs_2_ = bf16[4,144,128]{2,1,0:T(8,128)(2,1)S(1)} collective-permute-done((bf16[4,144,128]{2,1,0:T(8,128)(2,1)}, bf16[4,144,128]{2,1,0:T(8,128)(2,1)S(1)}, u32[]{:S(2)}, u32[]{:S(2)}) %collective-permute-start.9) | collective-permute-done | bytes 147488 | tf_op jit(solution)/shard_map/ppermute | solution.py:117
  22.2 0.0 copy-done.1
  22.2 0.0 copy-start
  22.2 0.1 sides.3
  22.3 0.7 %collective-permute-start.11 = (bf16[3,4,144,128]{3,2,1,0:T(8,128)(2,1)S(1)}, bf16[3,4,144,128]{3,2,1,0:T(8,128)(2,1)S(1)}, u32[]{:S(2)}, u32[]{:S(2)}) collective-permute-start(bf16[3,4,144,128]{3,2,1,0:T(8,128)(2,1)S(1)} %get-tuple-element.52), channel_id=1, source_target_pairs={{4,8},{12,16},{20,24},{8,4},{16,12},{24,20},{5,9},{13,17},{21,25},... | collective-permute-start | bytes 1327112 | tf_op jit(solution)/shard_map/ppermute | solution.py:117
  23.0 3.1 %collective-permute-start.12 = (bf16[3,4,144,128]{3,2,1,0:T(8,128)(2,1)S(1)}, bf16[3,4,144,128]{3,2,1,0:T(8,128)(2,1)S(1)}, u32[]{:S(2)}, u32[]{:S(2)}) collective-permute-start(bf16[3,4,144,128]{3,2,1,0:T(8,128)(2,1)S(1)} %get-tuple-element.53), channel_id=1, source_target_pairs={{0,4},{8,12},{16,20},{24,28},{4,0},{12,8},{20,16},{28,24},{1,5},{9... | collective-permute-start | bytes 1327112 | tf_op jit(solution)/shard_map/ppermute | solution.py:117
  26.1 0.2 select_reduce_fusion.1
  26.3 0.0 collective-permute-done.refs_1_
  26.3 4.5 %collective-permute-done.1.refs_2_ = bf16[4,144,128]{2,1,0:T(8,128)(2,1)S(1)} collective-permute-done((bf16[4,144,128]{2,1,0:T(8,128)(2,1)}, bf16[4,144,128]{2,1,0:T(8,128)(2,1)S(1)}, u32[]{:S(2)}, u32[]{:S(2)}) %collective-permute-start.1) | collective-permute-done | bytes 147488 | tf_op jit(solution)/shard_map/ppermute | solution.py:117
  30.8 0.0 collective-permute-done.2.refs_3_
  30.8 0.0 copy-done
  30.8 0.1 sides.2
  31.0 0.7 %collective-permute-start.3 = (bf16[3,4,144,128]{3,2,1,0:T(8,128)(2,1)S(1)}, bf16[3,4,144,128]{3,2,1,0:T(8,128)(2,1)S(1)}, u32[]{:S(2)}, u32[]{:S(2)}) collective-permute-start(bf16[3,4,144,128]{3,2,1,0:T(8,128)(2,1)S(1)} %get-tuple-element.42), channel_id=1, source_target_pairs={{4,8},{12,16},{20,24},{8,4},{16,12},{24,20},{5,9},{13,17},{21,25},... | collective-permute-start | bytes 1327112 | tf_op jit(solution)/shard_map/ppermute | solution.py:117
  31.7 2.9 %collective-permute-start.4 = (bf16[3,4,144,128]{3,2,1,0:T(8,128)(2,1)S(1)}, bf16[3,4,144,128]{3,2,1,0:T(8,128)(2,1)S(1)}, u32[]{:S(2)}, u32[]{:S(2)}) collective-permute-start(bf16[3,4,144,128]{3,2,1,0:T(8,128)(2,1)S(1)} %get-tuple-element.43), channel_id=1, source_target_pairs={{0,4},{8,12},{16,20},{24,28},{4,0},{12,8},{20,16},{28,24},{1,5},{9... | collective-permute-start | bytes 1327112 | tf_op jit(solution)/shard_map/ppermute | solution.py:117
  34.6 0.0 collective-permute-done.11.refs_4_
  34.6 0.0 collective-permute-done.12.refs_5_
  34.6 1.4 %clips.3 = (bf16[3,144,128]{2,1,0:T(8,128)(2,1)S(1)}, bf16[3,144,128]{2,1,0:T(8,128)(2,1)S(1)}, bf16[3,144,128]{2,1,0:T(8,128)(2,1)S(1)}, bf16[3,144,128]{2,1,0:T(8,128)(2,1)S(1)}) custom-call(s32[2,10]{1,0:T(2,128)S(1)} %pad_add_fusion.given_bounds, bf16[4,144,128]{2,1,0:T(8,128)(2,1)S(1)} %copy-done.1, ...), custom_call_target="tpu_custom_call" | custom-call | flops 589824000 | bytes 1474560 | tf_op jit(solution)/shard_map/clips/pallas_call | solution.py:291
  36.0 2.7 %collective-permute-start.13 = (bf16[3,144,128]{2,1,0:T(8,128)(2,1)S(1)}, bf16[3,144,128]{2,1,0:T(8,128)(2,1)S(1)}, u32[]{:S(2)}, u32[]{:S(2)}) collective-permute-start(bf16[3,144,128]{2,1,0:T(8,128)(2,1)S(1)} %get-tuple-element.54), channel_id=1, source_target_pairs={{0,3},{1,2},{3,0},{2,1},{4,7},{5,6},{7,4},{6,5},{8,11},{9,10},{11,... | collective-permute-start | bytes 331784 | tf_op jit(solution)/shard_map/ppermute | solution.py:117
  38.7 1.6 %collective-permute-start.14 = (bf16[3,144,128]{2,1,0:T(8,128)(2,1)S(1)}, bf16[3,144,128]{2,1,0:T(8,128)(2,1)S(1)}, u32[]{:S(2)}, u32[]{:S(2)}) collective-permute-start(bf16[3,144,128]{2,1,0:T(8,128)(2,1)S(1)} %get-tuple-element.55), channel_id=1, source_target_pairs={{0,2},{1,3},{2,0},{3,1},{4,6},{5,7},{6,4},{7,5},{8,10},{9,11},{10,... | collective-permute-start | bytes 331784 | tf_op jit(solution)/shard_map/ppermute | solution.py:117
  40.3 0.2 collective-permute-start.15
  40.5 0.0 collective-permute-done.3.refs_4_
  40.5 0.0 collective-permute-done.4.refs_5_
  40.5 1.4 %clips.2 = (bf16[3,144,128]{2,1,0:T(8,128)(2,1)S(1)}, bf16[3,144,128]{2,1,0:T(8,128)(2,1)S(1)}, bf16[3,144,128]{2,1,0:T(8,128)(2,1)S(1)}, bf16[3,144,128]{2,1,0:T(8,128)(2,1)S(1)}) custom-call(s32[2,10]{1,0:T(2,128)S(1)} %pad_add_fusion.given_bounds, bf16[4,144,128]{2,1,0:T(8,128)(2,1)S(1)} %copy-done, ...), custom_call_target="tpu_custom_call" | custom-call | flops 589824000 | bytes 1474560 | tf_op jit(solution)/shard_map/clips/pallas_call | solution.py:291
  41.9 2.7 %collective-permute-start.5 = (bf16[3,144,128]{2,1,0:T(8,128)(2,1)S(1)}, bf16[3,144,128]{2,1,0:T(8,128)(2,1)S(1)}, u32[]{:S(2)}, u32[]{:S(2)}) collective-permute-start(bf16[3,144,128]{2,1,0:T(8,128)(2,1)S(1)} %get-tuple-element.44), channel_id=1, source_target_pairs={{0,3},{1,2},{3,0},{2,1},{4,7},{5,6},{7,4},{6,5},{8,11},{9,10},{11,... | collective-permute-start | bytes 331784 | tf_op jit(solution)/shard_map/ppermute | solution.py:117
  44.6 0.7 %collective-permute-start.6 = (bf16[3,144,128]{2,1,0:T(8,128)(2,1)S(1)}, bf16[3,144,128]{2,1,0:T(8,128)(2,1)S(1)}, u32[]{:S(2)}, u32[]{:S(2)}) collective-permute-start(bf16[3,144,128]{2,1,0:T(8,128)(2,1)S(1)} %get-tuple-element.45), channel_id=1, source_target_pairs={{0,2},{1,3},{2,0},{3,1},{4,6},{5,7},{6,4},{7,5},{8,10},{9,11},{10,... | collective-permute-start | bytes 331784 | tf_op jit(solution)/shard_map/ppermute | solution.py:117
  45.3 0.0 collective-permute-done.13.refs_0_
  45.3 3.9 %collective-permute-start.7 = (bf16[3,144,128]{2,1,0:T(8,128)(2,1)S(1)}, bf16[3,144,128]{2,1,0:T(8,128)(2,1)S(1)}, u32[]{:S(2)}, u32[]{:S(2)}) collective-permute-start(bf16[3,144,128]{2,1,0:T(8,128)(2,1)S(1)} %get-tuple-element.47), channel_id=1, source_target_pairs={{0,1},{2,3},{1,0},{3,2},{4,5},{6,7},{5,4},{7,6},{8,9},{10,11},{9,8... | collective-permute-start | bytes 331784 | tf_op jit(solution)/shard_map/ppermute | solution.py:117
  49.2 5.5 %space.1 = (bf16[1,576,256]{2,1,0:T(8,128)(2,1)}, bf16[1,576,256]{2,1,0:T(8,128)(2,1)}, bf16[1,576,256]{2,1,0:T(8,128)(2,1)}) custom-call(bf16[1,576,256]{2,1,0:T(8,128)(2,1)} %bitcast.29, bf16[1,576,256]{2,1,0:T(8,128)(2,1)} %bitcast.30, bf16[1,576,256]{2,1,0:T(8,128)(2,1)} %bitcast.31, bf16[1,576,256]{2,1,0:T(8,128)(2,1)} %bitcast.32), custom_call_target="tpu_custom_call" | custom-call | flops 1610612736 | bytes 2064384 | tf_op jit(solution)/shard_map/space/pallas_call | solution.py:58
  54.7 1.1 %collective-permute-done.14.refs_1_ = bf16[3,144,128]{2,1,0:T(8,128)(2,1)S(1)} collective-permute-done((bf16[3,144,128]{2,1,0:T(8,128)(2,1)S(1)}, bf16[3,144,128]{2,1,0:T(8,128)(2,1)S(1)}, u32[]{:S(2)}, u32[]{:S(2)}) %collective-permute-start.14) | collective-permute-done | bytes 110624 | tf_op jit(solution)/shard_map/ppermute | solution.py:117
  55.8 0.0 collective-permute-done.15.refs_3_
  55.8 0.9 %unpack.2 = (bf16[1,576,256]{2,1,0:T(8,128)(2,1)}, bf16[1,576,256]{2,1,0:T(8,128)(2,1)}, bf16[1,576,256]{2,1,0:T(8,128)(2,1)}) custom-call(bf16[3,144,128]{2,1,0:T(8,128)(2,1)S(1)} %collective-permute-done.13.refs_0_, bf16[3,144,128]{2,1,0:T(8,128)(2,1)S(1)} %collective-permute-done.14.refs_1_, bf16[3,144,128]{2,1,0:T(8,128)(2,1)S(1)} %get-tuple-element.56.refs_2_, ...), custom_call_target="tpu_custom_call" | custom-call | tf_op jit(solution)/shard_map/unpack/pallas_call | solution.py:185
  56.7 0.0 collective-permute-done.5.refs_0_
  56.7 3.5 %collective-permute-done.6.refs_1_ = bf16[3,144,128]{2,1,0:T(8,128)(2,1)S(1)} collective-permute-done((bf16[3,144,128]{2,1,0:T(8,128)(2,1)S(1)}, bf16[3,144,128]{2,1,0:T(8,128)(2,1)S(1)}, u32[]{:S(2)}, u32[]{:S(2)}) %collective-permute-start.6) | collective-permute-done | bytes 110624 | tf_op jit(solution)/shard_map/ppermute | solution.py:117
  60.1 0.0 collective-permute-done.7.refs_3_
  60.1 0.9 %unpack.3 = (bf16[1,576,256]{2,1,0:T(8,128)(2,1)}, bf16[1,576,256]{2,1,0:T(8,128)(2,1)}, bf16[1,576,256]{2,1,0:T(8,128)(2,1)}) custom-call(bf16[3,144,128]{2,1,0:T(8,128)(2,1)S(1)} %collective-permute-done.5.refs_0_, bf16[3,144,128]{2,1,0:T(8,128)(2,1)S(1)} %collective-permute-done.6.refs_1_, ...), custom_call_target="tpu_custom_call", output_to_operand_aliasing={{0}: (4, {}), {1}: (5, {}), {2}: (6, {})} | custom-call | tf_op jit(solution)/shard_map/unpack/pallas_call | solution.py:185
  (4 shorter events, 0.0 us)
Async XLA Ops:
  2.5 12.1 %collective-permute-start.10 = (bf16[4,144,128]{2,1,0:T(8,128)(2,1)}, bf16[4,144,128]{2,1,0:T(8,128)(2,1)S(1)}, u32[]{:S(2)}, u32[]{:S(2)}) collective-permute-start(bf16[4,144,128]{2,1,0:T(8,128)(2,1)} %get-tuple-element.51), channel_id=1, source_target_pairs={{0,3},{1,2},{3,0},{2,1},{4,7},{5,6},{7,4},{6,5},{8,11},{9,10},{11,... | collective-permute-start | bytes 442376 | tf_op jit(solution)/shard_map/ppermute | solution.py:117
  7.6 8.8 %collective-permute-start.8 = (bf16[4,144,128]{2,1,0:T(8,128)(2,1)}, bf16[4,144,128]{2,1,0:T(8,128)(2,1)S(1)}, u32[]{:S(2)}, u32[]{:S(2)}) collective-permute-start(bf16[4,144,128]{2,1,0:T(8,128)(2,1)} %get-tuple-element.49), channel_id=1, source_target_pairs={{0,1},{2,3},{1,0},{3,2},{4,5},{6,7},{5,4},{7,6},{8,9},{10,11},{9,8... | collective-permute-start | bytes 442376 | tf_op jit(solution)/shard_map/ppermute | solution.py:117
  7.7 14.5 %copy-start.1 = (bf16[4,144,128]{2,1,0:T(8,128)(2,1)S(1)}, bf16[4,144,128]{2,1,0:T(8,128)(2,1)}, u32[]{:S(2)}) copy-start(bf16[4,144,128]{2,1,0:T(8,128)(2,1)} %get-tuple-element.48.refs_0_) | copy-start | bytes 442372
  7.7 14.5 %collective-permute-start.9 = (bf16[4,144,128]{2,1,0:T(8,128)(2,1)}, bf16[4,144,128]{2,1,0:T(8,128)(2,1)S(1)}, u32[]{:S(2)}, u32[]{:S(2)}) collective-permute-start(bf16[4,144,128]{2,1,0:T(8,128)(2,1)} %get-tuple-element.50), channel_id=1, source_target_pairs={{0,2},{1,3},{2,0},{3,1},{4,6},{5,7},{6,4},{7,5},{8,10},{9,11},{10,... | collective-permute-start | bytes 442376 | tf_op jit(solution)/shard_map/ppermute | solution.py:117
  10.2 4.4 %copy-start.2 = (s32[16]{0:T(128)S(1)}, s32[16]{0:T(128)}, u32[]{:S(2)}) copy-start(s32[16]{0:T(128)} %param.17) | copy-start | bytes 196
  10.2 16.1 %collective-permute-start = (bf16[4,144,128]{2,1,0:T(8,128)(2,1)}, bf16[4,144,128]{2,1,0:T(8,128)(2,1)S(1)}, u32[]{:S(2)}, u32[]{:S(2)}) collective-permute-start(bf16[4,144,128]{2,1,0:T(8,128)(2,1)} %get-tuple-element.39), channel_id=1, source_target_pairs={{0,1},{2,3},{1,0},{3,2},{4,5},{6,7},{5,4},{7,6},{8,9},{10,11},{9,8... | collective-permute-start | bytes 442376 | tf_op jit(solution)/shard_map/ppermute | solution.py:117
  11.7 19.2 %collective-permute-start.1 = (bf16[4,144,128]{2,1,0:T(8,128)(2,1)}, bf16[4,144,128]{2,1,0:T(8,128)(2,1)S(1)}, u32[]{:S(2)}, u32[]{:S(2)}) collective-permute-start(bf16[4,144,128]{2,1,0:T(8,128)(2,1)} %get-tuple-element.40), channel_id=1, source_target_pairs={{0,2},{1,3},{2,0},{3,1},{4,6},{5,7},{6,4},{7,5},{8,10},{9,11},{10,... | collective-permute-start | bytes 442376 | tf_op jit(solution)/shard_map/ppermute | solution.py:117
  14.7 16.2 %collective-permute-start.2 = (bf16[4,144,128]{2,1,0:T(8,128)(2,1)}, bf16[4,144,128]{2,1,0:T(8,128)(2,1)S(1)}, u32[]{:S(2)}, u32[]{:S(2)}) collective-permute-start(bf16[4,144,128]{2,1,0:T(8,128)(2,1)} %get-tuple-element.41), channel_id=1, source_target_pairs={{0,3},{1,2},{3,0},{2,1},{4,7},{5,6},{7,4},{6,5},{8,11},{9,10},{11,... | collective-permute-start | bytes 442376 | tf_op jit(solution)/shard_map/ppermute | solution.py:117
  22.2 8.6 %copy-start = (bf16[4,144,128]{2,1,0:T(8,128)(2,1)S(1)}, bf16[4,144,128]{2,1,0:T(8,128)(2,1)}, u32[]{:S(2)}) copy-start(bf16[4,144,128]{2,1,0:T(8,128)(2,1)} %get-tuple-element.38.refs_0_) | copy-start | bytes 442372
  22.3 12.2 %collective-permute-start.11 = (bf16[3,4,144,128]{3,2,1,0:T(8,128)(2,1)S(1)}, bf16[3,4,144,128]{3,2,1,0:T(8,128)(2,1)S(1)}, u32[]{:S(2)}, u32[]{:S(2)}) collective-permute-start(bf16[3,4,144,128]{3,2,1,0:T(8,128)(2,1)S(1)} %get-tuple-element.52), channel_id=1, source_target_pairs={{4,8},{12,16},{20,24},{8,4},{16,12},{24,20},{5,9},{13,17},{21,25},... | collective-permute-start | bytes 1327112 | tf_op jit(solution)/shard_map/ppermute | solution.py:117
  23.0 11.6 %collective-permute-start.12 = (bf16[3,4,144,128]{3,2,1,0:T(8,128)(2,1)S(1)}, bf16[3,4,144,128]{3,2,1,0:T(8,128)(2,1)S(1)}, u32[]{:S(2)}, u32[]{:S(2)}) collective-permute-start(bf16[3,4,144,128]{3,2,1,0:T(8,128)(2,1)S(1)} %get-tuple-element.53), channel_id=1, source_target_pairs={{0,4},{8,12},{16,20},{24,28},{4,0},{12,8},{20,16},{28,24},{1,5},{9... | collective-permute-start | bytes 1327112 | tf_op jit(solution)/shard_map/ppermute | solution.py:117
  31.0 9.5 %collective-permute-start.3 = (bf16[3,4,144,128]{3,2,1,0:T(8,128)(2,1)S(1)}, bf16[3,4,144,128]{3,2,1,0:T(8,128)(2,1)S(1)}, u32[]{:S(2)}, u32[]{:S(2)}) collective-permute-start(bf16[3,4,144,128]{3,2,1,0:T(8,128)(2,1)S(1)} %get-tuple-element.42), channel_id=1, source_target_pairs={{4,8},{12,16},{20,24},{8,4},{16,12},{24,20},{5,9},{13,17},{21,25},... | collective-permute-start | bytes 1327112 | tf_op jit(solution)/shard_map/ppermute | solution.py:117
  31.7 8.8 %collective-permute-start.4 = (bf16[3,4,144,128]{3,2,1,0:T(8,128)(2,1)S(1)}, bf16[3,4,144,128]{3,2,1,0:T(8,128)(2,1)S(1)}, u32[]{:S(2)}, u32[]{:S(2)}) collective-permute-start(bf16[3,4,144,128]{3,2,1,0:T(8,128)(2,1)S(1)} %get-tuple-element.43), channel_id=1, source_target_pairs={{0,4},{8,12},{16,20},{24,28},{4,0},{12,8},{20,16},{28,24},{1,5},{9... | collective-permute-start | bytes 1327112 | tf_op jit(solution)/shard_map/ppermute | solution.py:117
  36.0 9.3 %collective-permute-start.13 = (bf16[3,144,128]{2,1,0:T(8,128)(2,1)S(1)}, bf16[3,144,128]{2,1,0:T(8,128)(2,1)S(1)}, u32[]{:S(2)}, u32[]{:S(2)}) collective-permute-start(bf16[3,144,128]{2,1,0:T(8,128)(2,1)S(1)} %get-tuple-element.54), channel_id=1, source_target_pairs={{0,3},{1,2},{3,0},{2,1},{4,7},{5,6},{7,4},{6,5},{8,11},{9,10},{11,... | collective-permute-start | bytes 331784 | tf_op jit(solution)/shard_map/ppermute | solution.py:117
  38.7 17.1 %collective-permute-start.14 = (bf16[3,144,128]{2,1,0:T(8,128)(2,1)S(1)}, bf16[3,144,128]{2,1,0:T(8,128)(2,1)S(1)}, u32[]{:S(2)}, u32[]{:S(2)}) collective-permute-start(bf16[3,144,128]{2,1,0:T(8,128)(2,1)S(1)} %get-tuple-element.55), channel_id=1, source_target_pairs={{0,2},{1,3},{2,0},{3,1},{4,6},{5,7},{6,4},{7,5},{8,10},{9,11},{10,... | collective-permute-start | bytes 331784 | tf_op jit(solution)/shard_map/ppermute | solution.py:117
  40.3 15.5 %collective-permute-start.15 = (bf16[3,144,128]{2,1,0:T(8,128)(2,1)S(1)}, bf16[3,144,128]{2,1,0:T(8,128)(2,1)S(1)}, u32[]{:S(2)}, u32[]{:S(2)}) collective-permute-start(bf16[3,144,128]{2,1,0:T(8,128)(2,1)S(1)} %get-tuple-element.57), channel_id=1, source_target_pairs={{0,1},{2,3},{1,0},{3,2},{4,5},{6,7},{5,4},{7,6},{8,9},{10,11},{9,8... | collective-permute-start | bytes 331784 | tf_op jit(solution)/shard_map/ppermute | solution.py:117
  41.9 14.7 %collective-permute-start.5 = (bf16[3,144,128]{2,1,0:T(8,128)(2,1)S(1)}, bf16[3,144,128]{2,1,0:T(8,128)(2,1)S(1)}, u32[]{:S(2)}, u32[]{:S(2)}) collective-permute-start(bf16[3,144,128]{2,1,0:T(8,128)(2,1)S(1)} %get-tuple-element.44), channel_id=1, source_target_pairs={{0,3},{1,2},{3,0},{2,1},{4,7},{5,6},{7,4},{6,5},{8,11},{9,10},{11,... | collective-permute-start | bytes 331784 | tf_op jit(solution)/shard_map/ppermute | solution.py:117
  44.6 15.5 %collective-permute-start.6 = (bf16[3,144,128]{2,1,0:T(8,128)(2,1)S(1)}, bf16[3,144,128]{2,1,0:T(8,128)(2,1)S(1)}, u32[]{:S(2)}, u32[]{:S(2)}) collective-permute-start(bf16[3,144,128]{2,1,0:T(8,128)(2,1)S(1)} %get-tuple-element.45), channel_id=1, source_target_pairs={{0,2},{1,3},{2,0},{3,1},{4,6},{5,7},{6,4},{7,5},{8,10},{9,11},{10,... | collective-permute-start | bytes 331784 | tf_op jit(solution)/shard_map/ppermute | solution.py:117
  45.3 14.8 %collective-permute-start.7 = (bf16[3,144,128]{2,1,0:T(8,128)(2,1)S(1)}, bf16[3,144,128]{2,1,0:T(8,128)(2,1)S(1)}, u32[]{:S(2)}, u32[]{:S(2)}) collective-permute-start(bf16[3,144,128]{2,1,0:T(8,128)(2,1)S(1)} %get-tuple-element.47), channel_id=1, source_target_pairs={{0,1},{2,3},{1,0},{3,2},{4,5},{6,7},{5,4},{7,6},{8,9},{10,11},{9,8... | collective-permute-start | bytes 331784 | tf_op jit(solution)/shard_map/ppermute | solution.py:117

commit v4 on v2

--- a/solution.py
+++ b/solution.py
@@ -159,7 +159,7 @@
 
 def neighbours(block, start):
     count = lax.axis_size("grp")
-    return swap(block, "grp", [(i, i + 1) for i in range(start, count - 1, 2)])
+    return swap(block, "grp", [(i, (i + 1) % count) for i in range(start, count, 2)])
 
 
 def join_kernel(sharing, span, *refs):
@@ -365,6 +365,8 @@
         tokens % LANES == 0
         and n % 4 == 0
         and n & (n - 1) == 0
+        and mesh.shape["grp"] % 2 == 0
+        and mesh.shape["grp"] > 2
         and sharing * tokens == n * LANES
         and all(heads % sharing == 0 and heads // sharing * HDIM % 16 == 0 for heads in CHUNKS)
     )

time: 60.5 us -> 59.7 us (0.987)
  starting transfers between devices: 28.4 us -> 23.9 us
  waiting for transfers between devices: 16.5 us -> 20 us
    ppermute x16, starting transfers between devices: 28.4 us -> 23.9 us  [swap(): lax.ppermute(block, axis, [(i, j) for i, j in pairs] + [(j, i) for i, j i...]
    ppermute x16, waiting for transfers between devices: 16.5 us -> 20 us  [swap(): lax.ppermute(block, axis, [(i, j) for i, j in pairs] + [(j, i) for i, j i...]
  transfers between devices with their start and end apart: 16 -> 16, of which waited for: 3 -> 5; matrix products, arithmetic and copies ran while one was open for 0% -> 0% of each run, Pallas kernels for 19% -> 20%
where the time goes in v4:
time: 59.7 us; the launch traced here: 59.3 us
  starting transfers between devices  23.9 us (40%)
  waiting for transfers between devices  20 us (34%)
  Pallas kernels  14.4 us (24%)
  between operations  0.75 us (1%)
    ppermute x16, starting transfers between devices, swap(): lax.ppermute(block, axis, [(i, j) for i, j in pairs] + [(j, i) for i, j i...  23.9 us
    ppermute x16, waiting for transfers between devices, swap(): lax.ppermute(block, axis, [(i, j) for i, j in pairs] + [(j, i) for i, j i...  20 us
    pallas_call x1, Pallas kernels, space_grads(): pl.pallas_call(frame_kernel, out_shape=(shape, shape, shape), compiler_pa...  5.58 us
    pallas_call x2, Pallas kernels, split(): pl.pallas_call(functools.partial(split_kernel, sharing, rows, span), in_s...  3.77 us
    pallas_call x2, Pallas kernels, clip_grads(): pl.pallas_call(functools.partial(clip_kernel, window, heads), out_shape=[...  3.02 us
    pallas_call x2, Pallas kernels, join(): pl.pallas_call(functools.partial(join_kernel, sharing, span), in_specs=[p...  1.71 us
  transfers between devices with their start and end apart: 16, of which 5 were waited for; matrix products, arithmetic and copies ran while one was open for 0% of the time, Pallas kernels for 20%

profile of v4, /device:TPU:0, one launch (start us, length us, event | category | flops | bytes accessed | tf_op | source)
XLA Modules:
  0.0 59.3 jit_solution(1935433401122795814)
XLA Ops:
  0.6 1.9 %pack.3 = (bf16[4,144,128]{2,1,0:T(8,128)(2,1)}, bf16[4,144,128]{2,1,0:T(8,128)(2,1)}, bf16[4,144,128]{2,1,0:T(8,128)(2,1)}, bf16[4,144,128]{2,1,0:T(8,128)(2,1)}) custom-call(bf16[1,576,256]{2,1,0:T(8,128)(2,1)} %bitcast.18, bf16[1,576,256]{2,1,0:T(8,128)(2,1)} %bitcast.20, bf16[1,576,256]{2,1,0:T(8,128)(2,1)} %bitcast.22, bf16[1,576,256]{2,1,0:T(8,128)(2,1)} %bitcast.24), custom_call_target="tpu_custom_call" | custom-call | tf_op jit(solution)/shard_map/pack/pallas_call | solution.py:97
  2.5 4.1 %collective-permute-start = (bf16[4,144,128]{2,1,0:T(8,128)(2,1)}, bf16[4,144,128]{2,1,0:T(8,128)(2,1)S(1)}, u32[]{:S(2)}, u32[]{:S(2)}) collective-permute-start(bf16[4,144,128]{2,1,0:T(8,128)(2,1)} %get-tuple-element.43), channel_id=1, source_target_pairs={{0,2},{1,3},{2,0},{3,1},{4,6},{5,7},{6,4},{7,5},{8,10},{9,11},{10,... | collective-permute-start | bytes 442376 | tf_op jit(solution)/shard_map/ppermute | solution.py:117
  6.6 1.6 %collective-permute-start.9 = (bf16[4,144,128]{2,1,0:T(8,128)(2,1)}, bf16[4,144,128]{2,1,0:T(8,128)(2,1)S(1)}, u32[]{:S(2)}, u32[]{:S(2)}) collective-permute-start(bf16[4,144,128]{2,1,0:T(8,128)(2,1)} %get-tuple-element.61), channel_id=1, source_target_pairs={{0,1},{2,3},{1,0},{3,2},{4,5},{6,7},{5,4},{7,6},{8,9},{10,11},{9,8... | collective-permute-start | bytes 442376 | tf_op jit(solution)/shard_map/ppermute | solution.py:117
  8.2 0.0 collective-permute-start.10
  8.2 1.9 %pack.2 = (bf16[4,144,128]{2,1,0:T(8,128)(2,1)}, bf16[4,144,128]{2,1,0:T(8,128)(2,1)}, bf16[4,144,128]{2,1,0:T(8,128)(2,1)}, bf16[4,144,128]{2,1,0:T(8,128)(2,1)}) custom-call(bf16[1,576,256]{2,1,0:T(8,128)(2,1)} %bitcast.19, bf16[1,576,256]{2,1,0:T(8,128)(2,1)} %bitcast.21, bf16[1,576,256]{2,1,0:T(8,128)(2,1)} %bitcast.23, bf16[1,576,256]{2,1,0:T(8,128)(2,1)} %bitcast.25), custom_call_target="tpu_custom_call" | custom-call | tf_op jit(solution)/shard_map/pack/pallas_call | solution.py:97
  10.1 1.0 %collective-permute-start.1 = (bf16[4,144,128]{2,1,0:T(8,128)(2,1)}, bf16[4,144,128]{2,1,0:T(8,128)(2,1)S(1)}, u32[]{:S(2)}, u32[]{:S(2)}) collective-permute-start(bf16[4,144,128]{2,1,0:T(8,128)(2,1)} %get-tuple-element.51), channel_id=1, source_target_pairs={{0,1},{2,3},{1,0},{3,2},{4,5},{6,7},{5,4},{7,6},{8,9},{10,11},{9,8... | collective-permute-start | bytes 442376 | tf_op jit(solution)/shard_map/ppermute | solution.py:117
  11.1 0.0 copy-start.4
  11.1 0.0 copy-start.3
  11.1 0.0 copy-start.2
  11.1 0.0 copy-start.1
  11.1 5.6 %space.1 = (bf16[1,576,256]{2,1,0:T(8,128)(2,1)}, bf16[1,576,256]{2,1,0:T(8,128)(2,1)}, bf16[1,576,256]{2,1,0:T(8,128)(2,1)}) custom-call(bf16[1,576,256]{2,1,0:T(8,128)(2,1)} %bitcast.29, bf16[1,576,256]{2,1,0:T(8,128)(2,1)} %bitcast.30, bf16[1,576,256]{2,1,0:T(8,128)(2,1)} %bitcast.31, bf16[1,576,256]{2,1,0:T(8,128)(2,1)} %bitcast.32), custom_call_target="tpu_custom_call" | custom-call | flops 1610612736 | bytes 2064384 | tf_op jit(solution)/shard_map/space/pallas_call | solution.py:58
  16.7 0.0 copy-done.4
  16.7 0.1 select_reduce_fusion.2
  16.7 0.0 collective-permute-done.refs_2_
  16.7 0.0 copy-done.3
  16.8 3.6 %collective-permute-start.2 = (bf16[4,144,128]{2,1,0:T(8,128)(2,1)S(1)}, bf16[4,144,128]{2,1,0:T(8,128)(2,1)S(1)}, u32[]{:S(2)}, u32[]{:S(2)}) collective-permute-start(bf16[4,144,128]{2,1,0:T(8,128)(2,1)S(1)} %copy-done.3), channel_id=1, source_target_pairs={{0,2},{1,3},{2,0},{3,1},{4,6},{5,7},{6,4},{7,5},{8,10},{9,11},{10,... | collective-permute-start | bytes 442376 | tf_op jit(solution)/shard_map/ppermute | solution.py:117
  20.3 0.0 copy-done.2
  20.3 0.0 collective-permute-start.3
  20.3 0.0 collective-permute-done.9.refs_1_
  20.3 0.0 collective-permute-done.10.refs_3_
  20.4 0.0 copy-done.1
  20.4 0.0 copy-start
  20.4 0.1 sides.3
  20.5 0.6 collective-permute-start.11
  21.1 1.3 %collective-permute-start.12 = (bf16[3,4,144,128]{3,2,1,0:T(8,128)(2,1)S(1)}, bf16[3,4,144,128]{3,2,1,0:T(8,128)(2,1)S(1)}, u32[]{:S(2)}, u32[]{:S(2)}) collective-permute-start(bf16[3,4,144,128]{3,2,1,0:T(8,128)(2,1)S(1)} %get-tuple-element.65), channel_id=1, source_target_pairs={{0,4},{8,12},{16,20},{24,28},{4,0},{12,8},{20,16},{28,24},{1,5},{9... | collective-permute-start | bytes 1327112 | tf_op jit(solution)/shard_map/ppermute | solution.py:117
  22.4 0.2 select_reduce_fusion.1
  22.6 0.0 collective-permute-done.1.refs_1_
  22.6 8.0 %collective-permute-done.2.refs_2_ = bf16[4,144,128]{2,1,0:T(8,128)(2,1)S(1)} collective-permute-done((bf16[4,144,128]{2,1,0:T(8,128)(2,1)S(1)}, bf16[4,144,128]{2,1,0:T(8,128)(2,1)S(1)}, u32[]{:S(2)}, u32[]{:S(2)}) %collective-permute-start.2) | collective-permute-done | bytes 147488 | tf_op jit(solution)/shard_map/ppermute | solution.py:117
  30.6 0.0 collective-permute-done.3.refs_3_
  30.6 0.0 copy-done
  30.6 0.1 sides.2
  30.7 0.5 collective-permute-start.4
  31.2 1.2 %collective-permute-start.5 = (bf16[3,4,144,128]{3,2,1,0:T(8,128)(2,1)S(1)}, bf16[3,4,144,128]{3,2,1,0:T(8,128)(2,1)S(1)}, u32[]{:S(2)}, u32[]{:S(2)}) collective-permute-start(bf16[3,4,144,128]{3,2,1,0:T(8,128)(2,1)S(1)} %get-tuple-element.55), channel_id=1, source_target_pairs={{0,4},{8,12},{16,20},{24,28},{4,0},{12,8},{20,16},{28,24},{1,5},{9... | collective-permute-start | bytes 1327112 | tf_op jit(solution)/shard_map/ppermute | solution.py:117
  32.4 1.2 %collective-permute-done.11.refs_4_ = bf16[3,4,144,128]{3,2,1,0:T(8,128)(2,1)S(1)} collective-permute-done((bf16[3,4,144,128]{3,2,1,0:T(8,128)(2,1)S(1)}, bf16[3,4,144,128]{3,2,1,0:T(8,128)(2,1)S(1)}, u32[]{:S(2)}, u32[]{:S(2)}) %collective-permute-start.11) | collective-permute-done | bytes 442400 | tf_op jit(solution)/shard_map/ppermute | solution.py:117
  33.6 0.0 collective-permute-done.12.refs_5_
  33.6 1.5 %clips.3 = (bf16[3,144,128]{2,1,0:T(8,128)(2,1)S(1)}, bf16[3,144,128]{2,1,0:T(8,128)(2,1)S(1)}, bf16[3,144,128]{2,1,0:T(8,128)(2,1)S(1)}, bf16[3,144,128]{2,1,0:T(8,128)(2,1)S(1)}) custom-call(s32[2,10]{1,0:T(2,128)S(1)} %pad_add_fusion.given_bounds, bf16[4,144,128]{2,1,0:T(8,128)(2,1)S(1)} %copy-done.1, ...), custom_call_target="tpu_custom_call" | custom-call | flops 589824000 | bytes 1474560 | tf_op jit(solution)/shard_map/clips/pallas_call | solution.py:291
  35.2 4.1 %collective-permute-start.13 = (bf16[3,144,128]{2,1,0:T(8,128)(2,1)S(1)}, bf16[3,144,128]{2,1,0:T(8,128)(2,1)S(1)}, u32[]{:S(2)}, u32[]{:S(2)}) collective-permute-start(bf16[3,144,128]{2,1,0:T(8,128)(2,1)S(1)} %get-tuple-element.66), channel_id=1, source_target_pairs={{0,3},{1,2},{3,0},{2,1},{4,7},{5,6},{7,4},{6,5},{8,11},{9,10},{11,... | collective-permute-start | bytes 331784 | tf_op jit(solution)/shard_map/ppermute | solution.py:117
  39.2 0.2 collective-permute-start.14
  39.4 0.5 collective-permute-start.15
  39.9 4.1 %collective-permute-done.4.refs_4_ = bf16[3,4,144,128]{3,2,1,0:T(8,128)(2,1)S(1)} collective-permute-done((bf16[3,4,144,128]{3,2,1,0:T(8,128)(2,1)S(1)}, bf16[3,4,144,128]{3,2,1,0:T(8,128)(2,1)S(1)}, u32[]{:S(2)}, u32[]{:S(2)}) %collective-permute-start.4) | collective-permute-done | bytes 442400 | tf_op jit(solution)/shard_map/ppermute | solution.py:117
  44.0 0.0 collective-permute-done.5.refs_5_
  44.0 1.5 %clips.2 = (bf16[3,144,128]{2,1,0:T(8,128)(2,1)S(1)}, bf16[3,144,128]{2,1,0:T(8,128)(2,1)S(1)}, bf16[3,144,128]{2,1,0:T(8,128)(2,1)S(1)}, bf16[3,144,128]{2,1,0:T(8,128)(2,1)S(1)}) custom-call(s32[2,10]{1,0:T(2,128)S(1)} %pad_add_fusion.given_bounds, bf16[4,144,128]{2,1,0:T(8,128)(2,1)S(1)} %copy-done, ...), custom_call_target="tpu_custom_call" | custom-call | flops 589824000 | bytes 1474560 | tf_op jit(solution)/shard_map/clips/pallas_call | solution.py:291
  45.6 3.2 %collective-permute-start.6 = (bf16[3,144,128]{2,1,0:T(8,128)(2,1)S(1)}, bf16[3,144,128]{2,1,0:T(8,128)(2,1)S(1)}, u32[]{:S(2)}, u32[]{:S(2)}) collective-permute-start(bf16[3,144,128]{2,1,0:T(8,128)(2,1)S(1)} %get-tuple-element.56), channel_id=1, source_target_pairs={{0,3},{1,2},{3,0},{2,1},{4,7},{5,6},{7,4},{6,5},{8,11},{9,10},{11,... | collective-permute-start | bytes 331784 | tf_op jit(solution)/shard_map/ppermute | solution.py:117
  48.7 1.8 %collective-permute-start.7 = (bf16[3,144,128]{2,1,0:T(8,128)(2,1)S(1)}, bf16[3,144,128]{2,1,0:T(8,128)(2,1)S(1)}, u32[]{:S(2)}, u32[]{:S(2)}) collective-permute-start(bf16[3,144,128]{2,1,0:T(8,128)(2,1)S(1)} %get-tuple-element.57), channel_id=1, source_target_pairs={{0,2},{1,3},{2,0},{3,1},{4,6},{5,7},{6,4},{7,5},{8,10},{9,11},{10,... | collective-permute-start | bytes 331784 | tf_op jit(solution)/shard_map/ppermute | solution.py:117
  50.5 0.0 collective-permute-done.13.refs_0_
  50.5 0.5 collective-permute-start.8
  51.0 0.0 collective-permute-done.14.refs_1_
  51.0 0.0 collective-permute-done.15.refs_3_
  51.0 0.9 %unpack.2 = (bf16[1,576,256]{2,1,0:T(8,128)(2,1)}, bf16[1,576,256]{2,1,0:T(8,128)(2,1)}, bf16[1,576,256]{2,1,0:T(8,128)(2,1)}) custom-call(bf16[3,144,128]{2,1,0:T(8,128)(2,1)S(1)} %collective-permute-done.13.refs_0_, bf16[3,144,128]{2,1,0:T(8,128)(2,1)S(1)} %collective-permute-done.14.refs_1_, bf16[3,144,128]{2,1,0:T(8,128)(2,1)S(1)} %get-tuple-element.68.refs_2_, ...), custom_call_target="tpu_custom_call" | custom-call | tf_op jit(solution)/shard_map/unpack/pallas_call | solution.py:185
  51.9 0.4 collective-permute-done.6.refs_0_
  52.3 6.1 %collective-permute-done.7.refs_1_ = bf16[3,144,128]{2,1,0:T(8,128)(2,1)S(1)} collective-permute-done((bf16[3,144,128]{2,1,0:T(8,128)(2,1)S(1)}, bf16[3,144,128]{2,1,0:T(8,128)(2,1)S(1)}, u32[]{:S(2)}, u32[]{:S(2)}) %collective-permute-start.7) | collective-permute-done | bytes 110624 | tf_op jit(solution)/shard_map/ppermute | solution.py:117
  58.5 0.0 collective-permute-done.8.refs_3_
  58.5 0.9 %unpack.3 = (bf16[1,576,256]{2,1,0:T(8,128)(2,1)}, bf16[1,576,256]{2,1,0:T(8,128)(2,1)}, bf16[1,576,256]{2,1,0:T(8,128)(2,1)}) custom-call(bf16[3,144,128]{2,1,0:T(8,128)(2,1)S(1)} %collective-permute-done.6.refs_0_, bf16[3,144,128]{2,1,0:T(8,128)(2,1)S(1)} %collective-permute-done.7.refs_1_, ...), custom_call_target="tpu_custom_call", output_to_operand_aliasing={{0}: (4, {}), {1}: (5, {}), {2}: (6, {})} | custom-call | tf_op jit(solution)/shard_map/unpack/pallas_call | solution.py:185
  (4 shorter events, 0.0 us)
Async XLA Ops:
  2.5 14.2 %collective-permute-start = (bf16[4,144,128]{2,1,0:T(8,128)(2,1)}, bf16[4,144,128]{2,1,0:T(8,128)(2,1)S(1)}, u32[]{:S(2)}, u32[]{:S(2)}) collective-permute-start(bf16[4,144,128]{2,1,0:T(8,128)(2,1)} %get-tuple-element.43), channel_id=1, source_target_pairs={{0,2},{1,3},{2,0},{3,1},{4,6},{5,7},{6,4},{7,5},{8,10},{9,11},{10,... | collective-permute-start | bytes 442376 | tf_op jit(solution)/shard_map/ppermute | solution.py:117
  6.6 13.7 %collective-permute-start.9 = (bf16[4,144,128]{2,1,0:T(8,128)(2,1)}, bf16[4,144,128]{2,1,0:T(8,128)(2,1)S(1)}, u32[]{:S(2)}, u32[]{:S(2)}) collective-permute-start(bf16[4,144,128]{2,1,0:T(8,128)(2,1)} %get-tuple-element.61), channel_id=1, source_target_pairs={{0,1},{2,3},{1,0},{3,2},{4,5},{6,7},{5,4},{7,6},{8,9},{10,11},{9,8... | collective-permute-start | bytes 442376 | tf_op jit(solution)/shard_map/ppermute | solution.py:117
  8.2 12.1 %collective-permute-start.10 = (bf16[4,144,128]{2,1,0:T(8,128)(2,1)}, bf16[4,144,128]{2,1,0:T(8,128)(2,1)S(1)}, u32[]{:S(2)}, u32[]{:S(2)}) collective-permute-start(bf16[4,144,128]{2,1,0:T(8,128)(2,1)} %get-tuple-element.63), channel_id=1, source_target_pairs={{0,3},{1,2},{3,0},{2,1},{4,7},{5,6},{7,4},{6,5},{8,11},{9,10},{11,... | collective-permute-start | bytes 442376 | tf_op jit(solution)/shard_map/ppermute | solution.py:117
  10.1 12.5 %collective-permute-start.1 = (bf16[4,144,128]{2,1,0:T(8,128)(2,1)}, bf16[4,144,128]{2,1,0:T(8,128)(2,1)S(1)}, u32[]{:S(2)}, u32[]{:S(2)}) collective-permute-start(bf16[4,144,128]{2,1,0:T(8,128)(2,1)} %get-tuple-element.51), channel_id=1, source_target_pairs={{0,1},{2,3},{1,0},{3,2},{4,5},{6,7},{5,4},{7,6},{8,9},{10,11},{9,8... | collective-permute-start | bytes 442376 | tf_op jit(solution)/shard_map/ppermute | solution.py:117
  11.1 5.6 %copy-start.4 = (s32[16]{0:T(128)S(1)}, s32[16]{0:T(128)}, u32[]{:S(2)}) copy-start(s32[16]{0:T(128)} %param.17) | copy-start | bytes 196
  11.1 5.7 %copy-start.3 = (bf16[4,144,128]{2,1,0:T(8,128)(2,1)S(1)}, bf16[4,144,128]{2,1,0:T(8,128)(2,1)}, u32[]{:S(2)}) copy-start(bf16[4,144,128]{2,1,0:T(8,128)(2,1)} %get-tuple-element.52) | copy-start | bytes 442372
  11.1 9.2 %copy-start.2 = (bf16[4,144,128]{2,1,0:T(8,128)(2,1)S(1)}, bf16[4,144,128]{2,1,0:T(8,128)(2,1)}, u32[]{:S(2)}) copy-start(bf16[4,144,128]{2,1,0:T(8,128)(2,1)} %get-tuple-element.53) | copy-start | bytes 442372
  11.1 9.3 %copy-start.1 = (bf16[4,144,128]{2,1,0:T(8,128)(2,1)S(1)}, bf16[4,144,128]{2,1,0:T(8,128)(2,1)}, u32[]{:S(2)}) copy-start(bf16[4,144,128]{2,1,0:T(8,128)(2,1)} %get-tuple-element.60.refs_0_) | copy-start | bytes 442372
  16.8 13.8 %collective-permute-start.2 = (bf16[4,144,128]{2,1,0:T(8,128)(2,1)S(1)}, bf16[4,144,128]{2,1,0:T(8,128)(2,1)S(1)}, u32[]{:S(2)}, u32[]{:S(2)}) collective-permute-start(bf16[4,144,128]{2,1,0:T(8,128)(2,1)S(1)} %copy-done.3), channel_id=1, source_target_pairs={{0,2},{1,3},{2,0},{3,1},{4,6},{5,7},{6,4},{7,5},{8,10},{9,11},{10,... | collective-permute-start | bytes 442376 | tf_op jit(solution)/shard_map/ppermute | solution.py:117
  20.3 10.3 %collective-permute-start.3 = (bf16[4,144,128]{2,1,0:T(8,128)(2,1)S(1)}, bf16[4,144,128]{2,1,0:T(8,128)(2,1)S(1)}, u32[]{:S(2)}, u32[]{:S(2)}) collective-permute-start(bf16[4,144,128]{2,1,0:T(8,128)(2,1)S(1)} %copy-done.2), channel_id=1, source_target_pairs={{0,3},{1,2},{3,0},{2,1},{4,7},{5,6},{7,4},{6,5},{8,11},{9,10},{11,... | collective-permute-start | bytes 442376 | tf_op jit(solution)/shard_map/ppermute | solution.py:117
  20.4 10.2 %copy-start = (bf16[4,144,128]{2,1,0:T(8,128)(2,1)S(1)}, bf16[4,144,128]{2,1,0:T(8,128)(2,1)}, u32[]{:S(2)}) copy-start(bf16[4,144,128]{2,1,0:T(8,128)(2,1)} %get-tuple-element.50.refs_0_) | copy-start | bytes 442372
  20.5 13.1 %collective-permute-start.11 = (bf16[3,4,144,128]{3,2,1,0:T(8,128)(2,1)S(1)}, bf16[3,4,144,128]{3,2,1,0:T(8,128)(2,1)S(1)}, u32[]{:S(2)}, u32[]{:S(2)}) collective-permute-start(bf16[3,4,144,128]{3,2,1,0:T(8,128)(2,1)S(1)} %get-tuple-element.64), channel_id=1, source_target_pairs={{4,8},{12,16},{20,24},{28,0},{8,4},{16,12},{24,20},{0,28},{5,9},{1... | collective-permute-start | bytes 1327112 | tf_op jit(solution)/shard_map/ppermute | solution.py:117
  21.1 12.6 %collective-permute-start.12 = (bf16[3,4,144,128]{3,2,1,0:T(8,128)(2,1)S(1)}, bf16[3,4,144,128]{3,2,1,0:T(8,128)(2,1)S(1)}, u32[]{:S(2)}, u32[]{:S(2)}) collective-permute-start(bf16[3,4,144,128]{3,2,1,0:T(8,128)(2,1)S(1)} %get-tuple-element.65), channel_id=1, source_target_pairs={{0,4},{8,12},{16,20},{24,28},{4,0},{12,8},{20,16},{28,24},{1,5},{9... | collective-permute-start | bytes 1327112 | tf_op jit(solution)/shard_map/ppermute | solution.py:117
  30.7 13.3 %collective-permute-start.4 = (bf16[3,4,144,128]{3,2,1,0:T(8,128)(2,1)S(1)}, bf16[3,4,144,128]{3,2,1,0:T(8,128)(2,1)S(1)}, u32[]{:S(2)}, u32[]{:S(2)}) collective-permute-start(bf16[3,4,144,128]{3,2,1,0:T(8,128)(2,1)S(1)} %get-tuple-element.54), channel_id=1, source_target_pairs={{4,8},{12,16},{20,24},{28,0},{8,4},{16,12},{24,20},{0,28},{5,9},{1... | collective-permute-start | bytes 1327112 | tf_op jit(solution)/shard_map/ppermute | solution.py:117
  31.2 12.8 %collective-permute-start.5 = (bf16[3,4,144,128]{3,2,1,0:T(8,128)(2,1)S(1)}, bf16[3,4,144,128]{3,2,1,0:T(8,128)(2,1)S(1)}, u32[]{:S(2)}, u32[]{:S(2)}) collective-permute-start(bf16[3,4,144,128]{3,2,1,0:T(8,128)(2,1)S(1)} %get-tuple-element.55), channel_id=1, source_target_pairs={{0,4},{8,12},{16,20},{24,28},{4,0},{12,8},{20,16},{28,24},{1,5},{9... | collective-permute-start | bytes 1327112 | tf_op jit(solution)/shard_map/ppermute | solution.py:117
  35.2 15.4 %collective-permute-start.13 = (bf16[3,144,128]{2,1,0:T(8,128)(2,1)S(1)}, bf16[3,144,128]{2,1,0:T(8,128)(2,1)S(1)}, u32[]{:S(2)}, u32[]{:S(2)}) collective-permute-start(bf16[3,144,128]{2,1,0:T(8,128)(2,1)S(1)} %get-tuple-element.66), channel_id=1, source_target_pairs={{0,3},{1,2},{3,0},{2,1},{4,7},{5,6},{7,4},{6,5},{8,11},{9,10},{11,... | collective-permute-start | bytes 331784 | tf_op jit(solution)/shard_map/ppermute | solution.py:117
  39.2 11.8 %collective-permute-start.14 = (bf16[3,144,128]{2,1,0:T(8,128)(2,1)S(1)}, bf16[3,144,128]{2,1,0:T(8,128)(2,1)S(1)}, u32[]{:S(2)}, u32[]{:S(2)}) collective-permute-start(bf16[3,144,128]{2,1,0:T(8,128)(2,1)S(1)} %get-tuple-element.67), channel_id=1, source_target_pairs={{0,2},{1,3},{2,0},{3,1},{4,6},{5,7},{6,4},{7,5},{8,10},{9,11},{10,... | collective-permute-start | bytes 331784 | tf_op jit(solution)/shard_map/ppermute | solution.py:117
  39.4 11.6 %collective-permute-start.15 = (bf16[3,144,128]{2,1,0:T(8,128)(2,1)S(1)}, bf16[3,144,128]{2,1,0:T(8,128)(2,1)S(1)}, u32[]{:S(2)}, u32[]{:S(2)}) collective-permute-start(bf16[3,144,128]{2,1,0:T(8,128)(2,1)S(1)} %get-tuple-element.69), channel_id=1, source_target_pairs={{0,1},{2,3},{1,0},{3,2},{4,5},{6,7},{5,4},{7,6},{8,9},{10,11},{9,8... | collective-permute-start | bytes 331784 | tf_op jit(solution)/shard_map/ppermute | solution.py:117
  45.6 6.8 %collective-permute-start.6 = (bf16[3,144,128]{2,1,0:T(8,128)(2,1)S(1)}, bf16[3,144,128]{2,1,0:T(8,128)(2,1)S(1)}, u32[]{:S(2)}, u32[]{:S(2)}) collective-permute-start(bf16[3,144,128]{2,1,0:T(8,128)(2,1)S(1)} %get-tuple-element.56), channel_id=1, source_target_pairs={{0,3},{1,2},{3,0},{2,1},{4,7},{5,6},{7,4},{6,5},{8,11},{9,10},{11,... | collective-permute-start | bytes 331784 | tf_op jit(solution)/shard_map/ppermute | solution.py:117
  48.7 9.8 %collective-permute-start.7 = (bf16[3,144,128]{2,1,0:T(8,128)(2,1)S(1)}, bf16[3,144,128]{2,1,0:T(8,128)(2,1)S(1)}, u32[]{:S(2)}, u32[]{:S(2)}) collective-permute-start(bf16[3,144,128]{2,1,0:T(8,128)(2,1)S(1)} %get-tuple-element.57), channel_id=1, source_target_pairs={{0,2},{1,3},{2,0},{3,1},{4,6},{5,7},{6,4},{7,5},{8,10},{9,11},{10,... | collective-permute-start | bytes 331784 | tf_op jit(solution)/shard_map/ppermute | solution.py:117
  50.5 7.9 %collective-permute-start.8 = (bf16[3,144,128]{2,1,0:T(8,128)(2,1)S(1)}, bf16[3,144,128]{2,1,0:T(8,128)(2,1)S(1)}, u32[]{:S(2)}, u32[]{:S(2)}) collective-permute-start(bf16[3,144,128]{2,1,0:T(8,128)(2,1)S(1)} %get-tuple-element.59), channel_id=1, source_target_pairs={{0,1},{2,3},{1,0},{3,2},{4,5},{6,7},{5,4},{7,6},{8,9},{10,11},{9,8... | collective-permute-start | bytes 331784 | tf_op jit(solution)/shard_map/ppermute | solution.py:117

commit v5 on v3

--- a/solution.py
+++ b/solution.py
@@ -159,7 +159,7 @@
 
 def neighbours(block, start):
     count = lax.axis_size("grp")
-    return swap(block, "grp", [(i, i + 1) for i in range(start, count - 1, 2)])
+    return swap(block, "grp", [(i, (i + 1) % count) for i in range(start, count, 2)])
 
 
 def join_kernel(sharing, span, *refs):
@@ -363,6 +363,8 @@
         tokens % LANES == 0
         and n % 4 == 0
         and n & (n - 1) == 0
+        and mesh.shape["grp"] % 2 == 0
+        and mesh.shape["grp"] > 2
         and sharing * tokens == n * LANES
         and all(heads % sharing == 0 and heads // sharing * HDIM % 16 == 0 for heads in CHUNKS)
     )

time: 61.2 us -> 59.6 us (0.974)
  starting transfers between devices: 30.9 us -> 24.3 us
  waiting for transfers between devices: 14.9 us -> 20 us
    ppermute x16, starting transfers between devices: 30.9 us -> 24.3 us  [swap(): lax.ppermute(block, axis, [(i, j) for i, j in pairs] + [(j, i) for i, j i...]
    ppermute x16, waiting for transfers between devices: 14.9 us -> 20 us  [swap(): lax.ppermute(block, axis, [(i, j) for i, j in pairs] + [(j, i) for i, j i...]
  transfers between devices with their start and end apart: 16 -> 16, of which waited for: 4 -> 5; matrix products, arithmetic and copies ran while one was open for 0% -> 0% of each run, Pallas kernels for 19% -> 19%
where the time goes in v5:
time: 59.6 us; the launch traced here: 59.3 us
  starting transfers between devices  24.3 us (41%)
  waiting for transfers between devices  20 us (34%)
  Pallas kernels  13.9 us (23%)
  between operations  0.74 us (1%)
    ppermute x16, starting transfers between devices, swap(): lax.ppermute(block, axis, [(i, j) for i, j in pairs] + [(j, i) for i, j i...  24.3 us
    ppermute x16, waiting for transfers between devices, swap(): lax.ppermute(block, axis, [(i, j) for i, j in pairs] + [(j, i) for i, j i...  20 us
    pallas_call x1, Pallas kernels, space_grads(): pl.pallas_call(frame_kernel, out_shape=(shape, shape, shape), compiler_pa...  5.53 us
    pallas_call x2, Pallas kernels, split(): pl.pallas_call(functools.partial(split_kernel, sharing, rows, span), in_s...  3.76 us
    pallas_call x2, Pallas kernels, clip_grads(): pl.pallas_call(functools.partial(clip_kernel, window, heads), out_shape=[...  2.67 us
    pallas_call x2, Pallas kernels, join(): pl.pallas_call(functools.partial(join_kernel, sharing, span), in_specs=[p...  1.73 us
  transfers between devices with their start and end apart: 16, of which 5 were waited for; matrix products, arithmetic and copies ran while one was open for 0% of the time, Pallas kernels for 19%

profile of v5, /device:TPU:0, one launch (start us, length us, event | category | flops | bytes accessed | tf_op | source)
XLA Modules:
  0.0 59.3 jit_solution(17433046660094151972)
XLA Ops:
  0.6 1.9 %pack.3 = (bf16[4,144,128]{2,1,0:T(8,128)(2,1)}, bf16[4,144,128]{2,1,0:T(8,128)(2,1)}, bf16[4,144,128]{2,1,0:T(8,128)(2,1)}, bf16[4,144,128]{2,1,0:T(8,128)(2,1)}) custom-call(bf16[1,576,256]{2,1,0:T(8,128)(2,1)} %bitcast.18, bf16[1,576,256]{2,1,0:T(8,128)(2,1)} %bitcast.20, bf16[1,576,256]{2,1,0:T(8,128)(2,1)} %bitcast.22, bf16[1,576,256]{2,1,0:T(8,128)(2,1)} %bitcast.24), custom_call_target="tpu_custom_call" | custom-call | tf_op jit(solution)/shard_map/pack/pallas_call | solution.py:97
  2.5 5.1 %collective-permute-start.10 = (bf16[4,144,128]{2,1,0:T(8,128)(2,1)}, bf16[4,144,128]{2,1,0:T(8,128)(2,1)S(1)}, u32[]{:S(2)}, u32[]{:S(2)}) collective-permute-start(bf16[4,144,128]{2,1,0:T(8,128)(2,1)} %get-tuple-element.51), channel_id=1, source_target_pairs={{0,3},{1,2},{3,0},{2,1},{4,7},{5,6},{7,4},{6,5},{8,11},{9,10},{11,... | collective-permute-start | bytes 442376 | tf_op jit(solution)/shard_map/ppermute | solution.py:117
  7.6 0.0 collective-permute-start.8
  7.7 0.0 copy-start.1
  7.7 0.6 %collective-permute-start.9 = (bf16[4,144,128]{2,1,0:T(8,128)(2,1)}, bf16[4,144,128]{2,1,0:T(8,128)(2,1)S(1)}, u32[]{:S(2)}, u32[]{:S(2)}) collective-permute-start(bf16[4,144,128]{2,1,0:T(8,128)(2,1)} %get-tuple-element.50), channel_id=1, source_target_pairs={{0,2},{1,3},{2,0},{3,1},{4,6},{5,7},{6,4},{7,5},{8,10},{9,11},{10,... | collective-permute-start | bytes 442376 | tf_op jit(solution)/shard_map/ppermute | solution.py:117
  8.3 1.9 %pack.2 = (bf16[4,144,128]{2,1,0:T(8,128)(2,1)}, bf16[4,144,128]{2,1,0:T(8,128)(2,1)}, bf16[4,144,128]{2,1,0:T(8,128)(2,1)}, bf16[4,144,128]{2,1,0:T(8,128)(2,1)}) custom-call(bf16[1,576,256]{2,1,0:T(8,128)(2,1)} %bitcast.19, bf16[1,576,256]{2,1,0:T(8,128)(2,1)} %bitcast.21, bf16[1,576,256]{2,1,0:T(8,128)(2,1)} %bitcast.23, bf16[1,576,256]{2,1,0:T(8,128)(2,1)} %bitcast.25), custom_call_target="tpu_custom_call" | custom-call | tf_op jit(solution)/shard_map/pack/pallas_call | solution.py:97
  10.2 0.0 copy-start.2
  10.2 1.5 %collective-permute-start = (bf16[4,144,128]{2,1,0:T(8,128)(2,1)}, bf16[4,144,128]{2,1,0:T(8,128)(2,1)S(1)}, u32[]{:S(2)}, u32[]{:S(2)}) collective-permute-start(bf16[4,144,128]{2,1,0:T(8,128)(2,1)} %get-tuple-element.39), channel_id=1, source_target_pairs={{0,1},{2,3},{1,0},{3,2},{4,5},{6,7},{5,4},{7,6},{8,9},{10,11},{9,8... | collective-permute-start | bytes 442376 | tf_op jit(solution)/shard_map/ppermute | solution.py:117
  11.7 2.9 %collective-permute-start.1 = (bf16[4,144,128]{2,1,0:T(8,128)(2,1)}, bf16[4,144,128]{2,1,0:T(8,128)(2,1)S(1)}, u32[]{:S(2)}, u32[]{:S(2)}) collective-permute-start(bf16[4,144,128]{2,1,0:T(8,128)(2,1)} %get-tuple-element.40), channel_id=1, source_target_pairs={{0,2},{1,3},{2,0},{3,1},{4,6},{5,7},{6,4},{7,5},{8,10},{9,11},{10,... | collective-permute-start | bytes 442376 | tf_op jit(solution)/shard_map/ppermute | solution.py:117
  14.6 0.0 copy-done.2
  14.6 0.1 select_reduce_fusion.2
  14.6 0.0 collective-permute-done.10.refs_3_
  14.7 1.7 %collective-permute-start.2 = (bf16[4,144,128]{2,1,0:T(8,128)(2,1)}, bf16[4,144,128]{2,1,0:T(8,128)(2,1)S(1)}, u32[]{:S(2)}, u32[]{:S(2)}) collective-permute-start(bf16[4,144,128]{2,1,0:T(8,128)(2,1)} %get-tuple-element.41), channel_id=1, source_target_pairs={{0,3},{1,2},{3,0},{2,1},{4,7},{5,6},{7,4},{6,5},{8,11},{9,10},{11,... | collective-permute-start | bytes 442376 | tf_op jit(solution)/shard_map/ppermute | solution.py:117
  16.4 0.0 collective-permute-done.8.refs_1_
  16.4 5.8 %collective-permute-done.9.refs_2_ = bf16[4,144,128]{2,1,0:T(8,128)(2,1)S(1)} collective-permute-done((bf16[4,144,128]{2,1,0:T(8,128)(2,1)}, bf16[4,144,128]{2,1,0:T(8,128)(2,1)S(1)}, u32[]{:S(2)}, u32[]{:S(2)}) %collective-permute-start.9) | collective-permute-done | bytes 147488 | tf_op jit(solution)/shard_map/ppermute | solution.py:117
  22.2 0.0 copy-done.1
  22.2 0.0 copy-start
  22.2 0.1 sides.3
  22.3 0.1 collective-permute-start.11
  22.4 1.8 %collective-permute-start.12 = (bf16[3,4,144,128]{3,2,1,0:T(8,128)(2,1)S(1)}, bf16[3,4,144,128]{3,2,1,0:T(8,128)(2,1)S(1)}, u32[]{:S(2)}, u32[]{:S(2)}) collective-permute-start(bf16[3,4,144,128]{3,2,1,0:T(8,128)(2,1)S(1)} %get-tuple-element.53), channel_id=1, source_target_pairs={{0,4},{8,12},{16,20},{24,28},{4,0},{12,8},{20,16},{28,24},{1,5},{9... | collective-permute-start | bytes 1327112 | tf_op jit(solution)/shard_map/ppermute | solution.py:117
  24.2 0.2 select_reduce_fusion.1
  24.4 0.0 collective-permute-done.refs_1_
  24.4 6.4 %collective-permute-done.1.refs_2_ = bf16[4,144,128]{2,1,0:T(8,128)(2,1)S(1)} collective-permute-done((bf16[4,144,128]{2,1,0:T(8,128)(2,1)}, bf16[4,144,128]{2,1,0:T(8,128)(2,1)S(1)}, u32[]{:S(2)}, u32[]{:S(2)}) %collective-permute-start.1) | collective-permute-done | bytes 147488 | tf_op jit(solution)/shard_map/ppermute | solution.py:117
  30.8 0.0 collective-permute-done.2.refs_3_
  30.8 0.0 copy-done
  30.8 0.1 sides.2
  31.0 0.3 collective-permute-start.3
  31.3 1.4 %collective-permute-start.4 = (bf16[3,4,144,128]{3,2,1,0:T(8,128)(2,1)S(1)}, bf16[3,4,144,128]{3,2,1,0:T(8,128)(2,1)S(1)}, u32[]{:S(2)}, u32[]{:S(2)}) collective-permute-start(bf16[3,4,144,128]{3,2,1,0:T(8,128)(2,1)S(1)} %get-tuple-element.43), channel_id=1, source_target_pairs={{0,4},{8,12},{16,20},{24,28},{4,0},{12,8},{20,16},{28,24},{1,5},{9... | collective-permute-start | bytes 1327112 | tf_op jit(solution)/shard_map/ppermute | solution.py:117
  32.6 2.8 %collective-permute-done.11.refs_4_ = bf16[3,4,144,128]{3,2,1,0:T(8,128)(2,1)S(1)} collective-permute-done((bf16[3,4,144,128]{3,2,1,0:T(8,128)(2,1)S(1)}, bf16[3,4,144,128]{3,2,1,0:T(8,128)(2,1)S(1)}, u32[]{:S(2)}, u32[]{:S(2)}) %collective-permute-start.11) | collective-permute-done | bytes 442400 | tf_op jit(solution)/shard_map/ppermute | solution.py:117
  35.5 0.0 collective-permute-done.12.refs_5_
  35.5 1.3 %clips.3 = (bf16[3,144,128]{2,1,0:T(8,128)(2,1)S(1)}, bf16[3,144,128]{2,1,0:T(8,128)(2,1)S(1)}, bf16[3,144,128]{2,1,0:T(8,128)(2,1)S(1)}, bf16[3,144,128]{2,1,0:T(8,128)(2,1)S(1)}) custom-call(s32[2,10]{1,0:T(2,128)S(1)} %pad_add_fusion.given_bounds, bf16[4,144,128]{2,1,0:T(8,128)(2,1)S(1)} %copy-done.1, ...), custom_call_target="tpu_custom_call" | custom-call | flops 589824000 | bytes 1474560 | tf_op jit(solution)/shard_map/clips/pallas_call | solution.py:291
  36.8 2.3 %collective-permute-start.13 = (bf16[3,144,128]{2,1,0:T(8,128)(2,1)S(1)}, bf16[3,144,128]{2,1,0:T(8,128)(2,1)S(1)}, u32[]{:S(2)}, u32[]{:S(2)}) collective-permute-start(bf16[3,144,128]{2,1,0:T(8,128)(2,1)S(1)} %get-tuple-element.54), channel_id=1, source_target_pairs={{0,3},{1,2},{3,0},{2,1},{4,7},{5,6},{7,4},{6,5},{8,11},{9,10},{11,... | collective-permute-start | bytes 331784 | tf_op jit(solution)/shard_map/ppermute | solution.py:117
  39.1 0.0 collective-permute-start.14
  39.1 2.1 %collective-permute-start.15 = (bf16[3,144,128]{2,1,0:T(8,128)(2,1)S(1)}, bf16[3,144,128]{2,1,0:T(8,128)(2,1)S(1)}, u32[]{:S(2)}, u32[]{:S(2)}) collective-permute-start(bf16[3,144,128]{2,1,0:T(8,128)(2,1)S(1)} %get-tuple-element.57), channel_id=1, source_target_pairs={{0,1},{2,3},{1,0},{3,2},{4,5},{6,7},{5,4},{7,6},{8,9},{10,11},{9,8... | collective-permute-start | bytes 331784 | tf_op jit(solution)/shard_map/ppermute | solution.py:117
  41.3 3.7 %collective-permute-done.3.refs_4_ = bf16[3,4,144,128]{3,2,1,0:T(8,128)(2,1)S(1)} collective-permute-done((bf16[3,4,144,128]{3,2,1,0:T(8,128)(2,1)S(1)}, bf16[3,4,144,128]{3,2,1,0:T(8,128)(2,1)S(1)}, u32[]{:S(2)}, u32[]{:S(2)}) %collective-permute-start.3) | collective-permute-done | bytes 442400 | tf_op jit(solution)/shard_map/ppermute | solution.py:117
  44.9 0.0 collective-permute-done.4.refs_5_
  44.9 1.3 %clips.2 = (bf16[3,144,128]{2,1,0:T(8,128)(2,1)S(1)}, bf16[3,144,128]{2,1,0:T(8,128)(2,1)S(1)}, bf16[3,144,128]{2,1,0:T(8,128)(2,1)S(1)}, bf16[3,144,128]{2,1,0:T(8,128)(2,1)S(1)}) custom-call(s32[2,10]{1,0:T(2,128)S(1)} %pad_add_fusion.given_bounds, bf16[4,144,128]{2,1,0:T(8,128)(2,1)S(1)} %copy-done, ...), custom_call_target="tpu_custom_call" | custom-call | flops 589824000 | bytes 1474560 | tf_op jit(solution)/shard_map/clips/pallas_call | solution.py:291
  46.3 2.3 %collective-permute-start.5 = (bf16[3,144,128]{2,1,0:T(8,128)(2,1)S(1)}, bf16[3,144,128]{2,1,0:T(8,128)(2,1)S(1)}, u32[]{:S(2)}, u32[]{:S(2)}) collective-permute-start(bf16[3,144,128]{2,1,0:T(8,128)(2,1)S(1)} %get-tuple-element.44), channel_id=1, source_target_pairs={{0,3},{1,2},{3,0},{2,1},{4,7},{5,6},{7,4},{6,5},{8,11},{9,10},{11,... | collective-permute-start | bytes 331784 | tf_op jit(solution)/shard_map/ppermute | solution.py:117
  48.6 1.3 %collective-permute-start.6 = (bf16[3,144,128]{2,1,0:T(8,128)(2,1)S(1)}, bf16[3,144,128]{2,1,0:T(8,128)(2,1)S(1)}, u32[]{:S(2)}, u32[]{:S(2)}) collective-permute-start(bf16[3,144,128]{2,1,0:T(8,128)(2,1)S(1)} %get-tuple-element.45), channel_id=1, source_target_pairs={{0,2},{1,3},{2,0},{3,1},{4,6},{5,7},{6,4},{7,5},{8,10},{9,11},{10,... | collective-permute-start | bytes 331784 | tf_op jit(solution)/shard_map/ppermute | solution.py:117
  49.9 0.0 collective-permute-done.13.refs_0_
  49.9 0.8 %collective-permute-start.7 = (bf16[3,144,128]{2,1,0:T(8,128)(2,1)S(1)}, bf16[3,144,128]{2,1,0:T(8,128)(2,1)S(1)}, u32[]{:S(2)}, u32[]{:S(2)}) collective-permute-start(bf16[3,144,128]{2,1,0:T(8,128)(2,1)S(1)} %get-tuple-element.47), channel_id=1, source_target_pairs={{0,1},{2,3},{1,0},{3,2},{4,5},{6,7},{5,4},{7,6},{8,9},{10,11},{9,8... | collective-permute-start | bytes 331784 | tf_op jit(solution)/shard_map/ppermute | solution.py:117
  50.7 5.5 %space.1 = (bf16[1,576,256]{2,1,0:T(8,128)(2,1)}, bf16[1,576,256]{2,1,0:T(8,128)(2,1)}, bf16[1,576,256]{2,1,0:T(8,128)(2,1)}) custom-call(bf16[1,576,256]{2,1,0:T(8,128)(2,1)} %bitcast.29, bf16[1,576,256]{2,1,0:T(8,128)(2,1)} %bitcast.30, bf16[1,576,256]{2,1,0:T(8,128)(2,1)} %bitcast.31, bf16[1,576,256]{2,1,0:T(8,128)(2,1)} %bitcast.32), custom_call_target="tpu_custom_call" | custom-call | flops 1610612736 | bytes 2064384 | tf_op jit(solution)/shard_map/space/pallas_call | solution.py:58
  56.3 0.0 collective-permute-done.14.refs_1_
  56.3 0.0 collective-permute-done.15.refs_3_
  56.3 0.9 %unpack.2 = (bf16[1,576,256]{2,1,0:T(8,128)(2,1)}, bf16[1,576,256]{2,1,0:T(8,128)(2,1)}, bf16[1,576,256]{2,1,0:T(8,128)(2,1)}) custom-call(bf16[3,144,128]{2,1,0:T(8,128)(2,1)S(1)} %collective-permute-done.13.refs_0_, bf16[3,144,128]{2,1,0:T(8,128)(2,1)S(1)} %collective-permute-done.14.refs_1_, bf16[3,144,128]{2,1,0:T(8,128)(2,1)S(1)} %get-tuple-element.56.refs_2_, ...), custom_call_target="tpu_custom_call" | custom-call | tf_op jit(solution)/shard_map/unpack/pallas_call | solution.py:185
  57.2 0.0 collective-permute-done.5.refs_0_
  57.2 1.3 %collective-permute-done.6.refs_1_ = bf16[3,144,128]{2,1,0:T(8,128)(2,1)S(1)} collective-permute-done((bf16[3,144,128]{2,1,0:T(8,128)(2,1)S(1)}, bf16[3,144,128]{2,1,0:T(8,128)(2,1)S(1)}, u32[]{:S(2)}, u32[]{:S(2)}) %collective-permute-start.6) | collective-permute-done | bytes 110624 | tf_op jit(solution)/shard_map/ppermute | solution.py:117
  58.4 0.0 collective-permute-done.7.refs_3_
  58.4 0.9 %unpack.3 = (bf16[1,576,256]{2,1,0:T(8,128)(2,1)}, bf16[1,576,256]{2,1,0:T(8,128)(2,1)}, bf16[1,576,256]{2,1,0:T(8,128)(2,1)}) custom-call(bf16[3,144,128]{2,1,0:T(8,128)(2,1)S(1)} %collective-permute-done.5.refs_0_, bf16[3,144,128]{2,1,0:T(8,128)(2,1)S(1)} %collective-permute-done.6.refs_1_, ...), custom_call_target="tpu_custom_call", output_to_operand_aliasing={{0}: (4, {}), {1}: (5, {}), {2}: (6, {})} | custom-call | tf_op jit(solution)/shard_map/unpack/pallas_call | solution.py:185
  (4 shorter events, 0.0 us)
Async XLA Ops:
  2.5 12.1 %collective-permute-start.10 = (bf16[4,144,128]{2,1,0:T(8,128)(2,1)}, bf16[4,144,128]{2,1,0:T(8,128)(2,1)S(1)}, u32[]{:S(2)}, u32[]{:S(2)}) collective-permute-start(bf16[4,144,128]{2,1,0:T(8,128)(2,1)} %get-tuple-element.51), channel_id=1, source_target_pairs={{0,3},{1,2},{3,0},{2,1},{4,7},{5,6},{7,4},{6,5},{8,11},{9,10},{11,... | collective-permute-start | bytes 442376 | tf_op jit(solution)/shard_map/ppermute | solution.py:117
  7.6 8.8 %collective-permute-start.8 = (bf16[4,144,128]{2,1,0:T(8,128)(2,1)}, bf16[4,144,128]{2,1,0:T(8,128)(2,1)S(1)}, u32[]{:S(2)}, u32[]{:S(2)}) collective-permute-start(bf16[4,144,128]{2,1,0:T(8,128)(2,1)} %get-tuple-element.49), channel_id=1, source_target_pairs={{0,1},{2,3},{1,0},{3,2},{4,5},{6,7},{5,4},{7,6},{8,9},{10,11},{9,8... | collective-permute-start | bytes 442376 | tf_op jit(solution)/shard_map/ppermute | solution.py:117
  7.7 14.5 %copy-start.1 = (bf16[4,144,128]{2,1,0:T(8,128)(2,1)S(1)}, bf16[4,144,128]{2,1,0:T(8,128)(2,1)}, u32[]{:S(2)}) copy-start(bf16[4,144,128]{2,1,0:T(8,128)(2,1)} %get-tuple-element.48.refs_0_) | copy-start | bytes 442372
  7.7 14.5 %collective-permute-start.9 = (bf16[4,144,128]{2,1,0:T(8,128)(2,1)}, bf16[4,144,128]{2,1,0:T(8,128)(2,1)S(1)}, u32[]{:S(2)}, u32[]{:S(2)}) collective-permute-start(bf16[4,144,128]{2,1,0:T(8,128)(2,1)} %get-tuple-element.50), channel_id=1, source_target_pairs={{0,2},{1,3},{2,0},{3,1},{4,6},{5,7},{6,4},{7,5},{8,10},{9,11},{10,... | collective-permute-start | bytes 442376 | tf_op jit(solution)/shard_map/ppermute | solution.py:117
  10.2 4.4 %copy-start.2 = (s32[16]{0:T(128)S(1)}, s32[16]{0:T(128)}, u32[]{:S(2)}) copy-start(s32[16]{0:T(128)} %param.17) | copy-start | bytes 196
  10.2 14.2 %collective-permute-start = (bf16[4,144,128]{2,1,0:T(8,128)(2,1)}, bf16[4,144,128]{2,1,0:T(8,128)(2,1)S(1)}, u32[]{:S(2)}, u32[]{:S(2)}) collective-permute-start(bf16[4,144,128]{2,1,0:T(8,128)(2,1)} %get-tuple-element.39), channel_id=1, source_target_pairs={{0,1},{2,3},{1,0},{3,2},{4,5},{6,7},{5,4},{7,6},{8,9},{10,11},{9,8... | collective-permute-start | bytes 442376 | tf_op jit(solution)/shard_map/ppermute | solution.py:117
  11.7 19.2 %collective-permute-start.1 = (bf16[4,144,128]{2,1,0:T(8,128)(2,1)}, bf16[4,144,128]{2,1,0:T(8,128)(2,1)S(1)}, u32[]{:S(2)}, u32[]{:S(2)}) collective-permute-start(bf16[4,144,128]{2,1,0:T(8,128)(2,1)} %get-tuple-element.40), channel_id=1, source_target_pairs={{0,2},{1,3},{2,0},{3,1},{4,6},{5,7},{6,4},{7,5},{8,10},{9,11},{10,... | collective-permute-start | bytes 442376 | tf_op jit(solution)/shard_map/ppermute | solution.py:117
  14.7 16.2 %collective-permute-start.2 = (bf16[4,144,128]{2,1,0:T(8,128)(2,1)}, bf16[4,144,128]{2,1,0:T(8,128)(2,1)S(1)}, u32[]{:S(2)}, u32[]{:S(2)}) collective-permute-start(bf16[4,144,128]{2,1,0:T(8,128)(2,1)} %get-tuple-element.41), channel_id=1, source_target_pairs={{0,3},{1,2},{3,0},{2,1},{4,7},{5,6},{7,4},{6,5},{8,11},{9,10},{11,... | collective-permute-start | bytes 442376 | tf_op jit(solution)/shard_map/ppermute | solution.py:117
  22.2 8.6 %copy-start = (bf16[4,144,128]{2,1,0:T(8,128)(2,1)S(1)}, bf16[4,144,128]{2,1,0:T(8,128)(2,1)}, u32[]{:S(2)}) copy-start(bf16[4,144,128]{2,1,0:T(8,128)(2,1)} %get-tuple-element.38.refs_0_) | copy-start | bytes 442372
  22.3 13.1 %collective-permute-start.11 = (bf16[3,4,144,128]{3,2,1,0:T(8,128)(2,1)S(1)}, bf16[3,4,144,128]{3,2,1,0:T(8,128)(2,1)S(1)}, u32[]{:S(2)}, u32[]{:S(2)}) collective-permute-start(bf16[3,4,144,128]{3,2,1,0:T(8,128)(2,1)S(1)} %get-tuple-element.52), channel_id=1, source_target_pairs={{4,8},{12,16},{20,24},{28,0},{8,4},{16,12},{24,20},{0,28},{5,9},{1... | collective-permute-start | bytes 1327112 | tf_op jit(solution)/shard_map/ppermute | solution.py:117
  22.4 13.1 %collective-permute-start.12 = (bf16[3,4,144,128]{3,2,1,0:T(8,128)(2,1)S(1)}, bf16[3,4,144,128]{3,2,1,0:T(8,128)(2,1)S(1)}, u32[]{:S(2)}, u32[]{:S(2)}) collective-permute-start(bf16[3,4,144,128]{3,2,1,0:T(8,128)(2,1)S(1)} %get-tuple-element.53), channel_id=1, source_target_pairs={{0,4},{8,12},{16,20},{24,28},{4,0},{12,8},{20,16},{28,24},{1,5},{9... | collective-permute-start | bytes 1327112 | tf_op jit(solution)/shard_map/ppermute | solution.py:117
  31.0 14.0 %collective-permute-start.3 = (bf16[3,4,144,128]{3,2,1,0:T(8,128)(2,1)S(1)}, bf16[3,4,144,128]{3,2,1,0:T(8,128)(2,1)S(1)}, u32[]{:S(2)}, u32[]{:S(2)}) collective-permute-start(bf16[3,4,144,128]{3,2,1,0:T(8,128)(2,1)S(1)} %get-tuple-element.42), channel_id=1, source_target_pairs={{4,8},{12,16},{20,24},{28,0},{8,4},{16,12},{24,20},{0,28},{5,9},{1... | collective-permute-start | bytes 1327112 | tf_op jit(solution)/shard_map/ppermute | solution.py:117
  31.3 13.7 %collective-permute-start.4 = (bf16[3,4,144,128]{3,2,1,0:T(8,128)(2,1)S(1)}, bf16[3,4,144,128]{3,2,1,0:T(8,128)(2,1)S(1)}, u32[]{:S(2)}, u32[]{:S(2)}) collective-permute-start(bf16[3,4,144,128]{3,2,1,0:T(8,128)(2,1)S(1)} %get-tuple-element.43), channel_id=1, source_target_pairs={{0,4},{8,12},{16,20},{24,28},{4,0},{12,8},{20,16},{28,24},{1,5},{9... | collective-permute-start | bytes 1327112 | tf_op jit(solution)/shard_map/ppermute | solution.py:117
  36.8 13.1 %collective-permute-start.13 = (bf16[3,144,128]{2,1,0:T(8,128)(2,1)S(1)}, bf16[3,144,128]{2,1,0:T(8,128)(2,1)S(1)}, u32[]{:S(2)}, u32[]{:S(2)}) collective-permute-start(bf16[3,144,128]{2,1,0:T(8,128)(2,1)S(1)} %get-tuple-element.54), channel_id=1, source_target_pairs={{0,3},{1,2},{3,0},{2,1},{4,7},{5,6},{7,4},{6,5},{8,11},{9,10},{11,... | collective-permute-start | bytes 331784 | tf_op jit(solution)/shard_map/ppermute | solution.py:117
  39.1 17.2 %collective-permute-start.14 = (bf16[3,144,128]{2,1,0:T(8,128)(2,1)S(1)}, bf16[3,144,128]{2,1,0:T(8,128)(2,1)S(1)}, u32[]{:S(2)}, u32[]{:S(2)}) collective-permute-start(bf16[3,144,128]{2,1,0:T(8,128)(2,1)S(1)} %get-tuple-element.55), channel_id=1, source_target_pairs={{0,2},{1,3},{2,0},{3,1},{4,6},{5,7},{6,4},{7,5},{8,10},{9,11},{10,... | collective-permute-start | bytes 331784 | tf_op jit(solution)/shard_map/ppermute | solution.py:117
  39.1 17.2 %collective-permute-start.15 = (bf16[3,144,128]{2,1,0:T(8,128)(2,1)S(1)}, bf16[3,144,128]{2,1,0:T(8,128)(2,1)S(1)}, u32[]{:S(2)}, u32[]{:S(2)}) collective-permute-start(bf16[3,144,128]{2,1,0:T(8,128)(2,1)S(1)} %get-tuple-element.57), channel_id=1, source_target_pairs={{0,1},{2,3},{1,0},{3,2},{4,5},{6,7},{5,4},{7,6},{8,9},{10,11},{9,8... | collective-permute-start | bytes 331784 | tf_op jit(solution)/shard_map/ppermute | solution.py:117
  46.3 10.9 %collective-permute-start.5 = (bf16[3,144,128]{2,1,0:T(8,128)(2,1)S(1)}, bf16[3,144,128]{2,1,0:T(8,128)(2,1)S(1)}, u32[]{:S(2)}, u32[]{:S(2)}) collective-permute-start(bf16[3,144,128]{2,1,0:T(8,128)(2,1)S(1)} %get-tuple-element.44), channel_id=1, source_target_pairs={{0,3},{1,2},{3,0},{2,1},{4,7},{5,6},{7,4},{6,5},{8,11},{9,10},{11,... | collective-permute-start | bytes 331784 | tf_op jit(solution)/shard_map/ppermute | solution.py:117
  48.6 9.8 %collective-permute-start.6 = (bf16[3,144,128]{2,1,0:T(8,128)(2,1)S(1)}, bf16[3,144,128]{2,1,0:T(8,128)(2,1)S(1)}, u32[]{:S(2)}, u32[]{:S(2)}) collective-permute-start(bf16[3,144,128]{2,1,0:T(8,128)(2,1)S(1)} %get-tuple-element.45), channel_id=1, source_target_pairs={{0,2},{1,3},{2,0},{3,1},{4,6},{5,7},{6,4},{7,5},{8,10},{9,11},{10,... | collective-permute-start | bytes 331784 | tf_op jit(solution)/shard_map/ppermute | solution.py:117
  49.9 8.5 %collective-permute-start.7 = (bf16[3,144,128]{2,1,0:T(8,128)(2,1)S(1)}, bf16[3,144,128]{2,1,0:T(8,128)(2,1)S(1)}, u32[]{:S(2)}, u32[]{:S(2)}) collective-permute-start(bf16[3,144,128]{2,1,0:T(8,128)(2,1)S(1)} %get-tuple-element.47), channel_id=1, source_target_pairs={{0,1},{2,3},{1,0},{3,2},{4,5},{6,7},{5,4},{7,6},{8,9},{10,11},{9,8... | collective-permute-start | bytes 331784 | tf_op jit(solution)/shard_map/ppermute | solution.py:117

commit v6 on v4

--- a/solution.py
+++ b/solution.py
@@ -210,14 +210,12 @@
 
     for step, ref in enumerate(own):
         widen(ref, halo + (lax.axis_index("seq") ^ step))
-    copy.wait()
-    lowest, highest = bounds[0, halo], bounds[1, halo + window - 1]
     for start, ref in zip((1, 0), sides_of):
         is_next = (lax.axis_index("grp") & 1) == start
         for at in range(halo):
-            frame = at + jnp.where(is_next, halo + window, 0)
-            needed = (frame >= lowest) & (frame < highest)
-            pl.when(needed)(functools.partial(widen, ref.at[at], frame))
+            widen(ref.at[at], at + jnp.where(is_next, halo + window, 0))
+    copy.wait()
+    lowest, highest = bounds[0, halo], bounds[1, halo + window - 1]
 
     def partners(frame):
         first, last = bounds[0, frame], bounds[1, frame]
@@ -344,9 +342,9 @@
     space_in = turned(q_space, k_space, v_space, cot_space)
     packed = [list(split(time, span, n, sharing)) for span in spans]
     own = [exchange(packed[0])]
+    packed[1][n // 2 :], own[0][-1] = gated(packed[1][n // 2 :], own[0][-1])
+    own.append(exchange(packed[1]))
     space = space_grads(*space_in)
-    packed[1][2:], own[0][2], space = gated(packed[1][2:], own[0][2], space)
-    own.append(exchange(packed[1]))
     beside = [
         [neighbours(ends, start) for ends, start in zip(sides(blocks), (1, 0))] for blocks in own
     ]

time: 59.7 us -> 64.1 us (1.074)
  starting transfers between devices: 23.9 us -> 27.8 us
  waiting for transfers between devices: 20 us -> 20.8 us
    ppermute x16, starting transfers between devices: 23.9 us -> 27.8 us  [swap(): lax.ppermute(block, axis, [(i, j) for i, j in pairs] + [(j, i) for i, j i...]
    ppermute x16, waiting for transfers between devices: 20 us -> 20.8 us  [swap(): lax.ppermute(block, axis, [(i, j) for i, j in pairs] + [(j, i) for i, j i...]
  transfers between devices with their start and end apart: 16 -> 16, of which waited for: 5 -> 5; matrix products, arithmetic and copies ran while one was open for 0% -> 0% of each run, Pallas kernels for 20% -> 18%
where the time goes in v6:
time: 64.1 us; the launch traced here: 63.8 us
  starting transfers between devices  27.8 us (43%)
  waiting for transfers between devices  20.8 us (32%)
  Pallas kernels  14.1 us (22%)
  between operations  0.79 us (1%)
    ppermute x16, starting transfers between devices, swap(): lax.ppermute(block, axis, [(i, j) for i, j in pairs] + [(j, i) for i, j i...  27.8 us
    ppermute x16, waiting for transfers between devices, swap(): lax.ppermute(block, axis, [(i, j) for i, j in pairs] + [(j, i) for i, j i...  20.8 us
    pallas_call x1, Pallas kernels, space_grads(): pl.pallas_call(frame_kernel, out_shape=(shape, shape, shape), compiler_pa...  5.52 us
    pallas_call x2, Pallas kernels, split(): pl.pallas_call(functools.partial(split_kernel, sharing, rows, span), in_s...  3.76 us
    pallas_call x2, Pallas kernels, clip_grads(): pl.pallas_call(functools.partial(clip_kernel, window, heads), out_shape=[...  2.77 us
    pallas_call x2, Pallas kernels, join(): pl.pallas_call(functools.partial(join_kernel, sharing, span), in_specs=[p...  1.75 us
  transfers between devices with their start and end apart: 16, of which 5 were waited for; matrix products, arithmetic and copies ran while one was open for 0% of the time, Pallas kernels for 18%

profile of v6, /device:TPU:0, one launch (start us, length us, event | category | flops | bytes accessed | tf_op | source)
XLA Modules:
  0.0 63.8 jit_solution(8258383942041455506)
XLA Ops:
  0.6 1.9 %pack.3 = (bf16[4,144,128]{2,1,0:T(8,128)(2,1)}, bf16[4,144,128]{2,1,0:T(8,128)(2,1)}, bf16[4,144,128]{2,1,0:T(8,128)(2,1)}, bf16[4,144,128]{2,1,0:T(8,128)(2,1)}) custom-call(bf16[1,576,256]{2,1,0:T(8,128)(2,1)} %bitcast.18, bf16[1,576,256]{2,1,0:T(8,128)(2,1)} %bitcast.20, bf16[1,576,256]{2,1,0:T(8,128)(2,1)} %bitcast.22, bf16[1,576,256]{2,1,0:T(8,128)(2,1)} %bitcast.24), custom_call_target="tpu_custom_call" | custom-call | tf_op jit(solution)/shard_map/pack/pallas_call | solution.py:97
  2.5 5.1 %collective-permute-start.1 = (bf16[4,144,128]{2,1,0:T(8,128)(2,1)}, bf16[4,144,128]{2,1,0:T(8,128)(2,1)S(1)}, u32[]{:S(2)}, u32[]{:S(2)}) collective-permute-start(bf16[4,144,128]{2,1,0:T(8,128)(2,1)} %get-tuple-element.45), channel_id=1, source_target_pairs={{0,3},{1,2},{3,0},{2,1},{4,7},{5,6},{7,4},{6,5},{8,11},{9,10},{11,... | collective-permute-start | bytes 442376 | tf_op jit(solution)/shard_map/ppermute | solution.py:117
  7.6 0.0 collective-permute-start.10
  7.7 0.0 copy-start.1
  7.7 0.6 %collective-permute-start.9 = (bf16[4,144,128]{2,1,0:T(8,128)(2,1)}, bf16[4,144,128]{2,1,0:T(8,128)(2,1)S(1)}, u32[]{:S(2)}, u32[]{:S(2)}) collective-permute-start(bf16[4,144,128]{2,1,0:T(8,128)(2,1)} %get-tuple-element.55), channel_id=1, source_target_pairs={{0,1},{2,3},{1,0},{3,2},{4,5},{6,7},{5,4},{7,6},{8,9},{10,11},{9,8... | collective-permute-start | bytes 442376 | tf_op jit(solution)/shard_map/ppermute | solution.py:117
  8.3 1.9 %pack.2 = (bf16[4,144,128]{2,1,0:T(8,128)(2,1)}, bf16[4,144,128]{2,1,0:T(8,128)(2,1)}, bf16[4,144,128]{2,1,0:T(8,128)(2,1)}, bf16[4,144,128]{2,1,0:T(8,128)(2,1)}) custom-call(bf16[1,576,256]{2,1,0:T(8,128)(2,1)} %bitcast.19, bf16[1,576,256]{2,1,0:T(8,128)(2,1)} %bitcast.21, bf16[1,576,256]{2,1,0:T(8,128)(2,1)} %bitcast.23, bf16[1,576,256]{2,1,0:T(8,128)(2,1)} %bitcast.25), custom_call_target="tpu_custom_call" | custom-call | tf_op jit(solution)/shard_map/pack/pallas_call | solution.py:97
  10.2 0.0 copy-start.2
  10.2 1.5 %collective-permute-start = (bf16[4,144,128]{2,1,0:T(8,128)(2,1)}, bf16[4,144,128]{2,1,0:T(8,128)(2,1)S(1)}, u32[]{:S(2)}, u32[]{:S(2)}) collective-permute-start(bf16[4,144,128]{2,1,0:T(8,128)(2,1)} %get-tuple-element.42), channel_id=1, source_target_pairs={{0,1},{2,3},{1,0},{3,2},{4,5},{6,7},{5,4},{7,6},{8,9},{10,11},{9,8... | collective-permute-start | bytes 442376 | tf_op jit(solution)/shard_map/ppermute | solution.py:117
  11.6 0.0 copy-done.2
  11.6 0.1 select_reduce_fusion.2
  11.7 0.9 %collective-permute-done.1.refs_3_ = bf16[4,144,128]{2,1,0:T(8,128)(2,1)S(1)} collective-permute-done((bf16[4,144,128]{2,1,0:T(8,128)(2,1)}, bf16[4,144,128]{2,1,0:T(8,128)(2,1)S(1)}, u32[]{:S(2)}, u32[]{:S(2)}) %collective-permute-start.1) | collective-permute-done | bytes 147488 | tf_op jit(solution)/shard_map/ppermute | solution.py:117
  12.6 7.3 %collective-permute-start.2 = (bf16[4,144,128]{2,1,0:T(8,128)(2,1)}, bf16[4,144,128]{2,1,0:T(8,128)(2,1)S(1)}, u32[]{:S(2)}, u32[]{:S(2)}) collective-permute-start(bf16[4,144,128]{2,1,0:T(8,128)(2,1)} %get-tuple-element.46), channel_id=1, source_target_pairs={{0,2},{1,3},{2,0},{3,1},{4,6},{5,7},{6,4},{7,5},{8,10},{9,11},{10,... | collective-permute-start | bytes 442376 | tf_op jit(solution)/shard_map/ppermute | solution.py:117
  19.9 1.1 %collective-permute-start.3 = (bf16[4,144,128]{2,1,0:T(8,128)(2,1)}, bf16[4,144,128]{2,1,0:T(8,128)(2,1)S(1)}, u32[]{:S(2)}, u32[]{:S(2)}) collective-permute-start(bf16[4,144,128]{2,1,0:T(8,128)(2,1)} %get-tuple-element.47), channel_id=1, source_target_pairs={{0,3},{1,2},{3,0},{2,1},{4,7},{5,6},{7,4},{6,5},{8,11},{9,10},{11,... | collective-permute-start | bytes 442376 | tf_op jit(solution)/shard_map/ppermute | solution.py:117
  21.1 6.6 %collective-permute-done.10.refs_2_ = bf16[4,144,128]{2,1,0:T(8,128)(2,1)S(1)} collective-permute-done((bf16[4,144,128]{2,1,0:T(8,128)(2,1)}, bf16[4,144,128]{2,1,0:T(8,128)(2,1)S(1)}, u32[]{:S(2)}, u32[]{:S(2)}) %collective-permute-start.10) | collective-permute-done | bytes 147488 | tf_op jit(solution)/shard_map/ppermute | solution.py:117
  27.7 0.0 collective-permute-done.9.refs_1_
  27.7 0.0 copy-done.1
  27.7 0.0 copy-start
  27.7 0.1 sides.3
  27.8 0.1 collective-permute-start.11
  27.9 1.6 %collective-permute-start.12 = (bf16[3,4,144,128]{3,2,1,0:T(8,128)(2,1)S(1)}, bf16[3,4,144,128]{3,2,1,0:T(8,128)(2,1)S(1)}, u32[]{:S(2)}, u32[]{:S(2)}) collective-permute-start(bf16[3,4,144,128]{3,2,1,0:T(8,128)(2,1)S(1)} %get-tuple-element.59), channel_id=1, source_target_pairs={{0,4},{8,12},{16,20},{24,28},{4,0},{12,8},{20,16},{28,24},{1,5},{9... | collective-permute-start | bytes 1327112 | tf_op jit(solution)/shard_map/ppermute | solution.py:117
  29.5 0.2 select_reduce_fusion.1
  29.7 0.0 collective-permute-done.refs_1_
  29.7 1.1 %collective-permute-done.2.refs_2_ = bf16[4,144,128]{2,1,0:T(8,128)(2,1)S(1)} collective-permute-done((bf16[4,144,128]{2,1,0:T(8,128)(2,1)}, bf16[4,144,128]{2,1,0:T(8,128)(2,1)S(1)}, u32[]{:S(2)}, u32[]{:S(2)}) %collective-permute-start.2) | collective-permute-done | bytes 147488 | tf_op jit(solution)/shard_map/ppermute | solution.py:117
  30.8 0.0 collective-permute-done.3.refs_3_
  30.8 0.0 copy-done
  30.8 0.1 sides.2
  31.0 0.3 collective-permute-start.4
  31.3 1.4 %collective-permute-start.5 = (bf16[3,4,144,128]{3,2,1,0:T(8,128)(2,1)S(1)}, bf16[3,4,144,128]{3,2,1,0:T(8,128)(2,1)S(1)}, u32[]{:S(2)}, u32[]{:S(2)}) collective-permute-start(bf16[3,4,144,128]{3,2,1,0:T(8,128)(2,1)S(1)} %get-tuple-element.49), channel_id=1, source_target_pairs={{0,4},{8,12},{16,20},{24,28},{4,0},{12,8},{20,16},{28,24},{1,5},{9... | collective-permute-start | bytes 1327112 | tf_op jit(solution)/shard_map/ppermute | solution.py:117
  32.6 8.5 %collective-permute-done.11.refs_4_ = bf16[3,4,144,128]{3,2,1,0:T(8,128)(2,1)S(1)} collective-permute-done((bf16[3,4,144,128]{3,2,1,0:T(8,128)(2,1)S(1)}, bf16[3,4,144,128]{3,2,1,0:T(8,128)(2,1)S(1)}, u32[]{:S(2)}, u32[]{:S(2)}) %collective-permute-start.11) | collective-permute-done | bytes 442400 | tf_op jit(solution)/shard_map/ppermute | solution.py:117
  41.1 0.0 collective-permute-done.12.refs_5_
  41.2 1.4 %clips.3 = (bf16[3,144,128]{2,1,0:T(8,128)(2,1)S(1)}, bf16[3,144,128]{2,1,0:T(8,128)(2,1)S(1)}, bf16[3,144,128]{2,1,0:T(8,128)(2,1)S(1)}, bf16[3,144,128]{2,1,0:T(8,128)(2,1)S(1)}) custom-call(s32[2,10]{1,0:T(2,128)S(1)} %pad_add_fusion.given_bounds, bf16[4,144,128]{2,1,0:T(8,128)(2,1)S(1)} %copy-done.1, ...), custom_call_target="tpu_custom_call" | custom-call | flops 589824000 | bytes 1474560 | tf_op jit(solution)/shard_map/clips/pallas_call | solution.py:289
  42.5 0.1 collective-permute-start.13
  42.6 0.1 collective-permute-start.14
  42.7 4.3 %collective-permute-start.15 = (bf16[3,144,128]{2,1,0:T(8,128)(2,1)S(1)}, bf16[3,144,128]{2,1,0:T(8,128)(2,1)S(1)}, u32[]{:S(2)}, u32[]{:S(2)}) collective-permute-start(bf16[3,144,128]{2,1,0:T(8,128)(2,1)S(1)} %get-tuple-element.63), channel_id=1, source_target_pairs={{0,1},{2,3},{1,0},{3,2},{4,5},{6,7},{5,4},{7,6},{8,9},{10,11},{9,8... | collective-permute-start | bytes 331784 | tf_op jit(solution)/shard_map/ppermute | solution.py:117
  47.0 3.6 %collective-permute-done.4.refs_4_ = bf16[3,4,144,128]{3,2,1,0:T(8,128)(2,1)S(1)} collective-permute-done((bf16[3,4,144,128]{3,2,1,0:T(8,128)(2,1)S(1)}, bf16[3,4,144,128]{3,2,1,0:T(8,128)(2,1)S(1)}, u32[]{:S(2)}, u32[]{:S(2)}) %collective-permute-start.4) | collective-permute-done | bytes 442400 | tf_op jit(solution)/shard_map/ppermute | solution.py:117
  50.6 0.0 collective-permute-done.5.refs_5_
  50.6 1.4 %clips.2 = (bf16[3,144,128]{2,1,0:T(8,128)(2,1)S(1)}, bf16[3,144,128]{2,1,0:T(8,128)(2,1)S(1)}, bf16[3,144,128]{2,1,0:T(8,128)(2,1)S(1)}, bf16[3,144,128]{2,1,0:T(8,128)(2,1)S(1)}) custom-call(s32[2,10]{1,0:T(2,128)S(1)} %pad_add_fusion.given_bounds, bf16[4,144,128]{2,1,0:T(8,128)(2,1)S(1)} %copy-done, ...), custom_call_target="tpu_custom_call" | custom-call | flops 589824000 | bytes 1474560 | tf_op jit(solution)/shard_map/clips/pallas_call | solution.py:289
  52.0 0.1 collective-permute-start.6
  52.1 0.1 collective-permute-start.7
  52.2 0.0 collective-permute-done.13.refs_0_
  52.2 4.3 %collective-permute-start.8 = (bf16[3,144,128]{2,1,0:T(8,128)(2,1)S(1)}, bf16[3,144,128]{2,1,0:T(8,128)(2,1)S(1)}, u32[]{:S(2)}, u32[]{:S(2)}) collective-permute-start(bf16[3,144,128]{2,1,0:T(8,128)(2,1)S(1)} %get-tuple-element.53), channel_id=1, source_target_pairs={{0,1},{2,3},{1,0},{3,2},{4,5},{6,7},{5,4},{7,6},{8,9},{10,11},{9,8... | collective-permute-start | bytes 331784 | tf_op jit(solution)/shard_map/ppermute | solution.py:117
  56.5 5.5 %space.1 = (bf16[1,576,256]{2,1,0:T(8,128)(2,1)}, bf16[1,576,256]{2,1,0:T(8,128)(2,1)}, bf16[1,576,256]{2,1,0:T(8,128)(2,1)}) custom-call(bf16[1,576,256]{2,1,0:T(8,128)(2,1)} %bitcast.29, bf16[1,576,256]{2,1,0:T(8,128)(2,1)} %bitcast.30, bf16[1,576,256]{2,1,0:T(8,128)(2,1)} %bitcast.31, bf16[1,576,256]{2,1,0:T(8,128)(2,1)} %bitcast.32), custom_call_target="tpu_custom_call" | custom-call | flops 1610612736 | bytes 2064384 | tf_op jit(solution)/shard_map/space/pallas_call | solution.py:58
  62.0 0.0 collective-permute-done.14.refs_1_
  62.0 0.0 collective-permute-done.15.refs_3_
  62.0 0.9 %unpack.2 = (bf16[1,576,256]{2,1,0:T(8,128)(2,1)}, bf16[1,576,256]{2,1,0:T(8,128)(2,1)}, bf16[1,576,256]{2,1,0:T(8,128)(2,1)}) custom-call(bf16[3,144,128]{2,1,0:T(8,128)(2,1)S(1)} %collective-permute-done.13.refs_0_, bf16[3,144,128]{2,1,0:T(8,128)(2,1)S(1)} %collective-permute-done.14.refs_1_, bf16[3,144,128]{2,1,0:T(8,128)(2,1)S(1)} %get-tuple-element.62.refs_2_, ...), custom_call_target="tpu_custom_call" | custom-call | tf_op jit(solution)/shard_map/unpack/pallas_call | solution.py:185
  62.9 0.0 collective-permute-done.6.refs_0_
  62.9 0.0 collective-permute-done.7.refs_1_
  62.9 0.0 collective-permute-done.8.refs_3_
  62.9 0.9 %unpack.3 = (bf16[1,576,256]{2,1,0:T(8,128)(2,1)}, bf16[1,576,256]{2,1,0:T(8,128)(2,1)}, bf16[1,576,256]{2,1,0:T(8,128)(2,1)}) custom-call(bf16[3,144,128]{2,1,0:T(8,128)(2,1)S(1)} %collective-permute-done.6.refs_0_, bf16[3,144,128]{2,1,0:T(8,128)(2,1)S(1)} %collective-permute-done.7.refs_1_, ...), custom_call_target="tpu_custom_call", output_to_operand_aliasing={{0}: (4, {}), {1}: (5, {}), {2}: (6, {})} | custom-call | tf_op jit(solution)/shard_map/unpack/pallas_call | solution.py:185
  (4 shorter events, 0.0 us)
Async XLA Ops:
  2.5 10.1 %collective-permute-start.1 = (bf16[4,144,128]{2,1,0:T(8,128)(2,1)}, bf16[4,144,128]{2,1,0:T(8,128)(2,1)S(1)}, u32[]{:S(2)}, u32[]{:S(2)}) collective-permute-start(bf16[4,144,128]{2,1,0:T(8,128)(2,1)} %get-tuple-element.45), channel_id=1, source_target_pairs={{0,3},{1,2},{3,0},{2,1},{4,7},{5,6},{7,4},{6,5},{8,11},{9,10},{11,... | collective-permute-start | bytes 442376 | tf_op jit(solution)/shard_map/ppermute | solution.py:117
  7.6 20.0 %collective-permute-start.10 = (bf16[4,144,128]{2,1,0:T(8,128)(2,1)}, bf16[4,144,128]{2,1,0:T(8,128)(2,1)S(1)}, u32[]{:S(2)}, u32[]{:S(2)}) collective-permute-start(bf16[4,144,128]{2,1,0:T(8,128)(2,1)} %get-tuple-element.56), channel_id=1, source_target_pairs={{0,2},{1,3},{2,0},{3,1},{4,6},{5,7},{6,4},{7,5},{8,10},{9,11},{10,... | collective-permute-start | bytes 442376 | tf_op jit(solution)/shard_map/ppermute | solution.py:117
  7.7 20.0 %copy-start.1 = (bf16[4,144,128]{2,1,0:T(8,128)(2,1)S(1)}, bf16[4,144,128]{2,1,0:T(8,128)(2,1)}, u32[]{:S(2)}) copy-start(bf16[4,144,128]{2,1,0:T(8,128)(2,1)} %get-tuple-element.54.refs_0_) | copy-start | bytes 442372
  7.7 20.0 %collective-permute-start.9 = (bf16[4,144,128]{2,1,0:T(8,128)(2,1)}, bf16[4,144,128]{2,1,0:T(8,128)(2,1)S(1)}, u32[]{:S(2)}, u32[]{:S(2)}) collective-permute-start(bf16[4,144,128]{2,1,0:T(8,128)(2,1)} %get-tuple-element.55), channel_id=1, source_target_pairs={{0,1},{2,3},{1,0},{3,2},{4,5},{6,7},{5,4},{7,6},{8,9},{10,11},{9,8... | collective-permute-start | bytes 442376 | tf_op jit(solution)/shard_map/ppermute | solution.py:117
  10.2 1.5 %copy-start.2 = (s32[16]{0:T(128)S(1)}, s32[16]{0:T(128)}, u32[]{:S(2)}) copy-start(s32[16]{0:T(128)} %param.17) | copy-start | bytes 196
  10.2 19.5 %collective-permute-start = (bf16[4,144,128]{2,1,0:T(8,128)(2,1)}, bf16[4,144,128]{2,1,0:T(8,128)(2,1)S(1)}, u32[]{:S(2)}, u32[]{:S(2)}) collective-permute-start(bf16[4,144,128]{2,1,0:T(8,128)(2,1)} %get-tuple-element.42), channel_id=1, source_target_pairs={{0,1},{2,3},{1,0},{3,2},{4,5},{6,7},{5,4},{7,6},{8,9},{10,11},{9,8... | collective-permute-start | bytes 442376 | tf_op jit(solution)/shard_map/ppermute | solution.py:117
  12.6 18.2 %collective-permute-start.2 = (bf16[4,144,128]{2,1,0:T(8,128)(2,1)}, bf16[4,144,128]{2,1,0:T(8,128)(2,1)S(1)}, u32[]{:S(2)}, u32[]{:S(2)}) collective-permute-start(bf16[4,144,128]{2,1,0:T(8,128)(2,1)} %get-tuple-element.46), channel_id=1, source_target_pairs={{0,2},{1,3},{2,0},{3,1},{4,6},{5,7},{6,4},{7,5},{8,10},{9,11},{10,... | collective-permute-start | bytes 442376 | tf_op jit(solution)/shard_map/ppermute | solution.py:117
  19.9 10.9 %collective-permute-start.3 = (bf16[4,144,128]{2,1,0:T(8,128)(2,1)}, bf16[4,144,128]{2,1,0:T(8,128)(2,1)S(1)}, u32[]{:S(2)}, u32[]{:S(2)}) collective-permute-start(bf16[4,144,128]{2,1,0:T(8,128)(2,1)} %get-tuple-element.47), channel_id=1, source_target_pairs={{0,3},{1,2},{3,0},{2,1},{4,7},{5,6},{7,4},{6,5},{8,11},{9,10},{11,... | collective-permute-start | bytes 442376 | tf_op jit(solution)/shard_map/ppermute | solution.py:117
  27.7 3.2 %copy-start = (bf16[4,144,128]{2,1,0:T(8,128)(2,1)S(1)}, bf16[4,144,128]{2,1,0:T(8,128)(2,1)}, u32[]{:S(2)}) copy-start(bf16[4,144,128]{2,1,0:T(8,128)(2,1)} %get-tuple-element.41.refs_0_) | copy-start | bytes 442372
  27.8 13.3 %collective-permute-start.11 = (bf16[3,4,144,128]{3,2,1,0:T(8,128)(2,1)S(1)}, bf16[3,4,144,128]{3,2,1,0:T(8,128)(2,1)S(1)}, u32[]{:S(2)}, u32[]{:S(2)}) collective-permute-start(bf16[3,4,144,128]{3,2,1,0:T(8,128)(2,1)S(1)} %get-tuple-element.58), channel_id=1, source_target_pairs={{4,8},{12,16},{20,24},{28,0},{8,4},{16,12},{24,20},{0,28},{5,9},{1... | collective-permute-start | bytes 1327112 | tf_op jit(solution)/shard_map/ppermute | solution.py:117
  27.9 13.3 %collective-permute-start.12 = (bf16[3,4,144,128]{3,2,1,0:T(8,128)(2,1)S(1)}, bf16[3,4,144,128]{3,2,1,0:T(8,128)(2,1)S(1)}, u32[]{:S(2)}, u32[]{:S(2)}) collective-permute-start(bf16[3,4,144,128]{3,2,1,0:T(8,128)(2,1)S(1)} %get-tuple-element.59), channel_id=1, source_target_pairs={{0,4},{8,12},{16,20},{24,28},{4,0},{12,8},{20,16},{28,24},{1,5},{9... | collective-permute-start | bytes 1327112 | tf_op jit(solution)/shard_map/ppermute | solution.py:117
  31.0 19.7 %collective-permute-start.4 = (bf16[3,4,144,128]{3,2,1,0:T(8,128)(2,1)S(1)}, bf16[3,4,144,128]{3,2,1,0:T(8,128)(2,1)S(1)}, u32[]{:S(2)}, u32[]{:S(2)}) collective-permute-start(bf16[3,4,144,128]{3,2,1,0:T(8,128)(2,1)S(1)} %get-tuple-element.48), channel_id=1, source_target_pairs={{4,8},{12,16},{20,24},{28,0},{8,4},{16,12},{24,20},{0,28},{5,9},{1... | collective-permute-start | bytes 1327112 | tf_op jit(solution)/shard_map/ppermute | solution.py:117
  31.3 19.4 %collective-permute-start.5 = (bf16[3,4,144,128]{3,2,1,0:T(8,128)(2,1)S(1)}, bf16[3,4,144,128]{3,2,1,0:T(8,128)(2,1)S(1)}, u32[]{:S(2)}, u32[]{:S(2)}) collective-permute-start(bf16[3,4,144,128]{3,2,1,0:T(8,128)(2,1)S(1)} %get-tuple-element.49), channel_id=1, source_target_pairs={{0,4},{8,12},{16,20},{24,28},{4,0},{12,8},{20,16},{28,24},{1,5},{9... | collective-permute-start | bytes 1327112 | tf_op jit(solution)/shard_map/ppermute | solution.py:117
  42.5 9.6 %collective-permute-start.13 = (bf16[3,144,128]{2,1,0:T(8,128)(2,1)S(1)}, bf16[3,144,128]{2,1,0:T(8,128)(2,1)S(1)}, u32[]{:S(2)}, u32[]{:S(2)}) collective-permute-start(bf16[3,144,128]{2,1,0:T(8,128)(2,1)S(1)} %get-tuple-element.60), channel_id=1, source_target_pairs={{0,3},{1,2},{3,0},{2,1},{4,7},{5,6},{7,4},{6,5},{8,11},{9,10},{11,... | collective-permute-start | bytes 331784 | tf_op jit(solution)/shard_map/ppermute | solution.py:117
  42.6 19.4 %collective-permute-start.14 = (bf16[3,144,128]{2,1,0:T(8,128)(2,1)S(1)}, bf16[3,144,128]{2,1,0:T(8,128)(2,1)S(1)}, u32[]{:S(2)}, u32[]{:S(2)}) collective-permute-start(bf16[3,144,128]{2,1,0:T(8,128)(2,1)S(1)} %get-tuple-element.61), channel_id=1, source_target_pairs={{0,2},{1,3},{2,0},{3,1},{4,6},{5,7},{6,4},{7,5},{8,10},{9,11},{10,... | collective-permute-start | bytes 331784 | tf_op jit(solution)/shard_map/ppermute | solution.py:117
  42.7 19.3 %collective-permute-start.15 = (bf16[3,144,128]{2,1,0:T(8,128)(2,1)S(1)}, bf16[3,144,128]{2,1,0:T(8,128)(2,1)S(1)}, u32[]{:S(2)}, u32[]{:S(2)}) collective-permute-start(bf16[3,144,128]{2,1,0:T(8,128)(2,1)S(1)} %get-tuple-element.63), channel_id=1, source_target_pairs={{0,1},{2,3},{1,0},{3,2},{4,5},{6,7},{5,4},{7,6},{8,9},{10,11},{9,8... | collective-permute-start | bytes 331784 | tf_op jit(solution)/shard_map/ppermute | solution.py:117
  52.0 10.9 %collective-permute-start.6 = (bf16[3,144,128]{2,1,0:T(8,128)(2,1)S(1)}, bf16[3,144,128]{2,1,0:T(8,128)(2,1)S(1)}, u32[]{:S(2)}, u32[]{:S(2)}) collective-permute-start(bf16[3,144,128]{2,1,0:T(8,128)(2,1)S(1)} %get-tuple-element.50), channel_id=1, source_target_pairs={{0,3},{1,2},{3,0},{2,1},{4,7},{5,6},{7,4},{6,5},{8,11},{9,10},{11,... | collective-permute-start | bytes 331784 | tf_op jit(solution)/shard_map/ppermute | solution.py:117
  52.1 10.8 %collective-permute-start.7 = (bf16[3,144,128]{2,1,0:T(8,128)(2,1)S(1)}, bf16[3,144,128]{2,1,0:T(8,128)(2,1)S(1)}, u32[]{:S(2)}, u32[]{:S(2)}) collective-permute-start(bf16[3,144,128]{2,1,0:T(8,128)(2,1)S(1)} %get-tuple-element.51), channel_id=1, source_target_pairs={{0,2},{1,3},{2,0},{3,1},{4,6},{5,7},{6,4},{7,5},{8,10},{9,11},{10,... | collective-permute-start | bytes 331784 | tf_op jit(solution)/shard_map/ppermute | solution.py:117
  52.2 10.7 %collective-permute-start.8 = (bf16[3,144,128]{2,1,0:T(8,128)(2,1)S(1)}, bf16[3,144,128]{2,1,0:T(8,128)(2,1)S(1)}, u32[]{:S(2)}, u32[]{:S(2)}) collective-permute-start(bf16[3,144,128]{2,1,0:T(8,128)(2,1)S(1)} %get-tuple-element.53), channel_id=1, source_target_pairs={{0,1},{2,3},{1,0},{3,2},{4,5},{6,7},{5,4},{7,6},{8,9},{10,11},{9,8... | collective-permute-start | bytes 331784 | tf_op jit(solution)/shard_map/ppermute | solution.py:117

commit v7 on v6

--- a/solution.py
+++ b/solution.py
@@ -129,7 +129,7 @@
 def sides_kernel(n, *refs):
     ins, outs = refs[:n], refs[n:]
     is_odd = lax.axis_index("grp") & 1
-    for step, ref in enumerate(ins):
+    for step, ref in zip(far_first(n), ins):
         frame = lax.axis_index("seq") ^ step
         for start, out in zip((1, 0), outs):
             at = frame - jnp.where(is_odd == start, 1, 0)
@@ -150,7 +150,7 @@
         out_shape=[shape] * 2,
         compiler_params=pltpu.CompilerParams(vmem_limit_bytes=24 * 2**20),
         name="sides",
-    )(*blocks)
+    )(*(blocks[step] for step in far_first(n)))
 
 
 def gated(values, *earlier):
@@ -208,7 +208,7 @@
         for i in range(4):
             wide[i, frame] = ref[i].astype(jnp.float32)
 
-    for step, ref in enumerate(own):
+    for step, ref in zip(far_first(window), own):
         widen(ref, halo + (lax.axis_index("seq") ^ step))
     for start, ref in zip((1, 0), sides_of):
         is_next = (lax.axis_index("grp") & 1) == start
@@ -307,7 +307,7 @@
             transcendentals=extent * window * heads * lanes,
         ),
         name="clips",
-    )(bounds, *own, *beside)
+    )(bounds, *(own[step] for step in far_first(window)), *beside)
 
 
 def clip_bounds(clip_len, window):
@@ -342,9 +342,9 @@
     space_in = turned(q_space, k_space, v_space, cot_space)
     packed = [list(split(time, span, n, sharing)) for span in spans]
     own = [exchange(packed[0])]
-    packed[1][n // 2 :], own[0][-1] = gated(packed[1][n // 2 :], own[0][-1])
+    space = space_grads(*space_in)
+    packed[1][2:], own[0][2], space = gated(packed[1][2:], own[0][2], space)
     own.append(exchange(packed[1]))
-    space = space_grads(*space_in)
     beside = [
         [neighbours(ends, start) for ends, start in zip(sides(blocks), (1, 0))] for blocks in own
     ]

time: 64.1 us -> 60.4 us (0.942)
  starting transfers between devices: 27.8 us -> 22.9 us
  waiting for transfers between devices: 20.8 us -> 22.2 us
    ppermute x16, starting transfers between devices: 27.8 us -> 22.9 us  [swap(): lax.ppermute(block, axis, [(i, j) for i, j in pairs] + [(j, i) for i, j i...]
    ppermute x16, waiting for transfers between devices: 20.8 us -> 22.2 us  [swap(): lax.ppermute(block, axis, [(i, j) for i, j in pairs] + [(j, i) for i, j i...]
  transfers between devices with their start and end apart: 16 -> 16, of which waited for: 5 -> 6; matrix products, arithmetic and copies ran while one was open for 0% -> 0% of each run, Pallas kernels for 18% -> 19%
where the time goes in v7:
time: 60.4 us; the launch traced here: 60 us
  starting transfers between devices  22.9 us (38%)
  waiting for transfers between devices  22.2 us (37%)
  Pallas kernels  13.9 us (23%)
  between operations  0.77 us (1%)
    ppermute x16, starting transfers between devices, swap(): lax.ppermute(block, axis, [(i, j) for i, j in pairs] + [(j, i) for i, j i...  22.9 us
    ppermute x16, waiting for transfers between devices, swap(): lax.ppermute(block, axis, [(i, j) for i, j in pairs] + [(j, i) for i, j i...  22.2 us
    pallas_call x1, Pallas kernels, space_grads(): pl.pallas_call(frame_kernel, out_shape=(shape, shape, shape), compiler_pa...  5.58 us
    pallas_call x2, Pallas kernels, split(): pl.pallas_call(functools.partial(split_kernel, sharing, rows, span), in_s...  3.77 us
    pallas_call x2, Pallas kernels, clip_grads(): pl.pallas_call(functools.partial(clip_kernel, window, heads), out_shape=[...  2.59 us
    pallas_call x2, Pallas kernels, join(): pl.pallas_call(functools.partial(join_kernel, sharing, span), in_specs=[p...  1.71 us
  transfers between devices with their start and end apart: 16, of which 6 were waited for; matrix products, arithmetic and copies ran while one was open for 0% of the time, Pallas kernels for 19%

profile of v7, /device:TPU:0, one launch (start us, length us, event | category | flops | bytes accessed | tf_op | source)
XLA Modules:
  0.0 60.0 jit_solution(6379148515451338446)
XLA Ops:
  0.6 1.9 %pack.3 = (bf16[4,144,128]{2,1,0:T(8,128)(2,1)}, bf16[4,144,128]{2,1,0:T(8,128)(2,1)}, bf16[4,144,128]{2,1,0:T(8,128)(2,1)}, bf16[4,144,128]{2,1,0:T(8,128)(2,1)}) custom-call(bf16[1,576,256]{2,1,0:T(8,128)(2,1)} %bitcast.18, bf16[1,576,256]{2,1,0:T(8,128)(2,1)} %bitcast.20, bf16[1,576,256]{2,1,0:T(8,128)(2,1)} %bitcast.22, bf16[1,576,256]{2,1,0:T(8,128)(2,1)} %bitcast.24), custom_call_target="tpu_custom_call" | custom-call | tf_op jit(solution)/shard_map/pack/pallas_call | solution.py:97
  2.5 4.1 %collective-permute-start = (bf16[4,144,128]{2,1,0:T(8,128)(2,1)}, bf16[4,144,128]{2,1,0:T(8,128)(2,1)S(1)}, u32[]{:S(2)}, u32[]{:S(2)}) collective-permute-start(bf16[4,144,128]{2,1,0:T(8,128)(2,1)} %get-tuple-element.43), channel_id=1, source_target_pairs={{0,2},{1,3},{2,0},{3,1},{4,6},{5,7},{6,4},{7,5},{8,10},{9,11},{10,... | collective-permute-start | bytes 442376 | tf_op jit(solution)/shard_map/ppermute | solution.py:117
  6.6 1.3 %collective-permute-start.9 = (bf16[4,144,128]{2,1,0:T(8,128)(2,1)}, bf16[4,144,128]{2,1,0:T(8,128)(2,1)S(1)}, u32[]{:S(2)}, u32[]{:S(2)}) collective-permute-start(bf16[4,144,128]{2,1,0:T(8,128)(2,1)} %get-tuple-element.60), channel_id=1, source_target_pairs={{0,3},{1,2},{3,0},{2,1},{4,7},{5,6},{7,4},{6,5},{8,11},{9,10},{11,... | collective-permute-start | bytes 442376 | tf_op jit(solution)/shard_map/ppermute | solution.py:117
  8.0 0.2 collective-permute-start.10
  8.2 1.9 %pack.2 = (bf16[4,144,128]{2,1,0:T(8,128)(2,1)}, bf16[4,144,128]{2,1,0:T(8,128)(2,1)}, bf16[4,144,128]{2,1,0:T(8,128)(2,1)}, bf16[4,144,128]{2,1,0:T(8,128)(2,1)}) custom-call(bf16[1,576,256]{2,1,0:T(8,128)(2,1)} %bitcast.19, bf16[1,576,256]{2,1,0:T(8,128)(2,1)} %bitcast.21, bf16[1,576,256]{2,1,0:T(8,128)(2,1)} %bitcast.23, bf16[1,576,256]{2,1,0:T(8,128)(2,1)} %bitcast.25), custom_call_target="tpu_custom_call" | custom-call | tf_op jit(solution)/shard_map/pack/pallas_call | solution.py:97
  10.1 1.9 %collective-permute-start.3 = (bf16[4,144,128]{2,1,0:T(8,128)(2,1)}, bf16[4,144,128]{2,1,0:T(8,128)(2,1)S(1)}, u32[]{:S(2)}, u32[]{:S(2)}) collective-permute-start(bf16[4,144,128]{2,1,0:T(8,128)(2,1)} %get-tuple-element.53), channel_id=1, source_target_pairs={{0,1},{2,3},{1,0},{3,2},{4,5},{6,7},{5,4},{7,6},{8,9},{10,11},{9,8... | collective-permute-start | bytes 442376 | tf_op jit(solution)/shard_map/ppermute | solution.py:117
  12.0 0.0 copy-start.4
  12.0 0.0 copy-start.3
  12.0 0.0 copy-start.2
  12.0 0.0 copy-start.1
  12.0 5.6 %space.1 = (bf16[1,576,256]{2,1,0:T(8,128)(2,1)}, bf16[1,576,256]{2,1,0:T(8,128)(2,1)}, bf16[1,576,256]{2,1,0:T(8,128)(2,1)}) custom-call(bf16[1,576,256]{2,1,0:T(8,128)(2,1)} %bitcast.29, bf16[1,576,256]{2,1,0:T(8,128)(2,1)} %bitcast.30, bf16[1,576,256]{2,1,0:T(8,128)(2,1)} %bitcast.31, bf16[1,576,256]{2,1,0:T(8,128)(2,1)} %bitcast.32), custom_call_target="tpu_custom_call" | custom-call | flops 1610612736 | bytes 2064384 | tf_op jit(solution)/shard_map/space/pallas_call | solution.py:58
  17.6 0.0 copy-done.4
  17.6 0.1 select_reduce_fusion.2
  17.6 0.2 collective-permute-done.refs_1_
  17.9 0.0 copy-done.3
  17.9 2.8 %collective-permute-start.1 = (bf16[4,144,128]{2,1,0:T(8,128)(2,1)S(1)}, bf16[4,144,128]{2,1,0:T(8,128)(2,1)S(1)}, u32[]{:S(2)}, u32[]{:S(2)}) collective-permute-start(bf16[4,144,128]{2,1,0:T(8,128)(2,1)S(1)} %copy-done.3), channel_id=1, source_target_pairs={{0,3},{1,2},{3,0},{2,1},{4,7},{5,6},{7,4},{6,5},{8,11},{9,10},{11,... | collective-permute-start | bytes 442376 | tf_op jit(solution)/shard_map/ppermute | solution.py:117
  20.7 0.0 copy-done.2
  20.7 0.0 collective-permute-start.2
  20.7 0.0 collective-permute-done.9.refs_0_
  20.7 0.0 collective-permute-done.10.refs_3_
  20.7 0.0 copy-done.1
  20.8 0.0 copy-start
  20.8 0.1 sides.3
  20.9 1.8 %collective-permute-start.11 = (bf16[3,4,144,128]{3,2,1,0:T(8,128)(2,1)S(1)}, bf16[3,4,144,128]{3,2,1,0:T(8,128)(2,1)S(1)}, u32[]{:S(2)}, u32[]{:S(2)}) collective-permute-start(bf16[3,4,144,128]{3,2,1,0:T(8,128)(2,1)S(1)} %get-tuple-element.64), channel_id=1, source_target_pairs={{4,8},{12,16},{20,24},{28,0},{8,4},{16,12},{24,20},{0,28},{5,9},{1... | collective-permute-start | bytes 1327112 | tf_op jit(solution)/shard_map/ppermute | solution.py:117
  22.7 0.0 collective-permute-start.12
  22.7 0.2 select_reduce_fusion.1
  22.9 0.0 collective-permute-done.3.refs_3_
  22.9 3.5 %collective-permute-done.1.refs_0_ = bf16[4,144,128]{2,1,0:T(8,128)(2,1)S(1)} collective-permute-done((bf16[4,144,128]{2,1,0:T(8,128)(2,1)S(1)}, bf16[4,144,128]{2,1,0:T(8,128)(2,1)S(1)}, u32[]{:S(2)}, u32[]{:S(2)}) %collective-permute-start.1) | collective-permute-done | bytes 147488 | tf_op jit(solution)/shard_map/ppermute | solution.py:117
  26.3 6.5 %collective-permute-done.2.refs_1_ = bf16[4,144,128]{2,1,0:T(8,128)(2,1)S(1)} collective-permute-done((bf16[4,144,128]{2,1,0:T(8,128)(2,1)S(1)}, bf16[4,144,128]{2,1,0:T(8,128)(2,1)S(1)}, u32[]{:S(2)}, u32[]{:S(2)}) %collective-permute-start.2) | collective-permute-done | bytes 147488 | tf_op jit(solution)/shard_map/ppermute | solution.py:117
  32.9 0.0 copy-done
  32.9 0.1 sides.2
  33.0 1.6 %collective-permute-start.4 = (bf16[3,4,144,128]{3,2,1,0:T(8,128)(2,1)S(1)}, bf16[3,4,144,128]{3,2,1,0:T(8,128)(2,1)S(1)}, u32[]{:S(2)}, u32[]{:S(2)}) collective-permute-start(bf16[3,4,144,128]{3,2,1,0:T(8,128)(2,1)S(1)} %get-tuple-element.54), channel_id=1, source_target_pairs={{4,8},{12,16},{20,24},{28,0},{8,4},{16,12},{24,20},{0,28},{5,9},{1... | collective-permute-start | bytes 1327112 | tf_op jit(solution)/shard_map/ppermute | solution.py:117
  34.6 0.1 collective-permute-start.5
  34.7 0.0 collective-permute-done.11.refs_4_
  34.7 0.0 collective-permute-done.12.refs_5_
  34.7 1.3 %clips.3 = (bf16[3,144,128]{2,1,0:T(8,128)(2,1)S(1)}, bf16[3,144,128]{2,1,0:T(8,128)(2,1)S(1)}, bf16[3,144,128]{2,1,0:T(8,128)(2,1)S(1)}, bf16[3,144,128]{2,1,0:T(8,128)(2,1)S(1)}) custom-call(s32[2,10]{1,0:T(2,128)S(1)} %pad_add_fusion.given_bounds, bf16[4,144,128]{2,1,0:T(8,128)(2,1)S(1)} %collective-permute-done.9.refs_0_, ...), custom_call_target="tpu_custom_call" | custom-call | flops 589824000 | bytes 1474560 | tf_op jit(solution)/shard_map/clips/pallas_call | solution.py:289
  36.1 3.9 %collective-permute-start.13 = (bf16[3,144,128]{2,1,0:T(8,128)(2,1)S(1)}, bf16[3,144,128]{2,1,0:T(8,128)(2,1)S(1)}, u32[]{:S(2)}, u32[]{:S(2)}) collective-permute-start(bf16[3,144,128]{2,1,0:T(8,128)(2,1)S(1)} %get-tuple-element.66), channel_id=1, source_target_pairs={{0,3},{1,2},{3,0},{2,1},{4,7},{5,6},{7,4},{6,5},{8,11},{9,10},{11,... | collective-permute-start | bytes 331784 | tf_op jit(solution)/shard_map/ppermute | solution.py:117
  40.0 0.0 collective-permute-start.14
  40.0 0.7 %collective-permute-start.15 = (bf16[3,144,128]{2,1,0:T(8,128)(2,1)S(1)}, bf16[3,144,128]{2,1,0:T(8,128)(2,1)S(1)}, u32[]{:S(2)}, u32[]{:S(2)}) collective-permute-start(bf16[3,144,128]{2,1,0:T(8,128)(2,1)S(1)} %get-tuple-element.69), channel_id=1, source_target_pairs={{0,1},{2,3},{1,0},{3,2},{4,5},{6,7},{5,4},{7,6},{8,9},{10,11},{9,8... | collective-permute-start | bytes 331784 | tf_op jit(solution)/shard_map/ppermute | solution.py:117
  40.6 5.6 %collective-permute-done.4.refs_4_ = bf16[3,4,144,128]{3,2,1,0:T(8,128)(2,1)S(1)} collective-permute-done((bf16[3,4,144,128]{3,2,1,0:T(8,128)(2,1)S(1)}, bf16[3,4,144,128]{3,2,1,0:T(8,128)(2,1)S(1)}, u32[]{:S(2)}, u32[]{:S(2)}) %collective-permute-start.4) | collective-permute-done | bytes 442400 | tf_op jit(solution)/shard_map/ppermute | solution.py:117
  46.3 0.0 collective-permute-done.5.refs_5_
  46.3 1.3 %clips.2 = (bf16[3,144,128]{2,1,0:T(8,128)(2,1)S(1)}, bf16[3,144,128]{2,1,0:T(8,128)(2,1)S(1)}, bf16[3,144,128]{2,1,0:T(8,128)(2,1)S(1)}, bf16[3,144,128]{2,1,0:T(8,128)(2,1)S(1)}) custom-call(s32[2,10]{1,0:T(2,128)S(1)} %pad_add_fusion.given_bounds, bf16[4,144,128]{2,1,0:T(8,128)(2,1)S(1)} %collective-permute-done.1.refs_0_, ...), custom_call_target="tpu_custom_call" | custom-call | flops 589824000 | bytes 1474560 | tf_op jit(solution)/shard_map/clips/pallas_call | solution.py:289
  47.6 3.6 %collective-permute-start.6 = (bf16[3,144,128]{2,1,0:T(8,128)(2,1)S(1)}, bf16[3,144,128]{2,1,0:T(8,128)(2,1)S(1)}, u32[]{:S(2)}, u32[]{:S(2)}) collective-permute-start(bf16[3,144,128]{2,1,0:T(8,128)(2,1)S(1)} %get-tuple-element.56), channel_id=1, source_target_pairs={{0,3},{1,2},{3,0},{2,1},{4,7},{5,6},{7,4},{6,5},{8,11},{9,10},{11,... | collective-permute-start | bytes 331784 | tf_op jit(solution)/shard_map/ppermute | solution.py:117
  51.2 0.0 collective-permute-start.7
  51.2 0.0 collective-permute-done.13.refs_0_
  51.2 0.8 %collective-permute-start.8 = (bf16[3,144,128]{2,1,0:T(8,128)(2,1)S(1)}, bf16[3,144,128]{2,1,0:T(8,128)(2,1)S(1)}, u32[]{:S(2)}, u32[]{:S(2)}) collective-permute-start(bf16[3,144,128]{2,1,0:T(8,128)(2,1)S(1)} %get-tuple-element.59), channel_id=1, source_target_pairs={{0,1},{2,3},{1,0},{3,2},{4,5},{6,7},{5,4},{7,6},{8,9},{10,11},{9,8... | collective-permute-start | bytes 331784 | tf_op jit(solution)/shard_map/ppermute | solution.py:117
  52.0 0.0 collective-permute-done.14.refs_1_
  52.0 0.0 collective-permute-done.15.refs_3_
  52.0 0.9 %unpack.2 = (bf16[1,576,256]{2,1,0:T(8,128)(2,1)}, bf16[1,576,256]{2,1,0:T(8,128)(2,1)}, bf16[1,576,256]{2,1,0:T(8,128)(2,1)}) custom-call(bf16[3,144,128]{2,1,0:T(8,128)(2,1)S(1)} %collective-permute-done.13.refs_0_, bf16[3,144,128]{2,1,0:T(8,128)(2,1)S(1)} %collective-permute-done.14.refs_1_, bf16[3,144,128]{2,1,0:T(8,128)(2,1)S(1)} %get-tuple-element.68.refs_2_, ...), custom_call_target="tpu_custom_call" | custom-call | tf_op jit(solution)/shard_map/unpack/pallas_call | solution.py:185
  52.9 1.8 %collective-permute-done.6.refs_0_ = bf16[3,144,128]{2,1,0:T(8,128)(2,1)S(1)} collective-permute-done((bf16[3,144,128]{2,1,0:T(8,128)(2,1)S(1)}, bf16[3,144,128]{2,1,0:T(8,128)(2,1)S(1)}, u32[]{:S(2)}, u32[]{:S(2)}) %collective-permute-start.6) | collective-permute-done | bytes 110624 | tf_op jit(solution)/shard_map/ppermute | solution.py:117
  54.7 4.5 %collective-permute-done.7.refs_1_ = bf16[3,144,128]{2,1,0:T(8,128)(2,1)S(1)} collective-permute-done((bf16[3,144,128]{2,1,0:T(8,128)(2,1)S(1)}, bf16[3,144,128]{2,1,0:T(8,128)(2,1)S(1)}, u32[]{:S(2)}, u32[]{:S(2)}) %collective-permute-start.7) | collective-permute-done | bytes 110624 | tf_op jit(solution)/shard_map/ppermute | solution.py:117
  59.2 0.0 collective-permute-done.8.refs_3_
  59.2 0.9 %unpack.3 = (bf16[1,576,256]{2,1,0:T(8,128)(2,1)}, bf16[1,576,256]{2,1,0:T(8,128)(2,1)}, bf16[1,576,256]{2,1,0:T(8,128)(2,1)}) custom-call(bf16[3,144,128]{2,1,0:T(8,128)(2,1)S(1)} %collective-permute-done.6.refs_0_, bf16[3,144,128]{2,1,0:T(8,128)(2,1)S(1)} %collective-permute-done.7.refs_1_, ...), custom_call_target="tpu_custom_call", output_to_operand_aliasing={{0}: (4, {}), {1}: (5, {}), {2}: (6, {})} | custom-call | tf_op jit(solution)/shard_map/unpack/pallas_call | solution.py:185
  (4 shorter events, 0.0 us)
Async XLA Ops:
  2.5 15.4 %collective-permute-start = (bf16[4,144,128]{2,1,0:T(8,128)(2,1)}, bf16[4,144,128]{2,1,0:T(8,128)(2,1)S(1)}, u32[]{:S(2)}, u32[]{:S(2)}) collective-permute-start(bf16[4,144,128]{2,1,0:T(8,128)(2,1)} %get-tuple-element.43), channel_id=1, source_target_pairs={{0,2},{1,3},{2,0},{3,1},{4,6},{5,7},{6,4},{7,5},{8,10},{9,11},{10,... | collective-permute-start | bytes 442376 | tf_op jit(solution)/shard_map/ppermute | solution.py:117
  6.6 14.1 %collective-permute-start.9 = (bf16[4,144,128]{2,1,0:T(8,128)(2,1)}, bf16[4,144,128]{2,1,0:T(8,128)(2,1)S(1)}, u32[]{:S(2)}, u32[]{:S(2)}) collective-permute-start(bf16[4,144,128]{2,1,0:T(8,128)(2,1)} %get-tuple-element.60), channel_id=1, source_target_pairs={{0,3},{1,2},{3,0},{2,1},{4,7},{5,6},{7,4},{6,5},{8,11},{9,10},{11,... | collective-permute-start | bytes 442376 | tf_op jit(solution)/shard_map/ppermute | solution.py:117
  8.0 12.7 %collective-permute-start.10 = (bf16[4,144,128]{2,1,0:T(8,128)(2,1)}, bf16[4,144,128]{2,1,0:T(8,128)(2,1)S(1)}, u32[]{:S(2)}, u32[]{:S(2)}) collective-permute-start(bf16[4,144,128]{2,1,0:T(8,128)(2,1)} %get-tuple-element.63), channel_id=1, source_target_pairs={{0,1},{2,3},{1,0},{3,2},{4,5},{6,7},{5,4},{7,6},{8,9},{10,11},{9,8... | collective-permute-start | bytes 442376 | tf_op jit(solution)/shard_map/ppermute | solution.py:117
  10.1 12.8 %collective-permute-start.3 = (bf16[4,144,128]{2,1,0:T(8,128)(2,1)}, bf16[4,144,128]{2,1,0:T(8,128)(2,1)S(1)}, u32[]{:S(2)}, u32[]{:S(2)}) collective-permute-start(bf16[4,144,128]{2,1,0:T(8,128)(2,1)} %get-tuple-element.53), channel_id=1, source_target_pairs={{0,1},{2,3},{1,0},{3,2},{4,5},{6,7},{5,4},{7,6},{8,9},{10,11},{9,8... | collective-permute-start | bytes 442376 | tf_op jit(solution)/shard_map/ppermute | solution.py:117
  12.0 5.6 %copy-start.4 = (s32[16]{0:T(128)S(1)}, s32[16]{0:T(128)}, u32[]{:S(2)}) copy-start(s32[16]{0:T(128)} %param.17) | copy-start | bytes 196
  12.0 5.9 %copy-start.3 = (bf16[4,144,128]{2,1,0:T(8,128)(2,1)S(1)}, bf16[4,144,128]{2,1,0:T(8,128)(2,1)}, u32[]{:S(2)}) copy-start(bf16[4,144,128]{2,1,0:T(8,128)(2,1)} %get-tuple-element.50) | copy-start | bytes 442372
  12.0 8.7 %copy-start.2 = (bf16[4,144,128]{2,1,0:T(8,128)(2,1)S(1)}, bf16[4,144,128]{2,1,0:T(8,128)(2,1)}, u32[]{:S(2)}) copy-start(bf16[4,144,128]{2,1,0:T(8,128)(2,1)} %get-tuple-element.51) | copy-start | bytes 442372
  12.0 8.8 %copy-start.1 = (bf16[4,144,128]{2,1,0:T(8,128)(2,1)S(1)}, bf16[4,144,128]{2,1,0:T(8,128)(2,1)}, u32[]{:S(2)}) copy-start(bf16[4,144,128]{2,1,0:T(8,128)(2,1)} %get-tuple-element.62.refs_2_) | copy-start | bytes 442372
  17.9 8.4 %collective-permute-start.1 = (bf16[4,144,128]{2,1,0:T(8,128)(2,1)S(1)}, bf16[4,144,128]{2,1,0:T(8,128)(2,1)S(1)}, u32[]{:S(2)}, u32[]{:S(2)}) collective-permute-start(bf16[4,144,128]{2,1,0:T(8,128)(2,1)S(1)} %copy-done.3), channel_id=1, source_target_pairs={{0,3},{1,2},{3,0},{2,1},{4,7},{5,6},{7,4},{6,5},{8,11},{9,10},{11,... | collective-permute-start | bytes 442376 | tf_op jit(solution)/shard_map/ppermute | solution.py:117
  20.7 12.2 %collective-permute-start.2 = (bf16[4,144,128]{2,1,0:T(8,128)(2,1)S(1)}, bf16[4,144,128]{2,1,0:T(8,128)(2,1)S(1)}, u32[]{:S(2)}, u32[]{:S(2)}) collective-permute-start(bf16[4,144,128]{2,1,0:T(8,128)(2,1)S(1)} %copy-done.2), channel_id=1, source_target_pairs={{0,2},{1,3},{2,0},{3,1},{4,6},{5,7},{6,4},{7,5},{8,10},{9,11},{10,... | collective-permute-start | bytes 442376 | tf_op jit(solution)/shard_map/ppermute | solution.py:117
  20.8 12.1 %copy-start = (bf16[4,144,128]{2,1,0:T(8,128)(2,1)S(1)}, bf16[4,144,128]{2,1,0:T(8,128)(2,1)}, u32[]{:S(2)}) copy-start(bf16[4,144,128]{2,1,0:T(8,128)(2,1)} %get-tuple-element.52.refs_2_) | copy-start | bytes 442372
  20.9 13.8 %collective-permute-start.11 = (bf16[3,4,144,128]{3,2,1,0:T(8,128)(2,1)S(1)}, bf16[3,4,144,128]{3,2,1,0:T(8,128)(2,1)S(1)}, u32[]{:S(2)}, u32[]{:S(2)}) collective-permute-start(bf16[3,4,144,128]{3,2,1,0:T(8,128)(2,1)S(1)} %get-tuple-element.64), channel_id=1, source_target_pairs={{4,8},{12,16},{20,24},{28,0},{8,4},{16,12},{24,20},{0,28},{5,9},{1... | collective-permute-start | bytes 1327112 | tf_op jit(solution)/shard_map/ppermute | solution.py:117
  22.7 12.1 %collective-permute-start.12 = (bf16[3,4,144,128]{3,2,1,0:T(8,128)(2,1)S(1)}, bf16[3,4,144,128]{3,2,1,0:T(8,128)(2,1)S(1)}, u32[]{:S(2)}, u32[]{:S(2)}) collective-permute-start(bf16[3,4,144,128]{3,2,1,0:T(8,128)(2,1)S(1)} %get-tuple-element.65), channel_id=1, source_target_pairs={{0,4},{8,12},{16,20},{24,28},{4,0},{12,8},{20,16},{28,24},{1,5},{9... | collective-permute-start | bytes 1327112 | tf_op jit(solution)/shard_map/ppermute | solution.py:117
  33.0 13.3 %collective-permute-start.4 = (bf16[3,4,144,128]{3,2,1,0:T(8,128)(2,1)S(1)}, bf16[3,4,144,128]{3,2,1,0:T(8,128)(2,1)S(1)}, u32[]{:S(2)}, u32[]{:S(2)}) collective-permute-start(bf16[3,4,144,128]{3,2,1,0:T(8,128)(2,1)S(1)} %get-tuple-element.54), channel_id=1, source_target_pairs={{4,8},{12,16},{20,24},{28,0},{8,4},{16,12},{24,20},{0,28},{5,9},{1... | collective-permute-start | bytes 1327112 | tf_op jit(solution)/shard_map/ppermute | solution.py:117
  34.6 11.7 %collective-permute-start.5 = (bf16[3,4,144,128]{3,2,1,0:T(8,128)(2,1)S(1)}, bf16[3,4,144,128]{3,2,1,0:T(8,128)(2,1)S(1)}, u32[]{:S(2)}, u32[]{:S(2)}) collective-permute-start(bf16[3,4,144,128]{3,2,1,0:T(8,128)(2,1)S(1)} %get-tuple-element.55), channel_id=1, source_target_pairs={{0,4},{8,12},{16,20},{24,28},{4,0},{12,8},{20,16},{28,24},{1,5},{9... | collective-permute-start | bytes 1327112 | tf_op jit(solution)/shard_map/ppermute | solution.py:117
  36.1 15.1 %collective-permute-start.13 = (bf16[3,144,128]{2,1,0:T(8,128)(2,1)S(1)}, bf16[3,144,128]{2,1,0:T(8,128)(2,1)S(1)}, u32[]{:S(2)}, u32[]{:S(2)}) collective-permute-start(bf16[3,144,128]{2,1,0:T(8,128)(2,1)S(1)} %get-tuple-element.66), channel_id=1, source_target_pairs={{0,3},{1,2},{3,0},{2,1},{4,7},{5,6},{7,4},{6,5},{8,11},{9,10},{11,... | collective-permute-start | bytes 331784 | tf_op jit(solution)/shard_map/ppermute | solution.py:117
  40.0 12.0 %collective-permute-start.14 = (bf16[3,144,128]{2,1,0:T(8,128)(2,1)S(1)}, bf16[3,144,128]{2,1,0:T(8,128)(2,1)S(1)}, u32[]{:S(2)}, u32[]{:S(2)}) collective-permute-start(bf16[3,144,128]{2,1,0:T(8,128)(2,1)S(1)} %get-tuple-element.67), channel_id=1, source_target_pairs={{0,2},{1,3},{2,0},{3,1},{4,6},{5,7},{6,4},{7,5},{8,10},{9,11},{10,... | collective-permute-start | bytes 331784 | tf_op jit(solution)/shard_map/ppermute | solution.py:117
  40.0 12.0 %collective-permute-start.15 = (bf16[3,144,128]{2,1,0:T(8,128)(2,1)S(1)}, bf16[3,144,128]{2,1,0:T(8,128)(2,1)S(1)}, u32[]{:S(2)}, u32[]{:S(2)}) collective-permute-start(bf16[3,144,128]{2,1,0:T(8,128)(2,1)S(1)} %get-tuple-element.69), channel_id=1, source_target_pairs={{0,1},{2,3},{1,0},{3,2},{4,5},{6,7},{5,4},{7,6},{8,9},{10,11},{9,8... | collective-permute-start | bytes 331784 | tf_op jit(solution)/shard_map/ppermute | solution.py:117
  47.6 7.1 %collective-permute-start.6 = (bf16[3,144,128]{2,1,0:T(8,128)(2,1)S(1)}, bf16[3,144,128]{2,1,0:T(8,128)(2,1)S(1)}, u32[]{:S(2)}, u32[]{:S(2)}) collective-permute-start(bf16[3,144,128]{2,1,0:T(8,128)(2,1)S(1)} %get-tuple-element.56), channel_id=1, source_target_pairs={{0,3},{1,2},{3,0},{2,1},{4,7},{5,6},{7,4},{6,5},{8,11},{9,10},{11,... | collective-permute-start | bytes 331784 | tf_op jit(solution)/shard_map/ppermute | solution.py:117
  51.2 8.0 %collective-permute-start.7 = (bf16[3,144,128]{2,1,0:T(8,128)(2,1)S(1)}, bf16[3,144,128]{2,1,0:T(8,128)(2,1)S(1)}, u32[]{:S(2)}, u32[]{:S(2)}) collective-permute-start(bf16[3,144,128]{2,1,0:T(8,128)(2,1)S(1)} %get-tuple-element.57), channel_id=1, source_target_pairs={{0,2},{1,3},{2,0},{3,1},{4,6},{5,7},{6,4},{7,5},{8,10},{9,11},{10,... | collective-permute-start | bytes 331784 | tf_op jit(solution)/shard_map/ppermute | solution.py:117
  51.2 8.0 %collective-permute-start.8 = (bf16[3,144,128]{2,1,0:T(8,128)(2,1)S(1)}, bf16[3,144,128]{2,1,0:T(8,128)(2,1)S(1)}, u32[]{:S(2)}, u32[]{:S(2)}) collective-permute-start(bf16[3,144,128]{2,1,0:T(8,128)(2,1)S(1)} %get-tuple-element.59), channel_id=1, source_target_pairs={{0,1},{2,3},{1,0},{3,2},{4,5},{6,7},{5,4},{7,6},{8,9},{10,11},{9,8... | collective-permute-start | bytes 331784 | tf_op jit(solution)/shard_map/ppermute | solution.py:117

commit v8 on v6

--- a/solution.py
+++ b/solution.py
@@ -159,7 +159,10 @@
 
 def neighbours(block, start):
     count = lax.axis_size("grp")
-    return swap(block, "grp", [(i, (i + 1) % count) for i in range(start, count, 2)])
+    pairs = [(i, i + 1) for i in range(start, count - 1, 2)]
+    alone = set(range(count)) - {i for pair in pairs for i in pair}
+    links = pairs + [(j, i) for i, j in pairs] + [(i, i) for i in sorted(alone)]
+    return lax.ppermute(block, "grp", links)
 
 
 def join_kernel(sharing, span, *refs):
@@ -342,9 +345,9 @@
     space_in = turned(q_space, k_space, v_space, cot_space)
     packed = [list(split(time, span, n, sharing)) for span in spans]
     own = [exchange(packed[0])]
-    packed[1][n // 2 :], own[0][-1] = gated(packed[1][n // 2 :], own[0][-1])
+    space = space_grads(*space_in)
+    packed[1][2:], own[0][2], space = gated(packed[1][2:], own[0][2], space)
     own.append(exchange(packed[1]))
-    space = space_grads(*space_in)
     beside = [
         [neighbours(ends, start) for ends, start in zip(sides(blocks), (1, 0))] for blocks in own
     ]
@@ -364,7 +367,6 @@
         and n % 4 == 0
         and n & (n - 1) == 0
         and mesh.shape["grp"] % 2 == 0
-        and mesh.shape["grp"] > 2
         and sharing * tokens == n * LANES
         and all(heads % sharing == 0 and heads // sharing * HDIM % 16 == 0 for heads in CHUNKS)
     )

time: 64.1 us -> 60.4 us (0.942)
  waiting for transfers between devices: 20.8 us -> 16.5 us
    ppermute x0 -> x4, starting transfers between devices: none -> 7.36 us  [neighbours(): return lax.ppermute(block, 'grp', links)]
    ppermute x16 -> x12, starting transfers between devices: 27.8 us -> 20.8 us  [swap(): lax.ppermute(block, axis, [(i, j) for i, j in pairs] + [(j, i) for i, j i...]
    ppermute x16 -> x12, waiting for transfers between devices: 20.8 us -> 16.5 us  [swap(): lax.ppermute(block, axis, [(i, j) for i, j in pairs] + [(j, i) for i, j i...]
  transfers between devices with their start and end apart: 16 -> 16, of which waited for: 5 -> 3; matrix products, arithmetic and copies ran while one was open for 0% -> 0% of each run, Pallas kernels for 18% -> 19%
where the time goes in v8:
time: 60.4 us; the launch traced here: 60.1 us
  starting transfers between devices  28.1 us (47%)
  waiting for transfers between devices  16.5 us (27%)
  Pallas kernels  14.4 us (24%)
  between operations  0.79 us (1%)
    ppermute x12, starting transfers between devices, swap(): lax.ppermute(block, axis, [(i, j) for i, j in pairs] + [(j, i) for i, j i...  20.8 us
    ppermute x12, waiting for transfers between devices, swap(): lax.ppermute(block, axis, [(i, j) for i, j in pairs] + [(j, i) for i, j i...  16.5 us
    ppermute x4, starting transfers between devices, neighbours(): return lax.ppermute(block, 'grp', links)  7.36 us
    pallas_call x1, Pallas kernels, space_grads(): pl.pallas_call(frame_kernel, out_shape=(shape, shape, shape), compiler_pa...  5.58 us
    pallas_call x2, Pallas kernels, split(): pl.pallas_call(functools.partial(split_kernel, sharing, rows, span), in_s...  3.77 us
    pallas_call x2, Pallas kernels, clip_grads(): pl.pallas_call(functools.partial(clip_kernel, window, heads), out_shape=[...  3.07 us
    pallas_call x2, Pallas kernels, join(): pl.pallas_call(functools.partial(join_kernel, sharing, span), in_specs=[p...  1.71 us
  transfers between devices with their start and end apart: 16, of which 3 were waited for; matrix products, arithmetic and copies ran while one was open for 0% of the time, Pallas kernels for 19%

profile of v8, /device:TPU:0, one launch (start us, length us, event | category | flops | bytes accessed | tf_op | source)
XLA Modules:
  0.0 60.1 jit_solution(13330490768047535390)
XLA Ops:
  0.6 1.9 %pack.3 = (bf16[4,144,128]{2,1,0:T(8,128)(2,1)}, bf16[4,144,128]{2,1,0:T(8,128)(2,1)}, bf16[4,144,128]{2,1,0:T(8,128)(2,1)}, bf16[4,144,128]{2,1,0:T(8,128)(2,1)}) custom-call(bf16[1,576,256]{2,1,0:T(8,128)(2,1)} %bitcast.18, bf16[1,576,256]{2,1,0:T(8,128)(2,1)} %bitcast.20, bf16[1,576,256]{2,1,0:T(8,128)(2,1)} %bitcast.22, bf16[1,576,256]{2,1,0:T(8,128)(2,1)} %bitcast.24), custom_call_target="tpu_custom_call" | custom-call | tf_op jit(solution)/shard_map/pack/pallas_call | solution.py:97
  2.5 4.1 %collective-permute-start = (bf16[4,144,128]{2,1,0:T(8,128)(2,1)}, bf16[4,144,128]{2,1,0:T(8,128)(2,1)S(1)}, u32[]{:S(2)}, u32[]{:S(2)}) collective-permute-start(bf16[4,144,128]{2,1,0:T(8,128)(2,1)} %get-tuple-element.43), channel_id=1, source_target_pairs={{0,2},{1,3},{2,0},{3,1},{4,6},{5,7},{6,4},{7,5},{8,10},{9,11},{10,... | collective-permute-start | bytes 442376 | tf_op jit(solution)/shard_map/ppermute | solution.py:117
  6.6 1.6 %collective-permute-start.9 = (bf16[4,144,128]{2,1,0:T(8,128)(2,1)}, bf16[4,144,128]{2,1,0:T(8,128)(2,1)S(1)}, u32[]{:S(2)}, u32[]{:S(2)}) collective-permute-start(bf16[4,144,128]{2,1,0:T(8,128)(2,1)} %get-tuple-element.61), channel_id=1, source_target_pairs={{0,1},{2,3},{1,0},{3,2},{4,5},{6,7},{5,4},{7,6},{8,9},{10,11},{9,8... | collective-permute-start | bytes 442376 | tf_op jit(solution)/shard_map/ppermute | solution.py:117
  8.2 0.0 collective-permute-start.10
  8.2 1.9 %pack.2 = (bf16[4,144,128]{2,1,0:T(8,128)(2,1)}, bf16[4,144,128]{2,1,0:T(8,128)(2,1)}, bf16[4,144,128]{2,1,0:T(8,128)(2,1)}, bf16[4,144,128]{2,1,0:T(8,128)(2,1)}) custom-call(bf16[1,576,256]{2,1,0:T(8,128)(2,1)} %bitcast.19, bf16[1,576,256]{2,1,0:T(8,128)(2,1)} %bitcast.21, bf16[1,576,256]{2,1,0:T(8,128)(2,1)} %bitcast.23, bf16[1,576,256]{2,1,0:T(8,128)(2,1)} %bitcast.25), custom_call_target="tpu_custom_call" | custom-call | tf_op jit(solution)/shard_map/pack/pallas_call | solution.py:97
  10.1 1.0 %collective-permute-start.1 = (bf16[4,144,128]{2,1,0:T(8,128)(2,1)}, bf16[4,144,128]{2,1,0:T(8,128)(2,1)S(1)}, u32[]{:S(2)}, u32[]{:S(2)}) collective-permute-start(bf16[4,144,128]{2,1,0:T(8,128)(2,1)} %get-tuple-element.51), channel_id=1, source_target_pairs={{0,1},{2,3},{1,0},{3,2},{4,5},{6,7},{5,4},{7,6},{8,9},{10,11},{9,8... | collective-permute-start | bytes 442376 | tf_op jit(solution)/shard_map/ppermute | solution.py:117
  11.1 0.0 copy-start.4
  11.1 0.0 copy-start.3
  11.1 0.0 copy-start.2
  11.1 0.0 copy-start.1
  11.1 5.6 %space.1 = (bf16[1,576,256]{2,1,0:T(8,128)(2,1)}, bf16[1,576,256]{2,1,0:T(8,128)(2,1)}, bf16[1,576,256]{2,1,0:T(8,128)(2,1)}) custom-call(bf16[1,576,256]{2,1,0:T(8,128)(2,1)} %bitcast.29, bf16[1,576,256]{2,1,0:T(8,128)(2,1)} %bitcast.30, bf16[1,576,256]{2,1,0:T(8,128)(2,1)} %bitcast.31, bf16[1,576,256]{2,1,0:T(8,128)(2,1)} %bitcast.32), custom_call_target="tpu_custom_call" | custom-call | flops 1610612736 | bytes 2064384 | tf_op jit(solution)/shard_map/space/pallas_call | solution.py:58
  16.7 0.0 copy-done.4
  16.7 0.1 select_reduce_fusion.2
  16.7 0.0 collective-permute-done.refs_2_
  16.7 0.0 copy-done.3
  16.8 3.6 %collective-permute-start.2 = (bf16[4,144,128]{2,1,0:T(8,128)(2,1)S(1)}, bf16[4,144,128]{2,1,0:T(8,128)(2,1)S(1)}, u32[]{:S(2)}, u32[]{:S(2)}) collective-permute-start(bf16[4,144,128]{2,1,0:T(8,128)(2,1)S(1)} %copy-done.3), channel_id=1, source_target_pairs={{0,2},{1,3},{2,0},{3,1},{4,6},{5,7},{6,4},{7,5},{8,10},{9,11},{10,... | collective-permute-start | bytes 442376 | tf_op jit(solution)/shard_map/ppermute | solution.py:117
  20.3 0.0 copy-done.2
  20.3 0.0 collective-permute-start.3
  20.3 0.0 collective-permute-done.9.refs_1_
  20.3 0.0 collective-permute-done.10.refs_3_
  20.4 0.0 copy-done.1
  20.4 0.0 copy-start
  20.4 0.1 sides.3
  20.5 0.7 %collective-permute-start.11 = (bf16[3,4,144,128]{3,2,1,0:T(8,128)(2,1)S(1)}, bf16[3,4,144,128]{3,2,1,0:T(8,128)(2,1)S(1)}, u32[]{:S(2)}, u32[]{:S(2)}) collective-permute-start(bf16[3,4,144,128]{3,2,1,0:T(8,128)(2,1)S(1)} %get-tuple-element.64), channel_id=1, source_target_pairs={{4,8},{12,16},{20,24},{8,4},{16,12},{24,20},{0,0},{28,28},{5,9},{1... | collective-permute-start | bytes 1327112 | tf_op jit(solution)/shard_map/ppermute | solution.py:165
  21.2 3.1 %collective-permute-start.12 = (bf16[3,4,144,128]{3,2,1,0:T(8,128)(2,1)S(1)}, bf16[3,4,144,128]{3,2,1,0:T(8,128)(2,1)S(1)}, u32[]{:S(2)}, u32[]{:S(2)}) collective-permute-start(bf16[3,4,144,128]{3,2,1,0:T(8,128)(2,1)S(1)} %get-tuple-element.65), channel_id=1, source_target_pairs={{0,4},{8,12},{16,20},{24,28},{4,0},{12,8},{20,16},{28,24},{1,5},{9... | collective-permute-start | bytes 1327112 | tf_op jit(solution)/shard_map/ppermute | solution.py:165
  24.3 0.2 select_reduce_fusion.1
  24.5 0.0 collective-permute-done.1.refs_1_
  24.5 6.1 %collective-permute-done.2.refs_2_ = bf16[4,144,128]{2,1,0:T(8,128)(2,1)S(1)} collective-permute-done((bf16[4,144,128]{2,1,0:T(8,128)(2,1)S(1)}, bf16[4,144,128]{2,1,0:T(8,128)(2,1)S(1)}, u32[]{:S(2)}, u32[]{:S(2)}) %collective-permute-start.2) | collective-permute-done | bytes 147488 | tf_op jit(solution)/shard_map/ppermute | solution.py:117
  30.6 0.0 collective-permute-done.3.refs_3_
  30.6 0.0 copy-done
  30.6 0.1 sides.2
  30.7 0.7 %collective-permute-start.4 = (bf16[3,4,144,128]{3,2,1,0:T(8,128)(2,1)S(1)}, bf16[3,4,144,128]{3,2,1,0:T(8,128)(2,1)S(1)}, u32[]{:S(2)}, u32[]{:S(2)}) collective-permute-start(bf16[3,4,144,128]{3,2,1,0:T(8,128)(2,1)S(1)} %get-tuple-element.54), channel_id=1, source_target_pairs={{4,8},{12,16},{20,24},{8,4},{16,12},{24,20},{0,0},{28,28},{5,9},{1... | collective-permute-start | bytes 1327112 | tf_op jit(solution)/shard_map/ppermute | solution.py:165
  31.4 2.9 %collective-permute-start.5 = (bf16[3,4,144,128]{3,2,1,0:T(8,128)(2,1)S(1)}, bf16[3,4,144,128]{3,2,1,0:T(8,128)(2,1)S(1)}, u32[]{:S(2)}, u32[]{:S(2)}) collective-permute-start(bf16[3,4,144,128]{3,2,1,0:T(8,128)(2,1)S(1)} %get-tuple-element.55), channel_id=1, source_target_pairs={{0,4},{8,12},{16,20},{24,28},{4,0},{12,8},{20,16},{28,24},{1,5},{9... | collective-permute-start | bytes 1327112 | tf_op jit(solution)/shard_map/ppermute | solution.py:165
  34.3 0.0 collective-permute-done.11.refs_4_
  34.3 0.0 collective-permute-done.12.refs_5_
  34.3 1.5 %clips.3 = (bf16[3,144,128]{2,1,0:T(8,128)(2,1)S(1)}, bf16[3,144,128]{2,1,0:T(8,128)(2,1)S(1)}, bf16[3,144,128]{2,1,0:T(8,128)(2,1)S(1)}, bf16[3,144,128]{2,1,0:T(8,128)(2,1)S(1)}) custom-call(s32[2,10]{1,0:T(2,128)S(1)} %pad_add_fusion.given_bounds, bf16[4,144,128]{2,1,0:T(8,128)(2,1)S(1)} %copy-done.1, ...), custom_call_target="tpu_custom_call" | custom-call | flops 589824000 | bytes 1474560 | tf_op jit(solution)/shard_map/clips/pallas_call | solution.py:292
  35.9 2.9 %collective-permute-start.13 = (bf16[3,144,128]{2,1,0:T(8,128)(2,1)S(1)}, bf16[3,144,128]{2,1,0:T(8,128)(2,1)S(1)}, u32[]{:S(2)}, u32[]{:S(2)}) collective-permute-start(bf16[3,144,128]{2,1,0:T(8,128)(2,1)S(1)} %get-tuple-element.66), channel_id=1, source_target_pairs={{0,3},{1,2},{3,0},{2,1},{4,7},{5,6},{7,4},{6,5},{8,11},{9,10},{11,... | collective-permute-start | bytes 331784 | tf_op jit(solution)/shard_map/ppermute | solution.py:117
  38.8 2.2 %collective-permute-start.14 = (bf16[3,144,128]{2,1,0:T(8,128)(2,1)S(1)}, bf16[3,144,128]{2,1,0:T(8,128)(2,1)S(1)}, u32[]{:S(2)}, u32[]{:S(2)}) collective-permute-start(bf16[3,144,128]{2,1,0:T(8,128)(2,1)S(1)} %get-tuple-element.67), channel_id=1, source_target_pairs={{0,2},{1,3},{2,0},{3,1},{4,6},{5,7},{6,4},{7,5},{8,10},{9,11},{10,... | collective-permute-start | bytes 331784 | tf_op jit(solution)/shard_map/ppermute | solution.py:117
  40.9 0.5 collective-permute-start.15
  41.4 0.0 collective-permute-done.4.refs_4_
  41.4 0.0 collective-permute-done.5.refs_5_
  41.4 1.5 %clips.2 = (bf16[3,144,128]{2,1,0:T(8,128)(2,1)S(1)}, bf16[3,144,128]{2,1,0:T(8,128)(2,1)S(1)}, bf16[3,144,128]{2,1,0:T(8,128)(2,1)S(1)}, bf16[3,144,128]{2,1,0:T(8,128)(2,1)S(1)}) custom-call(s32[2,10]{1,0:T(2,128)S(1)} %pad_add_fusion.given_bounds, bf16[4,144,128]{2,1,0:T(8,128)(2,1)S(1)} %copy-done, ...), custom_call_target="tpu_custom_call" | custom-call | flops 589824000 | bytes 1474560 | tf_op jit(solution)/shard_map/clips/pallas_call | solution.py:292
  43.0 2.4 %collective-permute-start.6 = (bf16[3,144,128]{2,1,0:T(8,128)(2,1)S(1)}, bf16[3,144,128]{2,1,0:T(8,128)(2,1)S(1)}, u32[]{:S(2)}, u32[]{:S(2)}) collective-permute-start(bf16[3,144,128]{2,1,0:T(8,128)(2,1)S(1)} %get-tuple-element.56), channel_id=1, source_target_pairs={{0,3},{1,2},{3,0},{2,1},{4,7},{5,6},{7,4},{6,5},{8,11},{9,10},{11,... | collective-permute-start | bytes 331784 | tf_op jit(solution)/shard_map/ppermute | solution.py:117
  45.4 0.6 %collective-permute-start.7 = (bf16[3,144,128]{2,1,0:T(8,128)(2,1)S(1)}, bf16[3,144,128]{2,1,0:T(8,128)(2,1)S(1)}, u32[]{:S(2)}, u32[]{:S(2)}) collective-permute-start(bf16[3,144,128]{2,1,0:T(8,128)(2,1)S(1)} %get-tuple-element.57), channel_id=1, source_target_pairs={{0,2},{1,3},{2,0},{3,1},{4,6},{5,7},{6,4},{7,5},{8,10},{9,11},{10,... | collective-permute-start | bytes 331784 | tf_op jit(solution)/shard_map/ppermute | solution.py:117
  46.0 0.0 collective-permute-done.13.refs_0_
  46.0 2.0 %collective-permute-start.8 = (bf16[3,144,128]{2,1,0:T(8,128)(2,1)S(1)}, bf16[3,144,128]{2,1,0:T(8,128)(2,1)S(1)}, u32[]{:S(2)}, u32[]{:S(2)}) collective-permute-start(bf16[3,144,128]{2,1,0:T(8,128)(2,1)S(1)} %get-tuple-element.59), channel_id=1, source_target_pairs={{0,1},{2,3},{1,0},{3,2},{4,5},{6,7},{5,4},{7,6},{8,9},{10,11},{9,8... | collective-permute-start | bytes 331784 | tf_op jit(solution)/shard_map/ppermute | solution.py:117
  48.0 5.4 %collective-permute-done.14.refs_1_ = bf16[3,144,128]{2,1,0:T(8,128)(2,1)S(1)} collective-permute-done((bf16[3,144,128]{2,1,0:T(8,128)(2,1)S(1)}, bf16[3,144,128]{2,1,0:T(8,128)(2,1)S(1)}, u32[]{:S(2)}, u32[]{:S(2)}) %collective-permute-start.14) | collective-permute-done | bytes 110624 | tf_op jit(solution)/shard_map/ppermute | solution.py:117
  53.4 0.0 collective-permute-done.15.refs_3_
  53.4 0.9 %unpack.2 = (bf16[1,576,256]{2,1,0:T(8,128)(2,1)}, bf16[1,576,256]{2,1,0:T(8,128)(2,1)}, bf16[1,576,256]{2,1,0:T(8,128)(2,1)}) custom-call(bf16[3,144,128]{2,1,0:T(8,128)(2,1)S(1)} %collective-permute-done.13.refs_0_, bf16[3,144,128]{2,1,0:T(8,128)(2,1)S(1)} %collective-permute-done.14.refs_1_, bf16[3,144,128]{2,1,0:T(8,128)(2,1)S(1)} %get-tuple-element.68.refs_2_, ...), custom_call_target="tpu_custom_call" | custom-call | tf_op jit(solution)/shard_map/unpack/pallas_call | solution.py:188
  54.3 0.0 collective-permute-done.6.refs_0_
  54.3 5.0 %collective-permute-done.7.refs_1_ = bf16[3,144,128]{2,1,0:T(8,128)(2,1)S(1)} collective-permute-done((bf16[3,144,128]{2,1,0:T(8,128)(2,1)S(1)}, bf16[3,144,128]{2,1,0:T(8,128)(2,1)S(1)}, u32[]{:S(2)}, u32[]{:S(2)}) %collective-permute-start.7) | collective-permute-done | bytes 110624 | tf_op jit(solution)/shard_map/ppermute | solution.py:117
  59.3 0.0 collective-permute-done.8.refs_3_
  59.3 0.9 %unpack.3 = (bf16[1,576,256]{2,1,0:T(8,128)(2,1)}, bf16[1,576,256]{2,1,0:T(8,128)(2,1)}, bf16[1,576,256]{2,1,0:T(8,128)(2,1)}) custom-call(bf16[3,144,128]{2,1,0:T(8,128)(2,1)S(1)} %collective-permute-done.6.refs_0_, bf16[3,144,128]{2,1,0:T(8,128)(2,1)S(1)} %collective-permute-done.7.refs_1_, ...), custom_call_target="tpu_custom_call", output_to_operand_aliasing={{0}: (4, {}), {1}: (5, {}), {2}: (6, {})} | custom-call | tf_op jit(solution)/shard_map/unpack/pallas_call | solution.py:188
  (4 shorter events, 0.0 us)
Async XLA Ops:
  2.5 14.2 %collective-permute-start = (bf16[4,144,128]{2,1,0:T(8,128)(2,1)}, bf16[4,144,128]{2,1,0:T(8,128)(2,1)S(1)}, u32[]{:S(2)}, u32[]{:S(2)}) collective-permute-start(bf16[4,144,128]{2,1,0:T(8,128)(2,1)} %get-tuple-element.43), channel_id=1, source_target_pairs={{0,2},{1,3},{2,0},{3,1},{4,6},{5,7},{6,4},{7,5},{8,10},{9,11},{10,... | collective-permute-start | bytes 442376 | tf_op jit(solution)/shard_map/ppermute | solution.py:117
  6.6 13.7 %collective-permute-start.9 = (bf16[4,144,128]{2,1,0:T(8,128)(2,1)}, bf16[4,144,128]{2,1,0:T(8,128)(2,1)S(1)}, u32[]{:S(2)}, u32[]{:S(2)}) collective-permute-start(bf16[4,144,128]{2,1,0:T(8,128)(2,1)} %get-tuple-element.61), channel_id=1, source_target_pairs={{0,1},{2,3},{1,0},{3,2},{4,5},{6,7},{5,4},{7,6},{8,9},{10,11},{9,8... | collective-permute-start | bytes 442376 | tf_op jit(solution)/shard_map/ppermute | solution.py:117
  8.2 12.1 %collective-permute-start.10 = (bf16[4,144,128]{2,1,0:T(8,128)(2,1)}, bf16[4,144,128]{2,1,0:T(8,128)(2,1)S(1)}, u32[]{:S(2)}, u32[]{:S(2)}) collective-permute-start(bf16[4,144,128]{2,1,0:T(8,128)(2,1)} %get-tuple-element.63), channel_id=1, source_target_pairs={{0,3},{1,2},{3,0},{2,1},{4,7},{5,6},{7,4},{6,5},{8,11},{9,10},{11,... | collective-permute-start | bytes 442376 | tf_op jit(solution)/shard_map/ppermute | solution.py:117
  10.1 14.4 %collective-permute-start.1 = (bf16[4,144,128]{2,1,0:T(8,128)(2,1)}, bf16[4,144,128]{2,1,0:T(8,128)(2,1)S(1)}, u32[]{:S(2)}, u32[]{:S(2)}) collective-permute-start(bf16[4,144,128]{2,1,0:T(8,128)(2,1)} %get-tuple-element.51), channel_id=1, source_target_pairs={{0,1},{2,3},{1,0},{3,2},{4,5},{6,7},{5,4},{7,6},{8,9},{10,11},{9,8... | collective-permute-start | bytes 442376 | tf_op jit(solution)/shard_map/ppermute | solution.py:117
  11.1 5.6 %copy-start.4 = (s32[16]{0:T(128)S(1)}, s32[16]{0:T(128)}, u32[]{:S(2)}) copy-start(s32[16]{0:T(128)} %param.17) | copy-start | bytes 196
  11.1 5.7 %copy-start.3 = (bf16[4,144,128]{2,1,0:T(8,128)(2,1)S(1)}, bf16[4,144,128]{2,1,0:T(8,128)(2,1)}, u32[]{:S(2)}) copy-start(bf16[4,144,128]{2,1,0:T(8,128)(2,1)} %get-tuple-element.52) | copy-start | bytes 442372
  11.1 9.2 %copy-start.2 = (bf16[4,144,128]{2,1,0:T(8,128)(2,1)S(1)}, bf16[4,144,128]{2,1,0:T(8,128)(2,1)}, u32[]{:S(2)}) copy-start(bf16[4,144,128]{2,1,0:T(8,128)(2,1)} %get-tuple-element.53) | copy-start | bytes 442372
  11.1 9.3 %copy-start.1 = (bf16[4,144,128]{2,1,0:T(8,128)(2,1)S(1)}, bf16[4,144,128]{2,1,0:T(8,128)(2,1)}, u32[]{:S(2)}) copy-start(bf16[4,144,128]{2,1,0:T(8,128)(2,1)} %get-tuple-element.60.refs_0_) | copy-start | bytes 442372
  16.8 13.8 %collective-permute-start.2 = (bf16[4,144,128]{2,1,0:T(8,128)(2,1)S(1)}, bf16[4,144,128]{2,1,0:T(8,128)(2,1)S(1)}, u32[]{:S(2)}, u32[]{:S(2)}) collective-permute-start(bf16[4,144,128]{2,1,0:T(8,128)(2,1)S(1)} %copy-done.3), channel_id=1, source_target_pairs={{0,2},{1,3},{2,0},{3,1},{4,6},{5,7},{6,4},{7,5},{8,10},{9,11},{10,... | collective-permute-start | bytes 442376 | tf_op jit(solution)/shard_map/ppermute | solution.py:117
  20.3 10.3 %collective-permute-start.3 = (bf16[4,144,128]{2,1,0:T(8,128)(2,1)S(1)}, bf16[4,144,128]{2,1,0:T(8,128)(2,1)S(1)}, u32[]{:S(2)}, u32[]{:S(2)}) collective-permute-start(bf16[4,144,128]{2,1,0:T(8,128)(2,1)S(1)} %copy-done.2), channel_id=1, source_target_pairs={{0,3},{1,2},{3,0},{2,1},{4,7},{5,6},{7,4},{6,5},{8,11},{9,10},{11,... | collective-permute-start | bytes 442376 | tf_op jit(solution)/shard_map/ppermute | solution.py:117
  20.4 10.2 %copy-start = (bf16[4,144,128]{2,1,0:T(8,128)(2,1)S(1)}, bf16[4,144,128]{2,1,0:T(8,128)(2,1)}, u32[]{:S(2)}) copy-start(bf16[4,144,128]{2,1,0:T(8,128)(2,1)} %get-tuple-element.50.refs_0_) | copy-start | bytes 442372
  20.5 13.8 %collective-permute-start.11 = (bf16[3,4,144,128]{3,2,1,0:T(8,128)(2,1)S(1)}, bf16[3,4,144,128]{3,2,1,0:T(8,128)(2,1)S(1)}, u32[]{:S(2)}, u32[]{:S(2)}) collective-permute-start(bf16[3,4,144,128]{3,2,1,0:T(8,128)(2,1)S(1)} %get-tuple-element.64), channel_id=1, source_target_pairs={{4,8},{12,16},{20,24},{8,4},{16,12},{24,20},{0,0},{28,28},{5,9},{1... | collective-permute-start | bytes 1327112 | tf_op jit(solution)/shard_map/ppermute | solution.py:165
  21.2 13.1 %collective-permute-start.12 = (bf16[3,4,144,128]{3,2,1,0:T(8,128)(2,1)S(1)}, bf16[3,4,144,128]{3,2,1,0:T(8,128)(2,1)S(1)}, u32[]{:S(2)}, u32[]{:S(2)}) collective-permute-start(bf16[3,4,144,128]{3,2,1,0:T(8,128)(2,1)S(1)} %get-tuple-element.65), channel_id=1, source_target_pairs={{0,4},{8,12},{16,20},{24,28},{4,0},{12,8},{20,16},{28,24},{1,5},{9... | collective-permute-start | bytes 1327112 | tf_op jit(solution)/shard_map/ppermute | solution.py:165
  30.7 10.7 %collective-permute-start.4 = (bf16[3,4,144,128]{3,2,1,0:T(8,128)(2,1)S(1)}, bf16[3,4,144,128]{3,2,1,0:T(8,128)(2,1)S(1)}, u32[]{:S(2)}, u32[]{:S(2)}) collective-permute-start(bf16[3,4,144,128]{3,2,1,0:T(8,128)(2,1)S(1)} %get-tuple-element.54), channel_id=1, source_target_pairs={{4,8},{12,16},{20,24},{8,4},{16,12},{24,20},{0,0},{28,28},{5,9},{1... | collective-permute-start | bytes 1327112 | tf_op jit(solution)/shard_map/ppermute | solution.py:165
  31.4 10.0 %collective-permute-start.5 = (bf16[3,4,144,128]{3,2,1,0:T(8,128)(2,1)S(1)}, bf16[3,4,144,128]{3,2,1,0:T(8,128)(2,1)S(1)}, u32[]{:S(2)}, u32[]{:S(2)}) collective-permute-start(bf16[3,4,144,128]{3,2,1,0:T(8,128)(2,1)S(1)} %get-tuple-element.55), channel_id=1, source_target_pairs={{0,4},{8,12},{16,20},{24,28},{4,0},{12,8},{20,16},{28,24},{1,5},{9... | collective-permute-start | bytes 1327112 | tf_op jit(solution)/shard_map/ppermute | solution.py:165
  35.9 10.2 %collective-permute-start.13 = (bf16[3,144,128]{2,1,0:T(8,128)(2,1)S(1)}, bf16[3,144,128]{2,1,0:T(8,128)(2,1)S(1)}, u32[]{:S(2)}, u32[]{:S(2)}) collective-permute-start(bf16[3,144,128]{2,1,0:T(8,128)(2,1)S(1)} %get-tuple-element.66), channel_id=1, source_target_pairs={{0,3},{1,2},{3,0},{2,1},{4,7},{5,6},{7,4},{6,5},{8,11},{9,10},{11,... | collective-permute-start | bytes 331784 | tf_op jit(solution)/shard_map/ppermute | solution.py:117
  38.8 14.6 %collective-permute-start.14 = (bf16[3,144,128]{2,1,0:T(8,128)(2,1)S(1)}, bf16[3,144,128]{2,1,0:T(8,128)(2,1)S(1)}, u32[]{:S(2)}, u32[]{:S(2)}) collective-permute-start(bf16[3,144,128]{2,1,0:T(8,128)(2,1)S(1)} %get-tuple-element.67), channel_id=1, source_target_pairs={{0,2},{1,3},{2,0},{3,1},{4,6},{5,7},{6,4},{7,5},{8,10},{9,11},{10,... | collective-permute-start | bytes 331784 | tf_op jit(solution)/shard_map/ppermute | solution.py:117
  40.9 12.5 %collective-permute-start.15 = (bf16[3,144,128]{2,1,0:T(8,128)(2,1)S(1)}, bf16[3,144,128]{2,1,0:T(8,128)(2,1)S(1)}, u32[]{:S(2)}, u32[]{:S(2)}) collective-permute-start(bf16[3,144,128]{2,1,0:T(8,128)(2,1)S(1)} %get-tuple-element.69), channel_id=1, source_target_pairs={{0,1},{2,3},{1,0},{3,2},{4,5},{6,7},{5,4},{7,6},{8,9},{10,11},{9,8... | collective-permute-start | bytes 331784 | tf_op jit(solution)/shard_map/ppermute | solution.py:117
  43.0 11.3 %collective-permute-start.6 = (bf16[3,144,128]{2,1,0:T(8,128)(2,1)S(1)}, bf16[3,144,128]{2,1,0:T(8,128)(2,1)S(1)}, u32[]{:S(2)}, u32[]{:S(2)}) collective-permute-start(bf16[3,144,128]{2,1,0:T(8,128)(2,1)S(1)} %get-tuple-element.56), channel_id=1, source_target_pairs={{0,3},{1,2},{3,0},{2,1},{4,7},{5,6},{7,4},{6,5},{8,11},{9,10},{11,... | collective-permute-start | bytes 331784 | tf_op jit(solution)/shard_map/ppermute | solution.py:117
  45.4 13.9 %collective-permute-start.7 = (bf16[3,144,128]{2,1,0:T(8,128)(2,1)S(1)}, bf16[3,144,128]{2,1,0:T(8,128)(2,1)S(1)}, u32[]{:S(2)}, u32[]{:S(2)}) collective-permute-start(bf16[3,144,128]{2,1,0:T(8,128)(2,1)S(1)} %get-tuple-element.57), channel_id=1, source_target_pairs={{0,2},{1,3},{2,0},{3,1},{4,6},{5,7},{6,4},{7,5},{8,10},{9,11},{10,... | collective-permute-start | bytes 331784 | tf_op jit(solution)/shard_map/ppermute | solution.py:117
  46.0 13.2 %collective-permute-start.8 = (bf16[3,144,128]{2,1,0:T(8,128)(2,1)S(1)}, bf16[3,144,128]{2,1,0:T(8,128)(2,1)S(1)}, u32[]{:S(2)}, u32[]{:S(2)}) collective-permute-start(bf16[3,144,128]{2,1,0:T(8,128)(2,1)S(1)} %get-tuple-element.59), channel_id=1, source_target_pairs={{0,1},{2,3},{1,0},{3,2},{4,5},{6,7},{5,4},{7,6},{8,9},{10,11},{9,8... | collective-permute-start | bytes 331784 | tf_op jit(solution)/shard_map/ppermute | solution.py:117

commit v9 on v6

--- a/solution.py
+++ b/solution.py
@@ -73,36 +73,36 @@
     return row, pl.ds(pl.multiple_of(device // sharing * LANES, LANES), LANES)
 
 
-def split_kernel(sharing, rows, span, *refs):
+def split_kernel(sharing, rows, jobs, *refs):
     ins, outs, (held, arrived, sent) = refs[:4], refs[4:-3], refs[-3:]
     loads, stores = {}, []
-    for step in far_first(len(outs)):
+    for at, (begin, step) in enumerate(jobs):
         row, tokens = part_of(lax.axis_index("seq") ^ step, sharing, rows)
         for i, array in enumerate(ins):
-            given = array.at[0, pl.ds(span.start + row, rows), tokens]
-            loads[step, i] = pltpu.make_async_copy(given, held.at[step, i], arrived.at[step, i])
-            loads[step, i].start()
-    for step in far_first(len(outs)):
+            given = array.at[0, pl.ds(begin + row, rows), tokens]
+            loads[at, i] = pltpu.make_async_copy(given, held.at[at, i], arrived.at[at, i])
+            loads[at, i].start()
+    for at, out in enumerate(outs):
         for i in range(len(ins)):
-            loads[step, i].wait()
-        stores.append(pltpu.make_async_copy(held.at[step], outs[step], sent.at[step]))
+            loads[at, i].wait()
+        stores.append(pltpu.make_async_copy(held.at[at], out, sent.at[at]))
         stores[-1].start()
     for copy in stores:
         copy.wait()
 
 
-def split(arrays, span, n, sharing):
-    rows = (span.stop - span.start) // sharing
+def split(arrays, jobs, rows, sharing):
+    count = len(jobs)
     hbm = pl.BlockSpec(memory_space=pltpu.HBM)
     return pl.pallas_call(
-        functools.partial(split_kernel, sharing, rows, span),
+        functools.partial(split_kernel, sharing, rows, jobs),
         in_specs=[hbm] * 4,
-        out_specs=[hbm] * n,
-        out_shape=[jax.ShapeDtypeStruct((4, rows, LANES), jnp.bfloat16)] * n,
+        out_specs=[hbm] * count,
+        out_shape=[jax.ShapeDtypeStruct((4, rows, LANES), jnp.bfloat16)] * count,
         scratch_shapes=[
-            pltpu.VMEM((n, 4, rows, LANES), jnp.bfloat16),
-            pltpu.SemaphoreType.DMA((n, 4)),
-            pltpu.SemaphoreType.DMA((n,)),
+            pltpu.VMEM((count, 4, rows, LANES), jnp.bfloat16),
+            pltpu.SemaphoreType.DMA((count, 4)),
+            pltpu.SemaphoreType.DMA((count,)),
         ],
         compiler_params=pltpu.CompilerParams(vmem_limit_bytes=60 * 2**20),
         name="pack",
@@ -340,11 +340,16 @@
         spans.append(slice(head * HDIM, (head + heads) * HDIM))
         head += heads
     space_in = turned(q_space, k_space, v_space, cot_space)
-    packed = [list(split(time, span, n, sharing)) for span in spans]
+    rows = CHUNKS[0] // sharing * HDIM
+    jobs = [(span.start, step) for span in spans for step in far_first(n)]
+    blocks = {}
+    for part in (jobs[: n // 2], jobs[n // 2 :]):
+        blocks.update(zip(part, split(time, part, rows, sharing)))
+    packed = [[blocks[span.start, step] for step in range(n)] for span in spans]
     own = [exchange(packed[0])]
-    packed[1][n // 2 :], own[0][-1] = gated(packed[1][n // 2 :], own[0][-1])
+    space = space_grads(*space_in)
+    packed[1][2:], own[0][2], space = gated(packed[1][2:], own[0][2], space)
     own.append(exchange(packed[1]))
-    space = space_grads(*space_in)
     beside = [
         [neighbours(ends, start) for ends, start in zip(sides(blocks), (1, 0))] for blocks in own
     ]
@@ -366,6 +371,7 @@
         and mesh.shape["grp"] % 2 == 0
         and mesh.shape["grp"] > 2
         and sharing * tokens == n * LANES
+        and len(set(CHUNKS)) == 1
         and all(heads % sharing == 0 and heads // sharing * HDIM % 16 == 0 for heads in CHUNKS)
     )
 

time: 64.1 us -> 61 us (0.952)
  starting transfers between devices: 27.8 us -> 22.6 us
  waiting for transfers between devices: 20.8 us -> 23.2 us
    ppermute x16, starting transfers between devices: 27.8 us -> 22.6 us  [swap(): lax.ppermute(block, axis, [(i, j) for i, j in pairs] + [(j, i) for i, j i...]
    ppermute x16, waiting for transfers between devices: 20.8 us -> 23.2 us  [swap(): lax.ppermute(block, axis, [(i, j) for i, j in pairs] + [(j, i) for i, j i...]
  transfers between devices with their start and end apart: 16 -> 16, of which waited for: 5 -> 7; matrix products, arithmetic and copies ran while one was open for 0% -> 0% of each run, Pallas kernels for 18% -> 19%
where the time goes in v9:
time: 61 us; the launch traced here: 60.7 us
  waiting for transfers between devices  23.2 us (38%)
  starting transfers between devices  22.6 us (37%)
  Pallas kernels  13.8 us (23%)
  between operations  0.72 us (1%)
    ppermute x16, waiting for transfers between devices, swap(): lax.ppermute(block, axis, [(i, j) for i, j in pairs] + [(j, i) for i, j i...  23.2 us
    ppermute x16, starting transfers between devices, swap(): lax.ppermute(block, axis, [(i, j) for i, j in pairs] + [(j, i) for i, j i...  22.6 us
    pallas_call x1, Pallas kernels, space_grads(): pl.pallas_call(frame_kernel, out_shape=(shape, shape, shape), compiler_pa...  5.59 us
    pallas_call x2, Pallas kernels, split(): pl.pallas_call(functools.partial(split_kernel, sharing, rows, jobs), in_s...  3.71 us
    pallas_call x2, Pallas kernels, clip_grads(): pl.pallas_call(functools.partial(clip_kernel, window, heads), out_shape=[...  2.58 us
    pallas_call x2, Pallas kernels, join(): pl.pallas_call(functools.partial(join_kernel, sharing, span), in_specs=[p...  1.71 us
  transfers between devices with their start and end apart: 16, of which 7 were waited for; matrix products, arithmetic and copies ran while one was open for 0% of the time, Pallas kernels for 19%

profile of v9, /device:TPU:0, one launch (start us, length us, event | category | flops | bytes accessed | tf_op | source)
XLA Modules:
  0.0 60.7 jit_solution(5267451481763720359)
XLA Ops:
  0.6 1.7 %pack.3 = (bf16[4,144,128]{2,1,0:T(8,128)(2,1)}, bf16[4,144,128]{2,1,0:T(8,128)(2,1)}) custom-call(bf16[1,576,256]{2,1,0:T(8,128)(2,1)} %bitcast.18, bf16[1,576,256]{2,1,0:T(8,128)(2,1)} %bitcast.20, bf16[1,576,256]{2,1,0:T(8,128)(2,1)} %bitcast.22, bf16[1,576,256]{2,1,0:T(8,128)(2,1)} %bitcast.24), custom_call_target="tpu_custom_call" | custom-call | tf_op jit(solution)/shard_map/pack/pallas_call | solution.py:97
  2.3 4.1 %collective-permute-start = (bf16[4,144,128]{2,1,0:T(8,128)(2,1)}, bf16[4,144,128]{2,1,0:T(8,128)(2,1)S(1)}, u32[]{:S(2)}, u32[]{:S(2)}) collective-permute-start(bf16[4,144,128]{2,1,0:T(8,128)(2,1)} %get-tuple-element.43), channel_id=1, source_target_pairs={{0,2},{1,3},{2,0},{3,1},{4,6},{5,7},{6,4},{7,5},{8,10},{9,11},{10,... | collective-permute-start | bytes 442376 | tf_op jit(solution)/shard_map/ppermute | solution.py:117
  6.4 1.3 %collective-permute-start.10 = (bf16[4,144,128]{2,1,0:T(8,128)(2,1)}, bf16[4,144,128]{2,1,0:T(8,128)(2,1)S(1)}, u32[]{:S(2)}, u32[]{:S(2)}) collective-permute-start(bf16[4,144,128]{2,1,0:T(8,128)(2,1)} %get-tuple-element.63), channel_id=1, source_target_pairs={{0,3},{1,2},{3,0},{2,1},{4,7},{5,6},{7,4},{6,5},{8,11},{9,10},{11,... | collective-permute-start | bytes 442376 | tf_op jit(solution)/shard_map/ppermute | solution.py:117
  7.8 2.0 %pack.2 = (bf16[4,144,128]{2,1,0:T(8,128)(2,1)}, bf16[4,144,128]{2,1,0:T(8,128)(2,1)}, bf16[4,144,128]{2,1,0:T(8,128)(2,1)}, bf16[4,144,128]{2,1,0:T(8,128)(2,1)...) custom-call(bf16[1,576,256]{2,1,0:T(8,128)(2,1)} %bitcast.19, bf16[1,576,256]{2,1,0:T(8,128)(2,1)} %bitcast.21, ...), custom_call_target="tpu_custom_call" | custom-call | tf_op jit(solution)/shard_map/pack/pallas_call | solution.py:97
  9.8 0.3 collective-permute-start.1
  10.1 1.8 %collective-permute-start.9 = (bf16[4,144,128]{2,1,0:T(8,128)(2,1)}, bf16[4,144,128]{2,1,0:T(8,128)(2,1)S(1)}, u32[]{:S(2)}, u32[]{:S(2)}) collective-permute-start(bf16[4,144,128]{2,1,0:T(8,128)(2,1)} %get-tuple-element.61), channel_id=1, source_target_pairs={{0,1},{2,3},{1,0},{3,2},{4,5},{6,7},{5,4},{7,6},{8,9},{10,11},{9,8... | collective-permute-start | bytes 442376 | tf_op jit(solution)/shard_map/ppermute | solution.py:117
  11.9 0.0 copy-start.4
  11.9 0.0 copy-start.3
  11.9 0.0 copy-start.2
  11.9 0.0 copy-start.1
  11.9 5.6 %space.1 = (bf16[1,576,256]{2,1,0:T(8,128)(2,1)}, bf16[1,576,256]{2,1,0:T(8,128)(2,1)}, bf16[1,576,256]{2,1,0:T(8,128)(2,1)}) custom-call(bf16[1,576,256]{2,1,0:T(8,128)(2,1)} %bitcast.29, bf16[1,576,256]{2,1,0:T(8,128)(2,1)} %bitcast.30, bf16[1,576,256]{2,1,0:T(8,128)(2,1)} %bitcast.31, bf16[1,576,256]{2,1,0:T(8,128)(2,1)} %bitcast.32), custom_call_target="tpu_custom_call" | custom-call | flops 1610612736 | bytes 2064384 | tf_op jit(solution)/shard_map/space/pallas_call | solution.py:58
  17.5 0.0 copy-done.4
  17.5 0.1 select_reduce_fusion.2
  17.6 0.1 collective-permute-done.refs_2_
  17.7 0.0 copy-done.3
  17.7 1.7 %collective-permute-start.2 = (bf16[4,144,128]{2,1,0:T(8,128)(2,1)S(1)}, bf16[4,144,128]{2,1,0:T(8,128)(2,1)S(1)}, u32[]{:S(2)}, u32[]{:S(2)}) collective-permute-start(bf16[4,144,128]{2,1,0:T(8,128)(2,1)S(1)} %copy-done.3), channel_id=1, source_target_pairs={{0,2},{1,3},{2,0},{3,1},{4,6},{5,7},{6,4},{7,5},{8,10},{9,11},{10,... | collective-permute-start | bytes 442376 | tf_op jit(solution)/shard_map/ppermute | solution.py:117
  19.3 0.0 copy-done.2
  19.3 1.2 %collective-permute-start.3 = (bf16[4,144,128]{2,1,0:T(8,128)(2,1)S(1)}, bf16[4,144,128]{2,1,0:T(8,128)(2,1)S(1)}, u32[]{:S(2)}, u32[]{:S(2)}) collective-permute-start(bf16[4,144,128]{2,1,0:T(8,128)(2,1)S(1)} %copy-done.2), channel_id=1, source_target_pairs={{0,3},{1,2},{3,0},{2,1},{4,7},{5,6},{7,4},{6,5},{8,11},{9,10},{11,... | collective-permute-start | bytes 442376 | tf_op jit(solution)/shard_map/ppermute | solution.py:117
  20.5 0.0 collective-permute-done.10.refs_3_
  20.5 3.8 %collective-permute-done.9.refs_1_ = bf16[4,144,128]{2,1,0:T(8,128)(2,1)S(1)} collective-permute-done((bf16[4,144,128]{2,1,0:T(8,128)(2,1)}, bf16[4,144,128]{2,1,0:T(8,128)(2,1)S(1)}, u32[]{:S(2)}, u32[]{:S(2)}) %collective-permute-start.9) | collective-permute-done | bytes 147488 | tf_op jit(solution)/shard_map/ppermute | solution.py:117
  24.4 0.0 copy-done.1
  24.4 0.0 copy-start
  24.4 0.1 sides.3
  24.5 1.4 %collective-permute-start.11 = (bf16[3,4,144,128]{3,2,1,0:T(8,128)(2,1)S(1)}, bf16[3,4,144,128]{3,2,1,0:T(8,128)(2,1)S(1)}, u32[]{:S(2)}, u32[]{:S(2)}) collective-permute-start(bf16[3,4,144,128]{3,2,1,0:T(8,128)(2,1)S(1)} %get-tuple-element.64), channel_id=1, source_target_pairs={{4,8},{12,16},{20,24},{28,0},{8,4},{16,12},{24,20},{0,28},{5,9},{1... | collective-permute-start | bytes 1327112 | tf_op jit(solution)/shard_map/ppermute | solution.py:117
  25.9 0.3 collective-permute-start.12
  26.2 0.2 select_reduce_fusion.1
  26.4 0.0 collective-permute-done.1.refs_1_
  26.4 4.5 %collective-permute-done.2.refs_2_ = bf16[4,144,128]{2,1,0:T(8,128)(2,1)S(1)} collective-permute-done((bf16[4,144,128]{2,1,0:T(8,128)(2,1)S(1)}, bf16[4,144,128]{2,1,0:T(8,128)(2,1)S(1)}, u32[]{:S(2)}, u32[]{:S(2)}) %collective-permute-start.2) | collective-permute-done | bytes 147488 | tf_op jit(solution)/shard_map/ppermute | solution.py:117
  30.9 0.0 collective-permute-done.3.refs_3_
  30.9 0.0 copy-done
  30.9 0.1 sides.2
  31.0 0.1 collective-permute-start.4
  31.1 1.6 %collective-permute-start.5 = (bf16[3,4,144,128]{3,2,1,0:T(8,128)(2,1)S(1)}, bf16[3,4,144,128]{3,2,1,0:T(8,128)(2,1)S(1)}, u32[]{:S(2)}, u32[]{:S(2)}) collective-permute-start(bf16[3,4,144,128]{3,2,1,0:T(8,128)(2,1)S(1)} %get-tuple-element.55), channel_id=1, source_target_pairs={{0,4},{8,12},{16,20},{24,28},{4,0},{12,8},{20,16},{28,24},{1,5},{9... | collective-permute-start | bytes 1327112 | tf_op jit(solution)/shard_map/ppermute | solution.py:117
  32.7 5.2 %collective-permute-done.11.refs_4_ = bf16[3,4,144,128]{3,2,1,0:T(8,128)(2,1)S(1)} collective-permute-done((bf16[3,4,144,128]{3,2,1,0:T(8,128)(2,1)S(1)}, bf16[3,4,144,128]{3,2,1,0:T(8,128)(2,1)S(1)}, u32[]{:S(2)}, u32[]{:S(2)}) %collective-permute-start.11) | collective-permute-done | bytes 442400 | tf_op jit(solution)/shard_map/ppermute | solution.py:117
  37.9 0.0 collective-permute-done.12.refs_5_
  37.9 1.3 %clips.3 = (bf16[3,144,128]{2,1,0:T(8,128)(2,1)S(1)}, bf16[3,144,128]{2,1,0:T(8,128)(2,1)S(1)}, bf16[3,144,128]{2,1,0:T(8,128)(2,1)S(1)}, bf16[3,144,128]{2,1,0:T(8,128)(2,1)S(1)}) custom-call(s32[2,10]{1,0:T(2,128)S(1)} %pad_add_fusion.given_bounds, bf16[4,144,128]{2,1,0:T(8,128)(2,1)S(1)} %copy-done.1, ...), custom_call_target="tpu_custom_call" | custom-call | flops 589824000 | bytes 1474560 | tf_op jit(solution)/shard_map/clips/pallas_call | solution.py:289
  39.2 2.8 %collective-permute-start.13 = (bf16[3,144,128]{2,1,0:T(8,128)(2,1)S(1)}, bf16[3,144,128]{2,1,0:T(8,128)(2,1)S(1)}, u32[]{:S(2)}, u32[]{:S(2)}) collective-permute-start(bf16[3,144,128]{2,1,0:T(8,128)(2,1)S(1)} %get-tuple-element.66), channel_id=1, source_target_pairs={{0,3},{1,2},{3,0},{2,1},{4,7},{5,6},{7,4},{6,5},{8,11},{9,10},{11,... | collective-permute-start | bytes 331784 | tf_op jit(solution)/shard_map/ppermute | solution.py:117
  41.9 0.0 collective-permute-start.14
  41.9 1.7 %collective-permute-start.15 = (bf16[3,144,128]{2,1,0:T(8,128)(2,1)S(1)}, bf16[3,144,128]{2,1,0:T(8,128)(2,1)S(1)}, u32[]{:S(2)}, u32[]{:S(2)}) collective-permute-start(bf16[3,144,128]{2,1,0:T(8,128)(2,1)S(1)} %get-tuple-element.69), channel_id=1, source_target_pairs={{0,1},{2,3},{1,0},{3,2},{4,5},{6,7},{5,4},{7,6},{8,9},{10,11},{9,8... | collective-permute-start | bytes 331784 | tf_op jit(solution)/shard_map/ppermute | solution.py:117
  43.6 3.7 %collective-permute-done.4.refs_4_ = bf16[3,4,144,128]{3,2,1,0:T(8,128)(2,1)S(1)} collective-permute-done((bf16[3,4,144,128]{3,2,1,0:T(8,128)(2,1)S(1)}, bf16[3,4,144,128]{3,2,1,0:T(8,128)(2,1)S(1)}, u32[]{:S(2)}, u32[]{:S(2)}) %collective-permute-start.4) | collective-permute-done | bytes 442400 | tf_op jit(solution)/shard_map/ppermute | solution.py:117
  47.3 0.0 collective-permute-done.5.refs_5_
  47.3 1.3 %clips.2 = (bf16[3,144,128]{2,1,0:T(8,128)(2,1)S(1)}, bf16[3,144,128]{2,1,0:T(8,128)(2,1)S(1)}, bf16[3,144,128]{2,1,0:T(8,128)(2,1)S(1)}, bf16[3,144,128]{2,1,0:T(8,128)(2,1)S(1)}) custom-call(s32[2,10]{1,0:T(2,128)S(1)} %pad_add_fusion.given_bounds, bf16[4,144,128]{2,1,0:T(8,128)(2,1)S(1)} %copy-done, ...), custom_call_target="tpu_custom_call" | custom-call | flops 589824000 | bytes 1474560 | tf_op jit(solution)/shard_map/clips/pallas_call | solution.py:289
  48.6 2.8 %collective-permute-start.6 = (bf16[3,144,128]{2,1,0:T(8,128)(2,1)S(1)}, bf16[3,144,128]{2,1,0:T(8,128)(2,1)S(1)}, u32[]{:S(2)}, u32[]{:S(2)}) collective-permute-start(bf16[3,144,128]{2,1,0:T(8,128)(2,1)S(1)} %get-tuple-element.56), channel_id=1, source_target_pairs={{0,3},{1,2},{3,0},{2,1},{4,7},{5,6},{7,4},{6,5},{8,11},{9,10},{11,... | collective-permute-start | bytes 331784 | tf_op jit(solution)/shard_map/ppermute | solution.py:117
  51.4 0.0 collective-permute-start.7
  51.4 0.0 collective-permute-done.13.refs_0_
  51.4 1.7 %collective-permute-start.8 = (bf16[3,144,128]{2,1,0:T(8,128)(2,1)S(1)}, bf16[3,144,128]{2,1,0:T(8,128)(2,1)S(1)}, u32[]{:S(2)}, u32[]{:S(2)}) collective-permute-start(bf16[3,144,128]{2,1,0:T(8,128)(2,1)S(1)} %get-tuple-element.59), channel_id=1, source_target_pairs={{0,1},{2,3},{1,0},{3,2},{4,5},{6,7},{5,4},{7,6},{8,9},{10,11},{9,8... | collective-permute-start | bytes 331784 | tf_op jit(solution)/shard_map/ppermute | solution.py:117
  53.1 0.0 collective-permute-done.14.refs_1_
  53.1 0.0 collective-permute-done.15.refs_3_
  53.1 0.9 %unpack.2 = (bf16[1,576,256]{2,1,0:T(8,128)(2,1)}, bf16[1,576,256]{2,1,0:T(8,128)(2,1)}, bf16[1,576,256]{2,1,0:T(8,128)(2,1)}) custom-call(bf16[3,144,128]{2,1,0:T(8,128)(2,1)S(1)} %collective-permute-done.13.refs_0_, bf16[3,144,128]{2,1,0:T(8,128)(2,1)S(1)} %collective-permute-done.14.refs_1_, bf16[3,144,128]{2,1,0:T(8,128)(2,1)S(1)} %get-tuple-element.68.refs_2_, ...), custom_call_target="tpu_custom_call" | custom-call | tf_op jit(solution)/shard_map/unpack/pallas_call | solution.py:185
  54.0 2.2 %collective-permute-done.6.refs_0_ = bf16[3,144,128]{2,1,0:T(8,128)(2,1)S(1)} collective-permute-done((bf16[3,144,128]{2,1,0:T(8,128)(2,1)S(1)}, bf16[3,144,128]{2,1,0:T(8,128)(2,1)S(1)}, u32[]{:S(2)}, u32[]{:S(2)}) %collective-permute-start.6) | collective-permute-done | bytes 110624 | tf_op jit(solution)/shard_map/ppermute | solution.py:117
  56.2 3.7 %collective-permute-done.7.refs_1_ = bf16[3,144,128]{2,1,0:T(8,128)(2,1)S(1)} collective-permute-done((bf16[3,144,128]{2,1,0:T(8,128)(2,1)S(1)}, bf16[3,144,128]{2,1,0:T(8,128)(2,1)S(1)}, u32[]{:S(2)}, u32[]{:S(2)}) %collective-permute-start.7) | collective-permute-done | bytes 110624 | tf_op jit(solution)/shard_map/ppermute | solution.py:117
  59.8 0.0 collective-permute-done.8.refs_3_
  59.8 0.9 %unpack.3 = (bf16[1,576,256]{2,1,0:T(8,128)(2,1)}, bf16[1,576,256]{2,1,0:T(8,128)(2,1)}, bf16[1,576,256]{2,1,0:T(8,128)(2,1)}) custom-call(bf16[3,144,128]{2,1,0:T(8,128)(2,1)S(1)} %collective-permute-done.6.refs_0_, bf16[3,144,128]{2,1,0:T(8,128)(2,1)S(1)} %collective-permute-done.7.refs_1_, ...), custom_call_target="tpu_custom_call", output_to_operand_aliasing={{0}: (4, {}), {1}: (5, {}), {2}: (6, {})} | custom-call | tf_op jit(solution)/shard_map/unpack/pallas_call | solution.py:185
  (4 shorter events, 0.0 us)
Async XLA Ops:
  2.3 15.4 %collective-permute-start = (bf16[4,144,128]{2,1,0:T(8,128)(2,1)}, bf16[4,144,128]{2,1,0:T(8,128)(2,1)S(1)}, u32[]{:S(2)}, u32[]{:S(2)}) collective-permute-start(bf16[4,144,128]{2,1,0:T(8,128)(2,1)} %get-tuple-element.43), channel_id=1, source_target_pairs={{0,2},{1,3},{2,0},{3,1},{4,6},{5,7},{6,4},{7,5},{8,10},{9,11},{10,... | collective-permute-start | bytes 442376 | tf_op jit(solution)/shard_map/ppermute | solution.py:117
  6.4 14.1 %collective-permute-start.10 = (bf16[4,144,128]{2,1,0:T(8,128)(2,1)}, bf16[4,144,128]{2,1,0:T(8,128)(2,1)S(1)}, u32[]{:S(2)}, u32[]{:S(2)}) collective-permute-start(bf16[4,144,128]{2,1,0:T(8,128)(2,1)} %get-tuple-element.63), channel_id=1, source_target_pairs={{0,3},{1,2},{3,0},{2,1},{4,7},{5,6},{7,4},{6,5},{8,11},{9,10},{11,... | collective-permute-start | bytes 442376 | tf_op jit(solution)/shard_map/ppermute | solution.py:117
  9.8 16.6 %collective-permute-start.1 = (bf16[4,144,128]{2,1,0:T(8,128)(2,1)}, bf16[4,144,128]{2,1,0:T(8,128)(2,1)S(1)}, u32[]{:S(2)}, u32[]{:S(2)}) collective-permute-start(bf16[4,144,128]{2,1,0:T(8,128)(2,1)} %get-tuple-element.51), channel_id=1, source_target_pairs={{0,1},{2,3},{1,0},{3,2},{4,5},{6,7},{5,4},{7,6},{8,9},{10,11},{9,8... | collective-permute-start | bytes 442376 | tf_op jit(solution)/shard_map/ppermute | solution.py:117
  10.1 14.3 %collective-permute-start.9 = (bf16[4,144,128]{2,1,0:T(8,128)(2,1)}, bf16[4,144,128]{2,1,0:T(8,128)(2,1)S(1)}, u32[]{:S(2)}, u32[]{:S(2)}) collective-permute-start(bf16[4,144,128]{2,1,0:T(8,128)(2,1)} %get-tuple-element.61), channel_id=1, source_target_pairs={{0,1},{2,3},{1,0},{3,2},{4,5},{6,7},{5,4},{7,6},{8,9},{10,11},{9,8... | collective-permute-start | bytes 442376 | tf_op jit(solution)/shard_map/ppermute | solution.py:117
  11.9 5.6 %copy-start.4 = (s32[16]{0:T(128)S(1)}, s32[16]{0:T(128)}, u32[]{:S(2)}) copy-start(s32[16]{0:T(128)} %param.17) | copy-start | bytes 196
  11.9 5.8 %copy-start.3 = (bf16[4,144,128]{2,1,0:T(8,128)(2,1)S(1)}, bf16[4,144,128]{2,1,0:T(8,128)(2,1)}, u32[]{:S(2)}) copy-start(bf16[4,144,128]{2,1,0:T(8,128)(2,1)} %get-tuple-element.52) | copy-start | bytes 442372
  11.9 7.4 %copy-start.2 = (bf16[4,144,128]{2,1,0:T(8,128)(2,1)S(1)}, bf16[4,144,128]{2,1,0:T(8,128)(2,1)}, u32[]{:S(2)}) copy-start(bf16[4,144,128]{2,1,0:T(8,128)(2,1)} %get-tuple-element.53) | copy-start | bytes 442372
  11.9 12.5 %copy-start.1 = (bf16[4,144,128]{2,1,0:T(8,128)(2,1)S(1)}, bf16[4,144,128]{2,1,0:T(8,128)(2,1)}, u32[]{:S(2)}) copy-start(bf16[4,144,128]{2,1,0:T(8,128)(2,1)} %get-tuple-element.60.refs_0_) | copy-start | bytes 442372
  17.7 13.2 %collective-permute-start.2 = (bf16[4,144,128]{2,1,0:T(8,128)(2,1)S(1)}, bf16[4,144,128]{2,1,0:T(8,128)(2,1)S(1)}, u32[]{:S(2)}, u32[]{:S(2)}) collective-permute-start(bf16[4,144,128]{2,1,0:T(8,128)(2,1)S(1)} %copy-done.3), channel_id=1, source_target_pairs={{0,2},{1,3},{2,0},{3,1},{4,6},{5,7},{6,4},{7,5},{8,10},{9,11},{10,... | collective-permute-start | bytes 442376 | tf_op jit(solution)/shard_map/ppermute | solution.py:117
  19.3 11.5 %collective-permute-start.3 = (bf16[4,144,128]{2,1,0:T(8,128)(2,1)S(1)}, bf16[4,144,128]{2,1,0:T(8,128)(2,1)S(1)}, u32[]{:S(2)}, u32[]{:S(2)}) collective-permute-start(bf16[4,144,128]{2,1,0:T(8,128)(2,1)S(1)} %copy-done.2), channel_id=1, source_target_pairs={{0,3},{1,2},{3,0},{2,1},{4,7},{5,6},{7,4},{6,5},{8,11},{9,10},{11,... | collective-permute-start | bytes 442376 | tf_op jit(solution)/shard_map/ppermute | solution.py:117
  24.4 6.5 %copy-start = (bf16[4,144,128]{2,1,0:T(8,128)(2,1)S(1)}, bf16[4,144,128]{2,1,0:T(8,128)(2,1)}, u32[]{:S(2)}) copy-start(bf16[4,144,128]{2,1,0:T(8,128)(2,1)} %get-tuple-element.50.refs_0_) | copy-start | bytes 442372
  24.5 13.3 %collective-permute-start.11 = (bf16[3,4,144,128]{3,2,1,0:T(8,128)(2,1)S(1)}, bf16[3,4,144,128]{3,2,1,0:T(8,128)(2,1)S(1)}, u32[]{:S(2)}, u32[]{:S(2)}) collective-permute-start(bf16[3,4,144,128]{3,2,1,0:T(8,128)(2,1)S(1)} %get-tuple-element.64), channel_id=1, source_target_pairs={{4,8},{12,16},{20,24},{28,0},{8,4},{16,12},{24,20},{0,28},{5,9},{1... | collective-permute-start | bytes 1327112 | tf_op jit(solution)/shard_map/ppermute | solution.py:117
  25.9 11.9 %collective-permute-start.12 = (bf16[3,4,144,128]{3,2,1,0:T(8,128)(2,1)S(1)}, bf16[3,4,144,128]{3,2,1,0:T(8,128)(2,1)S(1)}, u32[]{:S(2)}, u32[]{:S(2)}) collective-permute-start(bf16[3,4,144,128]{3,2,1,0:T(8,128)(2,1)S(1)} %get-tuple-element.65), channel_id=1, source_target_pairs={{0,4},{8,12},{16,20},{24,28},{4,0},{12,8},{20,16},{28,24},{1,5},{9... | collective-permute-start | bytes 1327112 | tf_op jit(solution)/shard_map/ppermute | solution.py:117
  31.0 16.3 %collective-permute-start.4 = (bf16[3,4,144,128]{3,2,1,0:T(8,128)(2,1)S(1)}, bf16[3,4,144,128]{3,2,1,0:T(8,128)(2,1)S(1)}, u32[]{:S(2)}, u32[]{:S(2)}) collective-permute-start(bf16[3,4,144,128]{3,2,1,0:T(8,128)(2,1)S(1)} %get-tuple-element.54), channel_id=1, source_target_pairs={{4,8},{12,16},{20,24},{28,0},{8,4},{16,12},{24,20},{0,28},{5,9},{1... | collective-permute-start | bytes 1327112 | tf_op jit(solution)/shard_map/ppermute | solution.py:117
  31.1 16.3 %collective-permute-start.5 = (bf16[3,4,144,128]{3,2,1,0:T(8,128)(2,1)S(1)}, bf16[3,4,144,128]{3,2,1,0:T(8,128)(2,1)S(1)}, u32[]{:S(2)}, u32[]{:S(2)}) collective-permute-start(bf16[3,4,144,128]{3,2,1,0:T(8,128)(2,1)S(1)} %get-tuple-element.55), channel_id=1, source_target_pairs={{0,4},{8,12},{16,20},{24,28},{4,0},{12,8},{20,16},{28,24},{1,5},{9... | collective-permute-start | bytes 1327112 | tf_op jit(solution)/shard_map/ppermute | solution.py:117
  39.2 12.3 %collective-permute-start.13 = (bf16[3,144,128]{2,1,0:T(8,128)(2,1)S(1)}, bf16[3,144,128]{2,1,0:T(8,128)(2,1)S(1)}, u32[]{:S(2)}, u32[]{:S(2)}) collective-permute-start(bf16[3,144,128]{2,1,0:T(8,128)(2,1)S(1)} %get-tuple-element.66), channel_id=1, source_target_pairs={{0,3},{1,2},{3,0},{2,1},{4,7},{5,6},{7,4},{6,5},{8,11},{9,10},{11,... | collective-permute-start | bytes 331784 | tf_op jit(solution)/shard_map/ppermute | solution.py:117
  41.9 11.2 %collective-permute-start.14 = (bf16[3,144,128]{2,1,0:T(8,128)(2,1)S(1)}, bf16[3,144,128]{2,1,0:T(8,128)(2,1)S(1)}, u32[]{:S(2)}, u32[]{:S(2)}) collective-permute-start(bf16[3,144,128]{2,1,0:T(8,128)(2,1)S(1)} %get-tuple-element.67), channel_id=1, source_target_pairs={{0,2},{1,3},{2,0},{3,1},{4,6},{5,7},{6,4},{7,5},{8,10},{9,11},{10,... | collective-permute-start | bytes 331784 | tf_op jit(solution)/shard_map/ppermute | solution.py:117
  41.9 11.2 %collective-permute-start.15 = (bf16[3,144,128]{2,1,0:T(8,128)(2,1)S(1)}, bf16[3,144,128]{2,1,0:T(8,128)(2,1)S(1)}, u32[]{:S(2)}, u32[]{:S(2)}) collective-permute-start(bf16[3,144,128]{2,1,0:T(8,128)(2,1)S(1)} %get-tuple-element.69), channel_id=1, source_target_pairs={{0,1},{2,3},{1,0},{3,2},{4,5},{6,7},{5,4},{7,6},{8,9},{10,11},{9,8... | collective-permute-start | bytes 331784 | tf_op jit(solution)/shard_map/ppermute | solution.py:117
  48.6 7.5 %collective-permute-start.6 = (bf16[3,144,128]{2,1,0:T(8,128)(2,1)S(1)}, bf16[3,144,128]{2,1,0:T(8,128)(2,1)S(1)}, u32[]{:S(2)}, u32[]{:S(2)}) collective-permute-start(bf16[3,144,128]{2,1,0:T(8,128)(2,1)S(1)} %get-tuple-element.56), channel_id=1, source_target_pairs={{0,3},{1,2},{3,0},{2,1},{4,7},{5,6},{7,4},{6,5},{8,11},{9,10},{11,... | collective-permute-start | bytes 331784 | tf_op jit(solution)/shard_map/ppermute | solution.py:117
  51.4 8.4 %collective-permute-start.7 = (bf16[3,144,128]{2,1,0:T(8,128)(2,1)S(1)}, bf16[3,144,128]{2,1,0:T(8,128)(2,1)S(1)}, u32[]{:S(2)}, u32[]{:S(2)}) collective-permute-start(bf16[3,144,128]{2,1,0:T(8,128)(2,1)S(1)} %get-tuple-element.57), channel_id=1, source_target_pairs={{0,2},{1,3},{2,0},{3,1},{4,6},{5,7},{6,4},{7,5},{8,10},{9,11},{10,... | collective-permute-start | bytes 331784 | tf_op jit(solution)/shard_map/ppermute | solution.py:117
  51.4 8.4 %collective-permute-start.8 = (bf16[3,144,128]{2,1,0:T(8,128)(2,1)S(1)}, bf16[3,144,128]{2,1,0:T(8,128)(2,1)S(1)}, u32[]{:S(2)}, u32[]{:S(2)}) collective-permute-start(bf16[3,144,128]{2,1,0:T(8,128)(2,1)S(1)} %get-tuple-element.59), channel_id=1, source_target_pairs={{0,1},{2,3},{1,0},{3,2},{4,5},{6,7},{5,4},{7,6},{8,9},{10,11},{9,8... | collective-permute-start | bytes 331784 | tf_op jit(solution)/shard_map/ppermute | solution.py:117

commit v10 on v6

--- a/solution.py
+++ b/solution.py
@@ -342,9 +342,9 @@
     space_in = turned(q_space, k_space, v_space, cot_space)
     packed = [list(split(time, span, n, sharing)) for span in spans]
     own = [exchange(packed[0])]
-    packed[1][n // 2 :], own[0][-1] = gated(packed[1][n // 2 :], own[0][-1])
+    space = space_grads(*space_in)
+    packed[1][2:], own[0][2], space = gated(packed[1][2:], own[0][2], space)
     own.append(exchange(packed[1]))
-    space = space_grads(*space_in)
     beside = [
         [neighbours(ends, start) for ends, start in zip(sides(blocks), (1, 0))] for blocks in own
     ]

time: 64.1 us -> 59.5 us (0.928)
  starting transfers between devices: 27.8 us -> 24 us
  waiting for transfers between devices: 20.8 us -> 20.1 us
    ppermute x16, starting transfers between devices: 27.8 us -> 24 us  [swap(): lax.ppermute(block, axis, [(i, j) for i, j in pairs] + [(j, i) for i, j i...]
    ppermute x16, waiting for transfers between devices: 20.8 us -> 20.1 us  [swap(): lax.ppermute(block, axis, [(i, j) for i, j in pairs] + [(j, i) for i, j i...]
  transfers between devices with their start and end apart: 16 -> 16, of which waited for: 5 -> 5; matrix products, arithmetic and copies ran while one was open for 0% -> 0% of each run, Pallas kernels for 18% -> 19%
where the time goes in v10:
time: 59.5 us; the launch traced here: 59.1 us
  starting transfers between devices  24 us (40%)
  waiting for transfers between devices  20.1 us (34%)
  Pallas kernels  14 us (24%)
  between operations  0.75 us (1%)
    ppermute x16, starting transfers between devices, swap(): lax.ppermute(block, axis, [(i, j) for i, j in pairs] + [(j, i) for i, j i...  24 us
    ppermute x16, waiting for transfers between devices, swap(): lax.ppermute(block, axis, [(i, j) for i, j in pairs] + [(j, i) for i, j i...  20.1 us
    pallas_call x1, Pallas kernels, space_grads(): pl.pallas_call(frame_kernel, out_shape=(shape, shape, shape), compiler_pa...  5.58 us
    pallas_call x2, Pallas kernels, split(): pl.pallas_call(functools.partial(split_kernel, sharing, rows, span), in_s...  3.77 us
    pallas_call x2, Pallas kernels, clip_grads(): pl.pallas_call(functools.partial(clip_kernel, window, heads), out_shape=[...  2.65 us
    pallas_call x2, Pallas kernels, join(): pl.pallas_call(functools.partial(join_kernel, sharing, span), in_specs=[p...  1.71 us
  transfers between devices with their start and end apart: 16, of which 5 were waited for; matrix products, arithmetic and copies ran while one was open for 0% of the time, Pallas kernels for 19%

profile of v10, /device:TPU:0, one launch (start us, length us, event | category | flops | bytes accessed | tf_op | source)
XLA Modules:
  0.0 59.1 jit_solution(12446006956414229472)
XLA Ops:
  0.6 1.9 %pack.3 = (bf16[4,144,128]{2,1,0:T(8,128)(2,1)}, bf16[4,144,128]{2,1,0:T(8,128)(2,1)}, bf16[4,144,128]{2,1,0:T(8,128)(2,1)}, bf16[4,144,128]{2,1,0:T(8,128)(2,1)}) custom-call(bf16[1,576,256]{2,1,0:T(8,128)(2,1)} %bitcast.18, bf16[1,576,256]{2,1,0:T(8,128)(2,1)} %bitcast.20, bf16[1,576,256]{2,1,0:T(8,128)(2,1)} %bitcast.22, bf16[1,576,256]{2,1,0:T(8,128)(2,1)} %bitcast.24), custom_call_target="tpu_custom_call" | custom-call | tf_op jit(solution)/shard_map/pack/pallas_call | solution.py:97
  2.5 4.1 %collective-permute-start = (bf16[4,144,128]{2,1,0:T(8,128)(2,1)}, bf16[4,144,128]{2,1,0:T(8,128)(2,1)S(1)}, u32[]{:S(2)}, u32[]{:S(2)}) collective-permute-start(bf16[4,144,128]{2,1,0:T(8,128)(2,1)} %get-tuple-element.43), channel_id=1, source_target_pairs={{0,2},{1,3},{2,0},{3,1},{4,6},{5,7},{6,4},{7,5},{8,10},{9,11},{10,... | collective-permute-start | bytes 442376 | tf_op jit(solution)/shard_map/ppermute | solution.py:117
  6.6 1.6 %collective-permute-start.9 = (bf16[4,144,128]{2,1,0:T(8,128)(2,1)}, bf16[4,144,128]{2,1,0:T(8,128)(2,1)S(1)}, u32[]{:S(2)}, u32[]{:S(2)}) collective-permute-start(bf16[4,144,128]{2,1,0:T(8,128)(2,1)} %get-tuple-element.61), channel_id=1, source_target_pairs={{0,1},{2,3},{1,0},{3,2},{4,5},{6,7},{5,4},{7,6},{8,9},{10,11},{9,8... | collective-permute-start | bytes 442376 | tf_op jit(solution)/shard_map/ppermute | solution.py:117
  8.2 0.0 collective-permute-start.10
  8.2 1.9 %pack.2 = (bf16[4,144,128]{2,1,0:T(8,128)(2,1)}, bf16[4,144,128]{2,1,0:T(8,128)(2,1)}, bf16[4,144,128]{2,1,0:T(8,128)(2,1)}, bf16[4,144,128]{2,1,0:T(8,128)(2,1)}) custom-call(bf16[1,576,256]{2,1,0:T(8,128)(2,1)} %bitcast.19, bf16[1,576,256]{2,1,0:T(8,128)(2,1)} %bitcast.21, bf16[1,576,256]{2,1,0:T(8,128)(2,1)} %bitcast.23, bf16[1,576,256]{2,1,0:T(8,128)(2,1)} %bitcast.25), custom_call_target="tpu_custom_call" | custom-call | tf_op jit(solution)/shard_map/pack/pallas_call | solution.py:97
  10.1 1.0 %collective-permute-start.1 = (bf16[4,144,128]{2,1,0:T(8,128)(2,1)}, bf16[4,144,128]{2,1,0:T(8,128)(2,1)S(1)}, u32[]{:S(2)}, u32[]{:S(2)}) collective-permute-start(bf16[4,144,128]{2,1,0:T(8,128)(2,1)} %get-tuple-element.51), channel_id=1, source_target_pairs={{0,1},{2,3},{1,0},{3,2},{4,5},{6,7},{5,4},{7,6},{8,9},{10,11},{9,8... | collective-permute-start | bytes 442376 | tf_op jit(solution)/shard_map/ppermute | solution.py:117
  11.1 0.0 copy-start.4
  11.1 0.0 copy-start.3
  11.1 0.0 copy-start.2
  11.1 0.0 copy-start.1
  11.1 5.6 %space.1 = (bf16[1,576,256]{2,1,0:T(8,128)(2,1)}, bf16[1,576,256]{2,1,0:T(8,128)(2,1)}, bf16[1,576,256]{2,1,0:T(8,128)(2,1)}) custom-call(bf16[1,576,256]{2,1,0:T(8,128)(2,1)} %bitcast.29, bf16[1,576,256]{2,1,0:T(8,128)(2,1)} %bitcast.30, bf16[1,576,256]{2,1,0:T(8,128)(2,1)} %bitcast.31, bf16[1,576,256]{2,1,0:T(8,128)(2,1)} %bitcast.32), custom_call_target="tpu_custom_call" | custom-call | flops 1610612736 | bytes 2064384 | tf_op jit(solution)/shard_map/space/pallas_call | solution.py:58
  16.7 0.0 copy-done.4
  16.7 0.1 select_reduce_fusion.2
  16.7 0.0 collective-permute-done.refs_2_
  16.7 0.0 copy-done.3
  16.8 3.6 %collective-permute-start.2 = (bf16[4,144,128]{2,1,0:T(8,128)(2,1)S(1)}, bf16[4,144,128]{2,1,0:T(8,128)(2,1)S(1)}, u32[]{:S(2)}, u32[]{:S(2)}) collective-permute-start(bf16[4,144,128]{2,1,0:T(8,128)(2,1)S(1)} %copy-done.3), channel_id=1, source_target_pairs={{0,2},{1,3},{2,0},{3,1},{4,6},{5,7},{6,4},{7,5},{8,10},{9,11},{10,... | collective-permute-start | bytes 442376 | tf_op jit(solution)/shard_map/ppermute | solution.py:117
  20.3 0.0 copy-done.2
  20.3 0.0 collective-permute-start.3
  20.3 0.0 collective-permute-done.9.refs_1_
  20.3 0.0 collective-permute-done.10.refs_3_
  20.4 0.0 copy-done.1
  20.4 0.0 copy-start
  20.4 0.1 sides.3
  20.5 0.6 collective-permute-start.11
  21.1 1.3 %collective-permute-start.12 = (bf16[3,4,144,128]{3,2,1,0:T(8,128)(2,1)S(1)}, bf16[3,4,144,128]{3,2,1,0:T(8,128)(2,1)S(1)}, u32[]{:S(2)}, u32[]{:S(2)}) collective-permute-start(bf16[3,4,144,128]{3,2,1,0:T(8,128)(2,1)S(1)} %get-tuple-element.65), channel_id=1, source_target_pairs={{0,4},{8,12},{16,20},{24,28},{4,0},{12,8},{20,16},{28,24},{1,5},{9... | collective-permute-start | bytes 1327112 | tf_op jit(solution)/shard_map/ppermute | solution.py:117
  22.4 0.2 select_reduce_fusion.1
  22.6 0.0 collective-permute-done.1.refs_1_
  22.6 8.0 %collective-permute-done.2.refs_2_ = bf16[4,144,128]{2,1,0:T(8,128)(2,1)S(1)} collective-permute-done((bf16[4,144,128]{2,1,0:T(8,128)(2,1)S(1)}, bf16[4,144,128]{2,1,0:T(8,128)(2,1)S(1)}, u32[]{:S(2)}, u32[]{:S(2)}) %collective-permute-start.2) | collective-permute-done | bytes 147488 | tf_op jit(solution)/shard_map/ppermute | solution.py:117
  30.6 0.0 collective-permute-done.3.refs_3_
  30.6 0.0 copy-done
  30.6 0.1 sides.2
  30.7 0.5 collective-permute-start.4
  31.2 1.2 %collective-permute-start.5 = (bf16[3,4,144,128]{3,2,1,0:T(8,128)(2,1)S(1)}, bf16[3,4,144,128]{3,2,1,0:T(8,128)(2,1)S(1)}, u32[]{:S(2)}, u32[]{:S(2)}) collective-permute-start(bf16[3,4,144,128]{3,2,1,0:T(8,128)(2,1)S(1)} %get-tuple-element.55), channel_id=1, source_target_pairs={{0,4},{8,12},{16,20},{24,28},{4,0},{12,8},{20,16},{28,24},{1,5},{9... | collective-permute-start | bytes 1327112 | tf_op jit(solution)/shard_map/ppermute | solution.py:117
  32.4 1.2 %collective-permute-done.11.refs_4_ = bf16[3,4,144,128]{3,2,1,0:T(8,128)(2,1)S(1)} collective-permute-done((bf16[3,4,144,128]{3,2,1,0:T(8,128)(2,1)S(1)}, bf16[3,4,144,128]{3,2,1,0:T(8,128)(2,1)S(1)}, u32[]{:S(2)}, u32[]{:S(2)}) %collective-permute-start.11) | collective-permute-done | bytes 442400 | tf_op jit(solution)/shard_map/ppermute | solution.py:117
  33.6 0.0 collective-permute-done.12.refs_5_
  33.6 1.3 %clips.3 = (bf16[3,144,128]{2,1,0:T(8,128)(2,1)S(1)}, bf16[3,144,128]{2,1,0:T(8,128)(2,1)S(1)}, bf16[3,144,128]{2,1,0:T(8,128)(2,1)S(1)}, bf16[3,144,128]{2,1,0:T(8,128)(2,1)S(1)}) custom-call(s32[2,10]{1,0:T(2,128)S(1)} %pad_add_fusion.given_bounds, bf16[4,144,128]{2,1,0:T(8,128)(2,1)S(1)} %copy-done.1, ...), custom_call_target="tpu_custom_call" | custom-call | flops 589824000 | bytes 1474560 | tf_op jit(solution)/shard_map/clips/pallas_call | solution.py:289
  35.0 4.1 %collective-permute-start.13 = (bf16[3,144,128]{2,1,0:T(8,128)(2,1)S(1)}, bf16[3,144,128]{2,1,0:T(8,128)(2,1)S(1)}, u32[]{:S(2)}, u32[]{:S(2)}) collective-permute-start(bf16[3,144,128]{2,1,0:T(8,128)(2,1)S(1)} %get-tuple-element.66), channel_id=1, source_target_pairs={{0,3},{1,2},{3,0},{2,1},{4,7},{5,6},{7,4},{6,5},{8,11},{9,10},{11,... | collective-permute-start | bytes 331784 | tf_op jit(solution)/shard_map/ppermute | solution.py:117
  39.1 0.2 collective-permute-start.14
  39.2 0.5 collective-permute-start.15
  39.7 4.3 %collective-permute-done.4.refs_4_ = bf16[3,4,144,128]{3,2,1,0:T(8,128)(2,1)S(1)} collective-permute-done((bf16[3,4,144,128]{3,2,1,0:T(8,128)(2,1)S(1)}, bf16[3,4,144,128]{3,2,1,0:T(8,128)(2,1)S(1)}, u32[]{:S(2)}, u32[]{:S(2)}) %collective-permute-start.4) | collective-permute-done | bytes 442400 | tf_op jit(solution)/shard_map/ppermute | solution.py:117
  44.0 0.0 collective-permute-done.5.refs_5_
  44.0 1.3 %clips.2 = (bf16[3,144,128]{2,1,0:T(8,128)(2,1)S(1)}, bf16[3,144,128]{2,1,0:T(8,128)(2,1)S(1)}, bf16[3,144,128]{2,1,0:T(8,128)(2,1)S(1)}, bf16[3,144,128]{2,1,0:T(8,128)(2,1)S(1)}) custom-call(s32[2,10]{1,0:T(2,128)S(1)} %pad_add_fusion.given_bounds, bf16[4,144,128]{2,1,0:T(8,128)(2,1)S(1)} %copy-done, ...), custom_call_target="tpu_custom_call" | custom-call | flops 589824000 | bytes 1474560 | tf_op jit(solution)/shard_map/clips/pallas_call | solution.py:289
  45.4 3.2 %collective-permute-start.6 = (bf16[3,144,128]{2,1,0:T(8,128)(2,1)S(1)}, bf16[3,144,128]{2,1,0:T(8,128)(2,1)S(1)}, u32[]{:S(2)}, u32[]{:S(2)}) collective-permute-start(bf16[3,144,128]{2,1,0:T(8,128)(2,1)S(1)} %get-tuple-element.56), channel_id=1, source_target_pairs={{0,3},{1,2},{3,0},{2,1},{4,7},{5,6},{7,4},{6,5},{8,11},{9,10},{11,... | collective-permute-start | bytes 331784 | tf_op jit(solution)/shard_map/ppermute | solution.py:117
  48.5 1.8 %collective-permute-start.7 = (bf16[3,144,128]{2,1,0:T(8,128)(2,1)S(1)}, bf16[3,144,128]{2,1,0:T(8,128)(2,1)S(1)}, u32[]{:S(2)}, u32[]{:S(2)}) collective-permute-start(bf16[3,144,128]{2,1,0:T(8,128)(2,1)S(1)} %get-tuple-element.57), channel_id=1, source_target_pairs={{0,2},{1,3},{2,0},{3,1},{4,6},{5,7},{6,4},{7,5},{8,10},{9,11},{10,... | collective-permute-start | bytes 331784 | tf_op jit(solution)/shard_map/ppermute | solution.py:117
  50.4 0.0 collective-permute-done.13.refs_0_
  50.4 0.5 collective-permute-start.8
  50.8 0.0 collective-permute-done.14.refs_1_
  50.9 0.0 collective-permute-done.15.refs_3_
  50.9 0.9 %unpack.2 = (bf16[1,576,256]{2,1,0:T(8,128)(2,1)}, bf16[1,576,256]{2,1,0:T(8,128)(2,1)}, bf16[1,576,256]{2,1,0:T(8,128)(2,1)}) custom-call(bf16[3,144,128]{2,1,0:T(8,128)(2,1)S(1)} %collective-permute-done.13.refs_0_, bf16[3,144,128]{2,1,0:T(8,128)(2,1)S(1)} %collective-permute-done.14.refs_1_, bf16[3,144,128]{2,1,0:T(8,128)(2,1)S(1)} %get-tuple-element.68.refs_2_, ...), custom_call_target="tpu_custom_call" | custom-call | tf_op jit(solution)/shard_map/unpack/pallas_call | solution.py:185
  51.7 0.4 collective-permute-done.6.refs_0_
  52.2 6.1 %collective-permute-done.7.refs_1_ = bf16[3,144,128]{2,1,0:T(8,128)(2,1)S(1)} collective-permute-done((bf16[3,144,128]{2,1,0:T(8,128)(2,1)S(1)}, bf16[3,144,128]{2,1,0:T(8,128)(2,1)S(1)}, u32[]{:S(2)}, u32[]{:S(2)}) %collective-permute-start.7) | collective-permute-done | bytes 110624 | tf_op jit(solution)/shard_map/ppermute | solution.py:117
  58.3 0.0 collective-permute-done.8.refs_3_
  58.3 0.9 %unpack.3 = (bf16[1,576,256]{2,1,0:T(8,128)(2,1)}, bf16[1,576,256]{2,1,0:T(8,128)(2,1)}, bf16[1,576,256]{2,1,0:T(8,128)(2,1)}) custom-call(bf16[3,144,128]{2,1,0:T(8,128)(2,1)S(1)} %collective-permute-done.6.refs_0_, bf16[3,144,128]{2,1,0:T(8,128)(2,1)S(1)} %collective-permute-done.7.refs_1_, ...), custom_call_target="tpu_custom_call", output_to_operand_aliasing={{0}: (4, {}), {1}: (5, {}), {2}: (6, {})} | custom-call | tf_op jit(solution)/shard_map/unpack/pallas_call | solution.py:185
  (4 shorter events, 0.0 us)
Async XLA Ops:
  2.5 14.2 %collective-permute-start = (bf16[4,144,128]{2,1,0:T(8,128)(2,1)}, bf16[4,144,128]{2,1,0:T(8,128)(2,1)S(1)}, u32[]{:S(2)}, u32[]{:S(2)}) collective-permute-start(bf16[4,144,128]{2,1,0:T(8,128)(2,1)} %get-tuple-element.43), channel_id=1, source_target_pairs={{0,2},{1,3},{2,0},{3,1},{4,6},{5,7},{6,4},{7,5},{8,10},{9,11},{10,... | collective-permute-start | bytes 442376 | tf_op jit(solution)/shard_map/ppermute | solution.py:117
  6.6 13.7 %collective-permute-start.9 = (bf16[4,144,128]{2,1,0:T(8,128)(2,1)}, bf16[4,144,128]{2,1,0:T(8,128)(2,1)S(1)}, u32[]{:S(2)}, u32[]{:S(2)}) collective-permute-start(bf16[4,144,128]{2,1,0:T(8,128)(2,1)} %get-tuple-element.61), channel_id=1, source_target_pairs={{0,1},{2,3},{1,0},{3,2},{4,5},{6,7},{5,4},{7,6},{8,9},{10,11},{9,8... | collective-permute-start | bytes 442376 | tf_op jit(solution)/shard_map/ppermute | solution.py:117
  8.2 12.1 %collective-permute-start.10 = (bf16[4,144,128]{2,1,0:T(8,128)(2,1)}, bf16[4,144,128]{2,1,0:T(8,128)(2,1)S(1)}, u32[]{:S(2)}, u32[]{:S(2)}) collective-permute-start(bf16[4,144,128]{2,1,0:T(8,128)(2,1)} %get-tuple-element.63), channel_id=1, source_target_pairs={{0,3},{1,2},{3,0},{2,1},{4,7},{5,6},{7,4},{6,5},{8,11},{9,10},{11,... | collective-permute-start | bytes 442376 | tf_op jit(solution)/shard_map/ppermute | solution.py:117
  10.1 12.5 %collective-permute-start.1 = (bf16[4,144,128]{2,1,0:T(8,128)(2,1)}, bf16[4,144,128]{2,1,0:T(8,128)(2,1)S(1)}, u32[]{:S(2)}, u32[]{:S(2)}) collective-permute-start(bf16[4,144,128]{2,1,0:T(8,128)(2,1)} %get-tuple-element.51), channel_id=1, source_target_pairs={{0,1},{2,3},{1,0},{3,2},{4,5},{6,7},{5,4},{7,6},{8,9},{10,11},{9,8... | collective-permute-start | bytes 442376 | tf_op jit(solution)/shard_map/ppermute | solution.py:117
  11.1 5.6 %copy-start.4 = (s32[16]{0:T(128)S(1)}, s32[16]{0:T(128)}, u32[]{:S(2)}) copy-start(s32[16]{0:T(128)} %param.17) | copy-start | bytes 196
  11.1 5.7 %copy-start.3 = (bf16[4,144,128]{2,1,0:T(8,128)(2,1)S(1)}, bf16[4,144,128]{2,1,0:T(8,128)(2,1)}, u32[]{:S(2)}) copy-start(bf16[4,144,128]{2,1,0:T(8,128)(2,1)} %get-tuple-element.52) | copy-start | bytes 442372
  11.1 9.2 %copy-start.2 = (bf16[4,144,128]{2,1,0:T(8,128)(2,1)S(1)}, bf16[4,144,128]{2,1,0:T(8,128)(2,1)}, u32[]{:S(2)}) copy-start(bf16[4,144,128]{2,1,0:T(8,128)(2,1)} %get-tuple-element.53) | copy-start | bytes 442372
  11.1 9.3 %copy-start.1 = (bf16[4,144,128]{2,1,0:T(8,128)(2,1)S(1)}, bf16[4,144,128]{2,1,0:T(8,128)(2,1)}, u32[]{:S(2)}) copy-start(bf16[4,144,128]{2,1,0:T(8,128)(2,1)} %get-tuple-element.60.refs_0_) | copy-start | bytes 442372
  16.8 13.8 %collective-permute-start.2 = (bf16[4,144,128]{2,1,0:T(8,128)(2,1)S(1)}, bf16[4,144,128]{2,1,0:T(8,128)(2,1)S(1)}, u32[]{:S(2)}, u32[]{:S(2)}) collective-permute-start(bf16[4,144,128]{2,1,0:T(8,128)(2,1)S(1)} %copy-done.3), channel_id=1, source_target_pairs={{0,2},{1,3},{2,0},{3,1},{4,6},{5,7},{6,4},{7,5},{8,10},{9,11},{10,... | collective-permute-start | bytes 442376 | tf_op jit(solution)/shard_map/ppermute | solution.py:117
  20.3 10.3 %collective-permute-start.3 = (bf16[4,144,128]{2,1,0:T(8,128)(2,1)S(1)}, bf16[4,144,128]{2,1,0:T(8,128)(2,1)S(1)}, u32[]{:S(2)}, u32[]{:S(2)}) collective-permute-start(bf16[4,144,128]{2,1,0:T(8,128)(2,1)S(1)} %copy-done.2), channel_id=1, source_target_pairs={{0,3},{1,2},{3,0},{2,1},{4,7},{5,6},{7,4},{6,5},{8,11},{9,10},{11,... | collective-permute-start | bytes 442376 | tf_op jit(solution)/shard_map/ppermute | solution.py:117
  20.4 10.2 %copy-start = (bf16[4,144,128]{2,1,0:T(8,128)(2,1)S(1)}, bf16[4,144,128]{2,1,0:T(8,128)(2,1)}, u32[]{:S(2)}) copy-start(bf16[4,144,128]{2,1,0:T(8,128)(2,1)} %get-tuple-element.50.refs_0_) | copy-start | bytes 442372
  20.5 13.1 %collective-permute-start.11 = (bf16[3,4,144,128]{3,2,1,0:T(8,128)(2,1)S(1)}, bf16[3,4,144,128]{3,2,1,0:T(8,128)(2,1)S(1)}, u32[]{:S(2)}, u32[]{:S(2)}) collective-permute-start(bf16[3,4,144,128]{3,2,1,0:T(8,128)(2,1)S(1)} %get-tuple-element.64), channel_id=1, source_target_pairs={{4,8},{12,16},{20,24},{28,0},{8,4},{16,12},{24,20},{0,28},{5,9},{1... | collective-permute-start | bytes 1327112 | tf_op jit(solution)/shard_map/ppermute | solution.py:117
  21.1 12.6 %collective-permute-start.12 = (bf16[3,4,144,128]{3,2,1,0:T(8,128)(2,1)S(1)}, bf16[3,4,144,128]{3,2,1,0:T(8,128)(2,1)S(1)}, u32[]{:S(2)}, u32[]{:S(2)}) collective-permute-start(bf16[3,4,144,128]{3,2,1,0:T(8,128)(2,1)S(1)} %get-tuple-element.65), channel_id=1, source_target_pairs={{0,4},{8,12},{16,20},{24,28},{4,0},{12,8},{20,16},{28,24},{1,5},{9... | collective-permute-start | bytes 1327112 | tf_op jit(solution)/shard_map/ppermute | solution.py:117
  30.7 13.3 %collective-permute-start.4 = (bf16[3,4,144,128]{3,2,1,0:T(8,128)(2,1)S(1)}, bf16[3,4,144,128]{3,2,1,0:T(8,128)(2,1)S(1)}, u32[]{:S(2)}, u32[]{:S(2)}) collective-permute-start(bf16[3,4,144,128]{3,2,1,0:T(8,128)(2,1)S(1)} %get-tuple-element.54), channel_id=1, source_target_pairs={{4,8},{12,16},{20,24},{28,0},{8,4},{16,12},{24,20},{0,28},{5,9},{1... | collective-permute-start | bytes 1327112 | tf_op jit(solution)/shard_map/ppermute | solution.py:117
  31.2 12.8 %collective-permute-start.5 = (bf16[3,4,144,128]{3,2,1,0:T(8,128)(2,1)S(1)}, bf16[3,4,144,128]{3,2,1,0:T(8,128)(2,1)S(1)}, u32[]{:S(2)}, u32[]{:S(2)}) collective-permute-start(bf16[3,4,144,128]{3,2,1,0:T(8,128)(2,1)S(1)} %get-tuple-element.55), channel_id=1, source_target_pairs={{0,4},{8,12},{16,20},{24,28},{4,0},{12,8},{20,16},{28,24},{1,5},{9... | collective-permute-start | bytes 1327112 | tf_op jit(solution)/shard_map/ppermute | solution.py:117
  35.0 15.4 %collective-permute-start.13 = (bf16[3,144,128]{2,1,0:T(8,128)(2,1)S(1)}, bf16[3,144,128]{2,1,0:T(8,128)(2,1)S(1)}, u32[]{:S(2)}, u32[]{:S(2)}) collective-permute-start(bf16[3,144,128]{2,1,0:T(8,128)(2,1)S(1)} %get-tuple-element.66), channel_id=1, source_target_pairs={{0,3},{1,2},{3,0},{2,1},{4,7},{5,6},{7,4},{6,5},{8,11},{9,10},{11,... | collective-permute-start | bytes 331784 | tf_op jit(solution)/shard_map/ppermute | solution.py:117
  39.1 11.8 %collective-permute-start.14 = (bf16[3,144,128]{2,1,0:T(8,128)(2,1)S(1)}, bf16[3,144,128]{2,1,0:T(8,128)(2,1)S(1)}, u32[]{:S(2)}, u32[]{:S(2)}) collective-permute-start(bf16[3,144,128]{2,1,0:T(8,128)(2,1)S(1)} %get-tuple-element.67), channel_id=1, source_target_pairs={{0,2},{1,3},{2,0},{3,1},{4,6},{5,7},{6,4},{7,5},{8,10},{9,11},{10,... | collective-permute-start | bytes 331784 | tf_op jit(solution)/shard_map/ppermute | solution.py:117
  39.2 11.6 %collective-permute-start.15 = (bf16[3,144,128]{2,1,0:T(8,128)(2,1)S(1)}, bf16[3,144,128]{2,1,0:T(8,128)(2,1)S(1)}, u32[]{:S(2)}, u32[]{:S(2)}) collective-permute-start(bf16[3,144,128]{2,1,0:T(8,128)(2,1)S(1)} %get-tuple-element.69), channel_id=1, source_target_pairs={{0,1},{2,3},{1,0},{3,2},{4,5},{6,7},{5,4},{7,6},{8,9},{10,11},{9,8... | collective-permute-start | bytes 331784 | tf_op jit(solution)/shard_map/ppermute | solution.py:117
  45.4 6.8 %collective-permute-start.6 = (bf16[3,144,128]{2,1,0:T(8,128)(2,1)S(1)}, bf16[3,144,128]{2,1,0:T(8,128)(2,1)S(1)}, u32[]{:S(2)}, u32[]{:S(2)}) collective-permute-start(bf16[3,144,128]{2,1,0:T(8,128)(2,1)S(1)} %get-tuple-element.56), channel_id=1, source_target_pairs={{0,3},{1,2},{3,0},{2,1},{4,7},{5,6},{7,4},{6,5},{8,11},{9,10},{11,... | collective-permute-start | bytes 331784 | tf_op jit(solution)/shard_map/ppermute | solution.py:117
  48.5 9.7 %collective-permute-start.7 = (bf16[3,144,128]{2,1,0:T(8,128)(2,1)S(1)}, bf16[3,144,128]{2,1,0:T(8,128)(2,1)S(1)}, u32[]{:S(2)}, u32[]{:S(2)}) collective-permute-start(bf16[3,144,128]{2,1,0:T(8,128)(2,1)S(1)} %get-tuple-element.57), channel_id=1, source_target_pairs={{0,2},{1,3},{2,0},{3,1},{4,6},{5,7},{6,4},{7,5},{8,10},{9,11},{10,... | collective-permute-start | bytes 331784 | tf_op jit(solution)/shard_map/ppermute | solution.py:117
  50.4 7.9 %collective-permute-start.8 = (bf16[3,144,128]{2,1,0:T(8,128)(2,1)S(1)}, bf16[3,144,128]{2,1,0:T(8,128)(2,1)S(1)}, u32[]{:S(2)}, u32[]{:S(2)}) collective-permute-start(bf16[3,144,128]{2,1,0:T(8,128)(2,1)S(1)} %get-tuple-element.59), channel_id=1, source_target_pairs={{0,1},{2,3},{1,0},{3,2},{4,5},{6,7},{5,4},{7,6},{8,9},{10,11},{9,8... | collective-permute-start | bytes 331784 | tf_op jit(solution)/shard_map/ppermute | solution.py:117

commit v11 on v10

--- a/solution.py
+++ b/solution.py
@@ -113,6 +113,10 @@
     return [*reversed(range(n // 2, n)), *range(n // 2)]
 
 
+def listed(n):
+    return [*range(n // 2, n), *range(n // 2)]
+
+
 def swap(block, axis, pairs):
     return lax.ppermute(block, axis, [(i, j) for i, j in pairs] + [(j, i) for i, j in pairs])
 
@@ -208,7 +212,7 @@
         for i in range(4):
             wide[i, frame] = ref[i].astype(jnp.float32)
 
-    for step, ref in enumerate(own):
+    for step, ref in zip(listed(window), own):
         widen(ref, halo + (lax.axis_index("seq") ^ step))
     for start, ref in zip((1, 0), sides_of):
         is_next = (lax.axis_index("grp") & 1) == start
@@ -307,7 +311,7 @@
             transcendentals=extent * window * heads * lanes,
         ),
         name="clips",
-    )(bounds, *own, *beside)
+    )(bounds, *(own[step] for step in listed(window)), *beside)
 
 
 def clip_bounds(clip_len, window):
@@ -343,7 +347,7 @@
     packed = [list(split(time, span, n, sharing)) for span in spans]
     own = [exchange(packed[0])]
     space = space_grads(*space_in)
-    packed[1][2:], own[0][2], space = gated(packed[1][2:], own[0][2], space)
+    packed[1][1:], own[0][2], space = gated(packed[1][1:], own[0][2], space)
     own.append(exchange(packed[1]))
     beside = [
         [neighbours(ends, start) for ends, start in zip(sides(blocks), (1, 0))] for blocks in own

time: 59.5 us -> 61.7 us (1.037)
  starting transfers between devices: 24 us -> 29.5 us
  waiting for transfers between devices: 20.1 us -> 16.5 us
    ppermute x16, starting transfers between devices: 24 us -> 29.5 us  [swap(): lax.ppermute(block, axis, [(i, j) for i, j in pairs] + [(j, i) for i, j i...]
    ppermute x16, waiting for transfers between devices: 20.1 us -> 16.5 us  [swap(): lax.ppermute(block, axis, [(i, j) for i, j in pairs] + [(j, i) for i, j i...]
  transfers between devices with their start and end apart: 16 -> 16, of which waited for: 5 -> 4; matrix products, arithmetic and copies ran while one was open for 0% -> 0% of each run, Pallas kernels for 19% -> 19%
where the time goes in v11:
time: 61.7 us; the launch traced here: 61.5 us
  starting transfers between devices  29.5 us (48%)
  waiting for transfers between devices  16.5 us (27%)
  Pallas kernels  14.4 us (23%)
  between operations  0.76 us (1%)
    ppermute x16, starting transfers between devices, swap(): lax.ppermute(block, axis, [(i, j) for i, j in pairs] + [(j, i) for i, j i...  29.5 us
    ppermute x16, waiting for transfers between devices, swap(): lax.ppermute(block, axis, [(i, j) for i, j in pairs] + [(j, i) for i, j i...  16.5 us
    pallas_call x1, Pallas kernels, space_grads(): pl.pallas_call(frame_kernel, out_shape=(shape, shape, shape), compiler_pa...  5.54 us
    pallas_call x2, Pallas kernels, split(): pl.pallas_call(functools.partial(split_kernel, sharing, rows, span), in_s...  3.81 us
    pallas_call x2, Pallas kernels, clip_grads(): pl.pallas_call(functools.partial(clip_kernel, window, heads), out_shape=[...  3.08 us
    pallas_call x2, Pallas kernels, join(): pl.pallas_call(functools.partial(join_kernel, sharing, span), in_specs=[p...  1.71 us
  transfers between devices with their start and end apart: 16, of which 4 were waited for; matrix products, arithmetic and copies ran while one was open for 0% of the time, Pallas kernels for 19%

profile of v11, /device:TPU:0, one launch (start us, length us, event | category | flops | bytes accessed | tf_op | source)
XLA Modules:
  0.0 61.5 jit_solution(7324575581987203758)
XLA Ops:
  0.6 1.9 %pack.3 = (bf16[4,144,128]{2,1,0:T(8,128)(2,1)}, bf16[4,144,128]{2,1,0:T(8,128)(2,1)}, bf16[4,144,128]{2,1,0:T(8,128)(2,1)}, bf16[4,144,128]{2,1,0:T(8,128)(2,1)}) custom-call(bf16[1,576,256]{2,1,0:T(8,128)(2,1)} %bitcast.18, bf16[1,576,256]{2,1,0:T(8,128)(2,1)} %bitcast.20, bf16[1,576,256]{2,1,0:T(8,128)(2,1)} %bitcast.22, bf16[1,576,256]{2,1,0:T(8,128)(2,1)} %bitcast.24), custom_call_target="tpu_custom_call" | custom-call | tf_op jit(solution)/shard_map/pack/pallas_call | solution.py:97
  2.5 4.1 %collective-permute-start = (bf16[4,144,128]{2,1,0:T(8,128)(2,1)}, bf16[4,144,128]{2,1,0:T(8,128)(2,1)S(1)}, u32[]{:S(2)}, u32[]{:S(2)}) collective-permute-start(bf16[4,144,128]{2,1,0:T(8,128)(2,1)} %get-tuple-element.45), channel_id=1, source_target_pairs={{0,2},{1,3},{2,0},{3,1},{4,6},{5,7},{6,4},{7,5},{8,10},{9,11},{10,... | collective-permute-start | bytes 442376 | tf_op jit(solution)/shard_map/ppermute | solution.py:121
  6.6 1.3 %collective-permute-start.9 = (bf16[4,144,128]{2,1,0:T(8,128)(2,1)}, bf16[4,144,128]{2,1,0:T(8,128)(2,1)S(1)}, u32[]{:S(2)}, u32[]{:S(2)}) collective-permute-start(bf16[4,144,128]{2,1,0:T(8,128)(2,1)} %get-tuple-element.63), channel_id=1, source_target_pairs={{0,3},{1,2},{3,0},{2,1},{4,7},{5,6},{7,4},{6,5},{8,11},{9,10},{11,... | collective-permute-start | bytes 442376 | tf_op jit(solution)/shard_map/ppermute | solution.py:121
  8.0 0.2 collective-permute-start.10
  8.2 0.0 copy-start.2
  8.2 5.5 %space.1 = (bf16[1,576,256]{2,1,0:T(8,128)(2,1)}, bf16[1,576,256]{2,1,0:T(8,128)(2,1)}, bf16[1,576,256]{2,1,0:T(8,128)(2,1)}) custom-call(bf16[1,576,256]{2,1,0:T(8,128)(2,1)} %bitcast.29, bf16[1,576,256]{2,1,0:T(8,128)(2,1)} %bitcast.30, bf16[1,576,256]{2,1,0:T(8,128)(2,1)} %bitcast.31, bf16[1,576,256]{2,1,0:T(8,128)(2,1)} %bitcast.32), custom_call_target="tpu_custom_call" | custom-call | flops 1610612736 | bytes 2064384 | tf_op jit(solution)/shard_map/space/pallas_call | solution.py:58
  13.8 0.0 copy-done.2
  13.8 0.1 select_reduce_fusion.2
  13.8 0.0 copy-start.1
  13.8 1.9 %pack.2 = (bf16[4,144,128]{2,1,0:T(8,128)(2,1)}, bf16[4,144,128]{2,1,0:T(8,128)(2,1)}, bf16[4,144,128]{2,1,0:T(8,128)(2,1)}, bf16[4,144,128]{2,1,0:T(8,128)(2,1)}) custom-call(bf16[1,576,256]{2,1,0:T(8,128)(2,1)} %bitcast.19, bf16[1,576,256]{2,1,0:T(8,128)(2,1)} %bitcast.21, bf16[1,576,256]{2,1,0:T(8,128)(2,1)} %bitcast.23, bf16[1,576,256]{2,1,0:T(8,128)(2,1)} %bitcast.25), custom_call_target="tpu_custom_call" | custom-call | tf_op jit(solution)/shard_map/pack/pallas_call | solution.py:97
  15.8 2.1 %collective-permute-done.refs_2_.refs_0_ = bf16[4,144,128]{2,1,0:T(8,128)(2,1)S(1)} collective-permute-done((bf16[4,144,128]{2,1,0:T(8,128)(2,1)}, bf16[4,144,128]{2,1,0:T(8,128)(2,1)S(1)}, u32[]{:S(2)}, u32[]{:S(2)}) %collective-permute-start) | collective-permute-done | bytes 147488 | tf_op jit(solution)/shard_map/ppermute | solution.py:121
  17.9 0.8 %collective-permute-start.1 = (bf16[4,144,128]{2,1,0:T(8,128)(2,1)}, bf16[4,144,128]{2,1,0:T(8,128)(2,1)S(1)}, u32[]{:S(2)}, u32[]{:S(2)}) collective-permute-start(bf16[4,144,128]{2,1,0:T(8,128)(2,1)} %get-tuple-element.52), channel_id=1, source_target_pairs={{0,2},{1,3},{2,0},{3,1},{4,6},{5,7},{6,4},{7,5},{8,10},{9,11},{10,... | collective-permute-start | bytes 442376 | tf_op jit(solution)/shard_map/ppermute | solution.py:121
  18.7 2.0 %collective-permute-start.2 = (bf16[4,144,128]{2,1,0:T(8,128)(2,1)}, bf16[4,144,128]{2,1,0:T(8,128)(2,1)S(1)}, u32[]{:S(2)}, u32[]{:S(2)}) collective-permute-start(bf16[4,144,128]{2,1,0:T(8,128)(2,1)} %get-tuple-element.53), channel_id=1, source_target_pairs={{0,3},{1,2},{3,0},{2,1},{4,7},{5,6},{7,4},{6,5},{8,11},{9,10},{11,... | collective-permute-start | bytes 442376 | tf_op jit(solution)/shard_map/ppermute | solution.py:121
  20.7 0.7 %collective-permute-start.3 = (bf16[4,144,128]{2,1,0:T(8,128)(2,1)}, bf16[4,144,128]{2,1,0:T(8,128)(2,1)S(1)}, u32[]{:S(2)}, u32[]{:S(2)}) collective-permute-start(bf16[4,144,128]{2,1,0:T(8,128)(2,1)} %get-tuple-element.55), channel_id=1, source_target_pairs={{0,1},{2,3},{1,0},{3,2},{4,5},{6,7},{5,4},{7,6},{8,9},{10,11},{9,8... | collective-permute-start | bytes 442376 | tf_op jit(solution)/shard_map/ppermute | solution.py:121
  21.4 0.0 collective-permute-done.9.refs_3_.refs_1_
  21.4 0.0 collective-permute-done.10.refs_1_.refs_3_
  21.4 0.0 copy-done.1
  21.4 0.0 copy-start
  21.4 0.1 sides.3
  21.6 1.4 %collective-permute-start.11 = (bf16[3,4,144,128]{3,2,1,0:T(8,128)(2,1)S(1)}, bf16[3,4,144,128]{3,2,1,0:T(8,128)(2,1)S(1)}, u32[]{:S(2)}, u32[]{:S(2)}) collective-permute-start(bf16[3,4,144,128]{3,2,1,0:T(8,128)(2,1)S(1)} %get-tuple-element.66), channel_id=1, source_target_pairs={{4,8},{12,16},{20,24},{28,0},{8,4},{16,12},{24,20},{0,28},{5,9},{1... | collective-permute-start | bytes 1327112 | tf_op jit(solution)/shard_map/ppermute | solution.py:121
  22.9 0.7 %collective-permute-start.12 = (bf16[3,4,144,128]{3,2,1,0:T(8,128)(2,1)S(1)}, bf16[3,4,144,128]{3,2,1,0:T(8,128)(2,1)S(1)}, u32[]{:S(2)}, u32[]{:S(2)}) collective-permute-start(bf16[3,4,144,128]{3,2,1,0:T(8,128)(2,1)S(1)} %get-tuple-element.67), channel_id=1, source_target_pairs={{0,4},{8,12},{16,20},{24,28},{4,0},{12,8},{20,16},{28,24},{1,5},{9... | collective-permute-start | bytes 1327112 | tf_op jit(solution)/shard_map/ppermute | solution.py:121
  23.6 0.2 select_reduce_fusion.1
  23.8 7.5 %collective-permute-done.1.refs_2_.refs_0_ = bf16[4,144,128]{2,1,0:T(8,128)(2,1)S(1)} collective-permute-done((bf16[4,144,128]{2,1,0:T(8,128)(2,1)}, bf16[4,144,128]{2,1,0:T(8,128)(2,1)S(1)}, u32[]{:S(2)}, u32[]{:S(2)}) %collective-permute-start.1) | collective-permute-done | bytes 147488 | tf_op jit(solution)/shard_map/ppermute | solution.py:121
  31.3 0.0 collective-permute-done.2.refs_3_.refs_1_
  31.3 0.0 collective-permute-done.3.refs_1_.refs_3_
  31.3 0.0 copy-done
  31.3 0.1 sides.2
  31.5 0.1 collective-permute-start.4
  31.6 1.6 %collective-permute-start.5 = (bf16[3,4,144,128]{3,2,1,0:T(8,128)(2,1)S(1)}, bf16[3,4,144,128]{3,2,1,0:T(8,128)(2,1)S(1)}, u32[]{:S(2)}, u32[]{:S(2)}) collective-permute-start(bf16[3,4,144,128]{3,2,1,0:T(8,128)(2,1)S(1)} %get-tuple-element.57), channel_id=1, source_target_pairs={{0,4},{8,12},{16,20},{24,28},{4,0},{12,8},{20,16},{28,24},{1,5},{9... | collective-permute-start | bytes 1327112 | tf_op jit(solution)/shard_map/ppermute | solution.py:121
  33.2 1.4 %collective-permute-done.11.refs_4_ = bf16[3,4,144,128]{3,2,1,0:T(8,128)(2,1)S(1)} collective-permute-done((bf16[3,4,144,128]{3,2,1,0:T(8,128)(2,1)S(1)}, bf16[3,4,144,128]{3,2,1,0:T(8,128)(2,1)S(1)}, u32[]{:S(2)}, u32[]{:S(2)}) %collective-permute-start.11) | collective-permute-done | bytes 442400 | tf_op jit(solution)/shard_map/ppermute | solution.py:121
  34.6 0.0 collective-permute-done.12.refs_5_
  34.6 1.5 %clips.3 = (bf16[3,144,128]{2,1,0:T(8,128)(2,1)S(1)}, bf16[3,144,128]{2,1,0:T(8,128)(2,1)S(1)}, bf16[3,144,128]{2,1,0:T(8,128)(2,1)S(1)}, bf16[3,144,128]{2,1,0:T(8,128)(2,1)S(1)}) custom-call(s32[2,10]{1,0:T(2,128)S(1)} %pad_add_fusion.given_bounds, bf16[4,144,128]{2,1,0:T(8,128)(2,1)S(1)} %collective-permute-done.refs_2_.refs_0_, ...), custom_call_target="tpu_custom_call" | custom-call | flops 589824000 | bytes 1474560 | tf_op jit(solution)/shard_map/clips/pallas_call | solution.py:293
  36.2 3.1 %collective-permute-start.13 = (bf16[3,144,128]{2,1,0:T(8,128)(2,1)S(1)}, bf16[3,144,128]{2,1,0:T(8,128)(2,1)S(1)}, u32[]{:S(2)}, u32[]{:S(2)}) collective-permute-start(bf16[3,144,128]{2,1,0:T(8,128)(2,1)S(1)} %get-tuple-element.68), channel_id=1, source_target_pairs={{0,3},{1,2},{3,0},{2,1},{4,7},{5,6},{7,4},{6,5},{8,11},{9,10},{11,... | collective-permute-start | bytes 331784 | tf_op jit(solution)/shard_map/ppermute | solution.py:121
  39.3 5.1 %collective-permute-start.14 = (bf16[3,144,128]{2,1,0:T(8,128)(2,1)S(1)}, bf16[3,144,128]{2,1,0:T(8,128)(2,1)S(1)}, u32[]{:S(2)}, u32[]{:S(2)}) collective-permute-start(bf16[3,144,128]{2,1,0:T(8,128)(2,1)S(1)} %get-tuple-element.69), channel_id=1, source_target_pairs={{0,2},{1,3},{2,0},{3,1},{4,6},{5,7},{6,4},{7,5},{8,10},{9,11},{10,... | collective-permute-start | bytes 331784 | tf_op jit(solution)/shard_map/ppermute | solution.py:121
  44.4 0.5 collective-permute-start.15
  44.9 0.0 collective-permute-done.4.refs_4_
  44.9 0.0 collective-permute-done.5.refs_5_
  44.9 1.5 %clips.2 = (bf16[3,144,128]{2,1,0:T(8,128)(2,1)S(1)}, bf16[3,144,128]{2,1,0:T(8,128)(2,1)S(1)}, bf16[3,144,128]{2,1,0:T(8,128)(2,1)S(1)}, bf16[3,144,128]{2,1,0:T(8,128)(2,1)S(1)}) custom-call(s32[2,10]{1,0:T(2,128)S(1)} %pad_add_fusion.given_bounds, bf16[4,144,128]{2,1,0:T(8,128)(2,1)S(1)} %collective-permute-done.1.refs_2_.refs_0_, ...), custom_call_target="tpu_custom_call" | custom-call | flops 589824000 | bytes 1474560 | tf_op jit(solution)/shard_map/clips/pallas_call | solution.py:293
  46.4 2.7 %collective-permute-start.6 = (bf16[3,144,128]{2,1,0:T(8,128)(2,1)S(1)}, bf16[3,144,128]{2,1,0:T(8,128)(2,1)S(1)}, u32[]{:S(2)}, u32[]{:S(2)}) collective-permute-start(bf16[3,144,128]{2,1,0:T(8,128)(2,1)S(1)} %get-tuple-element.58), channel_id=1, source_target_pairs={{0,3},{1,2},{3,0},{2,1},{4,7},{5,6},{7,4},{6,5},{8,11},{9,10},{11,... | collective-permute-start | bytes 331784 | tf_op jit(solution)/shard_map/ppermute | solution.py:121
  49.1 4.7 %collective-permute-start.7 = (bf16[3,144,128]{2,1,0:T(8,128)(2,1)S(1)}, bf16[3,144,128]{2,1,0:T(8,128)(2,1)S(1)}, u32[]{:S(2)}, u32[]{:S(2)}) collective-permute-start(bf16[3,144,128]{2,1,0:T(8,128)(2,1)S(1)} %get-tuple-element.59), channel_id=1, source_target_pairs={{0,2},{1,3},{2,0},{3,1},{4,6},{5,7},{6,4},{7,5},{8,10},{9,11},{10,... | collective-permute-start | bytes 331784 | tf_op jit(solution)/shard_map/ppermute | solution.py:121
  53.9 0.0 collective-permute-done.13.refs_0_
  53.9 0.5 collective-permute-start.8
  54.4 0.0 collective-permute-done.14.refs_1_
  54.4 0.0 collective-permute-done.15.refs_3_
  54.4 0.9 %unpack.2 = (bf16[1,576,256]{2,1,0:T(8,128)(2,1)}, bf16[1,576,256]{2,1,0:T(8,128)(2,1)}, bf16[1,576,256]{2,1,0:T(8,128)(2,1)}) custom-call(bf16[3,144,128]{2,1,0:T(8,128)(2,1)S(1)} %collective-permute-done.13.refs_0_, bf16[3,144,128]{2,1,0:T(8,128)(2,1)S(1)} %collective-permute-done.14.refs_1_, bf16[3,144,128]{2,1,0:T(8,128)(2,1)S(1)} %get-tuple-element.70.refs_2_, ...), custom_call_target="tpu_custom_call" | custom-call | tf_op jit(solution)/shard_map/unpack/pallas_call | solution.py:189
  55.2 0.0 collective-permute-done.6.refs_0_
  55.2 5.4 %collective-permute-done.7.refs_1_ = bf16[3,144,128]{2,1,0:T(8,128)(2,1)S(1)} collective-permute-done((bf16[3,144,128]{2,1,0:T(8,128)(2,1)S(1)}, bf16[3,144,128]{2,1,0:T(8,128)(2,1)S(1)}, u32[]{:S(2)}, u32[]{:S(2)}) %collective-permute-start.7) | collective-permute-done | bytes 110624 | tf_op jit(solution)/shard_map/ppermute | solution.py:121
  60.7 0.0 collective-permute-done.8.refs_3_
  60.7 0.9 %unpack.3 = (bf16[1,576,256]{2,1,0:T(8,128)(2,1)}, bf16[1,576,256]{2,1,0:T(8,128)(2,1)}, bf16[1,576,256]{2,1,0:T(8,128)(2,1)}) custom-call(bf16[3,144,128]{2,1,0:T(8,128)(2,1)S(1)} %collective-permute-done.6.refs_0_, bf16[3,144,128]{2,1,0:T(8,128)(2,1)S(1)} %collective-permute-done.7.refs_1_, ...), custom_call_target="tpu_custom_call", output_to_operand_aliasing={{0}: (4, {}), {1}: (5, {}), {2}: (6, {})} | custom-call | tf_op jit(solution)/shard_map/unpack/pallas_call | solution.py:189
  (4 shorter events, 0.0 us)
Async XLA Ops:
  2.5 15.4 %collective-permute-start = (bf16[4,144,128]{2,1,0:T(8,128)(2,1)}, bf16[4,144,128]{2,1,0:T(8,128)(2,1)S(1)}, u32[]{:S(2)}, u32[]{:S(2)}) collective-permute-start(bf16[4,144,128]{2,1,0:T(8,128)(2,1)} %get-tuple-element.45), channel_id=1, source_target_pairs={{0,2},{1,3},{2,0},{3,1},{4,6},{5,7},{6,4},{7,5},{8,10},{9,11},{10,... | collective-permute-start | bytes 442376 | tf_op jit(solution)/shard_map/ppermute | solution.py:121
  6.6 14.8 %collective-permute-start.9 = (bf16[4,144,128]{2,1,0:T(8,128)(2,1)}, bf16[4,144,128]{2,1,0:T(8,128)(2,1)S(1)}, u32[]{:S(2)}, u32[]{:S(2)}) collective-permute-start(bf16[4,144,128]{2,1,0:T(8,128)(2,1)} %get-tuple-element.63), channel_id=1, source_target_pairs={{0,3},{1,2},{3,0},{2,1},{4,7},{5,6},{7,4},{6,5},{8,11},{9,10},{11,... | collective-permute-start | bytes 442376 | tf_op jit(solution)/shard_map/ppermute | solution.py:121
  8.0 13.4 %collective-permute-start.10 = (bf16[4,144,128]{2,1,0:T(8,128)(2,1)}, bf16[4,144,128]{2,1,0:T(8,128)(2,1)S(1)}, u32[]{:S(2)}, u32[]{:S(2)}) collective-permute-start(bf16[4,144,128]{2,1,0:T(8,128)(2,1)} %get-tuple-element.65), channel_id=1, source_target_pairs={{0,1},{2,3},{1,0},{3,2},{4,5},{6,7},{5,4},{7,6},{8,9},{10,11},{9,8... | collective-permute-start | bytes 442376 | tf_op jit(solution)/shard_map/ppermute | solution.py:121
  8.2 5.5 %copy-start.2 = (s32[16]{0:T(128)S(1)}, s32[16]{0:T(128)}, u32[]{:S(2)}) copy-start(s32[16]{0:T(128)} %param.17) | copy-start | bytes 196
  13.8 7.6 %copy-start.1 = (bf16[4,144,128]{2,1,0:T(8,128)(2,1)S(1)}, bf16[4,144,128]{2,1,0:T(8,128)(2,1)}, u32[]{:S(2)}) copy-start(bf16[4,144,128]{2,1,0:T(8,128)(2,1)} %get-tuple-element.64.refs_0_.refs_2_) | copy-start | bytes 442372
  17.9 13.4 %collective-permute-start.1 = (bf16[4,144,128]{2,1,0:T(8,128)(2,1)}, bf16[4,144,128]{2,1,0:T(8,128)(2,1)S(1)}, u32[]{:S(2)}, u32[]{:S(2)}) collective-permute-start(bf16[4,144,128]{2,1,0:T(8,128)(2,1)} %get-tuple-element.52), channel_id=1, source_target_pairs={{0,2},{1,3},{2,0},{3,1},{4,6},{5,7},{6,4},{7,5},{8,10},{9,11},{10,... | collective-permute-start | bytes 442376 | tf_op jit(solution)/shard_map/ppermute | solution.py:121
  18.7 12.7 %collective-permute-start.2 = (bf16[4,144,128]{2,1,0:T(8,128)(2,1)}, bf16[4,144,128]{2,1,0:T(8,128)(2,1)S(1)}, u32[]{:S(2)}, u32[]{:S(2)}) collective-permute-start(bf16[4,144,128]{2,1,0:T(8,128)(2,1)} %get-tuple-element.53), channel_id=1, source_target_pairs={{0,3},{1,2},{3,0},{2,1},{4,7},{5,6},{7,4},{6,5},{8,11},{9,10},{11,... | collective-permute-start | bytes 442376 | tf_op jit(solution)/shard_map/ppermute | solution.py:121
  20.7 10.6 %collective-permute-start.3 = (bf16[4,144,128]{2,1,0:T(8,128)(2,1)}, bf16[4,144,128]{2,1,0:T(8,128)(2,1)S(1)}, u32[]{:S(2)}, u32[]{:S(2)}) collective-permute-start(bf16[4,144,128]{2,1,0:T(8,128)(2,1)} %get-tuple-element.55), channel_id=1, source_target_pairs={{0,1},{2,3},{1,0},{3,2},{4,5},{6,7},{5,4},{7,6},{8,9},{10,11},{9,8... | collective-permute-start | bytes 442376 | tf_op jit(solution)/shard_map/ppermute | solution.py:121
  21.4 9.9 %copy-start = (bf16[4,144,128]{2,1,0:T(8,128)(2,1)S(1)}, bf16[4,144,128]{2,1,0:T(8,128)(2,1)}, u32[]{:S(2)}) copy-start(bf16[4,144,128]{2,1,0:T(8,128)(2,1)} %get-tuple-element.54.refs_0_.refs_2_) | copy-start | bytes 442372
  21.6 13.1 %collective-permute-start.11 = (bf16[3,4,144,128]{3,2,1,0:T(8,128)(2,1)S(1)}, bf16[3,4,144,128]{3,2,1,0:T(8,128)(2,1)S(1)}, u32[]{:S(2)}, u32[]{:S(2)}) collective-permute-start(bf16[3,4,144,128]{3,2,1,0:T(8,128)(2,1)S(1)} %get-tuple-element.66), channel_id=1, source_target_pairs={{4,8},{12,16},{20,24},{28,0},{8,4},{16,12},{24,20},{0,28},{5,9},{1... | collective-permute-start | bytes 1327112 | tf_op jit(solution)/shard_map/ppermute | solution.py:121
  22.9 11.7 %collective-permute-start.12 = (bf16[3,4,144,128]{3,2,1,0:T(8,128)(2,1)S(1)}, bf16[3,4,144,128]{3,2,1,0:T(8,128)(2,1)S(1)}, u32[]{:S(2)}, u32[]{:S(2)}) collective-permute-start(bf16[3,4,144,128]{3,2,1,0:T(8,128)(2,1)S(1)} %get-tuple-element.67), channel_id=1, source_target_pairs={{0,4},{8,12},{16,20},{24,28},{4,0},{12,8},{20,16},{28,24},{1,5},{9... | collective-permute-start | bytes 1327112 | tf_op jit(solution)/shard_map/ppermute | solution.py:121
  31.5 13.4 %collective-permute-start.4 = (bf16[3,4,144,128]{3,2,1,0:T(8,128)(2,1)S(1)}, bf16[3,4,144,128]{3,2,1,0:T(8,128)(2,1)S(1)}, u32[]{:S(2)}, u32[]{:S(2)}) collective-permute-start(bf16[3,4,144,128]{3,2,1,0:T(8,128)(2,1)S(1)} %get-tuple-element.56), channel_id=1, source_target_pairs={{4,8},{12,16},{20,24},{28,0},{8,4},{16,12},{24,20},{0,28},{5,9},{1... | collective-permute-start | bytes 1327112 | tf_op jit(solution)/shard_map/ppermute | solution.py:121
  31.6 13.3 %collective-permute-start.5 = (bf16[3,4,144,128]{3,2,1,0:T(8,128)(2,1)S(1)}, bf16[3,4,144,128]{3,2,1,0:T(8,128)(2,1)S(1)}, u32[]{:S(2)}, u32[]{:S(2)}) collective-permute-start(bf16[3,4,144,128]{3,2,1,0:T(8,128)(2,1)S(1)} %get-tuple-element.57), channel_id=1, source_target_pairs={{0,4},{8,12},{16,20},{24,28},{4,0},{12,8},{20,16},{28,24},{1,5},{9... | collective-permute-start | bytes 1327112 | tf_op jit(solution)/shard_map/ppermute | solution.py:121
  36.2 17.7 %collective-permute-start.13 = (bf16[3,144,128]{2,1,0:T(8,128)(2,1)S(1)}, bf16[3,144,128]{2,1,0:T(8,128)(2,1)S(1)}, u32[]{:S(2)}, u32[]{:S(2)}) collective-permute-start(bf16[3,144,128]{2,1,0:T(8,128)(2,1)S(1)} %get-tuple-element.68), channel_id=1, source_target_pairs={{0,3},{1,2},{3,0},{2,1},{4,7},{5,6},{7,4},{6,5},{8,11},{9,10},{11,... | collective-permute-start | bytes 331784 | tf_op jit(solution)/shard_map/ppermute | solution.py:121
  39.3 15.1 %collective-permute-start.14 = (bf16[3,144,128]{2,1,0:T(8,128)(2,1)S(1)}, bf16[3,144,128]{2,1,0:T(8,128)(2,1)S(1)}, u32[]{:S(2)}, u32[]{:S(2)}) collective-permute-start(bf16[3,144,128]{2,1,0:T(8,128)(2,1)S(1)} %get-tuple-element.69), channel_id=1, source_target_pairs={{0,2},{1,3},{2,0},{3,1},{4,6},{5,7},{6,4},{7,5},{8,10},{9,11},{10,... | collective-permute-start | bytes 331784 | tf_op jit(solution)/shard_map/ppermute | solution.py:121
  44.4 10.0 %collective-permute-start.15 = (bf16[3,144,128]{2,1,0:T(8,128)(2,1)S(1)}, bf16[3,144,128]{2,1,0:T(8,128)(2,1)S(1)}, u32[]{:S(2)}, u32[]{:S(2)}) collective-permute-start(bf16[3,144,128]{2,1,0:T(8,128)(2,1)S(1)} %get-tuple-element.71), channel_id=1, source_target_pairs={{0,1},{2,3},{1,0},{3,2},{4,5},{6,7},{5,4},{7,6},{8,9},{10,11},{9,8... | collective-permute-start | bytes 331784 | tf_op jit(solution)/shard_map/ppermute | solution.py:121
  46.4 8.8 %collective-permute-start.6 = (bf16[3,144,128]{2,1,0:T(8,128)(2,1)S(1)}, bf16[3,144,128]{2,1,0:T(8,128)(2,1)S(1)}, u32[]{:S(2)}, u32[]{:S(2)}) collective-permute-start(bf16[3,144,128]{2,1,0:T(8,128)(2,1)S(1)} %get-tuple-element.58), channel_id=1, source_target_pairs={{0,3},{1,2},{3,0},{2,1},{4,7},{5,6},{7,4},{6,5},{8,11},{9,10},{11,... | collective-permute-start | bytes 331784 | tf_op jit(solution)/shard_map/ppermute | solution.py:121
  49.1 11.5 %collective-permute-start.7 = (bf16[3,144,128]{2,1,0:T(8,128)(2,1)S(1)}, bf16[3,144,128]{2,1,0:T(8,128)(2,1)S(1)}, u32[]{:S(2)}, u32[]{:S(2)}) collective-permute-start(bf16[3,144,128]{2,1,0:T(8,128)(2,1)S(1)} %get-tuple-element.59), channel_id=1, source_target_pairs={{0,2},{1,3},{2,0},{3,1},{4,6},{5,7},{6,4},{7,5},{8,10},{9,11},{10,... | collective-permute-start | bytes 331784 | tf_op jit(solution)/shard_map/ppermute | solution.py:121
  53.9 6.8 %collective-permute-start.8 = (bf16[3,144,128]{2,1,0:T(8,128)(2,1)S(1)}, bf16[3,144,128]{2,1,0:T(8,128)(2,1)S(1)}, u32[]{:S(2)}, u32[]{:S(2)}) collective-permute-start(bf16[3,144,128]{2,1,0:T(8,128)(2,1)S(1)} %get-tuple-element.61), channel_id=1, source_target_pairs={{0,1},{2,3},{1,0},{3,2},{4,5},{6,7},{5,4},{7,6},{8,9},{10,11},{9,8... | collective-permute-start | bytes 331784 | tf_op jit(solution)/shard_map/ppermute | solution.py:121

commit v12 on v10

--- a/solution.py
+++ b/solution.py
@@ -340,11 +340,9 @@
         spans.append(slice(head * HDIM, (head + heads) * HDIM))
         head += heads
     space_in = turned(q_space, k_space, v_space, cot_space)
-    packed = [list(split(time, span, n, sharing)) for span in spans]
-    own = [exchange(packed[0])]
+    packed = [split(time, span, n, sharing) for span in spans]
+    own = [exchange(blocks) for blocks in packed]
     space = space_grads(*space_in)
-    packed[1][2:], own[0][2], space = gated(packed[1][2:], own[0][2], space)
-    own.append(exchange(packed[1]))
     beside = [
         [neighbours(ends, start) for ends, start in zip(sides(blocks), (1, 0))] for blocks in own
     ]

time: 59.5 us -> 59.7 us (level)
  no operation moved by 1% of the time
where the time goes in v12:
time: 59.7 us; the launch traced here: 59.6 us
  starting transfers between devices  24.3 us (41%)
  waiting for transfers between devices  20.2 us (34%)
  Pallas kernels  14 us (23%)
  between operations  0.74 us (1%)
    ppermute x16, starting transfers between devices, swap(): lax.ppermute(block, axis, [(i, j) for i, j in pairs] + [(j, i) for i, j i...  24.3 us
    ppermute x16, waiting for transfers between devices, swap(): lax.ppermute(block, axis, [(i, j) for i, j in pairs] + [(j, i) for i, j i...  20.2 us
    pallas_call x1, Pallas kernels, space_grads(): pl.pallas_call(frame_kernel, out_shape=(shape, shape, shape), compiler_pa...  5.53 us
    pallas_call x2, Pallas kernels, split(): pl.pallas_call(functools.partial(split_kernel, sharing, rows, span), in_s...  3.76 us
    pallas_call x2, Pallas kernels, clip_grads(): pl.pallas_call(functools.partial(clip_kernel, window, heads), out_shape=[...  2.78 us
    pallas_call x2, Pallas kernels, join(): pl.pallas_call(functools.partial(join_kernel, sharing, span), in_specs=[p...  1.73 us
  transfers between devices with their start and end apart: 16, of which 5 were waited for; matrix products, arithmetic and copies ran while one was open for 0% of the time, Pallas kernels for 19%

profile of v12, /device:TPU:0, one launch (start us, length us, event | category | flops | bytes accessed | tf_op | source)
XLA Modules:
  0.0 59.6 jit_solution(2940450199483553405)
XLA Ops:
  0.6 1.9 %pack.3 = (bf16[4,144,128]{2,1,0:T(8,128)(2,1)}, bf16[4,144,128]{2,1,0:T(8,128)(2,1)}, bf16[4,144,128]{2,1,0:T(8,128)(2,1)}, bf16[4,144,128]{2,1,0:T(8,128)(2,1)}) custom-call(bf16[1,576,256]{2,1,0:T(8,128)(2,1)} %bitcast.18, bf16[1,576,256]{2,1,0:T(8,128)(2,1)} %bitcast.20, bf16[1,576,256]{2,1,0:T(8,128)(2,1)} %bitcast.22, bf16[1,576,256]{2,1,0:T(8,128)(2,1)} %bitcast.24), custom_call_target="tpu_custom_call" | custom-call | tf_op jit(solution)/shard_map/pack/pallas_call | solution.py:97
  2.5 5.1 %collective-permute-start.10 = (bf16[4,144,128]{2,1,0:T(8,128)(2,1)}, bf16[4,144,128]{2,1,0:T(8,128)(2,1)S(1)}, u32[]{:S(2)}, u32[]{:S(2)}) collective-permute-start(bf16[4,144,128]{2,1,0:T(8,128)(2,1)} %get-tuple-element.51), channel_id=1, source_target_pairs={{0,3},{1,2},{3,0},{2,1},{4,7},{5,6},{7,4},{6,5},{8,11},{9,10},{11,... | collective-permute-start | bytes 442376 | tf_op jit(solution)/shard_map/ppermute | solution.py:117
  7.6 0.0 collective-permute-start.8
  7.7 0.0 copy-start.1
  7.7 0.6 %collective-permute-start.9 = (bf16[4,144,128]{2,1,0:T(8,128)(2,1)}, bf16[4,144,128]{2,1,0:T(8,128)(2,1)S(1)}, u32[]{:S(2)}, u32[]{:S(2)}) collective-permute-start(bf16[4,144,128]{2,1,0:T(8,128)(2,1)} %get-tuple-element.50), channel_id=1, source_target_pairs={{0,2},{1,3},{2,0},{3,1},{4,6},{5,7},{6,4},{7,5},{8,10},{9,11},{10,... | collective-permute-start | bytes 442376 | tf_op jit(solution)/shard_map/ppermute | solution.py:117
  8.3 1.9 %pack.2 = (bf16[4,144,128]{2,1,0:T(8,128)(2,1)}, bf16[4,144,128]{2,1,0:T(8,128)(2,1)}, bf16[4,144,128]{2,1,0:T(8,128)(2,1)}, bf16[4,144,128]{2,1,0:T(8,128)(2,1)}) custom-call(bf16[1,576,256]{2,1,0:T(8,128)(2,1)} %bitcast.19, bf16[1,576,256]{2,1,0:T(8,128)(2,1)} %bitcast.21, bf16[1,576,256]{2,1,0:T(8,128)(2,1)} %bitcast.23, bf16[1,576,256]{2,1,0:T(8,128)(2,1)} %bitcast.25), custom_call_target="tpu_custom_call" | custom-call | tf_op jit(solution)/shard_map/pack/pallas_call | solution.py:97
  10.2 0.0 copy-start.2
  10.2 1.5 %collective-permute-start = (bf16[4,144,128]{2,1,0:T(8,128)(2,1)}, bf16[4,144,128]{2,1,0:T(8,128)(2,1)S(1)}, u32[]{:S(2)}, u32[]{:S(2)}) collective-permute-start(bf16[4,144,128]{2,1,0:T(8,128)(2,1)} %get-tuple-element.39), channel_id=1, source_target_pairs={{0,1},{2,3},{1,0},{3,2},{4,5},{6,7},{5,4},{7,6},{8,9},{10,11},{9,8... | collective-permute-start | bytes 442376 | tf_op jit(solution)/shard_map/ppermute | solution.py:117
  11.7 2.9 %collective-permute-start.1 = (bf16[4,144,128]{2,1,0:T(8,128)(2,1)}, bf16[4,144,128]{2,1,0:T(8,128)(2,1)S(1)}, u32[]{:S(2)}, u32[]{:S(2)}) collective-permute-start(bf16[4,144,128]{2,1,0:T(8,128)(2,1)} %get-tuple-element.40), channel_id=1, source_target_pairs={{0,2},{1,3},{2,0},{3,1},{4,6},{5,7},{6,4},{7,5},{8,10},{9,11},{10,... | collective-permute-start | bytes 442376 | tf_op jit(solution)/shard_map/ppermute | solution.py:117
  14.6 0.0 copy-done.2
  14.6 0.1 select_reduce_fusion.2
  14.6 0.0 collective-permute-done.10.refs_3_
  14.7 1.7 %collective-permute-start.2 = (bf16[4,144,128]{2,1,0:T(8,128)(2,1)}, bf16[4,144,128]{2,1,0:T(8,128)(2,1)S(1)}, u32[]{:S(2)}, u32[]{:S(2)}) collective-permute-start(bf16[4,144,128]{2,1,0:T(8,128)(2,1)} %get-tuple-element.41), channel_id=1, source_target_pairs={{0,3},{1,2},{3,0},{2,1},{4,7},{5,6},{7,4},{6,5},{8,11},{9,10},{11,... | collective-permute-start | bytes 442376 | tf_op jit(solution)/shard_map/ppermute | solution.py:117
  16.4 0.0 collective-permute-done.8.refs_1_
  16.4 5.8 %collective-permute-done.9.refs_2_ = bf16[4,144,128]{2,1,0:T(8,128)(2,1)S(1)} collective-permute-done((bf16[4,144,128]{2,1,0:T(8,128)(2,1)}, bf16[4,144,128]{2,1,0:T(8,128)(2,1)S(1)}, u32[]{:S(2)}, u32[]{:S(2)}) %collective-permute-start.9) | collective-permute-done | bytes 147488 | tf_op jit(solution)/shard_map/ppermute | solution.py:117
  22.2 0.0 copy-done.1
  22.2 0.0 copy-start
  22.2 0.1 sides.3
  22.3 0.1 collective-permute-start.11
  22.4 1.8 %collective-permute-start.12 = (bf16[3,4,144,128]{3,2,1,0:T(8,128)(2,1)S(1)}, bf16[3,4,144,128]{3,2,1,0:T(8,128)(2,1)S(1)}, u32[]{:S(2)}, u32[]{:S(2)}) collective-permute-start(bf16[3,4,144,128]{3,2,1,0:T(8,128)(2,1)S(1)} %get-tuple-element.53), channel_id=1, source_target_pairs={{0,4},{8,12},{16,20},{24,28},{4,0},{12,8},{20,16},{28,24},{1,5},{9... | collective-permute-start | bytes 1327112 | tf_op jit(solution)/shard_map/ppermute | solution.py:117
  24.2 0.2 select_reduce_fusion.1
  24.4 0.0 collective-permute-done.refs_1_
  24.4 6.4 %collective-permute-done.1.refs_2_ = bf16[4,144,128]{2,1,0:T(8,128)(2,1)S(1)} collective-permute-done((bf16[4,144,128]{2,1,0:T(8,128)(2,1)}, bf16[4,144,128]{2,1,0:T(8,128)(2,1)S(1)}, u32[]{:S(2)}, u32[]{:S(2)}) %collective-permute-start.1) | collective-permute-done | bytes 147488 | tf_op jit(solution)/shard_map/ppermute | solution.py:117
  30.8 0.0 collective-permute-done.2.refs_3_
  30.8 0.0 copy-done
  30.8 0.1 sides.2
  31.0 0.3 collective-permute-start.3
  31.3 1.4 %collective-permute-start.4 = (bf16[3,4,144,128]{3,2,1,0:T(8,128)(2,1)S(1)}, bf16[3,4,144,128]{3,2,1,0:T(8,128)(2,1)S(1)}, u32[]{:S(2)}, u32[]{:S(2)}) collective-permute-start(bf16[3,4,144,128]{3,2,1,0:T(8,128)(2,1)S(1)} %get-tuple-element.43), channel_id=1, source_target_pairs={{0,4},{8,12},{16,20},{24,28},{4,0},{12,8},{20,16},{28,24},{1,5},{9... | collective-permute-start | bytes 1327112 | tf_op jit(solution)/shard_map/ppermute | solution.py:117
  32.6 2.8 %collective-permute-done.11.refs_4_ = bf16[3,4,144,128]{3,2,1,0:T(8,128)(2,1)S(1)} collective-permute-done((bf16[3,4,144,128]{3,2,1,0:T(8,128)(2,1)S(1)}, bf16[3,4,144,128]{3,2,1,0:T(8,128)(2,1)S(1)}, u32[]{:S(2)}, u32[]{:S(2)}) %collective-permute-start.11) | collective-permute-done | bytes 442400 | tf_op jit(solution)/shard_map/ppermute | solution.py:117
  35.5 0.0 collective-permute-done.12.refs_5_
  35.5 1.4 %clips.3 = (bf16[3,144,128]{2,1,0:T(8,128)(2,1)S(1)}, bf16[3,144,128]{2,1,0:T(8,128)(2,1)S(1)}, bf16[3,144,128]{2,1,0:T(8,128)(2,1)S(1)}, bf16[3,144,128]{2,1,0:T(8,128)(2,1)S(1)}) custom-call(s32[2,10]{1,0:T(2,128)S(1)} %pad_add_fusion.given_bounds, bf16[4,144,128]{2,1,0:T(8,128)(2,1)S(1)} %copy-done.1, ...), custom_call_target="tpu_custom_call" | custom-call | flops 589824000 | bytes 1474560 | tf_op jit(solution)/shard_map/clips/pallas_call | solution.py:289
  36.9 2.3 %collective-permute-start.13 = (bf16[3,144,128]{2,1,0:T(8,128)(2,1)S(1)}, bf16[3,144,128]{2,1,0:T(8,128)(2,1)S(1)}, u32[]{:S(2)}, u32[]{:S(2)}) collective-permute-start(bf16[3,144,128]{2,1,0:T(8,128)(2,1)S(1)} %get-tuple-element.54), channel_id=1, source_target_pairs={{0,3},{1,2},{3,0},{2,1},{4,7},{5,6},{7,4},{6,5},{8,11},{9,10},{11,... | collective-permute-start | bytes 331784 | tf_op jit(solution)/shard_map/ppermute | solution.py:117
  39.2 0.0 collective-permute-start.14
  39.2 2.1 %collective-permute-start.15 = (bf16[3,144,128]{2,1,0:T(8,128)(2,1)S(1)}, bf16[3,144,128]{2,1,0:T(8,128)(2,1)S(1)}, u32[]{:S(2)}, u32[]{:S(2)}) collective-permute-start(bf16[3,144,128]{2,1,0:T(8,128)(2,1)S(1)} %get-tuple-element.57), channel_id=1, source_target_pairs={{0,1},{2,3},{1,0},{3,2},{4,5},{6,7},{5,4},{7,6},{8,9},{10,11},{9,8... | collective-permute-start | bytes 331784 | tf_op jit(solution)/shard_map/ppermute | solution.py:117
  41.3 3.6 %collective-permute-done.3.refs_4_ = bf16[3,4,144,128]{3,2,1,0:T(8,128)(2,1)S(1)} collective-permute-done((bf16[3,4,144,128]{3,2,1,0:T(8,128)(2,1)S(1)}, bf16[3,4,144,128]{3,2,1,0:T(8,128)(2,1)S(1)}, u32[]{:S(2)}, u32[]{:S(2)}) %collective-permute-start.3) | collective-permute-done | bytes 442400 | tf_op jit(solution)/shard_map/ppermute | solution.py:117
  44.9 0.0 collective-permute-done.4.refs_5_
  44.9 1.4 %clips.2 = (bf16[3,144,128]{2,1,0:T(8,128)(2,1)S(1)}, bf16[3,144,128]{2,1,0:T(8,128)(2,1)S(1)}, bf16[3,144,128]{2,1,0:T(8,128)(2,1)S(1)}, bf16[3,144,128]{2,1,0:T(8,128)(2,1)S(1)}) custom-call(s32[2,10]{1,0:T(2,128)S(1)} %pad_add_fusion.given_bounds, bf16[4,144,128]{2,1,0:T(8,128)(2,1)S(1)} %copy-done, ...), custom_call_target="tpu_custom_call" | custom-call | flops 589824000 | bytes 1474560 | tf_op jit(solution)/shard_map/clips/pallas_call | solution.py:289
  46.3 2.3 %collective-permute-start.5 = (bf16[3,144,128]{2,1,0:T(8,128)(2,1)S(1)}, bf16[3,144,128]{2,1,0:T(8,128)(2,1)S(1)}, u32[]{:S(2)}, u32[]{:S(2)}) collective-permute-start(bf16[3,144,128]{2,1,0:T(8,128)(2,1)S(1)} %get-tuple-element.44), channel_id=1, source_target_pairs={{0,3},{1,2},{3,0},{2,1},{4,7},{5,6},{7,4},{6,5},{8,11},{9,10},{11,... | collective-permute-start | bytes 331784 | tf_op jit(solution)/shard_map/ppermute | solution.py:117
  48.6 1.3 %collective-permute-start.6 = (bf16[3,144,128]{2,1,0:T(8,128)(2,1)S(1)}, bf16[3,144,128]{2,1,0:T(8,128)(2,1)S(1)}, u32[]{:S(2)}, u32[]{:S(2)}) collective-permute-start(bf16[3,144,128]{2,1,0:T(8,128)(2,1)S(1)} %get-tuple-element.45), channel_id=1, source_target_pairs={{0,2},{1,3},{2,0},{3,1},{4,6},{5,7},{6,4},{7,5},{8,10},{9,11},{10,... | collective-permute-start | bytes 331784 | tf_op jit(solution)/shard_map/ppermute | solution.py:117
  50.0 0.0 collective-permute-done.13.refs_0_
  50.0 0.8 %collective-permute-start.7 = (bf16[3,144,128]{2,1,0:T(8,128)(2,1)S(1)}, bf16[3,144,128]{2,1,0:T(8,128)(2,1)S(1)}, u32[]{:S(2)}, u32[]{:S(2)}) collective-permute-start(bf16[3,144,128]{2,1,0:T(8,128)(2,1)S(1)} %get-tuple-element.47), channel_id=1, source_target_pairs={{0,1},{2,3},{1,0},{3,2},{4,5},{6,7},{5,4},{7,6},{8,9},{10,11},{9,8... | collective-permute-start | bytes 331784 | tf_op jit(solution)/shard_map/ppermute | solution.py:117
  50.8 5.5 %space.1 = (bf16[1,576,256]{2,1,0:T(8,128)(2,1)}, bf16[1,576,256]{2,1,0:T(8,128)(2,1)}, bf16[1,576,256]{2,1,0:T(8,128)(2,1)}) custom-call(bf16[1,576,256]{2,1,0:T(8,128)(2,1)} %bitcast.29, bf16[1,576,256]{2,1,0:T(8,128)(2,1)} %bitcast.30, bf16[1,576,256]{2,1,0:T(8,128)(2,1)} %bitcast.31, bf16[1,576,256]{2,1,0:T(8,128)(2,1)} %bitcast.32), custom_call_target="tpu_custom_call" | custom-call | flops 1610612736 | bytes 2064384 | tf_op jit(solution)/shard_map/space/pallas_call | solution.py:58
  56.3 0.0 collective-permute-done.14.refs_1_
  56.3 0.0 collective-permute-done.15.refs_3_
  56.3 0.9 %unpack.2 = (bf16[1,576,256]{2,1,0:T(8,128)(2,1)}, bf16[1,576,256]{2,1,0:T(8,128)(2,1)}, bf16[1,576,256]{2,1,0:T(8,128)(2,1)}) custom-call(bf16[3,144,128]{2,1,0:T(8,128)(2,1)S(1)} %collective-permute-done.13.refs_0_, bf16[3,144,128]{2,1,0:T(8,128)(2,1)S(1)} %collective-permute-done.14.refs_1_, bf16[3,144,128]{2,1,0:T(8,128)(2,1)S(1)} %get-tuple-element.56.refs_2_, ...), custom_call_target="tpu_custom_call" | custom-call | tf_op jit(solution)/shard_map/unpack/pallas_call | solution.py:185
  57.2 0.0 collective-permute-done.5.refs_0_
  57.2 1.5 %collective-permute-done.6.refs_1_ = bf16[3,144,128]{2,1,0:T(8,128)(2,1)S(1)} collective-permute-done((bf16[3,144,128]{2,1,0:T(8,128)(2,1)S(1)}, bf16[3,144,128]{2,1,0:T(8,128)(2,1)S(1)}, u32[]{:S(2)}, u32[]{:S(2)}) %collective-permute-start.6) | collective-permute-done | bytes 110624 | tf_op jit(solution)/shard_map/ppermute | solution.py:117
  58.7 0.0 collective-permute-done.7.refs_3_
  58.7 0.9 %unpack.3 = (bf16[1,576,256]{2,1,0:T(8,128)(2,1)}, bf16[1,576,256]{2,1,0:T(8,128)(2,1)}, bf16[1,576,256]{2,1,0:T(8,128)(2,1)}) custom-call(bf16[3,144,128]{2,1,0:T(8,128)(2,1)S(1)} %collective-permute-done.5.refs_0_, bf16[3,144,128]{2,1,0:T(8,128)(2,1)S(1)} %collective-permute-done.6.refs_1_, ...), custom_call_target="tpu_custom_call", output_to_operand_aliasing={{0}: (4, {}), {1}: (5, {}), {2}: (6, {})} | custom-call | tf_op jit(solution)/shard_map/unpack/pallas_call | solution.py:185
  (4 shorter events, 0.0 us)
Async XLA Ops:
  2.5 12.1 %collective-permute-start.10 = (bf16[4,144,128]{2,1,0:T(8,128)(2,1)}, bf16[4,144,128]{2,1,0:T(8,128)(2,1)S(1)}, u32[]{:S(2)}, u32[]{:S(2)}) collective-permute-start(bf16[4,144,128]{2,1,0:T(8,128)(2,1)} %get-tuple-element.51), channel_id=1, source_target_pairs={{0,3},{1,2},{3,0},{2,1},{4,7},{5,6},{7,4},{6,5},{8,11},{9,10},{11,... | collective-permute-start | bytes 442376 | tf_op jit(solution)/shard_map/ppermute | solution.py:117
  7.6 8.8 %collective-permute-start.8 = (bf16[4,144,128]{2,1,0:T(8,128)(2,1)}, bf16[4,144,128]{2,1,0:T(8,128)(2,1)S(1)}, u32[]{:S(2)}, u32[]{:S(2)}) collective-permute-start(bf16[4,144,128]{2,1,0:T(8,128)(2,1)} %get-tuple-element.49), channel_id=1, source_target_pairs={{0,1},{2,3},{1,0},{3,2},{4,5},{6,7},{5,4},{7,6},{8,9},{10,11},{9,8... | collective-permute-start | bytes 442376 | tf_op jit(solution)/shard_map/ppermute | solution.py:117
  7.7 14.5 %copy-start.1 = (bf16[4,144,128]{2,1,0:T(8,128)(2,1)S(1)}, bf16[4,144,128]{2,1,0:T(8,128)(2,1)}, u32[]{:S(2)}) copy-start(bf16[4,144,128]{2,1,0:T(8,128)(2,1)} %get-tuple-element.48.refs_0_) | copy-start | bytes 442372
  7.7 14.5 %collective-permute-start.9 = (bf16[4,144,128]{2,1,0:T(8,128)(2,1)}, bf16[4,144,128]{2,1,0:T(8,128)(2,1)S(1)}, u32[]{:S(2)}, u32[]{:S(2)}) collective-permute-start(bf16[4,144,128]{2,1,0:T(8,128)(2,1)} %get-tuple-element.50), channel_id=1, source_target_pairs={{0,2},{1,3},{2,0},{3,1},{4,6},{5,7},{6,4},{7,5},{8,10},{9,11},{10,... | collective-permute-start | bytes 442376 | tf_op jit(solution)/shard_map/ppermute | solution.py:117
  10.2 4.4 %copy-start.2 = (s32[16]{0:T(128)S(1)}, s32[16]{0:T(128)}, u32[]{:S(2)}) copy-start(s32[16]{0:T(128)} %param.17) | copy-start | bytes 196
  10.2 14.2 %collective-permute-start = (bf16[4,144,128]{2,1,0:T(8,128)(2,1)}, bf16[4,144,128]{2,1,0:T(8,128)(2,1)S(1)}, u32[]{:S(2)}, u32[]{:S(2)}) collective-permute-start(bf16[4,144,128]{2,1,0:T(8,128)(2,1)} %get-tuple-element.39), channel_id=1, source_target_pairs={{0,1},{2,3},{1,0},{3,2},{4,5},{6,7},{5,4},{7,6},{8,9},{10,11},{9,8... | collective-permute-start | bytes 442376 | tf_op jit(solution)/shard_map/ppermute | solution.py:117
  11.7 19.2 %collective-permute-start.1 = (bf16[4,144,128]{2,1,0:T(8,128)(2,1)}, bf16[4,144,128]{2,1,0:T(8,128)(2,1)S(1)}, u32[]{:S(2)}, u32[]{:S(2)}) collective-permute-start(bf16[4,144,128]{2,1,0:T(8,128)(2,1)} %get-tuple-element.40), channel_id=1, source_target_pairs={{0,2},{1,3},{2,0},{3,1},{4,6},{5,7},{6,4},{7,5},{8,10},{9,11},{10,... | collective-permute-start | bytes 442376 | tf_op jit(solution)/shard_map/ppermute | solution.py:117
  14.7 16.2 %collective-permute-start.2 = (bf16[4,144,128]{2,1,0:T(8,128)(2,1)}, bf16[4,144,128]{2,1,0:T(8,128)(2,1)S(1)}, u32[]{:S(2)}, u32[]{:S(2)}) collective-permute-start(bf16[4,144,128]{2,1,0:T(8,128)(2,1)} %get-tuple-element.41), channel_id=1, source_target_pairs={{0,3},{1,2},{3,0},{2,1},{4,7},{5,6},{7,4},{6,5},{8,11},{9,10},{11,... | collective-permute-start | bytes 442376 | tf_op jit(solution)/shard_map/ppermute | solution.py:117
  22.2 8.6 %copy-start = (bf16[4,144,128]{2,1,0:T(8,128)(2,1)S(1)}, bf16[4,144,128]{2,1,0:T(8,128)(2,1)}, u32[]{:S(2)}) copy-start(bf16[4,144,128]{2,1,0:T(8,128)(2,1)} %get-tuple-element.38.refs_0_) | copy-start | bytes 442372
  22.3 13.1 %collective-permute-start.11 = (bf16[3,4,144,128]{3,2,1,0:T(8,128)(2,1)S(1)}, bf16[3,4,144,128]{3,2,1,0:T(8,128)(2,1)S(1)}, u32[]{:S(2)}, u32[]{:S(2)}) collective-permute-start(bf16[3,4,144,128]{3,2,1,0:T(8,128)(2,1)S(1)} %get-tuple-element.52), channel_id=1, source_target_pairs={{4,8},{12,16},{20,24},{28,0},{8,4},{16,12},{24,20},{0,28},{5,9},{1... | collective-permute-start | bytes 1327112 | tf_op jit(solution)/shard_map/ppermute | solution.py:117
  22.4 13.1 %collective-permute-start.12 = (bf16[3,4,144,128]{3,2,1,0:T(8,128)(2,1)S(1)}, bf16[3,4,144,128]{3,2,1,0:T(8,128)(2,1)S(1)}, u32[]{:S(2)}, u32[]{:S(2)}) collective-permute-start(bf16[3,4,144,128]{3,2,1,0:T(8,128)(2,1)S(1)} %get-tuple-element.53), channel_id=1, source_target_pairs={{0,4},{8,12},{16,20},{24,28},{4,0},{12,8},{20,16},{28,24},{1,5},{9... | collective-permute-start | bytes 1327112 | tf_op jit(solution)/shard_map/ppermute | solution.py:117
  31.0 14.0 %collective-permute-start.3 = (bf16[3,4,144,128]{3,2,1,0:T(8,128)(2,1)S(1)}, bf16[3,4,144,128]{3,2,1,0:T(8,128)(2,1)S(1)}, u32[]{:S(2)}, u32[]{:S(2)}) collective-permute-start(bf16[3,4,144,128]{3,2,1,0:T(8,128)(2,1)S(1)} %get-tuple-element.42), channel_id=1, source_target_pairs={{4,8},{12,16},{20,24},{28,0},{8,4},{16,12},{24,20},{0,28},{5,9},{1... | collective-permute-start | bytes 1327112 | tf_op jit(solution)/shard_map/ppermute | solution.py:117
  31.3 13.7 %collective-permute-start.4 = (bf16[3,4,144,128]{3,2,1,0:T(8,128)(2,1)S(1)}, bf16[3,4,144,128]{3,2,1,0:T(8,128)(2,1)S(1)}, u32[]{:S(2)}, u32[]{:S(2)}) collective-permute-start(bf16[3,4,144,128]{3,2,1,0:T(8,128)(2,1)S(1)} %get-tuple-element.43), channel_id=1, source_target_pairs={{0,4},{8,12},{16,20},{24,28},{4,0},{12,8},{20,16},{28,24},{1,5},{9... | collective-permute-start | bytes 1327112 | tf_op jit(solution)/shard_map/ppermute | solution.py:117
  36.9 13.1 %collective-permute-start.13 = (bf16[3,144,128]{2,1,0:T(8,128)(2,1)S(1)}, bf16[3,144,128]{2,1,0:T(8,128)(2,1)S(1)}, u32[]{:S(2)}, u32[]{:S(2)}) collective-permute-start(bf16[3,144,128]{2,1,0:T(8,128)(2,1)S(1)} %get-tuple-element.54), channel_id=1, source_target_pairs={{0,3},{1,2},{3,0},{2,1},{4,7},{5,6},{7,4},{6,5},{8,11},{9,10},{11,... | collective-permute-start | bytes 331784 | tf_op jit(solution)/shard_map/ppermute | solution.py:117
  39.2 17.2 %collective-permute-start.14 = (bf16[3,144,128]{2,1,0:T(8,128)(2,1)S(1)}, bf16[3,144,128]{2,1,0:T(8,128)(2,1)S(1)}, u32[]{:S(2)}, u32[]{:S(2)}) collective-permute-start(bf16[3,144,128]{2,1,0:T(8,128)(2,1)S(1)} %get-tuple-element.55), channel_id=1, source_target_pairs={{0,2},{1,3},{2,0},{3,1},{4,6},{5,7},{6,4},{7,5},{8,10},{9,11},{10,... | collective-permute-start | bytes 331784 | tf_op jit(solution)/shard_map/ppermute | solution.py:117
  39.2 17.2 %collective-permute-start.15 = (bf16[3,144,128]{2,1,0:T(8,128)(2,1)S(1)}, bf16[3,144,128]{2,1,0:T(8,128)(2,1)S(1)}, u32[]{:S(2)}, u32[]{:S(2)}) collective-permute-start(bf16[3,144,128]{2,1,0:T(8,128)(2,1)S(1)} %get-tuple-element.57), channel_id=1, source_target_pairs={{0,1},{2,3},{1,0},{3,2},{4,5},{6,7},{5,4},{7,6},{8,9},{10,11},{9,8... | collective-permute-start | bytes 331784 | tf_op jit(solution)/shard_map/ppermute | solution.py:117
  46.3 10.9 %collective-permute-start.5 = (bf16[3,144,128]{2,1,0:T(8,128)(2,1)S(1)}, bf16[3,144,128]{2,1,0:T(8,128)(2,1)S(1)}, u32[]{:S(2)}, u32[]{:S(2)}) collective-permute-start(bf16[3,144,128]{2,1,0:T(8,128)(2,1)S(1)} %get-tuple-element.44), channel_id=1, source_target_pairs={{0,3},{1,2},{3,0},{2,1},{4,7},{5,6},{7,4},{6,5},{8,11},{9,10},{11,... | collective-permute-start | bytes 331784 | tf_op jit(solution)/shard_map/ppermute | solution.py:117
  48.6 10.1 %collective-permute-start.6 = (bf16[3,144,128]{2,1,0:T(8,128)(2,1)S(1)}, bf16[3,144,128]{2,1,0:T(8,128)(2,1)S(1)}, u32[]{:S(2)}, u32[]{:S(2)}) collective-permute-start(bf16[3,144,128]{2,1,0:T(8,128)(2,1)S(1)} %get-tuple-element.45), channel_id=1, source_target_pairs={{0,2},{1,3},{2,0},{3,1},{4,6},{5,7},{6,4},{7,5},{8,10},{9,11},{10,... | collective-permute-start | bytes 331784 | tf_op jit(solution)/shard_map/ppermute | solution.py:117
  50.0 8.8 %collective-permute-start.7 = (bf16[3,144,128]{2,1,0:T(8,128)(2,1)S(1)}, bf16[3,144,128]{2,1,0:T(8,128)(2,1)S(1)}, u32[]{:S(2)}, u32[]{:S(2)}) collective-permute-start(bf16[3,144,128]{2,1,0:T(8,128)(2,1)S(1)} %get-tuple-element.47), channel_id=1, source_target_pairs={{0,1},{2,3},{1,0},{3,2},{4,5},{6,7},{5,4},{7,6},{8,9},{10,11},{9,8... | collective-permute-start | bytes 331784 | tf_op jit(solution)/shard_map/ppermute | solution.py:117

commit v13 on v10

--- a/solution.py
+++ b/solution.py
@@ -273,7 +273,7 @@
             found[at, i] = jnp.concatenate(parts, axis=0).astype(jnp.bfloat16)
         return carry
 
-    lax.fori_loop(0, window, gradients, 0)
+    lax.fori_loop(0, window, gradients, 0, unroll=2)
     for step, out in enumerate(outs):
         out[...] = found[lax.axis_index("seq") ^ step]
 

time: 59.5 us -> 59.4 us (level)
  no operation moved by 1% of the time
where the time goes in v13:
time: 59.4 us; the launch traced here: 59.2 us
  starting transfers between devices  23.9 us (40%)
  waiting for transfers between devices  20 us (34%)
  Pallas kernels  14.2 us (24%)
  between operations  0.75 us (1%)
    ppermute x16, starting transfers between devices, swap(): lax.ppermute(block, axis, [(i, j) for i, j in pairs] + [(j, i) for i, j i...  23.9 us
    ppermute x16, waiting for transfers between devices, swap(): lax.ppermute(block, axis, [(i, j) for i, j in pairs] + [(j, i) for i, j i...  20 us
    pallas_call x1, Pallas kernels, space_grads(): pl.pallas_call(frame_kernel, out_shape=(shape, shape, shape), compiler_pa...  5.58 us
    pallas_call x2, Pallas kernels, split(): pl.pallas_call(functools.partial(split_kernel, sharing, rows, span), in_s...  3.77 us
    pallas_call x2, Pallas kernels, clip_grads(): pl.pallas_call(functools.partial(clip_kernel, window, heads), out_shape=[...  2.84 us
    pallas_call x2, Pallas kernels, join(): pl.pallas_call(functools.partial(join_kernel, sharing, span), in_specs=[p...  1.71 us
  transfers between devices with their start and end apart: 16, of which 5 were waited for; matrix products, arithmetic and copies ran while one was open for 0% of the time, Pallas kernels for 19%

profile of v13, /device:TPU:0, one launch (start us, length us, event | category | flops | bytes accessed | tf_op | source)
XLA Modules:
  0.0 59.2 jit_solution(2331435836097697576)
XLA Ops:
  0.6 1.9 %pack.3 = (bf16[4,144,128]{2,1,0:T(8,128)(2,1)}, bf16[4,144,128]{2,1,0:T(8,128)(2,1)}, bf16[4,144,128]{2,1,0:T(8,128)(2,1)}, bf16[4,144,128]{2,1,0:T(8,128)(2,1)}) custom-call(bf16[1,576,256]{2,1,0:T(8,128)(2,1)} %bitcast.18, bf16[1,576,256]{2,1,0:T(8,128)(2,1)} %bitcast.20, bf16[1,576,256]{2,1,0:T(8,128)(2,1)} %bitcast.22, bf16[1,576,256]{2,1,0:T(8,128)(2,1)} %bitcast.24), custom_call_target="tpu_custom_call" | custom-call | tf_op jit(solution)/shard_map/pack/pallas_call | solution.py:97
  2.5 4.1 %collective-permute-start = (bf16[4,144,128]{2,1,0:T(8,128)(2,1)}, bf16[4,144,128]{2,1,0:T(8,128)(2,1)S(1)}, u32[]{:S(2)}, u32[]{:S(2)}) collective-permute-start(bf16[4,144,128]{2,1,0:T(8,128)(2,1)} %get-tuple-element.43), channel_id=1, source_target_pairs={{0,2},{1,3},{2,0},{3,1},{4,6},{5,7},{6,4},{7,5},{8,10},{9,11},{10,... | collective-permute-start | bytes 442376 | tf_op jit(solution)/shard_map/ppermute | solution.py:117
  6.6 1.6 %collective-permute-start.9 = (bf16[4,144,128]{2,1,0:T(8,128)(2,1)}, bf16[4,144,128]{2,1,0:T(8,128)(2,1)S(1)}, u32[]{:S(2)}, u32[]{:S(2)}) collective-permute-start(bf16[4,144,128]{2,1,0:T(8,128)(2,1)} %get-tuple-element.61), channel_id=1, source_target_pairs={{0,1},{2,3},{1,0},{3,2},{4,5},{6,7},{5,4},{7,6},{8,9},{10,11},{9,8... | collective-permute-start | bytes 442376 | tf_op jit(solution)/shard_map/ppermute | solution.py:117
  8.2 0.0 collective-permute-start.10
  8.2 1.9 %pack.2 = (bf16[4,144,128]{2,1,0:T(8,128)(2,1)}, bf16[4,144,128]{2,1,0:T(8,128)(2,1)}, bf16[4,144,128]{2,1,0:T(8,128)(2,1)}, bf16[4,144,128]{2,1,0:T(8,128)(2,1)}) custom-call(bf16[1,576,256]{2,1,0:T(8,128)(2,1)} %bitcast.19, bf16[1,576,256]{2,1,0:T(8,128)(2,1)} %bitcast.21, bf16[1,576,256]{2,1,0:T(8,128)(2,1)} %bitcast.23, bf16[1,576,256]{2,1,0:T(8,128)(2,1)} %bitcast.25), custom_call_target="tpu_custom_call" | custom-call | tf_op jit(solution)/shard_map/pack/pallas_call | solution.py:97
  10.1 1.0 %collective-permute-start.1 = (bf16[4,144,128]{2,1,0:T(8,128)(2,1)}, bf16[4,144,128]{2,1,0:T(8,128)(2,1)S(1)}, u32[]{:S(2)}, u32[]{:S(2)}) collective-permute-start(bf16[4,144,128]{2,1,0:T(8,128)(2,1)} %get-tuple-element.51), channel_id=1, source_target_pairs={{0,1},{2,3},{1,0},{3,2},{4,5},{6,7},{5,4},{7,6},{8,9},{10,11},{9,8... | collective-permute-start | bytes 442376 | tf_op jit(solution)/shard_map/ppermute | solution.py:117
  11.1 0.0 copy-start.4
  11.1 0.0 copy-start.3
  11.1 0.0 copy-start.2
  11.1 0.0 copy-start.1
  11.1 5.6 %space.1 = (bf16[1,576,256]{2,1,0:T(8,128)(2,1)}, bf16[1,576,256]{2,1,0:T(8,128)(2,1)}, bf16[1,576,256]{2,1,0:T(8,128)(2,1)}) custom-call(bf16[1,576,256]{2,1,0:T(8,128)(2,1)} %bitcast.29, bf16[1,576,256]{2,1,0:T(8,128)(2,1)} %bitcast.30, bf16[1,576,256]{2,1,0:T(8,128)(2,1)} %bitcast.31, bf16[1,576,256]{2,1,0:T(8,128)(2,1)} %bitcast.32), custom_call_target="tpu_custom_call" | custom-call | flops 1610612736 | bytes 2064384 | tf_op jit(solution)/shard_map/space/pallas_call | solution.py:58
  16.7 0.0 copy-done.4
  16.7 0.1 select_reduce_fusion.2
  16.7 0.0 collective-permute-done.refs_2_
  16.7 0.0 copy-done.3
  16.8 3.6 %collective-permute-start.2 = (bf16[4,144,128]{2,1,0:T(8,128)(2,1)S(1)}, bf16[4,144,128]{2,1,0:T(8,128)(2,1)S(1)}, u32[]{:S(2)}, u32[]{:S(2)}) collective-permute-start(bf16[4,144,128]{2,1,0:T(8,128)(2,1)S(1)} %copy-done.3), channel_id=1, source_target_pairs={{0,2},{1,3},{2,0},{3,1},{4,6},{5,7},{6,4},{7,5},{8,10},{9,11},{10,... | collective-permute-start | bytes 442376 | tf_op jit(solution)/shard_map/ppermute | solution.py:117
  20.3 0.0 copy-done.2
  20.3 0.0 collective-permute-start.3
  20.3 0.0 collective-permute-done.9.refs_1_
  20.3 0.0 collective-permute-done.10.refs_3_
  20.4 0.0 copy-done.1
  20.4 0.0 copy-start
  20.4 0.1 sides.3
  20.5 0.6 collective-permute-start.11
  21.1 1.3 %collective-permute-start.12 = (bf16[3,4,144,128]{3,2,1,0:T(8,128)(2,1)S(1)}, bf16[3,4,144,128]{3,2,1,0:T(8,128)(2,1)S(1)}, u32[]{:S(2)}, u32[]{:S(2)}) collective-permute-start(bf16[3,4,144,128]{3,2,1,0:T(8,128)(2,1)S(1)} %get-tuple-element.65), channel_id=1, source_target_pairs={{0,4},{8,12},{16,20},{24,28},{4,0},{12,8},{20,16},{28,24},{1,5},{9... | collective-permute-start | bytes 1327112 | tf_op jit(solution)/shard_map/ppermute | solution.py:117
  22.4 0.2 select_reduce_fusion.1
  22.6 0.0 collective-permute-done.1.refs_1_
  22.6 8.0 %collective-permute-done.2.refs_2_ = bf16[4,144,128]{2,1,0:T(8,128)(2,1)S(1)} collective-permute-done((bf16[4,144,128]{2,1,0:T(8,128)(2,1)S(1)}, bf16[4,144,128]{2,1,0:T(8,128)(2,1)S(1)}, u32[]{:S(2)}, u32[]{:S(2)}) %collective-permute-start.2) | collective-permute-done | bytes 147488 | tf_op jit(solution)/shard_map/ppermute | solution.py:117
  30.6 0.0 collective-permute-done.3.refs_3_
  30.6 0.0 copy-done
  30.6 0.1 sides.2
  30.7 0.5 collective-permute-start.4
  31.2 1.2 %collective-permute-start.5 = (bf16[3,4,144,128]{3,2,1,0:T(8,128)(2,1)S(1)}, bf16[3,4,144,128]{3,2,1,0:T(8,128)(2,1)S(1)}, u32[]{:S(2)}, u32[]{:S(2)}) collective-permute-start(bf16[3,4,144,128]{3,2,1,0:T(8,128)(2,1)S(1)} %get-tuple-element.55), channel_id=1, source_target_pairs={{0,4},{8,12},{16,20},{24,28},{4,0},{12,8},{20,16},{28,24},{1,5},{9... | collective-permute-start | bytes 1327112 | tf_op jit(solution)/shard_map/ppermute | solution.py:117
  32.4 1.2 %collective-permute-done.11.refs_4_ = bf16[3,4,144,128]{3,2,1,0:T(8,128)(2,1)S(1)} collective-permute-done((bf16[3,4,144,128]{3,2,1,0:T(8,128)(2,1)S(1)}, bf16[3,4,144,128]{3,2,1,0:T(8,128)(2,1)S(1)}, u32[]{:S(2)}, u32[]{:S(2)}) %collective-permute-start.11) | collective-permute-done | bytes 442400 | tf_op jit(solution)/shard_map/ppermute | solution.py:117
  33.6 0.0 collective-permute-done.12.refs_5_
  33.6 1.4 %clips.3 = (bf16[3,144,128]{2,1,0:T(8,128)(2,1)S(1)}, bf16[3,144,128]{2,1,0:T(8,128)(2,1)S(1)}, bf16[3,144,128]{2,1,0:T(8,128)(2,1)S(1)}, bf16[3,144,128]{2,1,0:T(8,128)(2,1)S(1)}) custom-call(s32[2,10]{1,0:T(2,128)S(1)} %pad_add_fusion.given_bounds, bf16[4,144,128]{2,1,0:T(8,128)(2,1)S(1)} %copy-done.1, ...), custom_call_target="tpu_custom_call" | custom-call | flops 589824000 | bytes 1474560 | tf_op jit(solution)/shard_map/clips/pallas_call | solution.py:289
  35.1 4.1 %collective-permute-start.13 = (bf16[3,144,128]{2,1,0:T(8,128)(2,1)S(1)}, bf16[3,144,128]{2,1,0:T(8,128)(2,1)S(1)}, u32[]{:S(2)}, u32[]{:S(2)}) collective-permute-start(bf16[3,144,128]{2,1,0:T(8,128)(2,1)S(1)} %get-tuple-element.66), channel_id=1, source_target_pairs={{0,3},{1,2},{3,0},{2,1},{4,7},{5,6},{7,4},{6,5},{8,11},{9,10},{11,... | collective-permute-start | bytes 331784 | tf_op jit(solution)/shard_map/ppermute | solution.py:117
  39.2 0.2 collective-permute-start.14
  39.3 0.5 collective-permute-start.15
  39.8 4.2 %collective-permute-done.4.refs_4_ = bf16[3,4,144,128]{3,2,1,0:T(8,128)(2,1)S(1)} collective-permute-done((bf16[3,4,144,128]{3,2,1,0:T(8,128)(2,1)S(1)}, bf16[3,4,144,128]{3,2,1,0:T(8,128)(2,1)S(1)}, u32[]{:S(2)}, u32[]{:S(2)}) %collective-permute-start.4) | collective-permute-done | bytes 442400 | tf_op jit(solution)/shard_map/ppermute | solution.py:117
  44.0 0.0 collective-permute-done.5.refs_5_
  44.0 1.4 %clips.2 = (bf16[3,144,128]{2,1,0:T(8,128)(2,1)S(1)}, bf16[3,144,128]{2,1,0:T(8,128)(2,1)S(1)}, bf16[3,144,128]{2,1,0:T(8,128)(2,1)S(1)}, bf16[3,144,128]{2,1,0:T(8,128)(2,1)S(1)}) custom-call(s32[2,10]{1,0:T(2,128)S(1)} %pad_add_fusion.given_bounds, bf16[4,144,128]{2,1,0:T(8,128)(2,1)S(1)} %copy-done, ...), custom_call_target="tpu_custom_call" | custom-call | flops 589824000 | bytes 1474560 | tf_op jit(solution)/shard_map/clips/pallas_call | solution.py:289
  45.5 3.2 %collective-permute-start.6 = (bf16[3,144,128]{2,1,0:T(8,128)(2,1)S(1)}, bf16[3,144,128]{2,1,0:T(8,128)(2,1)S(1)}, u32[]{:S(2)}, u32[]{:S(2)}) collective-permute-start(bf16[3,144,128]{2,1,0:T(8,128)(2,1)S(1)} %get-tuple-element.56), channel_id=1, source_target_pairs={{0,3},{1,2},{3,0},{2,1},{4,7},{5,6},{7,4},{6,5},{8,11},{9,10},{11,... | collective-permute-start | bytes 331784 | tf_op jit(solution)/shard_map/ppermute | solution.py:117
  48.6 1.8 %collective-permute-start.7 = (bf16[3,144,128]{2,1,0:T(8,128)(2,1)S(1)}, bf16[3,144,128]{2,1,0:T(8,128)(2,1)S(1)}, u32[]{:S(2)}, u32[]{:S(2)}) collective-permute-start(bf16[3,144,128]{2,1,0:T(8,128)(2,1)S(1)} %get-tuple-element.57), channel_id=1, source_target_pairs={{0,2},{1,3},{2,0},{3,1},{4,6},{5,7},{6,4},{7,5},{8,10},{9,11},{10,... | collective-permute-start | bytes 331784 | tf_op jit(solution)/shard_map/ppermute | solution.py:117
  50.5 0.0 collective-permute-done.13.refs_0_
  50.5 0.5 collective-permute-start.8
  50.9 0.0 collective-permute-done.14.refs_1_
  50.9 0.0 collective-permute-done.15.refs_3_
  51.0 0.9 %unpack.2 = (bf16[1,576,256]{2,1,0:T(8,128)(2,1)}, bf16[1,576,256]{2,1,0:T(8,128)(2,1)}, bf16[1,576,256]{2,1,0:T(8,128)(2,1)}) custom-call(bf16[3,144,128]{2,1,0:T(8,128)(2,1)S(1)} %collective-permute-done.13.refs_0_, bf16[3,144,128]{2,1,0:T(8,128)(2,1)S(1)} %collective-permute-done.14.refs_1_, bf16[3,144,128]{2,1,0:T(8,128)(2,1)S(1)} %get-tuple-element.68.refs_2_, ...), custom_call_target="tpu_custom_call" | custom-call | tf_op jit(solution)/shard_map/unpack/pallas_call | solution.py:185
  51.8 0.4 collective-permute-done.6.refs_0_
  52.3 6.0 %collective-permute-done.7.refs_1_ = bf16[3,144,128]{2,1,0:T(8,128)(2,1)S(1)} collective-permute-done((bf16[3,144,128]{2,1,0:T(8,128)(2,1)S(1)}, bf16[3,144,128]{2,1,0:T(8,128)(2,1)S(1)}, u32[]{:S(2)}, u32[]{:S(2)}) %collective-permute-start.7) | collective-permute-done | bytes 110624 | tf_op jit(solution)/shard_map/ppermute | solution.py:117
  58.3 0.0 collective-permute-done.8.refs_3_
  58.3 0.9 %unpack.3 = (bf16[1,576,256]{2,1,0:T(8,128)(2,1)}, bf16[1,576,256]{2,1,0:T(8,128)(2,1)}, bf16[1,576,256]{2,1,0:T(8,128)(2,1)}) custom-call(bf16[3,144,128]{2,1,0:T(8,128)(2,1)S(1)} %collective-permute-done.6.refs_0_, bf16[3,144,128]{2,1,0:T(8,128)(2,1)S(1)} %collective-permute-done.7.refs_1_, ...), custom_call_target="tpu_custom_call", output_to_operand_aliasing={{0}: (4, {}), {1}: (5, {}), {2}: (6, {})} | custom-call | tf_op jit(solution)/shard_map/unpack/pallas_call | solution.py:185
  (4 shorter events, 0.0 us)
Async XLA Ops:
  2.5 14.2 %collective-permute-start = (bf16[4,144,128]{2,1,0:T(8,128)(2,1)}, bf16[4,144,128]{2,1,0:T(8,128)(2,1)S(1)}, u32[]{:S(2)}, u32[]{:S(2)}) collective-permute-start(bf16[4,144,128]{2,1,0:T(8,128)(2,1)} %get-tuple-element.43), channel_id=1, source_target_pairs={{0,2},{1,3},{2,0},{3,1},{4,6},{5,7},{6,4},{7,5},{8,10},{9,11},{10,... | collective-permute-start | bytes 442376 | tf_op jit(solution)/shard_map/ppermute | solution.py:117
  6.6 13.7 %collective-permute-start.9 = (bf16[4,144,128]{2,1,0:T(8,128)(2,1)}, bf16[4,144,128]{2,1,0:T(8,128)(2,1)S(1)}, u32[]{:S(2)}, u32[]{:S(2)}) collective-permute-start(bf16[4,144,128]{2,1,0:T(8,128)(2,1)} %get-tuple-element.61), channel_id=1, source_target_pairs={{0,1},{2,3},{1,0},{3,2},{4,5},{6,7},{5,4},{7,6},{8,9},{10,11},{9,8... | collective-permute-start | bytes 442376 | tf_op jit(solution)/shard_map/ppermute | solution.py:117
  8.2 12.1 %collective-permute-start.10 = (bf16[4,144,128]{2,1,0:T(8,128)(2,1)}, bf16[4,144,128]{2,1,0:T(8,128)(2,1)S(1)}, u32[]{:S(2)}, u32[]{:S(2)}) collective-permute-start(bf16[4,144,128]{2,1,0:T(8,128)(2,1)} %get-tuple-element.63), channel_id=1, source_target_pairs={{0,3},{1,2},{3,0},{2,1},{4,7},{5,6},{7,4},{6,5},{8,11},{9,10},{11,... | collective-permute-start | bytes 442376 | tf_op jit(solution)/shard_map/ppermute | solution.py:117
  10.1 12.5 %collective-permute-start.1 = (bf16[4,144,128]{2,1,0:T(8,128)(2,1)}, bf16[4,144,128]{2,1,0:T(8,128)(2,1)S(1)}, u32[]{:S(2)}, u32[]{:S(2)}) collective-permute-start(bf16[4,144,128]{2,1,0:T(8,128)(2,1)} %get-tuple-element.51), channel_id=1, source_target_pairs={{0,1},{2,3},{1,0},{3,2},{4,5},{6,7},{5,4},{7,6},{8,9},{10,11},{9,8... | collective-permute-start | bytes 442376 | tf_op jit(solution)/shard_map/ppermute | solution.py:117
  11.1 5.6 %copy-start.4 = (s32[16]{0:T(128)S(1)}, s32[16]{0:T(128)}, u32[]{:S(2)}) copy-start(s32[16]{0:T(128)} %param.17) | copy-start | bytes 196
  11.1 5.7 %copy-start.3 = (bf16[4,144,128]{2,1,0:T(8,128)(2,1)S(1)}, bf16[4,144,128]{2,1,0:T(8,128)(2,1)}, u32[]{:S(2)}) copy-start(bf16[4,144,128]{2,1,0:T(8,128)(2,1)} %get-tuple-element.52) | copy-start | bytes 442372
  11.1 9.2 %copy-start.2 = (bf16[4,144,128]{2,1,0:T(8,128)(2,1)S(1)}, bf16[4,144,128]{2,1,0:T(8,128)(2,1)}, u32[]{:S(2)}) copy-start(bf16[4,144,128]{2,1,0:T(8,128)(2,1)} %get-tuple-element.53) | copy-start | bytes 442372
  11.1 9.3 %copy-start.1 = (bf16[4,144,128]{2,1,0:T(8,128)(2,1)S(1)}, bf16[4,144,128]{2,1,0:T(8,128)(2,1)}, u32[]{:S(2)}) copy-start(bf16[4,144,128]{2,1,0:T(8,128)(2,1)} %get-tuple-element.60.refs_0_) | copy-start | bytes 442372
  16.8 13.8 %collective-permute-start.2 = (bf16[4,144,128]{2,1,0:T(8,128)(2,1)S(1)}, bf16[4,144,128]{2,1,0:T(8,128)(2,1)S(1)}, u32[]{:S(2)}, u32[]{:S(2)}) collective-permute-start(bf16[4,144,128]{2,1,0:T(8,128)(2,1)S(1)} %copy-done.3), channel_id=1, source_target_pairs={{0,2},{1,3},{2,0},{3,1},{4,6},{5,7},{6,4},{7,5},{8,10},{9,11},{10,... | collective-permute-start | bytes 442376 | tf_op jit(solution)/shard_map/ppermute | solution.py:117
  20.3 10.3 %collective-permute-start.3 = (bf16[4,144,128]{2,1,0:T(8,128)(2,1)S(1)}, bf16[4,144,128]{2,1,0:T(8,128)(2,1)S(1)}, u32[]{:S(2)}, u32[]{:S(2)}) collective-permute-start(bf16[4,144,128]{2,1,0:T(8,128)(2,1)S(1)} %copy-done.2), channel_id=1, source_target_pairs={{0,3},{1,2},{3,0},{2,1},{4,7},{5,6},{7,4},{6,5},{8,11},{9,10},{11,... | collective-permute-start | bytes 442376 | tf_op jit(solution)/shard_map/ppermute | solution.py:117
  20.4 10.2 %copy-start = (bf16[4,144,128]{2,1,0:T(8,128)(2,1)S(1)}, bf16[4,144,128]{2,1,0:T(8,128)(2,1)}, u32[]{:S(2)}) copy-start(bf16[4,144,128]{2,1,0:T(8,128)(2,1)} %get-tuple-element.50.refs_0_) | copy-start | bytes 442372
  20.5 13.1 %collective-permute-start.11 = (bf16[3,4,144,128]{3,2,1,0:T(8,128)(2,1)S(1)}, bf16[3,4,144,128]{3,2,1,0:T(8,128)(2,1)S(1)}, u32[]{:S(2)}, u32[]{:S(2)}) collective-permute-start(bf16[3,4,144,128]{3,2,1,0:T(8,128)(2,1)S(1)} %get-tuple-element.64), channel_id=1, source_target_pairs={{4,8},{12,16},{20,24},{28,0},{8,4},{16,12},{24,20},{0,28},{5,9},{1... | collective-permute-start | bytes 1327112 | tf_op jit(solution)/shard_map/ppermute | solution.py:117
  21.1 12.6 %collective-permute-start.12 = (bf16[3,4,144,128]{3,2,1,0:T(8,128)(2,1)S(1)}, bf16[3,4,144,128]{3,2,1,0:T(8,128)(2,1)S(1)}, u32[]{:S(2)}, u32[]{:S(2)}) collective-permute-start(bf16[3,4,144,128]{3,2,1,0:T(8,128)(2,1)S(1)} %get-tuple-element.65), channel_id=1, source_target_pairs={{0,4},{8,12},{16,20},{24,28},{4,0},{12,8},{20,16},{28,24},{1,5},{9... | collective-permute-start | bytes 1327112 | tf_op jit(solution)/shard_map/ppermute | solution.py:117
  30.7 13.3 %collective-permute-start.4 = (bf16[3,4,144,128]{3,2,1,0:T(8,128)(2,1)S(1)}, bf16[3,4,144,128]{3,2,1,0:T(8,128)(2,1)S(1)}, u32[]{:S(2)}, u32[]{:S(2)}) collective-permute-start(bf16[3,4,144,128]{3,2,1,0:T(8,128)(2,1)S(1)} %get-tuple-element.54), channel_id=1, source_target_pairs={{4,8},{12,16},{20,24},{28,0},{8,4},{16,12},{24,20},{0,28},{5,9},{1... | collective-permute-start | bytes 1327112 | tf_op jit(solution)/shard_map/ppermute | solution.py:117
  31.2 12.8 %collective-permute-start.5 = (bf16[3,4,144,128]{3,2,1,0:T(8,128)(2,1)S(1)}, bf16[3,4,144,128]{3,2,1,0:T(8,128)(2,1)S(1)}, u32[]{:S(2)}, u32[]{:S(2)}) collective-permute-start(bf16[3,4,144,128]{3,2,1,0:T(8,128)(2,1)S(1)} %get-tuple-element.55), channel_id=1, source_target_pairs={{0,4},{8,12},{16,20},{24,28},{4,0},{12,8},{20,16},{28,24},{1,5},{9... | collective-permute-start | bytes 1327112 | tf_op jit(solution)/shard_map/ppermute | solution.py:117
  35.1 15.4 %collective-permute-start.13 = (bf16[3,144,128]{2,1,0:T(8,128)(2,1)S(1)}, bf16[3,144,128]{2,1,0:T(8,128)(2,1)S(1)}, u32[]{:S(2)}, u32[]{:S(2)}) collective-permute-start(bf16[3,144,128]{2,1,0:T(8,128)(2,1)S(1)} %get-tuple-element.66), channel_id=1, source_target_pairs={{0,3},{1,2},{3,0},{2,1},{4,7},{5,6},{7,4},{6,5},{8,11},{9,10},{11,... | collective-permute-start | bytes 331784 | tf_op jit(solution)/shard_map/ppermute | solution.py:117
  39.2 11.8 %collective-permute-start.14 = (bf16[3,144,128]{2,1,0:T(8,128)(2,1)S(1)}, bf16[3,144,128]{2,1,0:T(8,128)(2,1)S(1)}, u32[]{:S(2)}, u32[]{:S(2)}) collective-permute-start(bf16[3,144,128]{2,1,0:T(8,128)(2,1)S(1)} %get-tuple-element.67), channel_id=1, source_target_pairs={{0,2},{1,3},{2,0},{3,1},{4,6},{5,7},{6,4},{7,5},{8,10},{9,11},{10,... | collective-permute-start | bytes 331784 | tf_op jit(solution)/shard_map/ppermute | solution.py:117
  39.3 11.6 %collective-permute-start.15 = (bf16[3,144,128]{2,1,0:T(8,128)(2,1)S(1)}, bf16[3,144,128]{2,1,0:T(8,128)(2,1)S(1)}, u32[]{:S(2)}, u32[]{:S(2)}) collective-permute-start(bf16[3,144,128]{2,1,0:T(8,128)(2,1)S(1)} %get-tuple-element.69), channel_id=1, source_target_pairs={{0,1},{2,3},{1,0},{3,2},{4,5},{6,7},{5,4},{7,6},{8,9},{10,11},{9,8... | collective-permute-start | bytes 331784 | tf_op jit(solution)/shard_map/ppermute | solution.py:117
  45.5 6.8 %collective-permute-start.6 = (bf16[3,144,128]{2,1,0:T(8,128)(2,1)S(1)}, bf16[3,144,128]{2,1,0:T(8,128)(2,1)S(1)}, u32[]{:S(2)}, u32[]{:S(2)}) collective-permute-start(bf16[3,144,128]{2,1,0:T(8,128)(2,1)S(1)} %get-tuple-element.56), channel_id=1, source_target_pairs={{0,3},{1,2},{3,0},{2,1},{4,7},{5,6},{7,4},{6,5},{8,11},{9,10},{11,... | collective-permute-start | bytes 331784 | tf_op jit(solution)/shard_map/ppermute | solution.py:117
  48.6 9.7 %collective-permute-start.7 = (bf16[3,144,128]{2,1,0:T(8,128)(2,1)S(1)}, bf16[3,144,128]{2,1,0:T(8,128)(2,1)S(1)}, u32[]{:S(2)}, u32[]{:S(2)}) collective-permute-start(bf16[3,144,128]{2,1,0:T(8,128)(2,1)S(1)} %get-tuple-element.57), channel_id=1, source_target_pairs={{0,2},{1,3},{2,0},{3,1},{4,6},{5,7},{6,4},{7,5},{8,10},{9,11},{10,... | collective-permute-start | bytes 331784 | tf_op jit(solution)/shard_map/ppermute | solution.py:117
  50.5 7.9 %collective-permute-start.8 = (bf16[3,144,128]{2,1,0:T(8,128)(2,1)S(1)}, bf16[3,144,128]{2,1,0:T(8,128)(2,1)S(1)}, u32[]{:S(2)}, u32[]{:S(2)}) collective-permute-start(bf16[3,144,128]{2,1,0:T(8,128)(2,1)S(1)} %get-tuple-element.59), channel_id=1, source_target_pairs={{0,1},{2,3},{1,0},{3,2},{4,5},{6,7},{5,4},{7,6},{8,9},{10,11},{9,8... | collective-permute-start | bytes 331784 | tf_op jit(solution)/shard_map/ppermute | solution.py:117

commit v14 on v10

--- a/solution.py
+++ b/solution.py
@@ -343,7 +343,7 @@
     packed = [list(split(time, span, n, sharing)) for span in spans]
     own = [exchange(packed[0])]
     space = space_grads(*space_in)
-    packed[1][2:], own[0][2], space = gated(packed[1][2:], own[0][2], space)
+    packed[1][2:], space = gated(packed[1][2:], space)
     own.append(exchange(packed[1]))
     beside = [
         [neighbours(ends, start) for ends, start in zip(sides(blocks), (1, 0))] for blocks in own

time: 59.5 us -> 79.4 us (1.33)
  waiting for transfers between devices: 20.1 us -> 39.9 us
    ppermute x16, waiting for transfers between devices: 20.1 us -> 39.9 us  [swap(): lax.ppermute(block, axis, [(i, j) for i, j in pairs] + [(j, i) for i, j i...]
  transfers between devices with their start and end apart: 16 -> 16, of which waited for: 5 -> 5; matrix products, arithmetic and copies ran while one was open for 0% -> 0% of each run, Pallas kernels for 19% -> 14%
where the time goes in v14:
time: 79.4 us; the launch traced here: 79.2 us
  waiting for transfers between devices  39.9 us (50%)
  starting transfers between devices  24.1 us (30%)
  Pallas kernels  14.1 us (18%)
    ppermute x16, waiting for transfers between devices, swap(): lax.ppermute(block, axis, [(i, j) for i, j in pairs] + [(j, i) for i, j i...  39.9 us
    ppermute x16, starting transfers between devices, swap(): lax.ppermute(block, axis, [(i, j) for i, j in pairs] + [(j, i) for i, j i...  24.1 us
    pallas_call x1, Pallas kernels, space_grads(): pl.pallas_call(frame_kernel, out_shape=(shape, shape, shape), compiler_pa...  5.6 us
    pallas_call x2, Pallas kernels, split(): pl.pallas_call(functools.partial(split_kernel, sharing, rows, span), in_s...  3.76 us
    pallas_call x2, Pallas kernels, clip_grads(): pl.pallas_call(functools.partial(clip_kernel, window, heads), out_shape=[...  2.71 us
    pallas_call x2, Pallas kernels, join(): pl.pallas_call(functools.partial(join_kernel, sharing, span), in_specs=[p...  1.71 us
  transfers between devices with their start and end apart: 16, of which 5 were waited for; matrix products, arithmetic and copies ran while one was open for 0% of the time, Pallas kernels for 14%

profile of v14, /device:TPU:0, one launch (start us, length us, event | category | flops | bytes accessed | tf_op | source)
XLA Modules:
  0.0 79.2 jit_solution(15560481787604912721)
XLA Ops:
  0.6 1.9 %pack.2 = (bf16[4,144,128]{2,1,0:T(8,128)(2,1)}, bf16[4,144,128]{2,1,0:T(8,128)(2,1)}, bf16[4,144,128]{2,1,0:T(8,128)(2,1)}, bf16[4,144,128]{2,1,0:T(8,128)(2,1)}) custom-call(bf16[1,576,256]{2,1,0:T(8,128)(2,1)} %bitcast.18, bf16[1,576,256]{2,1,0:T(8,128)(2,1)} %bitcast.20, bf16[1,576,256]{2,1,0:T(8,128)(2,1)} %bitcast.22, bf16[1,576,256]{2,1,0:T(8,128)(2,1)} %bitcast.24), custom_call_target="tpu_custom_call" | custom-call | tf_op jit(solution)/shard_map/pack/pallas_call | solution.py:97
  2.5 3.1 %collective-permute-start = (bf16[4,144,128]{2,1,0:T(8,128)(2,1)}, bf16[4,144,128]{2,1,0:T(8,128)(2,1)S(1)}, u32[]{:S(2)}, u32[]{:S(2)}) collective-permute-start(bf16[4,144,128]{2,1,0:T(8,128)(2,1)} %get-tuple-element.49), channel_id=1, source_target_pairs={{0,1},{2,3},{1,0},{3,2},{4,5},{6,7},{5,4},{7,6},{8,9},{10,11},{9,8... | collective-permute-start | bytes 442376 | tf_op jit(solution)/shard_map/ppermute | solution.py:117
  5.6 1.9 %pack.3 = (bf16[4,144,128]{2,1,0:T(8,128)(2,1)}, bf16[4,144,128]{2,1,0:T(8,128)(2,1)}, bf16[4,144,128]{2,1,0:T(8,128)(2,1)}, bf16[4,144,128]{2,1,0:T(8,128)(2,1)}) custom-call(bf16[1,576,256]{2,1,0:T(8,128)(2,1)} %bitcast.19, bf16[1,576,256]{2,1,0:T(8,128)(2,1)} %bitcast.21, bf16[1,576,256]{2,1,0:T(8,128)(2,1)} %bitcast.23, bf16[1,576,256]{2,1,0:T(8,128)(2,1)} %bitcast.25), custom_call_target="tpu_custom_call" | custom-call | tf_op jit(solution)/shard_map/pack/pallas_call | solution.py:97
  7.5 0.1 collective-permute-start.8
  7.6 0.0 copy-start.3
  7.6 0.0 copy-start.5
  7.6 0.0 copy-start.4
  7.6 0.0 copy-start.2
  7.6 0.0 copy-start.1
  7.6 5.6 %space.1 = (bf16[1,576,256]{2,1,0:T(8,128)(2,1)}, bf16[1,576,256]{2,1,0:T(8,128)(2,1)}, bf16[1,576,256]{2,1,0:T(8,128)(2,1)}) custom-call(bf16[1,576,256]{2,1,0:T(8,128)(2,1)} %bitcast.29, bf16[1,576,256]{2,1,0:T(8,128)(2,1)} %bitcast.30, bf16[1,576,256]{2,1,0:T(8,128)(2,1)} %bitcast.31, bf16[1,576,256]{2,1,0:T(8,128)(2,1)} %bitcast.32), custom_call_target="tpu_custom_call" | custom-call | flops 1610612736 | bytes 2064384 | tf_op jit(solution)/shard_map/space/pallas_call | solution.py:58
  13.2 0.0 copy-done.3
  13.2 3.0 %collective-permute-start.1 = (bf16[4,144,128]{2,1,0:T(8,128)(2,1)S(1)}, bf16[4,144,128]{2,1,0:T(8,128)(2,1)S(1)}, u32[]{:S(2)}, u32[]{:S(2)}) collective-permute-start(bf16[4,144,128]{2,1,0:T(8,128)(2,1)S(1)} %copy-done.3), channel_id=1, source_target_pairs={{0,2},{1,3},{2,0},{3,1},{4,6},{5,7},{6,4},{7,5},{8,10},{9,11},{10,... | collective-permute-start | bytes 442376 | tf_op jit(solution)/shard_map/ppermute | solution.py:117
  16.2 0.0 copy-done.5
  16.2 0.0 copy-start.6
  16.2 0.1 collective-permute-start.9
  16.3 0.0 copy-done.4
  16.3 3.9 %collective-permute-start.10 = (bf16[4,144,128]{2,1,0:T(8,128)(2,1)S(1)}, bf16[4,144,128]{2,1,0:T(8,128)(2,1)S(1)}, u32[]{:S(2)}, u32[]{:S(2)}) collective-permute-start(bf16[4,144,128]{2,1,0:T(8,128)(2,1)S(1)} %copy-done.4), channel_id=1, source_target_pairs={{0,3},{1,2},{3,0},{2,1},{4,7},{5,6},{7,4},{6,5},{8,11},{9,10},{11,... | collective-permute-start | bytes 442376 | tf_op jit(solution)/shard_map/ppermute | solution.py:117
  20.2 0.0 copy-done.6
  20.2 0.1 select_reduce_fusion.2
  20.3 0.0 collective-permute-done.8.refs_1_
  20.3 0.0 copy-done.2
  20.3 0.1 collective-permute-start.2
  20.4 16.2 %collective-permute-done.9.refs_2_ = bf16[4,144,128]{2,1,0:T(8,128)(2,1)S(1)} collective-permute-done((bf16[4,144,128]{2,1,0:T(8,128)(2,1)S(1)}, bf16[4,144,128]{2,1,0:T(8,128)(2,1)S(1)}, u32[]{:S(2)}, u32[]{:S(2)}) %collective-permute-start.9) | collective-permute-done | bytes 147488 | tf_op jit(solution)/shard_map/ppermute | solution.py:117
  36.5 0.0 collective-permute-done.10.refs_3_
  36.5 0.0 copy-done.1
  36.5 0.0 copy-start
  36.5 0.1 sides.3
  36.7 0.1 collective-permute-start.11
  36.8 1.6 %collective-permute-start.12 = (bf16[3,4,144,128]{3,2,1,0:T(8,128)(2,1)S(1)}, bf16[3,4,144,128]{3,2,1,0:T(8,128)(2,1)S(1)}, u32[]{:S(2)}, u32[]{:S(2)}) collective-permute-start(bf16[3,4,144,128]{3,2,1,0:T(8,128)(2,1)S(1)} %get-tuple-element.63), channel_id=1, source_target_pairs={{0,4},{8,12},{16,20},{24,28},{4,0},{12,8},{20,16},{28,24},{1,5},{9... | collective-permute-start | bytes 1327112 | tf_op jit(solution)/shard_map/ppermute | solution.py:117
  38.4 0.2 select_reduce_fusion.1
  38.5 0.0 collective-permute-done.refs_1_
  38.5 0.0 collective-permute-done.1.refs_2_
  38.6 0.0 collective-permute-done.2.refs_3_
  38.6 0.0 copy-done
  38.6 0.1 sides.2
  38.7 1.1 %collective-permute-start.3 = (bf16[3,4,144,128]{3,2,1,0:T(8,128)(2,1)S(1)}, bf16[3,4,144,128]{3,2,1,0:T(8,128)(2,1)S(1)}, u32[]{:S(2)}, u32[]{:S(2)}) collective-permute-start(bf16[3,4,144,128]{3,2,1,0:T(8,128)(2,1)S(1)} %get-tuple-element.52), channel_id=1, source_target_pairs={{4,8},{12,16},{20,24},{28,0},{8,4},{16,12},{24,20},{0,28},{5,9},{1... | collective-permute-start | bytes 1327112 | tf_op jit(solution)/shard_map/ppermute | solution.py:117
  39.8 0.6 collective-permute-start.4
  40.4 9.6 %collective-permute-done.11.refs_4_ = bf16[3,4,144,128]{3,2,1,0:T(8,128)(2,1)S(1)} collective-permute-done((bf16[3,4,144,128]{3,2,1,0:T(8,128)(2,1)S(1)}, bf16[3,4,144,128]{3,2,1,0:T(8,128)(2,1)S(1)}, u32[]{:S(2)}, u32[]{:S(2)}) %collective-permute-start.11) | collective-permute-done | bytes 442400 | tf_op jit(solution)/shard_map/ppermute | solution.py:117
  50.0 0.0 collective-permute-done.12.refs_5_
  50.0 1.4 %clips.3 = (bf16[3,144,128]{2,1,0:T(8,128)(2,1)S(1)}, bf16[3,144,128]{2,1,0:T(8,128)(2,1)S(1)}, bf16[3,144,128]{2,1,0:T(8,128)(2,1)S(1)}, bf16[3,144,128]{2,1,0:T(8,128)(2,1)S(1)}) custom-call(s32[2,10]{1,0:T(2,128)S(1)} %pad_add_fusion.given_bounds, bf16[4,144,128]{2,1,0:T(8,128)(2,1)S(1)} %copy-done.1, ...), custom_call_target="tpu_custom_call" | custom-call | flops 589824000 | bytes 1474560 | tf_op jit(solution)/shard_map/clips/pallas_call | solution.py:289
  51.4 2.4 %collective-permute-start.13 = (bf16[3,144,128]{2,1,0:T(8,128)(2,1)S(1)}, bf16[3,144,128]{2,1,0:T(8,128)(2,1)S(1)}, u32[]{:S(2)}, u32[]{:S(2)}) collective-permute-start(bf16[3,144,128]{2,1,0:T(8,128)(2,1)S(1)} %get-tuple-element.64), channel_id=1, source_target_pairs={{0,3},{1,2},{3,0},{2,1},{4,7},{5,6},{7,4},{6,5},{8,11},{9,10},{11,... | collective-permute-start | bytes 331784 | tf_op jit(solution)/shard_map/ppermute | solution.py:117
  53.8 5.7 %collective-permute-done.3.refs_4_ = bf16[3,4,144,128]{3,2,1,0:T(8,128)(2,1)S(1)} collective-permute-done((bf16[3,4,144,128]{3,2,1,0:T(8,128)(2,1)S(1)}, bf16[3,4,144,128]{3,2,1,0:T(8,128)(2,1)S(1)}, u32[]{:S(2)}, u32[]{:S(2)}) %collective-permute-start.3) | collective-permute-done | bytes 442400 | tf_op jit(solution)/shard_map/ppermute | solution.py:117
  59.5 0.0 collective-permute-done.4.refs_5_
  59.5 1.4 %clips.2 = (bf16[3,144,128]{2,1,0:T(8,128)(2,1)S(1)}, bf16[3,144,128]{2,1,0:T(8,128)(2,1)S(1)}, bf16[3,144,128]{2,1,0:T(8,128)(2,1)S(1)}, bf16[3,144,128]{2,1,0:T(8,128)(2,1)S(1)}) custom-call(s32[2,10]{1,0:T(2,128)S(1)} %pad_add_fusion.given_bounds, bf16[4,144,128]{2,1,0:T(8,128)(2,1)S(1)} %copy-done, ...), custom_call_target="tpu_custom_call" | custom-call | flops 589824000 | bytes 1474560 | tf_op jit(solution)/shard_map/clips/pallas_call | solution.py:289
  60.8 2.4 %collective-permute-start.5 = (bf16[3,144,128]{2,1,0:T(8,128)(2,1)S(1)}, bf16[3,144,128]{2,1,0:T(8,128)(2,1)S(1)}, u32[]{:S(2)}, u32[]{:S(2)}) collective-permute-start(bf16[3,144,128]{2,1,0:T(8,128)(2,1)S(1)} %get-tuple-element.54), channel_id=1, source_target_pairs={{0,3},{1,2},{3,0},{2,1},{4,7},{5,6},{7,4},{6,5},{8,11},{9,10},{11,... | collective-permute-start | bytes 331784 | tf_op jit(solution)/shard_map/ppermute | solution.py:117
  63.3 2.8 %collective-permute-start.14 = (bf16[3,144,128]{2,1,0:T(8,128)(2,1)S(1)}, bf16[3,144,128]{2,1,0:T(8,128)(2,1)S(1)}, u32[]{:S(2)}, u32[]{:S(2)}) collective-permute-start(bf16[3,144,128]{2,1,0:T(8,128)(2,1)S(1)} %get-tuple-element.65), channel_id=1, source_target_pairs={{0,2},{1,3},{2,0},{3,1},{4,6},{5,7},{6,4},{7,5},{8,10},{9,11},{10,... | collective-permute-start | bytes 331784 | tf_op jit(solution)/shard_map/ppermute | solution.py:117
  66.1 0.0 collective-permute-start.15
  66.1 2.9 %collective-permute-start.6 = (bf16[3,144,128]{2,1,0:T(8,128)(2,1)S(1)}, bf16[3,144,128]{2,1,0:T(8,128)(2,1)S(1)}, u32[]{:S(2)}, u32[]{:S(2)}) collective-permute-start(bf16[3,144,128]{2,1,0:T(8,128)(2,1)S(1)} %get-tuple-element.55), channel_id=1, source_target_pairs={{0,2},{1,3},{2,0},{3,1},{4,6},{5,7},{6,4},{7,5},{8,10},{9,11},{10,... | collective-permute-start | bytes 331784 | tf_op jit(solution)/shard_map/ppermute | solution.py:117
  69.0 0.0 collective-permute-done.13.refs_0_
  69.0 0.0 collective-permute-start.7
  69.0 8.1 %collective-permute-done.14.refs_1_ = bf16[3,144,128]{2,1,0:T(8,128)(2,1)S(1)} collective-permute-done((bf16[3,144,128]{2,1,0:T(8,128)(2,1)S(1)}, bf16[3,144,128]{2,1,0:T(8,128)(2,1)S(1)}, u32[]{:S(2)}, u32[]{:S(2)}) %collective-permute-start.14) | collective-permute-done | bytes 110624 | tf_op jit(solution)/shard_map/ppermute | solution.py:117
  77.1 0.0 collective-permute-done.15.refs_3_
  77.1 0.9 %unpack.2 = (bf16[1,576,256]{2,1,0:T(8,128)(2,1)}, bf16[1,576,256]{2,1,0:T(8,128)(2,1)}, bf16[1,576,256]{2,1,0:T(8,128)(2,1)}) custom-call(bf16[3,144,128]{2,1,0:T(8,128)(2,1)S(1)} %collective-permute-done.13.refs_0_, bf16[3,144,128]{2,1,0:T(8,128)(2,1)S(1)} %collective-permute-done.14.refs_1_, bf16[3,144,128]{2,1,0:T(8,128)(2,1)S(1)} %get-tuple-element.66.refs_2_, ...), custom_call_target="tpu_custom_call" | custom-call | tf_op jit(solution)/shard_map/unpack/pallas_call | solution.py:185
  78.0 0.0 collective-permute-done.5.refs_0_
  78.0 0.3 collective-permute-done.6.refs_1_
  78.3 0.0 collective-permute-done.7.refs_3_
  78.3 0.9 %unpack.3 = (bf16[1,576,256]{2,1,0:T(8,128)(2,1)}, bf16[1,576,256]{2,1,0:T(8,128)(2,1)}, bf16[1,576,256]{2,1,0:T(8,128)(2,1)}) custom-call(bf16[3,144,128]{2,1,0:T(8,128)(2,1)S(1)} %collective-permute-done.5.refs_0_, bf16[3,144,128]{2,1,0:T(8,128)(2,1)S(1)} %collective-permute-done.6.refs_1_, ...), custom_call_target="tpu_custom_call", output_to_operand_aliasing={{0}: (4, {}), {1}: (5, {}), {2}: (6, {})} | custom-call | tf_op jit(solution)/shard_map/unpack/pallas_call | solution.py:185
  (4 shorter events, 0.0 us)
Async XLA Ops:
  2.5 36.0 %collective-permute-start = (bf16[4,144,128]{2,1,0:T(8,128)(2,1)}, bf16[4,144,128]{2,1,0:T(8,128)(2,1)S(1)}, u32[]{:S(2)}, u32[]{:S(2)}) collective-permute-start(bf16[4,144,128]{2,1,0:T(8,128)(2,1)} %get-tuple-element.49), channel_id=1, source_target_pairs={{0,1},{2,3},{1,0},{3,2},{4,5},{6,7},{5,4},{7,6},{8,9},{10,11},{9,8... | collective-permute-start | bytes 442376 | tf_op jit(solution)/shard_map/ppermute | solution.py:117
  7.5 12.8 %collective-permute-start.8 = (bf16[4,144,128]{2,1,0:T(8,128)(2,1)}, bf16[4,144,128]{2,1,0:T(8,128)(2,1)S(1)}, u32[]{:S(2)}, u32[]{:S(2)}) collective-permute-start(bf16[4,144,128]{2,1,0:T(8,128)(2,1)} %get-tuple-element.59), channel_id=1, source_target_pairs={{0,1},{2,3},{1,0},{3,2},{4,5},{6,7},{5,4},{7,6},{8,9},{10,11},{9,8... | collective-permute-start | bytes 442376 | tf_op jit(solution)/shard_map/ppermute | solution.py:117
  7.6 5.6 %copy-start.3 = (bf16[4,144,128]{2,1,0:T(8,128)(2,1)S(1)}, bf16[4,144,128]{2,1,0:T(8,128)(2,1)}, u32[]{:S(2)}) copy-start(bf16[4,144,128]{2,1,0:T(8,128)(2,1)} %get-tuple-element.50) | copy-start | bytes 442372
  7.6 8.6 %copy-start.5 = (bf16[4,144,128]{2,1,0:T(8,128)(2,1)S(1)}, bf16[4,144,128]{2,1,0:T(8,128)(2,1)}, u32[]{:S(2)}) copy-start(bf16[4,144,128]{2,1,0:T(8,128)(2,1)} %get-tuple-element.60) | copy-start | bytes 442372
  7.6 8.7 %copy-start.4 = (bf16[4,144,128]{2,1,0:T(8,128)(2,1)S(1)}, bf16[4,144,128]{2,1,0:T(8,128)(2,1)}, u32[]{:S(2)}) copy-start(bf16[4,144,128]{2,1,0:T(8,128)(2,1)} %get-tuple-element.61) | copy-start | bytes 442372
  7.6 12.7 %copy-start.2 = (bf16[4,144,128]{2,1,0:T(8,128)(2,1)S(1)}, bf16[4,144,128]{2,1,0:T(8,128)(2,1)}, u32[]{:S(2)}) copy-start(bf16[4,144,128]{2,1,0:T(8,128)(2,1)} %get-tuple-element.51) | copy-start | bytes 442372
  7.6 28.9 %copy-start.1 = (bf16[4,144,128]{2,1,0:T(8,128)(2,1)S(1)}, bf16[4,144,128]{2,1,0:T(8,128)(2,1)}, u32[]{:S(2)}) copy-start(bf16[4,144,128]{2,1,0:T(8,128)(2,1)} %get-tuple-element.58.refs_0_) | copy-start | bytes 442372
  13.2 25.3 %collective-permute-start.1 = (bf16[4,144,128]{2,1,0:T(8,128)(2,1)S(1)}, bf16[4,144,128]{2,1,0:T(8,128)(2,1)S(1)}, u32[]{:S(2)}, u32[]{:S(2)}) collective-permute-start(bf16[4,144,128]{2,1,0:T(8,128)(2,1)S(1)} %copy-done.3), channel_id=1, source_target_pairs={{0,2},{1,3},{2,0},{3,1},{4,6},{5,7},{6,4},{7,5},{8,10},{9,11},{10,... | collective-permute-start | bytes 442376 | tf_op jit(solution)/shard_map/ppermute | solution.py:117
  16.2 3.9 %copy-start.6 = (s32[16]{0:T(128)S(1)}, s32[16]{0:T(128)}, u32[]{:S(2)}) copy-start(s32[16]{0:T(128)} %param.17) | copy-start | bytes 196
  16.2 20.3 %collective-permute-start.9 = (bf16[4,144,128]{2,1,0:T(8,128)(2,1)S(1)}, bf16[4,144,128]{2,1,0:T(8,128)(2,1)S(1)}, u32[]{:S(2)}, u32[]{:S(2)}) collective-permute-start(bf16[4,144,128]{2,1,0:T(8,128)(2,1)S(1)} %copy-done.5), channel_id=1, source_target_pairs={{0,2},{1,3},{2,0},{3,1},{4,6},{5,7},{6,4},{7,5},{8,10},{9,11},{10,... | collective-permute-start | bytes 442376 | tf_op jit(solution)/shard_map/ppermute | solution.py:117
  16.3 20.2 %collective-permute-start.10 = (bf16[4,144,128]{2,1,0:T(8,128)(2,1)S(1)}, bf16[4,144,128]{2,1,0:T(8,128)(2,1)S(1)}, u32[]{:S(2)}, u32[]{:S(2)}) collective-permute-start(bf16[4,144,128]{2,1,0:T(8,128)(2,1)S(1)} %copy-done.4), channel_id=1, source_target_pairs={{0,3},{1,2},{3,0},{2,1},{4,7},{5,6},{7,4},{6,5},{8,11},{9,10},{11,... | collective-permute-start | bytes 442376 | tf_op jit(solution)/shard_map/ppermute | solution.py:117
  20.3 18.3 %collective-permute-start.2 = (bf16[4,144,128]{2,1,0:T(8,128)(2,1)S(1)}, bf16[4,144,128]{2,1,0:T(8,128)(2,1)S(1)}, u32[]{:S(2)}, u32[]{:S(2)}) collective-permute-start(bf16[4,144,128]{2,1,0:T(8,128)(2,1)S(1)} %copy-done.2), channel_id=1, source_target_pairs={{0,3},{1,2},{3,0},{2,1},{4,7},{5,6},{7,4},{6,5},{8,11},{9,10},{11,... | collective-permute-start | bytes 442376 | tf_op jit(solution)/shard_map/ppermute | solution.py:117
  36.5 2.0 %copy-start = (bf16[4,144,128]{2,1,0:T(8,128)(2,1)S(1)}, bf16[4,144,128]{2,1,0:T(8,128)(2,1)}, u32[]{:S(2)}) copy-start(bf16[4,144,128]{2,1,0:T(8,128)(2,1)} %get-tuple-element.48.refs_0_) | copy-start | bytes 442372
  36.7 13.3 %collective-permute-start.11 = (bf16[3,4,144,128]{3,2,1,0:T(8,128)(2,1)S(1)}, bf16[3,4,144,128]{3,2,1,0:T(8,128)(2,1)S(1)}, u32[]{:S(2)}, u32[]{:S(2)}) collective-permute-start(bf16[3,4,144,128]{3,2,1,0:T(8,128)(2,1)S(1)} %get-tuple-element.62), channel_id=1, source_target_pairs={{4,8},{12,16},{20,24},{28,0},{8,4},{16,12},{24,20},{0,28},{5,9},{1... | collective-permute-start | bytes 1327112 | tf_op jit(solution)/shard_map/ppermute | solution.py:117
  36.8 13.2 %collective-permute-start.12 = (bf16[3,4,144,128]{3,2,1,0:T(8,128)(2,1)S(1)}, bf16[3,4,144,128]{3,2,1,0:T(8,128)(2,1)S(1)}, u32[]{:S(2)}, u32[]{:S(2)}) collective-permute-start(bf16[3,4,144,128]{3,2,1,0:T(8,128)(2,1)S(1)} %get-tuple-element.63), channel_id=1, source_target_pairs={{0,4},{8,12},{16,20},{24,28},{4,0},{12,8},{20,16},{28,24},{1,5},{9... | collective-permute-start | bytes 1327112 | tf_op jit(solution)/shard_map/ppermute | solution.py:117
  38.7 20.7 %collective-permute-start.3 = (bf16[3,4,144,128]{3,2,1,0:T(8,128)(2,1)S(1)}, bf16[3,4,144,128]{3,2,1,0:T(8,128)(2,1)S(1)}, u32[]{:S(2)}, u32[]{:S(2)}) collective-permute-start(bf16[3,4,144,128]{3,2,1,0:T(8,128)(2,1)S(1)} %get-tuple-element.52), channel_id=1, source_target_pairs={{4,8},{12,16},{20,24},{28,0},{8,4},{16,12},{24,20},{0,28},{5,9},{1... | collective-permute-start | bytes 1327112 | tf_op jit(solution)/shard_map/ppermute | solution.py:117
  39.8 19.7 %collective-permute-start.4 = (bf16[3,4,144,128]{3,2,1,0:T(8,128)(2,1)S(1)}, bf16[3,4,144,128]{3,2,1,0:T(8,128)(2,1)S(1)}, u32[]{:S(2)}, u32[]{:S(2)}) collective-permute-start(bf16[3,4,144,128]{3,2,1,0:T(8,128)(2,1)S(1)} %get-tuple-element.53), channel_id=1, source_target_pairs={{0,4},{8,12},{16,20},{24,28},{4,0},{12,8},{20,16},{28,24},{1,5},{9... | collective-permute-start | bytes 1327112 | tf_op jit(solution)/shard_map/ppermute | solution.py:117
  51.4 17.6 %collective-permute-start.13 = (bf16[3,144,128]{2,1,0:T(8,128)(2,1)S(1)}, bf16[3,144,128]{2,1,0:T(8,128)(2,1)S(1)}, u32[]{:S(2)}, u32[]{:S(2)}) collective-permute-start(bf16[3,144,128]{2,1,0:T(8,128)(2,1)S(1)} %get-tuple-element.64), channel_id=1, source_target_pairs={{0,3},{1,2},{3,0},{2,1},{4,7},{5,6},{7,4},{6,5},{8,11},{9,10},{11,... | collective-permute-start | bytes 331784 | tf_op jit(solution)/shard_map/ppermute | solution.py:117
  60.8 17.1 %collective-permute-start.5 = (bf16[3,144,128]{2,1,0:T(8,128)(2,1)S(1)}, bf16[3,144,128]{2,1,0:T(8,128)(2,1)S(1)}, u32[]{:S(2)}, u32[]{:S(2)}) collective-permute-start(bf16[3,144,128]{2,1,0:T(8,128)(2,1)S(1)} %get-tuple-element.54), channel_id=1, source_target_pairs={{0,3},{1,2},{3,0},{2,1},{4,7},{5,6},{7,4},{6,5},{8,11},{9,10},{11,... | collective-permute-start | bytes 331784 | tf_op jit(solution)/shard_map/ppermute | solution.py:117
  63.3 13.8 %collective-permute-start.14 = (bf16[3,144,128]{2,1,0:T(8,128)(2,1)S(1)}, bf16[3,144,128]{2,1,0:T(8,128)(2,1)S(1)}, u32[]{:S(2)}, u32[]{:S(2)}) collective-permute-start(bf16[3,144,128]{2,1,0:T(8,128)(2,1)S(1)} %get-tuple-element.65), channel_id=1, source_target_pairs={{0,2},{1,3},{2,0},{3,1},{4,6},{5,7},{6,4},{7,5},{8,10},{9,11},{10,... | collective-permute-start | bytes 331784 | tf_op jit(solution)/shard_map/ppermute | solution.py:117
  66.1 11.0 %collective-permute-start.15 = (bf16[3,144,128]{2,1,0:T(8,128)(2,1)S(1)}, bf16[3,144,128]{2,1,0:T(8,128)(2,1)S(1)}, u32[]{:S(2)}, u32[]{:S(2)}) collective-permute-start(bf16[3,144,128]{2,1,0:T(8,128)(2,1)S(1)} %get-tuple-element.67), channel_id=1, source_target_pairs={{0,1},{2,3},{1,0},{3,2},{4,5},{6,7},{5,4},{7,6},{8,9},{10,11},{9,8... | collective-permute-start | bytes 331784 | tf_op jit(solution)/shard_map/ppermute | solution.py:117
  66.1 12.2 %collective-permute-start.6 = (bf16[3,144,128]{2,1,0:T(8,128)(2,1)S(1)}, bf16[3,144,128]{2,1,0:T(8,128)(2,1)S(1)}, u32[]{:S(2)}, u32[]{:S(2)}) collective-permute-start(bf16[3,144,128]{2,1,0:T(8,128)(2,1)S(1)} %get-tuple-element.55), channel_id=1, source_target_pairs={{0,2},{1,3},{2,0},{3,1},{4,6},{5,7},{6,4},{7,5},{8,10},{9,11},{10,... | collective-permute-start | bytes 331784 | tf_op jit(solution)/shard_map/ppermute | solution.py:117
  69.0 9.3 %collective-permute-start.7 = (bf16[3,144,128]{2,1,0:T(8,128)(2,1)S(1)}, bf16[3,144,128]{2,1,0:T(8,128)(2,1)S(1)}, u32[]{:S(2)}, u32[]{:S(2)}) collective-permute-start(bf16[3,144,128]{2,1,0:T(8,128)(2,1)S(1)} %get-tuple-element.57), channel_id=1, source_target_pairs={{0,1},{2,3},{1,0},{3,2},{4,5},{6,7},{5,4},{7,6},{8,9},{10,11},{9,8... | collective-permute-start | bytes 331784 | tf_op jit(solution)/shard_map/ppermute | solution.py:117
